TPU v7x, 32 devices: a whole 2x2x4 slice. The times are simulated.
32 devices in a mesh: dp: 4 (over z), fsdp: 8 (over y, x, core).
Axes of the slice: x: 2, y: 2, z: 4, core: 2. Of those that a mesh axis runs over, the one named last changes fastest.
Arguments:
- tokens: bfloat16 [12288, 2048], P(('dp', 'fsdp')), may hold values from -6 to 6
- lengths: int32 [32], P(('dp', 'fsdp')), may hold values from 1 to 384, 6144 in all
- cotangent: bfloat16 [12288, 2048], P(('dp', 'fsdp')), may hold values from -6 to 6
- attention_gain: bfloat16 [2048], P(('dp', 'fsdp')), may hold values from 0.099609375 to 1.8984375
- query_weight: bfloat16 [2048, 2048], P(('dp', 'fsdp')), may hold values from -0.125 to 0.125
- key_matrix: bfloat16 [2048, 1024], P(('dp', 'fsdp')), may hold values from -0.125 to 0.125
- value_matrix: bfloat16 [2048, 1024], P(('dp', 'fsdp')), may hold values from -0.125 to 0.125
- head_gate_weight: bfloat16 [2048, 16], P(('dp', 'fsdp')), may hold values from -0.125 to 0.125
- output_weight: bfloat16 [2048, 2048], P(('dp', 'fsdp')), may hold values from -2 to 2
- query_key_gain: bfloat16 [2, 128], P(None, ('dp', 'fsdp')), may hold values from 0.099609375 to 1.8984375
- feedforward_gain: bfloat16 [2048], P(('dp', 'fsdp')), may hold values from 0.099609375 to 1.8984375
- gate_weight: bfloat16 [2048, 6144], P(('dp', 'fsdp')), may hold values from -0.125 to 0.125
- up_weight: bfloat16 [2048, 6144], P(('dp', 'fsdp')), may hold values from -0.125 to 0.125
- down_weight: bfloat16 [6144, 2048], P(('dp', 'fsdp')), may hold values from -0.078125 to 0.078125
Outputs:
- layer_output: bfloat16 [12288, 2048], P(('dp', 'fsdp'))
- tokens_grad: bfloat16 [12288, 2048], P(('dp', 'fsdp'))
- attention_gain_grad: float32 [2048], P(('dp', 'fsdp'))
- query_grad: float32 [2048, 2048], P(('dp', 'fsdp'))
- key_grad: float32 [2048, 1024], P(('dp', 'fsdp'))
- value_grad: float32 [2048, 1024], P(('dp', 'fsdp'))
- head_gate_grad: float32 [2048, 16], P(('dp', 'fsdp'))
- output_grad: float32 [2048, 2048], P(('dp', 'fsdp'))
- query_key_gain_grad: float32 [2, 128], P(None, ('dp', 'fsdp'))
- feedforward_gain_grad: float32 [2048], P(('dp', 'fsdp'))
- gate_grad: float32 [2048, 6144], P(('dp', 'fsdp'))
- up_grad: float32 [2048, 6144], P(('dp', 'fsdp'))
- down_grad: float32 [6144, 2048], P(('dp', 'fsdp'))
Inputs may be any that keep to these rules, and one draw needn't show every extreme that they name: `lengths`: one length a sequence; they sum to 6144 and the longest is exactly 384.
All inputs are finite; a program needn't handle non-finite values. No bound on the sum of `lengths` on one device may be relied on, other than what follows from the above.
Results may differ from a plain program's by a relative error of at most 0.015.
Values may be sent and summed in bfloat16 or wider, within the bound.
A program may use at most 448 MiB of HBM per device.

v0:
```python
import jax
import jax.numpy as jnp
from jax import lax
from jax.experimental import pallas as pl
from jax.experimental.pallas import tpu as pltpu
from jax.sharding import PartitionSpec as P

EPSILON = 1e-06
ROPE_BASE = 1000000.0
TEAM = 8
ALL = ("dp", "fsdp")
F32 = jnp.float32
BF16 = jnp.bfloat16
TILE = 128
ORDER_BACK = (3, 1, 2, 0)
ORDER_LATE = (0, 1, 3, 2)
ANY = pl.BlockSpec(memory_space=pl.ANY)
VMEM = pl.BlockSpec(memory_space=pltpu.VMEM)
SMEM = pl.BlockSpec(memory_space=pltpu.SMEM)


def product(left, right):
    return jnp.dot(left, right, preferred_element_type=F32)


def product_nt(left, right):
    return lax.dot_general(left, right, (((1,), (1,)), ((), ())), preferred_element_type=F32)


def product_tn(left, right):
    return lax.dot_general(left, right, (((0,), (0,)), ((), ())), preferred_element_type=F32)


def world():
    return lax.axis_size(ALL)


def member():
    return lax.axis_index(ALL) % TEAM


def teams():
    return [[first + t for t in range(TEAM)] for first in range(0, world(), TEAM)]


def lines():
    return [list(range(t, world(), TEAM)) for t in range(TEAM)]


def permute(array, pairs):
    return lax.ppermute(
        array, ALL, [(team[a], team[b]) for team in teams() for a, b in pairs]
    )


def swap(array, bits):
    return permute(array, [(i, i ^ bits) for i in range(TEAM)])


def exchange(blocks):
    if lax.axis_size("fsdp") == TEAM:
        return lax.all_to_all(blocks, "fsdp", 0, 0, tiled=True)
    return lax.all_to_all(blocks, ALL, 0, 0, tiled=True, axis_index_groups=teams())


def line_gather(shard):
    if lax.axis_size("fsdp") == TEAM:
        return lax.all_gather(shard, "dp", axis=0, tiled=True)
    return lax.all_gather(shard, ALL, axis=0, tiled=True, axis_index_groups=lines())


def line_sum(array):
    if lax.axis_size("fsdp") == TEAM:
        return lax.psum_scatter(array, "dp", scatter_dimension=0, tiled=True)
    return lax.psum_scatter(array, ALL, scatter_dimension=0, tiled=True, axis_index_groups=lines())


class TeamGather:
    def __init__(self, own):
        self.own = own
        self.a1 = swap(own, 1)
        self.a2 = swap(own, 2)
        self.a4 = swap(own, 4)

    def blocks(self, tick=None):
        a2, a4 = self.a2, self.a4
        if tick is not None:
            a2, a4 = hold([a2, a4], tick)
        half = self.own.shape[0] // 2
        a6 = jnp.concatenate([swap(a4[:half], 2), swap(a2[half:], 4)], axis=0)
        return [self.own, self.a1, a2, swap(a2, 1), a4, swap(a4, 1), a6, swap(a6, 1)]


def team_gather(own):
    return TeamGather(own).blocks()


class TeamSum:
    def add(self, pair, even, odd):
        half = even.shape[0] // 2
        total = even.astype(F32) + swap(odd, 1).astype(F32)
        if pair == 3:
            self.low6 = total.astype(BF16)
            self.u4 = swap(self.low6[:half], 2)
            self.u2 = swap(self.low6[half:], 4)
        elif pair == 1:
            self.s2_low = total[half:]
            self.x_top = swap(total[:half].astype(BF16), 2)
        elif pair == 2:
            self.s4_top = total[:half]
            self.y_low = swap(total[half:].astype(BF16), 4)
        else:
            self.s0 = total

    def total(self):
        x_low = swap((self.s2_low + self.u2.astype(F32)).astype(BF16), 2).astype(F32)
        y_top = swap((self.s4_top + self.u4.astype(F32)).astype(BF16), 4).astype(F32)
        top = self.x_top.astype(F32) + y_top
        low = x_low + self.y_low.astype(F32)
        return self.s0 + jnp.concatenate([top, low], axis=0)


def team_sum(parts):
    total = TeamSum()
    for pair in ORDER_BACK:
        total.add(pair, parts[2 * pair], parts[2 * pair + 1])
    return total.total()


def out_weight_in(shard, groups):
    t = member()
    if groups < TEAM:
        gathered = line_gather(shard[None])
        per = TEAM // groups
        b, z = t % groups, t // per
        result = jnp.zeros_like(gathered)
        for j in range(groups):
            perm = [(i, per * ((i % groups + j) % groups) + i // groups) for i in range(TEAM)]
            piece = lax.dynamic_index_in_dim(gathered, (b + j) % groups, 0, keepdims=True)
            piece = permute(piece, perm)
            result = lax.dynamic_update_slice_in_dim(result, piece, (z - j + groups) % groups, 0)
        return result.reshape(-1, shard.shape[1])
    full = lax.all_gather(shard, ALL, axis=0, tiled=True)
    rows = full.shape[0] // TEAM
    return lax.dynamic_slice_in_dim(full, t * rows, rows, 0)


def out_weight_back(grad, groups, done):
    t = member()
    if groups < TEAM:
        per = TEAM // groups
        b, z = t % groups, t // per
        grad = grad.reshape(groups, -1, grad.shape[1])
        placed = jnp.zeros_like(grad)
        for j in range(groups):
            perm = [(per * ((i % groups + j) % groups) + i // groups, i) for i in range(TEAM)]
            piece = lax.dynamic_index_in_dim(grad, (z - j + groups) % groups, 0, keepdims=True)
            piece = permute(piece, perm)
            placed = lax.dynamic_update_slice_in_dim(placed, piece, (b + j) % groups, 0)
        placed = hold([placed], done)[0]
        return line_sum(placed)[0], hold([done], placed)[0]
    whole = jnp.zeros((grad.shape[0] * TEAM, grad.shape[1]), grad.dtype)
    whole = lax.dynamic_update_slice_in_dim(whole, grad, t * grad.shape[0], 0)
    return lax.psum_scatter(whole, ALL, scatter_dimension=0, tiled=True), done


def rms_pull(value, gain, grad):
    scale = lax.rsqrt(jnp.mean(value * value, axis=-1, keepdims=True) + EPSILON)
    weighted = grad * gain
    mean = jnp.mean(weighted * value, axis=-1, keepdims=True)
    return scale * weighted - scale * scale * scale * value * mean


def rms(value, gain):
    return value * lax.rsqrt(jnp.mean(value * value, axis=-1, keepdims=True) + EPSILON) * gain


def struct(shape, dtype):
    return jax.ShapeDtypeStruct(shape, dtype)


def hold(arrays, tick):
    def kernel(*refs):
        del refs

    count = len(arrays)
    return pl.pallas_call(
        kernel,
        out_shape=[struct(a.shape, a.dtype) for a in arrays],
        in_specs=[ANY] * count + [ANY],
        out_specs=[ANY] * count,
        input_output_aliases={i: i for i in range(count)},
    )(*arrays, tick)


def mark(arrays):
    def kernel(*refs):
        refs[-1][...] = jnp.zeros_like(refs[-1])

    return pl.pallas_call(
        kernel,
        out_shape=struct((8, 128), jnp.int32),
        in_specs=[ANY] * len(arrays),
        out_specs=VMEM,
    )(*arrays)


def for_tiles(tiles, most, body):
    for m in range(1, most + 1):

        @pl.when(tiles == m)
        def _(m=m):
            body(m * TILE)


def turned(u, cosine, sine):
    return u * cosine + pltpu.roll(u, u.shape[-1] // 2, 1) * sine


def head_norm(u):
    return lax.rsqrt(jnp.mean(u * u, axis=-1, keepdims=True) + EPSILON)


def head_back(grad, raw, gain, cosine, sine):
    e = turned(grad, cosine, -sine)
    scale = head_norm(raw)
    weighted = e * gain
    mean = jnp.mean(weighted * raw, axis=-1, keepdims=True)
    back = scale * weighted - scale * scale * scale * raw * mean
    return back, jnp.sum(e * raw * scale, axis=0, keepdims=True)


def weights_of(query, key, factor):
    scores = product_nt(query, key) * factor
    n = scores.shape[0]
    causal = lax.broadcasted_iota(jnp.int32, (n, n), 1) <= lax.broadcasted_iota(jnp.int32, (n, n), 0)
    scores = jnp.where(causal, scores, -jnp.inf)
    terms = jnp.exp(scores - jnp.max(scores, axis=-1, keepdims=True))
    return terms * (1.0 / jnp.sum(terms, axis=-1, keepdims=True))


def attend(pair, tiles, tokens, consts, kept, mine, after):
    weight_attn, weight_head, weight_out, gain, gains, cosine, sine = consts
    rows, width = tokens[0].shape
    size = gains.shape[1]
    q_cols = mine * size
    cols = weight_attn.shape[1]
    factor = size ** (-0.5)
    first = kept is None
    count = 0 if first else 4

    def kernel(*refs):
        tiles_ref, tok_a, tok_b, wa, wh, wo, gain_ref, gains_ref, cos_ref, sin_ref, _ = refs[:11]
        outs = refs[11 + count : 18 + count]
        part_a, part_b, normed_all, qkv_all, logit_all, gated_all, tick = outs
        tok_v, wa_v, wh_v, wo_v, part_v, normed_v, qkv_v, logit_v, gated_v, in_sem, out_sem = refs[
            18 + count :
        ]
        tick[...] = jnp.zeros_like(tick)
        loads = [
            pltpu.make_async_copy(src, dst, in_sem.at[j])
            for j, (src, dst) in enumerate(
                ((tok_a, tok_v.at[0]), (wa, wa_v), (wh, wh_v), (wo, wo_v), (tok_b, tok_v.at[1]))
            )
        ]
        for load in loads:
            load.start()
        stores = []
        for i in range(2):
            for load in loads[:4] if i == 0 else loads[4:]:
                load.wait()
            block = 2 * pair + i

            def body(n, i=i):
                value = tok_v[i, :n].astype(F32)
                normed = rms(value, gain_ref[...]).astype(BF16)
                normed_v[i, :n] = normed
                qkv = product(normed, wa_v[...])
                qkv_v[i, :n] = qkv
                logit = product_nt(normed, wh_v[...])
                logit_v[i, :n] = logit
                cos, sin = cos_ref[:n], sin_ref[:n]
                key = qkv[:, q_cols : q_cols + size]
                key = turned(key * head_norm(key) * gains_ref[1:2], cos, sin).astype(BF16)
                values = qkv[:, q_cols + size :].astype(BF16)
                for h in range(mine):
                    query = qkv[:, h * size : (h + 1) * size]
                    query = turned(query * head_norm(query) * gains_ref[0:1], cos, sin).astype(BF16)
                    attention = weights_of(query, key, factor)
                    mixture = product(attention.astype(BF16), values)
                    gate = jax.nn.sigmoid(logit[:, h : h + 1])
                    gated_v[i, :n, h * size : (h + 1) * size] = (mixture * gate).astype(BF16)
                part_v[i, :n] = product(gated_v[i, :n], wo_v[...]).astype(BF16)
                if n < rows:
                    part_v[i, n:] = jnp.zeros((rows - n, width), BF16)
                    normed_v[i, n:] = jnp.zeros((rows - n, width), BF16)
                    gated_v[i, n:] = jnp.zeros((rows - n, q_cols), BF16)

            for_tiles(tiles_ref[block], rows // TILE, body)
            span = pl.ds(block * rows, rows)
            for j, (src, dst) in enumerate(
                (
                    (part_v, (part_a, part_b)[i]),
                    (normed_v, normed_all.at[span]),
                    (qkv_v, qkv_all.at[span]),
                    (logit_v, logit_all.at[span]),
                    (gated_v, gated_all.at[span]),
                )
            ):
                store = pltpu.make_async_copy(src.at[i], dst, out_sem.at[5 * i + j])
                store.start()
                stores.append(store)
        for store in stores:
            store.wait()

    whole = TEAM * rows
    result = pl.pallas_call(
        kernel,
        out_shape=[
            struct((rows, width), BF16),
            struct((rows, width), BF16),
            struct((whole, width), BF16),
            struct((whole, cols), F32),
            struct((whole, TILE), F32),
            struct((whole, q_cols), BF16),
            struct((8, 128), jnp.int32),
        ],
        in_specs=[SMEM] + [ANY] * 5 + [VMEM] * 4 + [ANY] + [ANY] * count,
        out_specs=[ANY] * 6 + [VMEM],
        scratch_shapes=[
            pltpu.VMEM((2, rows, width), BF16),
            pltpu.VMEM(weight_attn.shape, BF16),
            pltpu.VMEM(weight_head.shape, BF16),
            pltpu.VMEM(weight_out.shape, BF16),
            pltpu.VMEM((2, rows, width), BF16),
            pltpu.VMEM((2, rows, width), BF16),
            pltpu.VMEM((2, rows, cols), F32),
            pltpu.VMEM((2, rows, TILE), F32),
            pltpu.VMEM((2, rows, q_cols), BF16),
            pltpu.SemaphoreType.DMA((5,)),
            pltpu.SemaphoreType.DMA((10,)),
        ],
        input_output_aliases={11 + j: 2 + j for j in range(count)},
        compiler_params=pltpu.CompilerParams(vmem_limit_bytes=48 << 20),
        cost_estimate=pl.CostEstimate(flops=8 << 30, bytes_accessed=16 << 20, transcendentals=1 << 20),
    )(tiles, *tokens, weight_attn, weight_head, weight_out, gain, gains, cosine, sine, after, *(kept or ()))
    return result[0], result[1], result[2:6], result[6]


def attend_back(pair, tiles, hidden, consts, saved, kept, mine, after):
    weight_attn, weight_head, weight_out, gain, gains, cosine, sine = consts
    rows, width = hidden[0].shape
    size = gains.shape[1]
    q_cols = mine * size
    cols = weight_attn.shape[1]
    factor = size ** (-0.5)
    first = kept is None
    count = 0 if first else 3

    def kernel(*refs):
        (
            tiles_ref, hid_a, hid_b, wa, wh, wo, normed_all, qkv_all, logit_all,
            gains_ref, cos_ref, sin_ref, _,
        ) = refs[:13]
        part_a, part_b, back_all, logit_back_all, hidden_all, gain_sum, gains_sum, tick = refs[
            13 + count : 21 + count
        ]
        (
            hid_v, wa_v, wh_v, wo_v, normed_v, qkv_v, logit_v, part_v, back_v, logit_back_v,
            in_sem, out_sem,
        ) = refs[21 + count :]
        tick[...] = jnp.zeros_like(tick)
        gain_sum[...] = jnp.zeros_like(gain_sum)
        gains_sum[...] = jnp.zeros_like(gains_sum)
        spans = [pl.ds((2 * pair + i) * rows, rows) for i in range(2)]
        moves = [(hid_a, hid_v.at[0]), (wo, wo_v)]
        for i in range(2):
            if i:
                moves.append((hid_b, hid_v.at[1]))
            moves.append((qkv_all.at[spans[i]], qkv_v.at[i]))
            moves.append((logit_all.at[spans[i]], logit_v.at[i]))
            moves.append((normed_all.at[spans[i]], normed_v.at[i]))
            if not i:
                moves.append((wa, wa_v))
                moves.append((wh, wh_v))
        loads = [pltpu.make_async_copy(src, dst, in_sem.at[j]) for j, (src, dst) in enumerate(moves)]
        for load in loads:
            load.start()
        stores = []
        for i in range(2):
            for load in loads[:7] if i == 0 else loads[7:]:
                load.wait()
            store = pltpu.make_async_copy(hid_v.at[i], hidden_all.at[spans[i]], out_sem.at[4 * i + 3])
            store.start()
            stores.append(store)

            def body(n, i=i):
                gated_grad = product_nt(hid_v[i, :n], wo_v[...])
                cos, sin = cos_ref[:n], sin_ref[:n]
                key_raw = qkv_v[i, :n, q_cols : q_cols + size]
                key = turned(key_raw * head_norm(key_raw) * gains_ref[1:2], cos, sin).astype(BF16)
                values = qkv_v[i, :n, q_cols + size :].astype(BF16)
                lane = lax.broadcasted_iota(jnp.int32, (n, TILE), 1)
                logit_back = jnp.zeros((n, TILE), F32)
                values_back = jnp.zeros((n, size), F32)
                key_grad = jnp.zeros((n, size), F32)
                query_sum = jnp.zeros((1, size), F32)
                for h in range(mine):
                    span = slice(h * size, (h + 1) * size)
                    query_raw = qkv_v[i, :n, span]
                    query = turned(query_raw * head_norm(query_raw) * gains_ref[0:1], cos, sin).astype(BF16)
                    attention = weights_of(query, key, factor)
                    attention_low = attention.astype(BF16)
                    mixture = product(attention_low, values)
                    gate = jax.nn.sigmoid(logit_v[i, :n, h : h + 1])
                    head_grad = gated_grad[:, span]
                    mixture_back = (head_grad * gate).astype(BF16)
                    one = jnp.sum(head_grad * mixture, axis=-1, keepdims=True) * gate * (1.0 - gate)
                    logit_back = jnp.where(lane == h, one, logit_back)
                    values_back += product_tn(attention_low, mixture_back)
                    attention_grad = product_nt(mixture_back, values)
                    scores_back = (
                        attention
                        * (attention_grad - jnp.sum(attention_grad * attention, axis=-1, keepdims=True))
                    ).astype(BF16)
                    query_grad = product(scores_back, key) * factor
                    key_grad += product_tn(scores_back, query)
                    back, total = head_back(query_grad, query_raw, gains_ref[0:1], cos, sin)
                    back_v[i, :n, span] = back.astype(BF16)
                    query_sum += total
                back, key_sum = head_back(key_grad * factor, key_raw, gains_ref[1:2], cos, sin)
                back_v[i, :n, q_cols : q_cols + size] = back.astype(BF16)
                back_v[i, :n, q_cols + size :] = values_back.astype(BF16)
                logit_back = logit_back.astype(BF16)
                logit_back_v[i, :n] = logit_back
                gains_sum[0:1] += query_sum
                gains_sum[1:2] += key_sum
                part = product_nt(back_v[i, :n], wa_v[...]) + product(logit_back, wh_v[...])
                part_v[i, :n] = part.astype(BF16)
                gain_sum[0:1] += jnp.sum(part * normed_v[i, :n].astype(F32), axis=0, keepdims=True)
                if n < rows:
                    part_v[i, n:] = jnp.zeros((rows - n, width), BF16)
                    back_v[i, n:] = jnp.zeros((rows - n, cols), BF16)
                    logit_back_v[i, n:] = jnp.zeros((rows - n, TILE), BF16)

            for_tiles(tiles_ref[2 * pair + i], rows // TILE, body)
            for j, (src, dst) in enumerate(
                (
                    (part_v, (part_a, part_b)[i]),
                    (back_v, back_all.at[spans[i]]),
                    (logit_back_v, logit_back_all.at[spans[i]]),
                )
            ):
                store = pltpu.make_async_copy(src.at[i], dst, out_sem.at[4 * i + j])
                store.start()
                stores.append(store)
        for store in stores:
            store.wait()

    whole = TEAM * rows
    result = pl.pallas_call(
        kernel,
        out_shape=[
            struct((rows, width), BF16),
            struct((rows, width), BF16),
            struct((whole, cols), BF16),
            struct((whole, TILE), BF16),
            struct((whole, width), BF16),
            struct((8, width), F32),
            struct((8, size), F32),
            struct((8, 128), jnp.int32),
        ],
        in_specs=[SMEM] + [ANY] * 8 + [VMEM] * 3 + [ANY] + [ANY] * count,
        out_specs=[ANY] * 5 + [VMEM] * 3,
        scratch_shapes=[
            pltpu.VMEM((2, rows, width), BF16),
            pltpu.VMEM(weight_attn.shape, BF16),
            pltpu.VMEM(weight_head.shape, BF16),
            pltpu.VMEM(weight_out.shape, BF16),
            pltpu.VMEM((2, rows, width), BF16),
            pltpu.VMEM((2, rows, cols), F32),
            pltpu.VMEM((2, rows, TILE), F32),
            pltpu.VMEM((2, rows, width), BF16),
            pltpu.VMEM((2, rows, cols), BF16),
            pltpu.VMEM((2, rows, TILE), BF16),
            pltpu.SemaphoreType.DMA((11,)),
            pltpu.SemaphoreType.DMA((8,)),
        ],
        input_output_aliases={13 + j: 2 + j for j in range(count)},
        compiler_params=pltpu.CompilerParams(vmem_limit_bytes=48 << 20),
        cost_estimate=pl.CostEstimate(flops=12 << 30, bytes_accessed=20 << 20, transcendentals=1 << 20),
    )(
        tiles, *hidden, weight_attn, weight_head, weight_out, *saved, gains, cosine, sine, after,
        *(kept or ()),
    )
    return result[0], result[1], result[2:5], result[5], result[6], result[7]


def tile_places(tiles_ref, rows):
    places, total = [], 0
    for r in range(TEAM):
        count = tiles_ref[r]
        for j in range(rows // TILE):
            places.append((r, j, j < count, total + j))
        total = total + count
    return places, total


def rows_of(tile, size=TILE):
    return pl.ds(pl.multiple_of(tile * size, size), size)


def feed_up(tiles, twos, upstreams, weight_gate, weight_up, after):
    rows, width = twos[0].shape
    ff_cols = weight_gate.shape[1]
    whole = TEAM * rows
    chunk = 2 * TILE
    chunks = whole // chunk

    def kernel(*refs):
        tiles_ref, twos_ref, ups_ref = refs[0], refs[1 : 1 + TEAM], refs[1 + TEAM : 1 + 2 * TEAM]
        weights_ref = refs[1 + 2 * TEAM : 3 + 2 * TEAM]
        inner_all, both_all, two_all, ups_all = refs[4 + 2 * TEAM : 8 + 2 * TEAM]
        two_v, ups_v, wg_v, wu_v, inner_v, both_v, zero_v, w_sem, load_sem, out_sem = refs[8 + 2 * TEAM :]
        places, total = tile_places(tiles_ref, rows)
        used = (total + 1) // 2

        def loads(sources, packed, which):
            for k, (r, j, live, place) in enumerate(places):
                yield live, pltpu.make_async_copy(
                    sources[r].at[rows_of(j)], packed.at[rows_of(place)], load_sem.at[which, k]
                )

        for live, copy in loads(twos_ref, two_v, 0):
            pl.when(live)(copy.start)
        weights = [
            pltpu.make_async_copy(weights_ref[0], wg_v, w_sem.at[0]),
            pltpu.make_async_copy(weights_ref[1], wu_v, w_sem.at[1]),
        ]
        for load in weights:
            load.start()
        for live, copy in loads(ups_ref, ups_v, 1):
            pl.when(live)(copy.start)
        zero_v[...] = jnp.zeros_like(zero_v)

        @pl.when(total % 2 == 1)
        def _():
            two_v[rows_of(total)] = jnp.zeros((TILE, width), BF16)
            ups_v[rows_of(total)] = jnp.zeros((TILE, width), BF16)

        for live, copy in loads(twos_ref, two_v, 0):
            pl.when(live)(copy.wait)
        for load in weights:
            load.wait()

        def stores(c, sources):
            for j, (src, dst) in enumerate(zip(sources, (two_all, ups_all, inner_all, both_all))):
                yield pltpu.make_async_copy(src, dst.at[rows_of(c, chunk)], out_sem.at[j, c])

        zeros = (zero_v, zero_v, zero_v.at[:, :ff_cols], zero_v.at[:, : 2 * ff_cols])
        for c in range(TEAM // 2, chunks):

            @pl.when(c >= used)
            def _(c=c):
                for store in stores(c, zeros):
                    store.start()

        for live, copy in loads(ups_ref, ups_v, 1):
            pl.when(live)(copy.wait)

        def body(c, carry):
            span = rows_of(c, chunk)
            gate_part = product(two_v[span], wg_v[...])
            up_part = product(two_v[span], wu_v[...])
            inner_v[span] = (gate_part * jax.nn.sigmoid(gate_part) * up_part).astype(BF16)
            both_v[span, :ff_cols] = gate_part.astype(BF16)
            both_v[span, ff_cols:] = up_part.astype(BF16)
            for store in stores(c, (two_v.at[span], ups_v.at[span], inner_v.at[span], both_v.at[span])):
                store.start()
            return carry

        lax.fori_loop(0, used, body, 0)
        for c in range(chunks):
            for store in stores(c, zeros):
                store.wait()

    count = whole // TILE
    return pl.pallas_call(
        kernel,
        out_shape=[
            struct((whole, ff_cols), BF16),
            struct((whole, 2 * ff_cols), BF16),
            struct((whole, width), BF16),
            struct((whole, width), BF16),
        ],
        in_specs=[SMEM] + [ANY] * (3 + 2 * TEAM),
        out_specs=[ANY] * 4,
        scratch_shapes=[
            pltpu.VMEM((whole, width), BF16),
            pltpu.VMEM((whole, width), BF16),
            pltpu.VMEM(weight_gate.shape, BF16),
            pltpu.VMEM(weight_up.shape, BF16),
            pltpu.VMEM((whole, ff_cols), BF16),
            pltpu.VMEM((whole, 2 * ff_cols), BF16),
            pltpu.VMEM((chunk, width), BF16),
            pltpu.SemaphoreType.DMA((2,)),
            pltpu.SemaphoreType.DMA((2, count)),
            pltpu.SemaphoreType.DMA((4, chunks)),
        ],
        compiler_params=pltpu.CompilerParams(vmem_limit_bytes=58 << 20),
        cost_estimate=pl.CostEstimate(flops=20 << 30, bytes_accessed=60 << 20, transcendentals=1 << 20),
    )(tiles, *twos, *upstreams, weight_gate, weight_up, after)


def feed_down(second, tiles, saved, weight_gate, weight_up, weight_down, kept, after):
    count = 2 * TEAM + 1 if second else 0
    ff_cols, width = weight_down.shape
    whole = saved[0].shape[0]
    rows = whole // TEAM
    chunk = 2 * TILE
    chunks = whole // chunk

    def kernel(*refs):
        tiles_ref, inner_all, both_all, ups_all, wg, wu, wd = refs[:7]
        outs_ref = refs[8 + count : 8 + count + TEAM]
        grads_ref = refs[8 + count + TEAM : 8 + count + 2 * TEAM]
        back_all = refs[8 + count + 2 * TEAM]
        (
            ups_v, both_v, inner_v, back_v, wg_v, wu_v, wd_v, out_v, grad_v, zero_v,
            in_sem, w_sem, out_sem, grad_sem, back_sem, zero_sem,
        ) = refs[9 + count + 2 * TEAM :]
        places, total = tile_places(tiles_ref, rows)
        used = (total + 1) // 2
        first_chunk = used // 2 if second else 0
        end_chunk = used if second else used // 2

        def loads(c):
            slot = c % 2
            for j, (src, dst) in enumerate(((ups_all, ups_v), (both_all, both_v), (inner_all, inner_v))):
                yield pltpu.make_async_copy(src.at[rows_of(c, chunk)], dst.at[slot], in_sem.at[j, slot])

        for load in loads(first_chunk):
            load.start()
        weights = [
            pltpu.make_async_copy(src, dst, w_sem.at[j])
            for j, (src, dst) in enumerate(((wd, wd_v), (wg, wg_v), (wu, wu_v)))
        ]
        for load in weights:
            load.start()
        if not second:
            zero_v[...] = jnp.zeros_like(zero_v)

        def tile_stores(k, r, j, sources):
            yield pltpu.make_async_copy(sources[0], grads_ref[r].at[rows_of(j)], grad_sem.at[k])
            yield pltpu.make_async_copy(sources[1], outs_ref[r].at[rows_of(j)], out_sem.at[k])

        zeros = (zero_v.at[:TILE], zero_v.at[:TILE])
        def now(live, place):
            in_span = jnp.logical_and(place // 2 >= first_chunk, place // 2 < end_chunk)
            if second:
                return jnp.logical_and(live, in_span)
            return jnp.logical_or(jnp.logical_not(live), in_span)

        for k, (r, j, live, place) in enumerate(places) if not second else ():

            @pl.when(jnp.logical_not(live))
            def _(k=k, r=r, j=j):
                for store in tile_stores(k, r, j, zeros):
                    store.start()

        def back_zero(c):
            return pltpu.make_async_copy(
                zero_v.at[:, : 2 * ff_cols], back_all.at[rows_of(c, chunk)], zero_sem.at[c]
            )

        for c in range(TEAM // 2, chunks) if not second else ():
            pl.when(c >= used)(back_zero(c).start)

        def back_store(c):
            return pltpu.make_async_copy(
                back_v.at[c % 2], back_all.at[rows_of(c, chunk)], back_sem.at[c % 2]
            )

        for load in weights:
            load.wait()

        def body(c, carry):
            slot = c % 2

            @pl.when(c + 1 < end_chunk)
            def _():
                for load in loads(c + 1):
                    load.start()

            for load in loads(c):
                load.wait()

            @pl.when(c >= first_chunk + 2)
            def _():
                back_store(c - 2).wait()

            span = rows_of(c, chunk)
            inner_grad = product_nt(ups_v[slot], wd_v[...])
            gate_part = both_v[slot, :, :ff_cols].astype(F32)
            up_part = both_v[slot, :, ff_cols:].astype(F32)
            sig = jax.nn.sigmoid(gate_part)
            silu = gate_part * sig
            back_v[slot, :, :ff_cols] = (inner_grad * up_part * (sig + silu * (1.0 - sig))).astype(BF16)
            back_v[slot, :, ff_cols:] = (inner_grad * silu).astype(BF16)
            back_store(c).start()
            grad = product_nt(back_v[slot, :, :ff_cols], wg_v[...]) + product_nt(back_v[slot, :, ff_cols:], wu_v[...])
            grad_v[span] = grad.astype(BF16)
            out_v[span] = product(inner_v[slot], wd_v[...]).astype(BF16)
            for k, (r, j, live, place) in enumerate(places):

                @pl.when(jnp.logical_and(live, place // 2 == c))
                def _(k=k, r=r, j=j, place=place):
                    here = rows_of(place)
                    for store in tile_stores(k, r, j, (grad_v.at[here], out_v.at[here])):
                        store.start()

            return carry

        lax.fori_loop(first_chunk, end_chunk, body, 0)
        back_store(end_chunk - 2).wait()
        back_store(end_chunk - 1).wait()
        for c in range(TEAM // 2, chunks) if not second else ():
            pl.when(c >= used)(back_zero(c).wait)
        for k, (r, j, live, place) in enumerate(places):

            @pl.when(now(live, place))
            def _(k=k, r=r, j=j):
                for store in tile_stores(k, r, j, zeros):
                    store.wait()

    tile_count = whole // TILE
    result = pl.pallas_call(
        kernel,
        out_shape=[struct((rows, width), BF16)] * (2 * TEAM) + [struct((whole, 2 * ff_cols), BF16)],
        in_specs=[SMEM] + [ANY] * (7 + count),
        out_specs=[ANY] * (2 * TEAM + 1),
        input_output_aliases={8 + j: j for j in range(count)},
        scratch_shapes=[
            pltpu.VMEM((2, chunk, width), BF16),
            pltpu.VMEM((2, chunk, 2 * ff_cols), BF16),
            pltpu.VMEM((2, chunk, ff_cols), BF16),
            pltpu.VMEM((2, chunk, 2 * ff_cols), BF16),
            pltpu.VMEM(weight_gate.shape, BF16),
            pltpu.VMEM(weight_up.shape, BF16),
            pltpu.VMEM(weight_down.shape, BF16),
            pltpu.VMEM((whole, width), BF16),
            pltpu.VMEM((whole, width), BF16),
            pltpu.VMEM((chunk, width), BF16),
            pltpu.SemaphoreType.DMA((3, 2)),
            pltpu.SemaphoreType.DMA((3,)),
            pltpu.SemaphoreType.DMA((tile_count,)),
            pltpu.SemaphoreType.DMA((tile_count,)),
            pltpu.SemaphoreType.DMA((2,)),
            pltpu.SemaphoreType.DMA((chunks,)),
        ],
        compiler_params=pltpu.CompilerParams(vmem_limit_bytes=56 << 20),
        cost_estimate=pl.CostEstimate(flops=40 << 30, bytes_accessed=80 << 20, transcendentals=1 << 20),
    )(tiles, *saved, weight_gate, weight_up, weight_down, after, *(kept or ()))
    return result


def local(
    groups,
    tokens,
    lengths,
    cotangent,
    attention_gain,
    query_weight,
    key_matrix,
    value_matrix,
    head_gate_weight,
    output_weight,
    query_key_gain,
    feedforward_gain,
    gate_weight,
    up_weight,
    down_weight,
):
    t = member()
    everyone = groups * TEAM
    rows, width = tokens.shape
    rho = query_weight.shape[0]
    phi = down_weight.shape[0]
    ff = gate_weight.shape[1]
    pair_cols = query_key_gain.shape[1]
    size = pair_cols * everyone
    heads = query_weight.shape[1] // size
    mine = heads // TEAM
    q_cols = query_weight.shape[1] // TEAM
    k_cols = key_matrix.shape[1] // TEAM
    ff_cols = ff // TEAM

    def everyone_in_team(vector):
        return jnp.broadcast_to(vector.reshape(1, -1), (TEAM, vector.size))

    live_tiles = (lengths + (TILE - 1)) // TILE
    row = jnp.concatenate(
        [
            head_gate_weight.reshape(rho, TEAM, mine).transpose(1, 2, 0).reshape(TEAM, -1),
            everyone_in_team(attention_gain),
            everyone_in_team(feedforward_gain),
            everyone_in_team(query_key_gain),
            everyone_in_team(live_tiles.astype(BF16)),
        ],
        axis=1,
    )
    cols = q_cols + 2 * k_cols
    row = jnp.pad(row, ((0, 0), (0, cols - row.shape[1])))[:, None, :]
    attn = jnp.concatenate(
        [
            query_weight.reshape(rho, TEAM, q_cols),
            key_matrix.reshape(rho, TEAM, k_cols),
            value_matrix.reshape(rho, TEAM, k_cols),
        ],
        axis=2,
    ).transpose(1, 0, 2)
    attn = jnp.concatenate([attn, jnp.pad(row, ((0, 0), (0, 7), (0, 0)))], axis=1)
    attn = exchange(attn)
    head_lanes = mine * rho
    at_one, at_two, at_pair = head_lanes, head_lanes + rho, head_lanes + 2 * rho
    at_tiles = at_pair + 2 * pair_cols
    team_tiles = attn[:, rho, at_tiles].astype(jnp.int32)
    order = jnp.arange(TEAM, dtype=jnp.int32)
    tiles = jnp.sum(jnp.where((order[:, None] ^ t) == order[None, :], team_tiles[None, :], 0), axis=1)
    attn = line_gather(attn.reshape(TEAM * (rho + 8), cols)).reshape(everyone, rho + 8, cols)
    weight_attn = attn[:, :rho].reshape(width, cols)
    rows_small = attn[:, rho]
    weight_head = jnp.pad(
        rows_small[:, :head_lanes].reshape(everyone, mine, rho).transpose(1, 0, 2).reshape(mine, width),
        ((0, TILE - mine), (0, 0)),
    )
    gain_one = rows_small[:, at_one:at_two].reshape(1, width).astype(F32)
    gain_two = rows_small[:, at_two:at_pair].reshape(1, width).astype(F32)
    gain_pair = (
        rows_small[:, at_pair:at_tiles]
        .reshape(everyone, 2, pair_cols)
        .transpose(1, 0, 2)
        .reshape(2, size)
        .astype(F32)
    )
    weight_out = out_weight_in(output_weight, groups)

    def ff_split(w):
        return w.reshape(rho, groups, TEAM, phi).transpose(2, 0, 1, 3).reshape(TEAM, rho, ff_cols)

    feed_shard = jnp.concatenate([ff_split(gate_weight), ff_split(up_weight)], axis=2)
    feed_shard = exchange(feed_shard).reshape(TEAM * rho, -1)
    weight_gate = line_gather(feed_shard[:, :ff_cols])

    exponent = jnp.arange(size // 2, dtype=F32) * (-2.0 / size)
    frequency = jnp.power(ROPE_BASE, exponent)
    angles = jnp.arange(rows, dtype=F32)[:, None] * frequency[None, :]
    cosine = jnp.concatenate([jnp.cos(angles), jnp.cos(angles)], axis=1)
    sine = jnp.concatenate([-jnp.sin(angles), jnp.sin(angles)], axis=1)
    consts = (weight_attn, weight_head, weight_out, gain_one, gain_pair, cosine, sine)
    team_tokens = team_gather(tokens)
    kept, arrived = None, TeamSum()
    live = lax.broadcasted_iota(jnp.int32, (rows, 1), 0) < lengths[0]
    live_rows = live.astype(F32)
    upstream = cotangent.astype(F32) * live_rows
    ticks = []
    for step, pair in enumerate(ORDER_BACK):
        if step == 0:
            after = mark([feed_shard])
        if step == 2:
            after = arrived.low6
        if step == 3:
            after = mark([team_upstream[1], team_upstream[2], team_upstream[4], weight_gate])
        a, b, kept, tick = attend(
            pair, tiles, team_tokens[2 * pair : 2 * pair + 2], consts, kept, mine, after
        )
        arrived.add(pair, a, b)
        if step == 0:
            weight_up = line_gather(hold([feed_shard[:, ff_cols:]], tick)[0])
            later = lax.broadcasted_iota(jnp.int32, (rows, 1), 0) < lengths[0] + tick[0, 0]
            team_upstream = team_gather(jnp.where(later, cotangent, jnp.zeros_like(cotangent)))
        if step == 1:
            weight_down = line_gather(hold([down_weight], tick)[0])
    normed, qkv, logit, gated = kept
    inputs = tokens.astype(F32)
    hidden_state = inputs + arrived.total()

    normed_two = rms(hidden_state, gain_two).astype(BF16)
    normed_two = hold([normed_two], mark(team_upstream + [weight_up]))[0]
    team_two = team_gather(normed_two)
    saved = feed_up(tiles, team_two, team_upstream, weight_gate, weight_up, weight_down)
    inner, both, two_all, ups_all = saved
    down_part = product_tn(inner, ups_all).astype(BF16)
    half_width = width // 2
    down_grads = [line_sum(down_part[:, :half_width])]
    kept = feed_down(
        False, tiles, (inner, both, ups_all), weight_gate, weight_up, weight_down, None, mark([down_part])
    )
    kept = feed_down(
        True, tiles, (inner, both, ups_all), weight_gate, weight_up, weight_down, kept, down_grads[0]
    )
    down_grads.append(line_sum(hold([down_part[:, half_width:]], down_grads[0])[0]))
    down_grad = jnp.concatenate(down_grads, axis=1)
    outs, grads, feed_back = kept[:TEAM], kept[TEAM : 2 * TEAM], kept[2 * TEAM]
    arrived = TeamSum()
    for pair in ORDER_BACK:
        arrived.add(pair, grads[2 * pair], grads[2 * pair + 1])
    two_grad = arrived.total()
    feed_back = hold([feed_back], arrived.low6)[0]
    gate_part = product_tn(two_all, feed_back[:, :ff_cols]).astype(BF16)
    up_part = product_tn(two_all, feed_back[:, ff_cols:]).astype(BF16)
    gate_part = hold([gate_part], down_grads[1])[0]
    after = mark([gate_part, up_part])
    gate_grad = line_sum(gate_part)
    up_grad = line_sum(hold([up_part], gate_grad)[0])

    hidden_grad = upstream + rms_pull(hidden_state, gain_two, two_grad)

    hidden_levels = TeamGather(hold([hidden_grad.astype(BF16)], after)[0])
    team_hidden = [hidden_levels.own, hidden_levels.a1]
    two_scale = lax.rsqrt(jnp.mean(hidden_state * hidden_state, axis=-1, keepdims=True) + EPSILON)
    two_sum = jnp.sum(two_grad * hidden_state * two_scale, axis=0)
    kept, one_sum, pair_sum, ticks, arrived = None, 0.0, 0.0, [], TeamSum()
    for step, pair in enumerate(ORDER_LATE):
        if step == 1:
            after = gate_grad
        if step == 2:
            after = up_grad
        if step == 3:
            after = mark([arrived.low6, fed.u2, fed.u4, fed.x_top, fed.y_low])
        a, b, kept, total, pair_total, tick = attend_back(
            pair, tiles, team_hidden[2 * pair : 2 * pair + 2], consts, (normed, qkv, logit), kept, mine, after
        )
        arrived.add(pair, a, b)
        one_sum = one_sum + total[0]
        pair_sum = pair_sum + pair_total[:2]
        if step == 0:
            team_hidden = hidden_levels.blocks(tick)
            outs = hold(outs, tick)
            fed = TeamSum()
            for other in ORDER_BACK:
                fed.add(other, outs[2 * other], outs[2 * other + 1])
    attn_back, logit_back, hidden_all = kept
    feed_done = up_grad
    layer_output = ((hidden_state + fed.total()) * live_rows).astype(BF16)
    normed_grad = arrived.total()
    feed_grad = jnp.concatenate([gate_grad, hold([up_grad], normed_grad)[0]], axis=1)
    feed_grad = exchange(feed_grad.reshape(TEAM, rho, 2 * ff_cols))
    def ff_join(w):
        return w.reshape(TEAM, rho, groups, phi).transpose(1, 2, 0, 3).reshape(rho, ff)

    gate_grad = ff_join(feed_grad[:, :, :ff_cols])
    up_grad = ff_join(feed_grad[:, :, ff_cols:])
    tokens_grad = (hidden_grad + rms_pull(inputs, gain_one, normed_grad)).astype(BF16)
    out_part = product_tn(gated, hidden_all).astype(BF16)
    attn_part = product_tn(normed, attn_back).astype(BF16)
    head_part = product_tn(logit_back, normed)[:mine]
    row = jnp.concatenate(
        [
            head_part.reshape(mine, everyone, rho).transpose(1, 0, 2).reshape(everyone, -1),
            (one_sum / gain_one[0]).reshape(everyone, rho),
            two_sum.reshape(everyone, rho),
            pair_sum.reshape(2, everyone, pair_cols).transpose(1, 0, 2).reshape(everyone, -1),
        ],
        axis=1,
    ).astype(BF16)
    row = jnp.pad(row, ((0, 0), (0, cols - row.shape[1])))[:, None, :]
    packed = jnp.concatenate(
        [attn_part.reshape(everyone, rho, cols), jnp.pad(row, ((0, 0), (0, 7), (0, 0)))], axis=1
    )
    packed = packed.reshape(everyone * (rho + 8), cols)
    packed = line_sum(hold([packed], feed_done)[0])
    output_grad, packed = out_weight_back(out_part, groups, packed)
    packed = exchange(packed.reshape(TEAM, rho + 8, cols))
    attn_grad = packed[:, :rho].transpose(1, 0, 2)
    rows_small = packed[:, rho].astype(F32)
    sums = jnp.sum(rows_small[:, head_lanes:], axis=0)
    head_gate_grad = rows_small[:, :head_lanes].reshape(heads, rho).T
    return (
        layer_output,
        tokens_grad,
        sums[:rho],
        attn_grad[:, :, :q_cols].reshape(rho, -1).astype(F32),
        attn_grad[:, :, q_cols : q_cols + k_cols].reshape(rho, -1).astype(F32),
        attn_grad[:, :, q_cols + k_cols :].reshape(rho, -1).astype(F32),
        head_gate_grad,
        output_grad.astype(F32),
        sums[2 * rho : 2 * rho + 2 * pair_cols].reshape(2, pair_cols),
        sums[rho : 2 * rho],
        gate_grad.astype(F32),
        up_grad.astype(F32),
        down_grad.astype(F32),
    )


def solution(mesh):
    groups = mesh.size // TEAM
    rows, vector, columns = P(ALL, None), P(ALL), P(None, ALL)

    def step(*args):
        return local(groups, *args)

    return jax.shard_map(
        step,
        mesh=mesh,
        in_specs=(
            rows, vector, rows, vector, rows, rows, rows, rows, rows, columns, vector, rows, rows, rows,
        ),
        out_specs=(
            rows, rows, vector, rows, rows, rows, rows, rows, columns, vector, rows, rows, rows,
        ),
        check_vma=False,
    )
```

profile of v0, /device:TPU:1, one launch (start us, length us, event | category | flops | bytes accessed | tf_op | source)
XLA Modules:
  0.0 907.5 jit_solution(7273165517425871393)
XLA Ops:
  11.0 15.1 %all_to_all.20 = bf16[8,72,512]{2,1,0:T(8,128)(2,1)} all-to-all(bf16[8,72,512]{2,1,0:T(8,128)(2,1)S(1)} %copy.162), channel_id=1, replica_groups=mesh['dp'=4,'fsdp'=8] {'fsdp'}, dimensions={0} | all-to-all | bytes 1179648 | tf_op jit(solution)/shard_map/all_to_all | solution.py:62
  33.6 4.0 all-to-all-start.1
  40.3 14.9 %all-to-all-done.1 = bf16[8,64,1536]{2,1,0:T(8,128)(2,1)S(1)} async-done(((bf16[8,64,1536]{2,1,0:T(8,128)(2,1)}), bf16[8,64,1536]{2,1,0:T(8,128)(2,1)S(1)}, u32[]{:S(2)}, u32[]{:S(2)}) %all-to-all-start.1) | async-done | bytes 1572896 | tf_op jit(solution)/shard_map/all_to_all | solution.py:62
  56.9 33.8 %collective-permute-done.5.refs_1_ = bf16[384,2048]{1,0:T(8,128)(2,1)} collective-permute-done((bf16[384,2048]{1,0:T(8,128)(2,1)}, bf16[384,2048]{1,0:T(8,128)(2,1)}, u32[]{:S(2)}, u32[]{:S(2)}) %collective-permute-start.5) | collective-permute-done | bytes 1572896 | tf_op jit(solution)/shard_map/ppermute | solution.py:51
  100.1 3.0 collective-permute-start.1
  103.2 7.4 collective-permute-done.6
  117.4 4.0 collective-permute-start.2
  122.2 3.8 collective-permute-start.4
  127.2 4.3 collective-permute-done.3
  132.2 3.5 slice.286
  138.1 11.3 %shard_map.238 = (bf16[384,2048]{1,0:T(8,128)(2,1)S(1)}, bf16[384,2048]{1,0:T(8,128)(2,1)}, bf16[3072,2048]{1,0:T(8,128)(2,1)}, f32[3072,512]{1,0:T(8,128)}, f32...) custom-call(s32[8]{0:T(128)S(1)} %select_reduce_fusion.refs_0_, ...), custom_call_target="tpu_custom_call" | custom-call | flops 8589934592 | bytes 16777216 | tf_op jit(solution)/shard_map/pallas_call | solution.py:317
  151.6 4.1 collective-permute-done.15.refs_2_
  159.8 12.2 %shard_map.240 = (bf16[384,2048]{1,0:T(8,128)(2,1)S(1)}, bf16[384,2048]{1,0:T(8,128)(2,1)}, bf16[3072,2048]{1,0:T(8,128)(2,1)}, f32[3072,512]{1,0:T(8,128)}, f32...) custom-call(s32[8]{0:T(128)S(1)} %copy-done.30, ...), custom_call_target="tpu_custom_call", output_to_operand_aliasing={{2}: (11, {}), {3}: (12, {}), {4}: (13, {}), {5}: (14, {})} | custom-call | flops 8589934592 | bytes 16777216 | tf_op jit(solution)/shard_map/pallas_call | solution.py:317
  174.5 2.7 broadcast_select_fusion.refs_0_.refs_9_
  179.2 3.3 add_convert_fusion.3.refs_10_
  183.6 11.3 %shard_map.241 = (bf16[384,2048]{1,0:T(8,128)(2,1)S(1)}, bf16[384,2048]{1,0:T(8,128)(2,1)}, bf16[3072,2048]{1,0:T(8,128)(2,1)}, f32[3072,512]{1,0:T(8,128)}, f32...) custom-call(s32[8]{0:T(128)S(1)} %copy-done.31, ...), custom_call_target="tpu_custom_call", output_to_operand_aliasing={{2}: (11, {}), {3}: (12, {}), {4}: (13, {}), {5}: (14, {})} | custom-call | flops 8589934592 | bytes 16777216 | tf_op jit(solution)/shard_map/pallas_call | solution.py:317
  201.2 17.5 %collective-permute-done.12.refs_2_.refs_4_.refs_13_ = bf16[384,2048]{1,0:T(8,128)(2,1)S(1)} collective-permute-done((bf16[384,2048]{1,0:T(8,128)(2,1)}, bf16[384,2048]{1,0:T(8,128)(2,1)S(1)}, u32[]{:S(2)}, u32[]{:S(2)}) %collective-permute-start.12) | collective-permute-done | bytes 1572896 | tf_op jit(solution)/shard_map/ppermute | solution.py:51
  225.9 16.7 %shard_map.242 = (bf16[384,2048]{1,0:T(8,128)(2,1)S(1)}, bf16[384,2048]{1,0:T(8,128)(2,1)S(1)}, bf16[3072,2048]{1,0:T(8,128)(2,1)}, f32[3072,512]{1,0:T(8,128)},...) custom-call(s32[8]{0:T(128)S(1)} %copy-done.31, ...), custom_call_target="tpu_custom_call", output_to_operand_aliasing={{2}: (11, {}), {3}: (12, {}), {4}: (13, {}), {5}: (14, {})} | custom-call | flops 8589934592 | bytes 16777216 | tf_op jit(solution)/shard_map/pallas_call | solution.py:317
  248.6 6.1 collective-permute-done.27
  258.5 13.0 %collective-permute-done.23 = bf16[192,2048]{1,0:T(8,128)(2,1)S(1)} collective-permute-done((bf16[192,2048]{1,0:T(8,128)(2,1)S(1)}, bf16[192,2048]{1,0:T(8,128)(2,1)S(1)}, u32[]{:S(2)}, u32[]{:S(2)}) %collective-permute-start.23) | collective-permute-done | bytes 786464 | tf_op jit(solution)/shard_map/ppermute | solution.py:51
  271.6 4.8 collective-permute-start.25
  276.6 11.7 %collective-permute-done.18 = bf16[192,2048]{1,0:T(8,128)(2,1)S(1)} collective-permute-done((bf16[192,2048]{1,0:T(8,128)(2,1)S(1)}, bf16[192,2048]{1,0:T(8,128)(2,1)S(1)}, u32[]{:S(2)}, u32[]{:S(2)}) %collective-permute-start.18) | collective-permute-done | bytes 786464 | tf_op jit(solution)/shard_map/ppermute | solution.py:51
  288.3 2.6 collective-permute-start.29
  300.8 34.2 %collective-permute-done.33.refs_5_ = bf16[384,2048]{1,0:T(8,128)(2,1)} collective-permute-done((bf16[384,2048]{1,0:T(8,128)(2,1)}, bf16[384,2048]{1,0:T(8,128)(2,1)}, u32[]{:S(2)}, u32[]{:S(2)}) %collective-permute-start.33) | collective-permute-done | bytes 1572896 | tf_op jit(solution)/shard_map/ppermute | solution.py:51
  341.5 13.0 %collective-permute-done.35 = bf16[192,2048]{1,0:T(8,128)(2,1)S(1)} collective-permute-done((bf16[192,2048]{1,0:T(8,128)(2,1)S(1)}, bf16[192,2048]{1,0:T(8,128)(2,1)S(1)}, u32[]{:S(2)}, u32[]{:S(2)}) %collective-permute-start.35) | collective-permute-done | bytes 786464 | tf_op jit(solution)/shard_map/ppermute | solution.py:51
  359.6 3.4 collective-permute-done.37.refs_8_
  363.0 27.0 %shard_map.247 = (bf16[3072,768]{1,0:T(8,128)(2,1)}, bf16[3072,1536]{1,0:T(8,128)(2,1)}, bf16[3072,2048]{1,0:T(8,128)(2,1)}, bf16[3072,2048]{1,0:T(8,128)(2,1)}) custom-call(s32[8]{0:T(128)} %copy-done.29, bf16[384,2048]{1,0:T(8,128)(2,1)} %shard_map.245.refs_1_, bf16[384,2048]{1,0:T(8,128)(2,1)} %collective-permute-done.30.refs_2_, ...), custom_call_target="tpu_custom_call" | custom-call | flops 21474836480 | bytes 62914560 | tf_op jit(solution)/shard_map/pallas_call | solution.py:588
  389.9 14.4 %convolution_convert_fusion.refs_0_ = bf16[768,2048]{1,0:T(8,128)(2,1)S(1)} fusion(bf16[3072,768]{1,0:T(8,128)(2,1)} %get-tuple-element.138.refs_1_, bf16[3072,2048]{1,0:T(8,128)(2,1)} %get-tuple-element.140.refs_3_), kind=kOutput, calls=%fused_computation.12 | convolution fusion | flops 9665249280 | bytes 20447232 | tf_op jit(solution)/shard_map/dot_general | solution.py:31
  408.6 26.6 %shard_map.249 = (bf16[384,2048]{1,0:T(8,128)(2,1)}, bf16[384,2048]{1,0:T(8,128)(2,1)}, bf16[384,2048]{1,0:T(8,128)(2,1)}, bf16[384,2048]{1,0:T(8,128)(2,1)}, bf...) custom-call(s32[8]{0:T(128)} %copy-done.29, ...), custom_call_target="tpu_custom_call" | custom-call | flops 42949672960 | bytes 83886080 | tf_op jit(solution)/shard_map/pallas_call | solution.py:737
  435.2 5.5 reduce-scatter.7.cloned.1.call-done.refs_7_.refs_1_
  440.7 27.2 %shard_map.250 = (bf16[384,2048]{1,0:T(8,128)(2,1)}, bf16[384,2048]{1,0:T(8,128)(2,1)}, bf16[384,2048]{1,0:T(8,128)(2,1)}, bf16[384,2048]{1,0:T(8,128)(2,1)}, bf...) custom-call(s32[8]{0:T(128)} %copy-done.29, ...), custom_call_target="tpu_custom_call", output_to_operand_aliasing={{0}: (8, {}), {1}: (9, {}), {2}: (10, {}), {3}: (11, {}), {... | custom-call | flops 42949672960 | bytes 83886080 | tf_op jit(solution)/shard_map/pallas_call | solution.py:737
  487.0 15.9 %fusion.5.refs_0_ = bf16[2048,768]{1,0:T(8,128)(2,1)} fusion(bf16[3072,2048]{1,0:T(8,128)(2,1)} %get-tuple-element.174, bf16[3072,1536]{1,0:T(8,128)(2,1)} %shard_map.251), kind=kOutput, calls=%fused_computation.10 | convolution fusion | flops 9665249280 | bytes 20447232 | tf_op jit(solution)/shard_map/dot_general | solution.py:31
  502.9 8.1 collective-permute-done.45
  518.1 16.0 %fusion.8.refs_1_.refs_0_ = bf16[2048,768]{1,0:T(8,128)(2,1)} fusion(bf16[3072,2048]{1,0:T(8,128)(2,1)} %get-tuple-element.174, bf16[3072,1536]{1,0:T(8,128)(2,1)} %shard_map.251), kind=kOutput, calls=%fused_computation.11 | convolution fusion | flops 9665249280 | bytes 20447232 | tf_op jit(solution)/shard_map/dot_general | solution.py:31
  538.7 3.3 multiply_reduce_fusion
  542.0 4.9 fusion.44
  549.2 26.4 %reduce-scatter.11.cloned.1.call-done.refs_12_.refs_1_ = bf16[512,768]{1,0:T(8,128)(2,1)} async-done(((bf16[2048,768]{1,0:T(8,128)(2,1)}), bf16[512,768]{1,0:T(8,128)(2,1)}) %reduce-scatter.11.cloned.1.call-update) | async-done | bytes 786448 | tf_op jit(solution)/shard_map/reduce_scatter | solution.py:74
  576.3 13.5 %shard_map.256 = (bf16[384,2048]{1,0:T(8,128)(2,1)S(1)}, bf16[384,2048]{1,0:T(8,128)(2,1)}, bf16[3072,512]{1,0:T(8,128)(2,1)}, bf16[3072,128]{1,0:T(8,128)(2,1)S...) custom-call(s32[8]{0:T(128)S(1)} %copy-done.32, ...), custom_call_target="tpu_custom_call" | custom-call | flops 12884901888 | bytes 20971520 | tf_op jit(solution)/shard_map/pallas_call | solution.py:461
  592.2 7.8 collective-permute-start.53
  610.3 11.3 %collective-permute-done.66 = bf16[192,2048]{1,0:T(8,128)(2,1)} collective-permute-done((bf16[192,2048]{1,0:T(8,128)(2,1)}, bf16[192,2048]{1,0:T(8,128)(2,1)}, u32[]{:S(2)}, u32[]{:S(2)}) %collective-permute-start.66) | collective-permute-done | bytes 786464 | tf_op jit(solution)/shard_map/ppermute | solution.py:51
  639.3 10.4 %collective-permute-done.56.refs_1_ = bf16[192,2048]{1,0:T(8,128)(2,1)S(1)} collective-permute-done((bf16[192,2048]{1,0:T(8,128)(2,1)S(1)}, bf16[192,2048]{1,0:T(8,128)(2,1)S(1)}, u32[]{:S(2)}, u32[]{:S(2)}) %collective-permute-start.56) | collective-permute-done | bytes 786464 | tf_op jit(solution)/shard_map/ppermute | solution.py:51
  659.0 18.1 %shard_map.259 = (bf16[384,2048]{1,0:T(8,128)(2,1)S(1)}, bf16[384,2048]{1,0:T(8,128)(2,1)}, bf16[3072,512]{1,0:T(8,128)(2,1)}, bf16[3072,128]{1,0:T(8,128)(2,1)S...) custom-call(s32[8]{0:T(128)S(1)} %copy-done.32, ...), custom_call_target="tpu_custom_call", output_to_operand_aliasing={{2}: (13, {}), {3}: (14, {}), {4}: (15, {})} | custom-call | flops 12884901888 | bytes 20971520 | tf_op jit(solution)/shard_map/pallas_call | solution.py:461
  683.6 19.6 %shard_map.261 = (bf16[384,2048]{1,0:T(8,128)(2,1)S(1)}, bf16[384,2048]{1,0:T(8,128)(2,1)}, bf16[3072,512]{1,0:T(8,128)(2,1)}, bf16[3072,128]{1,0:T(8,128)(2,1)S...) custom-call(s32[8]{0:T(128)S(1)} %copy-done.33, ...), custom_call_target="tpu_custom_call", output_to_operand_aliasing={{2}: (13, {}), {3}: (14, {}), {4}: (15, {})} | custom-call | flops 12884901888 | bytes 20971520 | tf_op jit(solution)/shard_map/pallas_call | solution.py:461
  703.8 2.8 convert_add_fusion.11
  706.8 2.8 convert_add_fusion.12
  719.7 23.0 %shard_map.263 = (bf16[384,2048]{1,0:T(8,128)(2,1)S(1)}, bf16[384,2048]{1,0:T(8,128)(2,1)}, bf16[3072,512]{1,0:T(8,128)(2,1)}, bf16[3072,128]{1,0:T(8,128)(2,1)S...) custom-call(s32[8]{0:T(128)S(1)} %copy-done.34, ...), custom_call_target="tpu_custom_call", output_to_operand_aliasing={{2}: (13, {}), {3}: (14, {}), {4}: (15, {})} | custom-call | flops 12884901888 | bytes 20971520 | tf_op jit(solution)/shard_map/pallas_call | solution.py:461
  743.6 11.6 %convolution_convert_fusion.1 = bf16[2048,512]{1,0:T(8,128)(2,1)} fusion(bf16[3072,2048]{1,0:T(8,128)(2,1)} %get-tuple-element.176.refs_6_, bf16[3072,512]{1,0:T(8,128)(2,1)} %get-tuple-element.207), kind=kOutput, calls=%fused_computation.43 | convolution fusion | flops 6443499520 | bytes 17825792 | tf_op jit(solution)/shard_map/dot_general | solution.py:31
  755.3 7.2 fusion.52
  765.7 3.2 fusion.20
  777.5 6.6 convolution_convert_fusion.2
  785.0 4.8 collective-permute-done.74
  792.9 6.1 collective-permute-start.76
  801.3 12.9 %collective-permute-done.72 = bf16[192,2048]{1,0:T(8,128)(2,1)S(1)} collective-permute-done((bf16[192,2048]{1,0:T(8,128)(2,1)S(1)}, bf16[192,2048]{1,0:T(8,128)(2,1)S(1)}, u32[]{:S(2)}, u32[]{:S(2)}) %collective-permute-start.72) | collective-permute-done | bytes 786464 | tf_op jit(solution)/shard_map/ppermute | solution.py:51
  815.7 4.7 fusion.11
  822.8 7.6 all-to-all-start.3
  830.5 5.1 fusion.19
  842.1 14.8 %collective-permute-done.78 = bf16[1,64,2048]{2,1,0:T(8,128)(2,1)S(1)} collective-permute-done((bf16[1,64,2048]{2,1,0:T(8,128)(2,1)S(1)}, bf16[1,64,2048]{2,1,0:T(8,128)(2,1)S(1)}, u32[]{:S(2)}, u32[]{:S(2)}) %collective-permute-start.78) | collective-permute-done | bytes 262176 | tf_op jit(solution)/shard_map/ppermute | solution.py:51
  858.0 10.4 %all-to-all-start.2 = ((bf16[8,72,512]{2,1,0:T(8,128)(2,1)}), bf16[8,72,512]{2,1,0:T(8,128)(2,1)}, u32[]{:S(2)}, u32[]{:S(2)}) async-start(bf16[8,72,512]{2,1,0:T(8,128)(2,1)} %bitcast.104), calls=%async_computation.7 | async-start | bytes 1179648 | tf_op jit(solution)/shard_map/all_to_all | solution.py:62
  868.4 4.4 fusion.15
  872.8 3.4 slice_convert_fusion.8
  876.2 2.7 reshape.311
  881.5 3.0 reshape.308
  884.4 2.7 reshape.312
  889.8 3.0 reshape.309
  (541 shorter events, 230.0 us)
Async XLA Ops:
  7.3 90.6 %all-gather.15.cloned.1.call-start = ((), (), s32[]{:S(2)}) async-start(), calls=%async_computation.20 | async-start | bytes 1310720 | tf_op jit(solution)/shard_map/all_gather | solution.py:68
  9.5 122.7 %all-gather.7.cloned.1.call-start = ((), (), s32[]{:S(2)}) async-start(), calls=%async_computation.10 | async-start | bytes 2949120 | tf_op jit(solution)/shard_map/all_gather | solution.py:68
  33.6 21.6 %all-to-all-start.1 = ((bf16[8,64,1536]{2,1,0:T(8,128)(2,1)}), bf16[8,64,1536]{2,1,0:T(8,128)(2,1)S(1)}, u32[]{:S(2)}, u32[]{:S(2)}) async-start(bf16[8,64,1536]{2,1,0:T(8,128)(2,1)} %pad_maximum_fusion), calls=%async_computation.1 | async-start | bytes 3145728 | tf_op jit(solution)/shard_map/all_to_all | solution.py:62
  37.7 185.9 %all-gather.9.cloned.1.call-start = ((), (), s32[]{:S(2)}) async-start(), calls=%async_computation.11 | async-start | bytes 3932160 | tf_op jit(solution)/shard_map/all_gather | solution.py:68
  37.7 53.0 %collective-permute-start.5 = (bf16[384,2048]{1,0:T(8,128)(2,1)}, bf16[384,2048]{1,0:T(8,128)(2,1)}, u32[]{:S(2)}, u32[]{:S(2)}) collective-permute-start(bf16[384,2048]{1,0:T(8,128)(2,1)} %refs_1_.1), channel_id=1, source_target_pairs={{0,4},{1,5},{2,6},{3,7},{4,0},{5,1},{6,2},{7,3},{8,12},{9,13},{10,... | collective-permute-start | bytes 4718600 | tf_op jit(solution)/shard_map/ppermute | solution.py:51
  39.1 54.5 %collective-permute-start.7 = (bf16[384,2048]{1,0:T(8,128)(2,1)}, bf16[384,2048]{1,0:T(8,128)(2,1)}, u32[]{:S(2)}, u32[]{:S(2)}) collective-permute-start(bf16[384,2048]{1,0:T(8,128)(2,1)} %refs_1_.1), channel_id=1, source_target_pairs={{0,2},{1,3},{2,0},{3,1},{4,6},{5,7},{6,4},{7,5},{8,10},{9,11},{10,... | collective-permute-start | bytes 4718600 | tf_op jit(solution)/shard_map/ppermute | solution.py:51
  56.9 241.1 %all-gather.11.cloned.1.call-start = ((), (), s32[]{:S(2)}) async-start(), calls=%async_computation.12 | async-start | bytes 3932160 | tf_op jit(solution)/shard_map/all_gather | solution.py:68
  100.1 25.9 %collective-permute-start.1 = (bf16[1,64,2048]{2,1,0:T(8,128)(2,1)}, bf16[1,64,2048]{2,1,0:T(8,128)(2,1)}, u32[]{:S(2)}, u32[]{:S(2)}) collective-permute-start(bf16[1,64,2048]{2,1,0:T(8,128)(2,1)} %get-tuple-element.249), channel_id=1, source_target_pairs={{0,0},{1,2},{2,4},{3,6},{4,1},{5,3},{6,5},{7,7},{8,8},{9,10},{10,1... | collective-permute-start | bytes 786440 | tf_op jit(solution)/shard_map/ppermute | solution.py:51
  114.3 23.8 %collective-permute-start.9 = (bf16[384,2048]{1,0:T(8,128)(2,1)}, bf16[384,2048]{1,0:T(8,128)(2,1)}, u32[]{:S(2)}, u32[]{:S(2)}) collective-permute-start(bf16[384,2048]{1,0:T(8,128)(2,1)} %constant_dynamic-update-slice_fusion.refs_1_), channel_id=1, source_target_pairs={{0,1},{1,0},{2,3},{3,2},{4,5},{5,4},{6,7},{7,6},{8,9},{9,8},{10,11... | collective-permute-start | bytes 4718600 | tf_op jit(solution)/shard_map/ppermute | solution.py:51
  150.1 209.5 %all-gather.13.cloned.1.call-start = ((), (), s32[]{:S(2)}) async-start(), calls=%async_computation.13 | async-start | bytes 3932160 | tf_op jit(solution)/shard_map/all_gather | solution.py:68
  150.6 28.5 %collective-permute-start.14 = (bf16[384,2048]{1,0:T(8,128)(2,1)}, bf16[384,2048]{1,0:T(8,128)(2,1)}, u32[]{:S(2)}, u32[]{:S(2)}) collective-permute-start(bf16[384,2048]{1,0:T(8,128)(2,1)} %get-tuple-element.118), channel_id=1, source_target_pairs={{0,1},{1,0},{2,3},{3,2},{4,5},{5,4},{6,7},{7,6},{8,9},{9,8},{10,11... | collective-permute-start | bytes 4718600 | tf_op jit(solution)/shard_map/ppermute | solution.py:51
  151.1 73.0 %collective-permute-start = (bf16[384,2048]{1,0:T(8,128)(2,1)}, bf16[384,2048]{1,0:T(8,128)(2,1)}, u32[]{:S(2)}, u32[]{:S(2)}) collective-permute-start(bf16[384,2048]{1,0:T(8,128)(2,1)} %refs_1_.1), channel_id=1, source_target_pairs={{0,1},{1,0},{2,3},{3,2},{4,5},{5,4},{6,7},{7,6},{8,9},{9,8},{10,11... | collective-permute-start | bytes 4718600 | tf_op jit(solution)/shard_map/ppermute | solution.py:51
  151.2 31.3 %collective-permute-start.13 = (bf16[384,2048]{1,0:T(8,128)(2,1)}, bf16[384,2048]{1,0:T(8,128)(2,1)}, u32[]{:S(2)}, u32[]{:S(2)}) collective-permute-start(bf16[384,2048]{1,0:T(8,128)(2,1)} %collective-permute-done.5.refs_1_), channel_id=1, source_target_pairs={{0,1},{1,0},{2,3},{3,2},{4,5},{5,4},{6,7},{7,6},{8,9},{9,8},{10,11... | collective-permute-start | bytes 4718600 | tf_op jit(solution)/shard_map/ppermute | solution.py:51
  177.3 45.1 %collective-permute-start.10 = (bf16[384,2048]{1,0:T(8,128)(2,1)}, bf16[384,2048]{1,0:T(8,128)(2,1)}, u32[]{:S(2)}, u32[]{:S(2)}) collective-permute-start(bf16[384,2048]{1,0:T(8,128)(2,1)} %broadcast_select_fusion.refs_0_.refs_9_), channel_id=1, source_target_pairs={{0,1},{1,0},{2,3},{3,2},{4,5},{5,4},{6,7},{7,6},{8,9},{9,8},{10,11... | collective-permute-start | bytes 4718600 | tf_op jit(solution)/shard_map/ppermute | solution.py:51
  179.1 261.6 %reduce-scatter.7.cloned.1.call-start = ((), (), s32[]{:S(2)}) async-start(), calls=%async_computation.14 | async-start | bytes 1966080 | tf_op jit(solution)/shard_map/reduce_scatter | solution.py:74
  179.1 41.1 %collective-permute-start.11 = (bf16[384,2048]{1,0:T(8,128)(2,1)}, bf16[384,2048]{1,0:T(8,128)(2,1)S(1)}, u32[]{:S(2)}, u32[]{:S(2)}) collective-permute-start(bf16[384,2048]{1,0:T(8,128)(2,1)} %broadcast_select_fusion.refs_0_.refs_9_), channel_id=1, source_target_pairs={{0,2},{1,3},{2,0},{3,1},{4,6},{5,7},{6,4},{7,5},{8,10},{9,11},{10,... | collective-permute-start | bytes 4718600 | tf_op jit(solution)/shard_map/ppermute | solution.py:51
  182.5 36.2 %collective-permute-start.12 = (bf16[384,2048]{1,0:T(8,128)(2,1)}, bf16[384,2048]{1,0:T(8,128)(2,1)S(1)}, u32[]{:S(2)}, u32[]{:S(2)}) collective-permute-start(bf16[384,2048]{1,0:T(8,128)(2,1)} %broadcast_select_fusion.refs_0_.refs_9_), channel_id=1, source_target_pairs={{0,4},{1,5},{2,6},{3,7},{4,0},{5,1},{6,2},{7,3},{8,12},{9,13},{10,... | collective-permute-start | bytes 4718600 | tf_op jit(solution)/shard_map/ppermute | solution.py:51
  194.9 50.0 %collective-permute-start.19 = (bf16[384,2048]{1,0:T(8,128)(2,1)}, bf16[384,2048]{1,0:T(8,128)(2,1)}, u32[]{:S(2)}, u32[]{:S(2)}) collective-permute-start(bf16[384,2048]{1,0:T(8,128)(2,1)} %get-tuple-element.136), channel_id=1, source_target_pairs={{0,1},{1,0},{2,3},{3,2},{4,5},{5,4},{6,7},{7,6},{8,9},{9,8},{10,11... | collective-permute-start | bytes 4718600 | tf_op jit(solution)/shard_map/ppermute | solution.py:51
  218.7 23.8 %collective-permute-start.22 = (bf16[192,2048]{1,0:T(8,128)(2,1)}, bf16[192,2048]{1,0:T(8,128)(2,1)}, u32[]{:S(2)}, u32[]{:S(2)}) collective-permute-start(bf16[192,2048]{1,0:T(8,128)(2,1)} %get-tuple-element.241), channel_id=1, source_target_pairs={{0,4},{1,5},{2,6},{3,7},{4,0},{5,1},{6,2},{7,3},{8,12},{9,13},{10,... | collective-permute-start | bytes 2359304 | tf_op jit(solution)/shard_map/ppermute | solution.py:51
  220.2 26.9 %collective-permute-start.20 = (bf16[192,2048]{1,0:T(8,128)(2,1)}, bf16[192,2048]{1,0:T(8,128)(2,1)}, u32[]{:S(2)}, u32[]{:S(2)}) collective-permute-start(bf16[192,2048]{1,0:T(8,128)(2,1)} %get-tuple-element.240), channel_id=1, source_target_pairs={{0,2},{1,3},{2,0},{3,1},{4,6},{5,7},{6,4},{7,5},{8,10},{9,11},{10,... | collective-permute-start | bytes 2359304 | tf_op jit(solution)/shard_map/ppermute | solution.py:51
  222.4 32.4 %collective-permute-start.27 = (bf16[192,2048]{1,0:T(8,128)(2,1)}, bf16[192,2048]{1,0:T(8,128)(2,1)}, u32[]{:S(2)}, u32[]{:S(2)}) collective-permute-start(bf16[192,2048]{1,0:T(8,128)(2,1)} %slice.301), channel_id=1, source_target_pairs={{0,2},{1,3},{2,0},{3,1},{4,6},{5,7},{6,4},{7,5},{8,10},{9,11},{10,... | collective-permute-start | bytes 2359304 | tf_op jit(solution)/shard_map/ppermute | solution.py:51
  224.2 31.8 %collective-permute-start.28 = (bf16[192,2048]{1,0:T(8,128)(2,1)}, bf16[192,2048]{1,0:T(8,128)(2,1)S(1)}, u32[]{:S(2)}, u32[]{:S(2)}) collective-permute-start(bf16[192,2048]{1,0:T(8,128)(2,1)} %slice.302), channel_id=1, source_target_pairs={{0,4},{1,5},{2,6},{3,7},{4,0},{5,1},{6,2},{7,3},{8,12},{9,13},{10,... | collective-permute-start | bytes 2359304 | tf_op jit(solution)/shard_map/ppermute | solution.py:51
  242.5 48.6 %collective-permute-start.16 = (bf16[384,2048]{1,0:T(8,128)(2,1)S(1)}, bf16[384,2048]{1,0:T(8,128)(2,1)S(1)}, u32[]{:S(2)}, u32[]{:S(2)}) collective-permute-start(bf16[384,2048]{1,0:T(8,128)(2,1)S(1)} %get-tuple-element.132), channel_id=1, source_target_pairs={{0,1},{1,0},{2,3},{3,2},{4,5},{5,4},{6,7},{7,6},{8,9},{9,8},{10,11... | collective-permute-start | bytes 4718600 | tf_op jit(solution)/shard_map/ppermute | solution.py:51
  245.0 26.6 %collective-permute-start.23 = (bf16[192,2048]{1,0:T(8,128)(2,1)S(1)}, bf16[192,2048]{1,0:T(8,128)(2,1)S(1)}, u32[]{:S(2)}, u32[]{:S(2)}) collective-permute-start(bf16[192,2048]{1,0:T(8,128)(2,1)S(1)} %fusion.27), channel_id=1, source_target_pairs={{0,2},{1,3},{2,0},{3,1},{4,6},{5,7},{6,4},{7,5},{8,10},{9,11},{10,... | collective-permute-start | bytes 2359304 | tf_op jit(solution)/shard_map/ppermute | solution.py:51
  247.1 29.2 %collective-permute-start.24 = (bf16[192,2048]{1,0:T(8,128)(2,1)S(1)}, bf16[192,2048]{1,0:T(8,128)(2,1)S(1)}, u32[]{:S(2)}, u32[]{:S(2)}) collective-permute-start(bf16[192,2048]{1,0:T(8,128)(2,1)S(1)} %slice.409), channel_id=1, source_target_pairs={{0,4},{1,5},{2,6},{3,7},{4,0},{5,1},{6,2},{7,3},{8,12},{9,13},{10,... | collective-permute-start | bytes 2359304 | tf_op jit(solution)/shard_map/ppermute | solution.py:51
  254.7 33.6 %collective-permute-start.18 = (bf16[192,2048]{1,0:T(8,128)(2,1)S(1)}, bf16[192,2048]{1,0:T(8,128)(2,1)S(1)}, u32[]{:S(2)}, u32[]{:S(2)}) collective-permute-start(bf16[192,2048]{1,0:T(8,128)(2,1)S(1)} %copy-done.75), channel_id=1, source_target_pairs={{0,2},{1,3},{2,0},{3,1},{4,6},{5,7},{6,4},{7,5},{8,10},{9,11},{10,... | collective-permute-start | bytes 2359304 | tf_op jit(solution)/shard_map/ppermute | solution.py:51
  255.9 35.0 %collective-permute-start.21 = (bf16[192,2048]{1,0:T(8,128)(2,1)S(1)}, bf16[192,2048]{1,0:T(8,128)(2,1)S(1)}, u32[]{:S(2)}, u32[]{:S(2)}) collective-permute-start(bf16[192,2048]{1,0:T(8,128)(2,1)S(1)} %fusion.28), channel_id=1, source_target_pairs={{0,4},{1,5},{2,6},{3,7},{4,0},{5,1},{6,2},{7,3},{8,12},{9,13},{10,... | collective-permute-start | bytes 2359304 | tf_op jit(solution)/shard_map/ppermute | solution.py:51
  271.6 24.2 %collective-permute-start.25 = (bf16[384,2048]{1,0:T(8,128)(2,1)S(1)}, bf16[384,2048]{1,0:T(8,128)(2,1)S(1)}, u32[]{:S(2)}, u32[]{:S(2)}) collective-permute-start(bf16[384,2048]{1,0:T(8,128)(2,1)S(1)} %copy-done.45), channel_id=1, source_target_pairs={{0,1},{1,0},{2,3},{3,2},{4,5},{5,4},{6,7},{7,6},{8,9},{9,8},{10,11... | collective-permute-start | bytes 4718600 | tf_op jit(solution)/shard_map/ppermute | solution.py:51
  298.6 36.3 %collective-permute-start.33 = (bf16[384,2048]{1,0:T(8,128)(2,1)}, bf16[384,2048]{1,0:T(8,128)(2,1)}, u32[]{:S(2)}, u32[]{:S(2)}) collective-permute-start(bf16[384,2048]{1,0:T(8,128)(2,1)} %shard_map.245.refs_1_), channel_id=1, source_target_pairs={{0,4},{1,5},{2,6},{3,7},{4,0},{5,1},{6,2},{7,3},{8,12},{9,13},{10,... | collective-permute-start | bytes 4718600 | tf_op jit(solution)/shard_map/ppermute | solution.py:51
  299.6 37.8 %collective-permute-start.31 = (bf16[384,2048]{1,0:T(8,128)(2,1)}, bf16[384,2048]{1,0:T(8,128)(2,1)}, u32[]{:S(2)}, u32[]{:S(2)}) collective-permute-start(bf16[384,2048]{1,0:T(8,128)(2,1)} %shard_map.245.refs_1_), channel_id=1, source_target_pairs={{0,2},{1,3},{2,0},{3,1},{4,6},{5,7},{6,4},{7,5},{8,10},{9,11},{10,... | collective-permute-start | bytes 4718600 | tf_op jit(solution)/shard_map/ppermute | solution.py:51
  408.6 109.3 %reduce-scatter.9.cloned.1.call-start = ((), (), s32[]{:S(2)}) async-start(), calls=%async_computation.15 | async-start | bytes 1966080 | tf_op jit(solution)/shard_map/reduce_scatter | solution.py:74
  469.8 68.2 %collective-permute-start.38 = (bf16[384,2048]{1,0:T(8,128)(2,1)}, bf16[384,2048]{1,0:T(8,128)(2,1)}, u32[]{:S(2)}, u32[]{:S(2)}) collective-permute-start(bf16[384,2048]{1,0:T(8,128)(2,1)} %get-tuple-element.167), channel_id=1, source_target_pairs={{0,1},{1,0},{2,3},{3,2},{4,5},{5,4},{6,7},{7,6},{8,9},{9,8},{10,11... | collective-permute-start | bytes 4718600 | tf_op jit(solution)/shard_map/ppermute | solution.py:51
  470.0 105.7 %reduce-scatter.11.cloned.1.call-start = ((), (), s32[]{:S(2)}) async-start(), calls=%async_computation.16 | async-start | bytes 3932160 | tf_op jit(solution)/shard_map/reduce_scatter | solution.py:74
  475.1 59.6 %collective-permute-start.47 = (bf16[192,2048]{1,0:T(8,128)(2,1)}, bf16[192,2048]{1,0:T(8,128)(2,1)}, u32[]{:S(2)}, u32[]{:S(2)}) collective-permute-start(bf16[192,2048]{1,0:T(8,128)(2,1)} %slice.407), channel_id=1, source_target_pairs={{0,4},{1,5},{2,6},{3,7},{4,0},{5,1},{6,2},{7,3},{8,12},{9,13},{10,... | collective-permute-start | bytes 2359304 | tf_op jit(solution)/shard_map/ppermute | solution.py:51
  480.4 30.6 %collective-permute-start.45 = (bf16[192,2048]{1,0:T(8,128)(2,1)}, bf16[192,2048]{1,0:T(8,128)(2,1)}, u32[]{:S(2)}, u32[]{:S(2)}) collective-permute-start(bf16[192,2048]{1,0:T(8,128)(2,1)} %get-tuple-element.237), channel_id=1, source_target_pairs={{0,4},{1,5},{2,6},{3,7},{4,0},{5,1},{6,2},{7,3},{8,12},{9,13},{10,... | collective-permute-start | bytes 2359304 | tf_op jit(solution)/shard_map/ppermute | solution.py:51
  481.7 32.8 %collective-permute-start.43 = (bf16[192,2048]{1,0:T(8,128)(2,1)}, bf16[192,2048]{1,0:T(8,128)(2,1)}, u32[]{:S(2)}, u32[]{:S(2)}) collective-permute-start(bf16[192,2048]{1,0:T(8,128)(2,1)} %get-tuple-element.236), channel_id=1, source_target_pairs={{0,2},{1,3},{2,0},{3,1},{4,6},{5,7},{6,4},{7,5},{8,10},{9,11},{10,... | collective-permute-start | bytes 2359304 | tf_op jit(solution)/shard_map/ppermute | solution.py:51
  486.6 49.9 %collective-permute-start.40 = (bf16[192,2048]{1,0:T(8,128)(2,1)S(1)}, bf16[192,2048]{1,0:T(8,128)(2,1)S(1)}, u32[]{:S(2)}, u32[]{:S(2)}) collective-permute-start(bf16[192,2048]{1,0:T(8,128)(2,1)S(1)} %slice.408), channel_id=1, source_target_pairs={{0,2},{1,3},{2,0},{3,1},{4,6},{5,7},{6,4},{7,5},{8,10},{9,11},{10,... | collective-permute-start | bytes 2359304 | tf_op jit(solution)/shard_map/ppermute | solution.py:51
  513.3 21.4 %collective-permute-start.46 = (bf16[192,2048]{1,0:T(8,128)(2,1)}, bf16[192,2048]{1,0:T(8,128)(2,1)}, u32[]{:S(2)}, u32[]{:S(2)}) collective-permute-start(bf16[192,2048]{1,0:T(8,128)(2,1)} %fusion.25), channel_id=1, source_target_pairs={{0,2},{1,3},{2,0},{3,1},{4,6},{5,7},{6,4},{7,5},{8,10},{9,11},{10,... | collective-permute-start | bytes 2359304 | tf_op jit(solution)/shard_map/ppermute | solution.py:51
  517.9 161.7 %reduce-scatter.13.cloned.1.call-start = ((), (), s32[]{:S(2)}) async-start(), calls=%async_computation.17 | async-start | bytes 3932160 | tf_op jit(solution)/shard_map/reduce_scatter | solution.py:74
  546.9 28.8 %collective-permute-start.48 = (bf16[384,2048]{1,0:T(8,128)(2,1)}, bf16[384,2048]{1,0:T(8,128)(2,1)}, u32[]{:S(2)}, u32[]{:S(2)}) collective-permute-start(bf16[384,2048]{1,0:T(8,128)(2,1)} %shard_map.255.refs_1_), channel_id=1, source_target_pairs={{0,1},{1,0},{2,3},{3,2},{4,5},{5,4},{6,7},{7,6},{8,9},{9,8},{10,11... | collective-permute-start | bytes 4718600 | tf_op jit(solution)/shard_map/ppermute | solution.py:51
  548.9 51.0 %collective-permute-start.60 = (bf16[384,2048]{1,0:T(8,128)(2,1)}, bf16[384,2048]{1,0:T(8,128)(2,1)}, u32[]{:S(2)}, u32[]{:S(2)}) collective-permute-start(bf16[384,2048]{1,0:T(8,128)(2,1)} %shard_map.255.refs_1_), channel_id=1, source_target_pairs={{0,2},{1,3},{2,0},{3,1},{4,6},{5,7},{6,4},{7,5},{8,10},{9,11},{10,... | collective-permute-start | bytes 4718600 | tf_op jit(solution)/shard_map/ppermute | solution.py:51
  549.2 50.7 %collective-permute-start.61 = (bf16[384,2048]{1,0:T(8,128)(2,1)}, bf16[384,2048]{1,0:T(8,128)(2,1)}, u32[]{:S(2)}, u32[]{:S(2)}) collective-permute-start(bf16[384,2048]{1,0:T(8,128)(2,1)} %shard_map.255.refs_1_), channel_id=1, source_target_pairs={{0,4},{1,5},{2,6},{3,7},{4,0},{5,1},{6,2},{7,3},{8,12},{9,13},{10,... | collective-permute-start | bytes 4718600 | tf_op jit(solution)/shard_map/ppermute | solution.py:51
  575.7 281.4 %reduce-scatter.15.cloned.1.call-start = ((), (), s32[]{:S(2)}) async-start(), calls=%async_computation.18 | async-start | bytes 2949120 | tf_op jit(solution)/shard_map/reduce_scatter | solution.py:74
  592.2 34.9 %collective-permute-start.53 = (bf16[384,2048]{1,0:T(8,128)(2,1)}, bf16[384,2048]{1,0:T(8,128)(2,1)S(1)}, u32[]{:S(2)}, u32[]{:S(2)}) collective-permute-start(bf16[384,2048]{1,0:T(8,128)(2,1)} %get-tuple-element.187), channel_id=1, source_target_pairs={{0,1},{1,0},{2,3},{3,2},{4,5},{5,4},{6,7},{7,6},{8,9},{9,8},{10,11... | collective-permute-start | bytes 4718600 | tf_op jit(solution)/shard_map/ppermute | solution.py:51
  607.5 24.5 %collective-permute-start.52 = (bf16[384,2048]{1,0:T(8,128)(2,1)}, bf16[384,2048]{1,0:T(8,128)(2,1)}, u32[]{:S(2)}, u32[]{:S(2)}) collective-permute-start(bf16[384,2048]{1,0:T(8,128)(2,1)} %get-tuple-element.185), channel_id=1, source_target_pairs={{0,1},{1,0},{2,3},{3,2},{4,5},{5,4},{6,7},{7,6},{8,9},{9,8},{10,11... | collective-permute-start | bytes 4718600 | tf_op jit(solution)/shard_map/ppermute | solution.py:51
  610.3 47.5 %collective-permute-start.62 = (bf16[384,2048]{1,0:T(8,128)(2,1)}, bf16[384,2048]{1,0:T(8,128)(2,1)S(1)}, u32[]{:S(2)}, u32[]{:S(2)}) collective-permute-start(bf16[384,2048]{1,0:T(8,128)(2,1)} %get-tuple-element.190.refs_1_), channel_id=1, source_target_pairs={{0,1},{1,0},{2,3},{3,2},{4,5},{5,4},{6,7},{7,6},{8,9},{9,8},{10,11... | collective-permute-start | bytes 4718600 | tf_op jit(solution)/shard_map/ppermute | solution.py:51
  626.6 51.1 %collective-permute-start.68 = (bf16[384,2048]{1,0:T(8,128)(2,1)}, bf16[384,2048]{1,0:T(8,128)(2,1)}, u32[]{:S(2)}, u32[]{:S(2)}) collective-permute-start(bf16[384,2048]{1,0:T(8,128)(2,1)} %constant_dynamic-update-slice_fusion.6.refs_1_), channel_id=1, source_target_pairs={{0,1},{1,0},{2,3},{3,2},{4,5},{5,4},{6,7},{7,6},{8,9},{9,8},{10,11... | collective-permute-start | bytes 4718600 | tf_op jit(solution)/shard_map/ppermute | solution.py:51
  635.0 68.2 %collective-permute-start.58 = (bf16[192,2048]{1,0:T(8,128)(2,1)}, bf16[192,2048]{1,0:T(8,128)(2,1)}, u32[]{:S(2)}, u32[]{:S(2)}) collective-permute-start(bf16[192,2048]{1,0:T(8,128)(2,1)} %slice.405), channel_id=1, source_target_pairs={{0,4},{1,5},{2,6},{3,7},{4,0},{5,1},{6,2},{7,3},{8,12},{9,13},{10,... | collective-permute-start | bytes 2359304 | tf_op jit(solution)/shard_map/ppermute | solution.py:51
  649.6 57.1 %collective-permute-start.51 = (bf16[192,2048]{1,0:T(8,128)(2,1)}, bf16[192,2048]{1,0:T(8,128)(2,1)}, u32[]{:S(2)}, u32[]{:S(2)}) collective-permute-start(bf16[192,2048]{1,0:T(8,128)(2,1)} %slice.406), channel_id=1, source_target_pairs={{0,2},{1,3},{2,0},{3,1},{4,6},{5,7},{6,4},{7,5},{8,10},{9,11},{10,... | collective-permute-start | bytes 2359304 | tf_op jit(solution)/shard_map/ppermute | solution.py:51
  654.8 48.6 %collective-permute-start.57 = (bf16[192,2048]{1,0:T(8,128)(2,1)}, bf16[192,2048]{1,0:T(8,128)(2,1)}, u32[]{:S(2)}, u32[]{:S(2)}) collective-permute-start(bf16[192,2048]{1,0:T(8,128)(2,1)} %fusion.23), channel_id=1, source_target_pairs={{0,2},{1,3},{2,0},{3,1},{4,6},{5,7},{6,4},{7,5},{8,10},{9,11},{10,... | collective-permute-start | bytes 2359304 | tf_op jit(solution)/shard_map/ppermute | solution.py:51
  657.8 49.0 %collective-permute-start.55 = (bf16[192,2048]{1,0:T(8,128)(2,1)}, bf16[192,2048]{1,0:T(8,128)(2,1)}, u32[]{:S(2)}, u32[]{:S(2)}) collective-permute-start(bf16[192,2048]{1,0:T(8,128)(2,1)} %fusion.24), channel_id=1, source_target_pairs={{0,4},{1,5},{2,6},{3,7},{4,0},{5,1},{6,2},{7,3},{8,12},{9,13},{10,... | collective-permute-start | bytes 2359304 | tf_op jit(solution)/shard_map/ppermute | solution.py:51
  677.7 31.8 %collective-permute-start.63 = (bf16[384,2048]{1,0:T(8,128)(2,1)}, bf16[384,2048]{1,0:T(8,128)(2,1)}, u32[]{:S(2)}, u32[]{:S(2)}) collective-permute-start(bf16[384,2048]{1,0:T(8,128)(2,1)} %get-tuple-element.195), channel_id=1, source_target_pairs={{0,1},{1,0},{2,3},{3,2},{4,5},{5,4},{6,7},{7,6},{8,9},{9,8},{10,11... | collective-permute-start | bytes 4718600 | tf_op jit(solution)/shard_map/ppermute | solution.py:51
  706.7 109.0 %collective-permute-start.59 = (bf16[384,2048]{1,0:T(8,128)(2,1)}, bf16[384,2048]{1,0:T(8,128)(2,1)}, u32[]{:S(2)}, u32[]{:S(2)}) collective-permute-start(bf16[384,2048]{1,0:T(8,128)(2,1)} %get-tuple-element.189), channel_id=1, source_target_pairs={{0,1},{1,0},{2,3},{3,2},{4,5},{5,4},{6,7},{7,6},{8,9},{9,8},{10,11... | collective-permute-start | bytes 4718600 | tf_op jit(solution)/shard_map/ppermute | solution.py:51
  712.6 86.7 %collective-permute-start.64 = (bf16[192,2048]{1,0:T(8,128)(2,1)}, bf16[192,2048]{1,0:T(8,128)(2,1)}, u32[]{:S(2)}, u32[]{:S(2)}) collective-permute-start(bf16[192,2048]{1,0:T(8,128)(2,1)} %slice.404), channel_id=1, source_target_pairs={{0,2},{1,3},{2,0},{3,1},{4,6},{5,7},{6,4},{7,5},{8,10},{9,11},{10,... | collective-permute-start | bytes 2359304 | tf_op jit(solution)/shard_map/ppermute | solution.py:51
  742.7 29.5 %collective-permute-start.70 = (bf16[384,2048]{1,0:T(8,128)(2,1)}, bf16[384,2048]{1,0:T(8,128)(2,1)}, u32[]{:S(2)}, u32[]{:S(2)}) collective-permute-start(bf16[384,2048]{1,0:T(8,128)(2,1)} %get-tuple-element.206), channel_id=1, source_target_pairs={{0,1},{1,0},{2,3},{3,2},{4,5},{5,4},{6,7},{7,6},{8,9},{9,8},{10,11... | collective-permute-start | bytes 4718600 | tf_op jit(solution)/shard_map/ppermute | solution.py:51
  743.6 25.3 %collective-permute-start.73 = (bf16[192,2048]{1,0:T(8,128)(2,1)}, bf16[192,2048]{1,0:T(8,128)(2,1)}, u32[]{:S(2)}, u32[]{:S(2)}) collective-permute-start(bf16[192,2048]{1,0:T(8,128)(2,1)} %get-tuple-element.233), channel_id=1, source_target_pairs={{0,4},{1,5},{2,6},{3,7},{4,0},{5,1},{6,2},{7,3},{8,12},{9,13},{10,... | collective-permute-start | bytes 2359304 | tf_op jit(solution)/shard_map/ppermute | solution.py:51
  743.6 32.3 %collective-permute-start.71 = (bf16[192,2048]{1,0:T(8,128)(2,1)}, bf16[192,2048]{1,0:T(8,128)(2,1)}, u32[]{:S(2)}, u32[]{:S(2)}) collective-permute-start(bf16[192,2048]{1,0:T(8,128)(2,1)} %get-tuple-element.232), channel_id=1, source_target_pairs={{0,2},{1,3},{2,0},{3,1},{4,6},{5,7},{6,4},{7,5},{8,10},{9,11},{10,... | collective-permute-start | bytes 2359304 | tf_op jit(solution)/shard_map/ppermute | solution.py:51
  777.4 36.9 %collective-permute-start.72 = (bf16[192,2048]{1,0:T(8,128)(2,1)S(1)}, bf16[192,2048]{1,0:T(8,128)(2,1)S(1)}, u32[]{:S(2)}, u32[]{:S(2)}) collective-permute-start(bf16[192,2048]{1,0:T(8,128)(2,1)S(1)} %fusion.22), channel_id=1, source_target_pairs={{0,4},{1,5},{2,6},{3,7},{4,0},{5,1},{6,2},{7,3},{8,12},{9,13},{10,... | collective-permute-start | bytes 2359304 | tf_op jit(solution)/shard_map/ppermute | solution.py:51
  789.9 40.6 %collective-permute-start.49 = (bf16[384,2048]{1,0:T(8,128)(2,1)}, bf16[384,2048]{1,0:T(8,128)(2,1)}, u32[]{:S(2)}, u32[]{:S(2)}) collective-permute-start(bf16[384,2048]{1,0:T(8,128)(2,1)} %get-tuple-element.181), channel_id=1, source_target_pairs={{0,1},{1,0},{2,3},{3,2},{4,5},{5,4},{6,7},{7,6},{8,9},{9,8},{10,11... | collective-permute-start | bytes 4718600 | tf_op jit(solution)/shard_map/ppermute | solution.py:51
  792.9 47.2 %collective-permute-start.76 = (bf16[1,64,2048]{2,1,0:T(8,128)(2,1)}, bf16[1,64,2048]{2,1,0:T(8,128)(2,1)}, u32[]{:S(2)}, u32[]{:S(2)}) collective-permute-start(bf16[1,64,2048]{2,1,0:T(8,128)(2,1)} %get-tuple-element.245), channel_id=1, source_target_pairs={{0,0},{2,1},{4,2},{6,3},{1,4},{3,5},{5,6},{7,7},{8,8},{10,9},{12,1... | collective-permute-start | bytes 786440 | tf_op jit(solution)/shard_map/ppermute | solution.py:51
  799.3 41.9 %collective-permute-start.77 = (bf16[1,64,2048]{2,1,0:T(8,128)(2,1)}, bf16[1,64,2048]{2,1,0:T(8,128)(2,1)}, u32[]{:S(2)}, u32[]{:S(2)}) collective-permute-start(bf16[1,64,2048]{2,1,0:T(8,128)(2,1)} %get-tuple-element.244), channel_id=1, source_target_pairs={{2,0},{4,1},{6,2},{0,3},{3,4},{5,5},{7,6},{1,7},{10,8},{12,9},{14,... | collective-permute-start | bytes 786440 | tf_op jit(solution)/shard_map/ppermute | solution.py:51
  822.8 35.3 %all-to-all-start.3 = ((bf16[8,64,1536]{2,1,0:T(8,128)(2,1)}), bf16[8,64,1536]{2,1,0:T(8,128)(2,1)}, u32[]{:S(2)}, u32[]{:S(2)}) async-start(bf16[8,64,1536]{2,1,0:T(8,128)(2,1)} %bitcast.103), calls=%async_computation.9 | async-start | bytes 3145728 | tf_op jit(solution)/shard_map/all_to_all | solution.py:62
  830.4 68.6 %reduce-scatter.17.cloned.1.call-start = ((), (), s32[]{:S(2)}) async-start(), calls=%async_computation.19 | async-start | bytes 1310720 | tf_op jit(solution)/shard_map/reduce_scatter | solution.py:74
  858.0 34.7 %all-to-all-start.2 = ((bf16[8,72,512]{2,1,0:T(8,128)(2,1)}), bf16[8,72,512]{2,1,0:T(8,128)(2,1)}, u32[]{:S(2)}, u32[]{:S(2)}) async-start(bf16[8,72,512]{2,1,0:T(8,128)(2,1)} %bitcast.104), calls=%async_computation.7 | async-start | bytes 1179648 | tf_op jit(solution)/shard_map/all_to_all | solution.py:62
  (130 other events, 1038.1 us)
Sparse Core Ops, SparseCore 0:
  9.7 29.8 all-gather.14
  41.1 50.0 all-gather.6
  92.8 62.2 all-gather.8
  156.6 62.1 all-gather.10
  220.2 62.1 all-gather.12
  408.7 31.9 reduce-scatter.6
  470.1 33.0 reduce-scatter.8
  518.0 57.5 reduce-scatter.10
  577.9 60.2 reduce-scatter.12
  769.0 49.1 reduce-scatter.14
  858.1 30.5 reduce-scatter.16
where the time goes:
time: 919 us; the launch traced here: 908 us
  waiting for transfers between devices  268 us (29%)
  Pallas kernels  210 us (23%)
  starting transfers between devices  120 us (13%)
  local copies, waits for them, and re-layouts  108 us (12%)
  other arithmetic  98 us (11%)
  matrix products  71.8 us (8%)
  between operations  17.1 us (2%)
  blocking collectives  15.1 us (2%)
    ppermute x80, waiting for transfers between devices, permute(): lax.ppermute(array, ALL, [(team[a], team[b]) for team in teams() for a, b...  221 us
    ppermute x80, starting transfers between devices, permute(): lax.ppermute(array, ALL, [(team[a], team[b]) for team in teams() for a, b...  96.4 us
    pallas_call x4, Pallas kernels, attend_back(): pl.pallas_call(kernel, out_shape=[struct((rows, width), BF16), struct((ro...  74.1 us
    dot_general x6, matrix products, product_tn(): lax.dot_general(left, right, (((0,), (0,)), ((), ())), preferred_element_...  71.8 us
    pallas_call x2, Pallas kernels, feed_down(): pl.pallas_call(kernel, out_shape=[struct((rows, width), BF16)] * (2 * TEA...  53.8 us
    pallas_call x4, Pallas kernels, attend(): pl.pallas_call(kernel, out_shape=[struct((rows, width), BF16), struct((ro...  51.4 us
    unnamed x212, local copies, waits for them, and re-layouts  34.2 us
    reduce_scatter x6, waiting for transfers between devices, line_sum(): return lax.psum_scatter(array, 'dp', scatter_dimension=0, tiled=True)  31.9 us
  transfers between devices with their start and end apart: 94, of which 26 were waited for; matrix products, arithmetic and copies ran while one was open for 25% of the time, Pallas kernels for 17%

commit v1 on v0

v1 whole, which is shorter than its diff:
```python
import jax
import jax.numpy as jnp
from jax import lax
from jax.experimental import pallas as pl
from jax.experimental.pallas import tpu as pltpu
from jax.sharding import PartitionSpec as P

EPSILON = 1e-06
ROPE_BASE = 1000000.0
TEAM = 8
ALL = ("dp", "fsdp")
F32 = jnp.float32
BF16 = jnp.bfloat16
TILE = 128
ANY = pl.BlockSpec(memory_space=pl.ANY)
VMEM = pl.BlockSpec(memory_space=pltpu.VMEM)
SMEM = pl.BlockSpec(memory_space=pltpu.SMEM)


def product(left, right):
    return jnp.dot(left, right, preferred_element_type=F32)


def product_nt(left, right):
    return lax.dot_general(left, right, (((1,), (1,)), ((), ())), preferred_element_type=F32)


def product_tn(left, right):
    return lax.dot_general(left, right, (((0,), (0,)), ((), ())), preferred_element_type=F32)


def world():
    return lax.axis_size(ALL)


def member():
    return lax.axis_index(ALL) % TEAM


def teams():
    return [[first + t for t in range(TEAM)] for first in range(0, world(), TEAM)]


def lines():
    return [list(range(t, world(), TEAM)) for t in range(TEAM)]


def permute(array, pairs):
    return lax.ppermute(
        array, ALL, [(team[a], team[b]) for team in teams() for a, b in pairs]
    )


def swap(array, bits):
    return permute(array, [(i, i ^ bits) for i in range(TEAM)])


def exchange(blocks):
    if lax.axis_size("fsdp") == TEAM:
        return lax.all_to_all(blocks, "fsdp", 0, 0, tiled=True)
    return lax.all_to_all(blocks, ALL, 0, 0, tiled=True, axis_index_groups=teams())


def line_gather(shard):
    if lax.axis_size("fsdp") == TEAM:
        return lax.all_gather(shard, "dp", axis=0, tiled=True)
    return lax.all_gather(shard, ALL, axis=0, tiled=True, axis_index_groups=lines())


def line_sum(array):
    if lax.axis_size("fsdp") == TEAM:
        return lax.psum_scatter(array, "dp", scatter_dimension=0, tiled=True)
    return lax.psum_scatter(array, ALL, scatter_dimension=0, tiled=True, axis_index_groups=lines())


class TeamGather:
    def __init__(self, own):
        self.own = own
        self.a1 = swap(own, 1)
        self.a2 = swap(own, 2)
        self.a4 = swap(own, 4)

    def blocks(self, tick=None):
        a2, a4 = self.a2, self.a4
        if tick is not None:
            a2, a4 = hold([a2, a4], tick)
        half = self.own.shape[0] // 2
        a6 = jnp.concatenate([swap(a4[:half], 2), swap(a2[half:], 4)], axis=0)
        return [self.own, self.a1, a2, swap(a2, 1), a4, swap(a4, 1), a6, swap(a6, 1)]


def team_gather(own):
    return TeamGather(own).blocks()


class TeamSum:
    def __init__(self, parts):
        half = parts[0].shape[0] // 2
        odd = {r: swap(parts[r + 1], 1) for r in (6, 2, 4, 0)}
        self.total6, self.total2, self.total4, self.total0 = (
            parts[r].astype(F32) + odd[r].astype(F32) for r in (6, 2, 4, 0)
        )
        self.half = half
        self.low6 = self.total6.astype(BF16)
        self.ready = [self.low6, self.total2[:half].astype(BF16), self.total4[half:].astype(BF16)]

    def first(self, tick=None):
        half = self.half
        low6, x_top, y_low = self.ready if tick is None else hold(self.ready, tick)
        self.u4 = swap(low6[:half], 2)
        self.u2 = swap(low6[half:], 4)
        self.x_top = swap(x_top, 2)
        self.y_low = swap(y_low, 4)
        self.sent = [low6, x_top, y_low]
        return [self.u4, self.u2, self.x_top, self.y_low]

    def total(self):
        half = self.half
        x_low = swap((self.total2[half:] + self.u2.astype(F32)).astype(BF16), 2).astype(F32)
        y_top = swap((self.total4[:half] + self.u4.astype(F32)).astype(BF16), 4).astype(F32)
        top = self.x_top.astype(F32) + y_top
        low = x_low + self.y_low.astype(F32)
        return self.total0 + jnp.concatenate([top, low], axis=0)


def out_weight_in(shard, groups):
    t = member()
    if groups < TEAM:
        gathered = line_gather(shard[None])
        per = TEAM // groups
        b, z = t % groups, t // per
        result = jnp.zeros_like(gathered)
        for j in range(groups):
            perm = [(i, per * ((i % groups + j) % groups) + i // groups) for i in range(TEAM)]
            piece = lax.dynamic_index_in_dim(gathered, (b + j) % groups, 0, keepdims=True)
            piece = permute(piece, perm)
            result = lax.dynamic_update_slice_in_dim(result, piece, (z - j + groups) % groups, 0)
        return result.reshape(-1, shard.shape[1])
    full = lax.all_gather(shard, ALL, axis=0, tiled=True)
    rows = full.shape[0] // TEAM
    return lax.dynamic_slice_in_dim(full, t * rows, rows, 0)


def out_weight_back(grad, groups, done):
    t = member()
    if groups < TEAM:
        per = TEAM // groups
        b, z = t % groups, t // per
        grad = grad.reshape(groups, -1, grad.shape[1])
        placed = jnp.zeros_like(grad)
        for j in range(groups):
            perm = [(per * ((i % groups + j) % groups) + i // groups, i) for i in range(TEAM)]
            piece = lax.dynamic_index_in_dim(grad, (z - j + groups) % groups, 0, keepdims=True)
            piece = permute(piece, perm)
            placed = lax.dynamic_update_slice_in_dim(placed, piece, (b + j) % groups, 0)
        placed = hold([placed], done)[0]
        return line_sum(placed)[0], hold([done], placed)[0]
    whole = jnp.zeros((grad.shape[0] * TEAM, grad.shape[1]), grad.dtype)
    whole = lax.dynamic_update_slice_in_dim(whole, grad, t * grad.shape[0], 0)
    return lax.psum_scatter(whole, ALL, scatter_dimension=0, tiled=True), done


def rms_pull(value, gain, grad):
    scale = lax.rsqrt(jnp.mean(value * value, axis=-1, keepdims=True) + EPSILON)
    weighted = grad * gain
    mean = jnp.mean(weighted * value, axis=-1, keepdims=True)
    return scale * weighted - scale * scale * scale * value * mean


def rms(value, gain):
    return value * lax.rsqrt(jnp.mean(value * value, axis=-1, keepdims=True) + EPSILON) * gain


def struct(shape, dtype):
    return jax.ShapeDtypeStruct(shape, dtype)


def hold(arrays, tick):
    def kernel(*refs):
        del refs

    count = len(arrays)
    return pl.pallas_call(
        kernel,
        out_shape=[struct(a.shape, a.dtype) for a in arrays],
        in_specs=[ANY] * count + [ANY],
        out_specs=[ANY] * count,
        input_output_aliases={i: i for i in range(count)},
    )(*arrays, tick)


def mark(arrays):
    def kernel(*refs):
        refs[-1][...] = jnp.zeros_like(refs[-1])

    return pl.pallas_call(
        kernel,
        out_shape=struct((8, 128), jnp.int32),
        in_specs=[ANY] * len(arrays),
        out_specs=VMEM,
    )(*arrays)


def for_tiles(tiles, most, body):
    for m in range(1, most + 1):

        @pl.when(tiles == m)
        def _(m=m):
            body(m * TILE)


def turned(u, cosine, sine):
    return u * cosine + pltpu.roll(u, u.shape[-1] // 2, 1) * sine


def head_norm(u):
    return lax.rsqrt(jnp.mean(u * u, axis=-1, keepdims=True) + EPSILON)


def head_back(grad, raw, gain, cosine, sine):
    e = turned(grad, cosine, -sine)
    scale = head_norm(raw)
    weighted = e * gain
    mean = jnp.mean(weighted * raw, axis=-1, keepdims=True)
    back = scale * weighted - scale * scale * scale * raw * mean
    return back, jnp.sum(e * raw * scale, axis=0, keepdims=True)


def weights_of(query, key, factor):
    scores = product_nt(query, key) * factor
    n = scores.shape[0]
    causal = lax.broadcasted_iota(jnp.int32, (n, n), 1) <= lax.broadcasted_iota(jnp.int32, (n, n), 0)
    scores = jnp.where(causal, scores, -jnp.inf)
    terms = jnp.exp(scores - jnp.max(scores, axis=-1, keepdims=True))
    return terms * (1.0 / jnp.sum(terms, axis=-1, keepdims=True))


def rows_of(tile, size=TILE):
    return pl.ds(pl.multiple_of(tile * size, size), size)


def each_block(r, body):
    for k in range(TEAM):
        pl.when(r == k)(lambda k=k: body(k))


def attend(tiles, tokens, consts, mine, after):
    weight_attn, weight_head, weight_out, gain, gains, cosine, sine = consts
    rows, width = tokens[0].shape
    size = gains.shape[1]
    q_cols = mine * size
    cols = weight_attn.shape[1]
    factor = size ** (-0.5)

    def kernel(*refs):
        tiles_ref, toks = refs[0], refs[1 : 1 + TEAM]
        wa, wh, wo, gain_ref, gains_ref, cos_ref, sin_ref, _ = refs[1 + TEAM : 9 + TEAM]
        parts = refs[9 + TEAM : 9 + 2 * TEAM]
        normed_all, qkv_all, logit_all, gated_all, tick = refs[9 + 2 * TEAM : 14 + 2 * TEAM]
        (
            tok_v, wa_v, wh_v, wo_v, part_v, normed_v, qkv_v, logit_v, gated_v, w_sem, in_sem, out_sem,
        ) = refs[14 + 2 * TEAM :]
        tick[...] = jnp.zeros_like(tick)

        def load(k, slot):
            return pltpu.make_async_copy(toks[k], tok_v.at[slot], in_sem.at[slot])

        def store(r, slot, j, k=0):
            src = (part_v, normed_v, qkv_v, logit_v, gated_v)[j].at[slot]
            dst = parts[k] if j == 0 else (normed_all, qkv_all, logit_all, gated_all)[j - 1].at[rows_of(r, rows)]
            return pltpu.make_async_copy(src, dst, out_sem.at[j, slot])

        load(0, 0).start()
        weights = [
            pltpu.make_async_copy(src, dst, w_sem.at[j])
            for j, (src, dst) in enumerate(((wa, wa_v), (wh, wh_v), (wo, wo_v)))
        ]
        for copy in weights:
            copy.start()
        for copy in weights:
            copy.wait()

        def step(r, carry):
            slot = r % 2

            @pl.when(r + 1 < TEAM)
            def _():
                each_block(r + 1, lambda k: load(k, 1 - slot).start())

            load(0, slot).wait()

            @pl.when(r >= 2)
            def _():
                for j in range(5):
                    store(r - 2, slot, j).wait()

            def body(n):
                value = tok_v[slot, :n].astype(F32)
                normed = rms(value, gain_ref[...]).astype(BF16)
                normed_v[slot, :n] = normed
                qkv = product(normed, wa_v[...])
                qkv_v[slot, :n] = qkv
                logit = product_nt(normed, wh_v[...])
                logit_v[slot, :n] = logit
                cos, sin = cos_ref[:n], sin_ref[:n]
                key = qkv[:, q_cols : q_cols + size]
                key = turned(key * head_norm(key) * gains_ref[1:2], cos, sin).astype(BF16)
                values = qkv[:, q_cols + size :].astype(BF16)
                for h in range(mine):
                    query = qkv[:, h * size : (h + 1) * size]
                    query = turned(query * head_norm(query) * gains_ref[0:1], cos, sin).astype(BF16)
                    attention = weights_of(query, key, factor)
                    mixture = product(attention.astype(BF16), values)
                    gate = jax.nn.sigmoid(logit[:, h : h + 1])
                    gated_v[slot, :n, h * size : (h + 1) * size] = (mixture * gate).astype(BF16)
                part_v[slot, :n] = product(gated_v[slot, :n], wo_v[...]).astype(BF16)
                if n < rows:
                    part_v[slot, n:] = jnp.zeros((rows - n, width), BF16)
                    normed_v[slot, n:] = jnp.zeros((rows - n, width), BF16)
                    gated_v[slot, n:] = jnp.zeros((rows - n, q_cols), BF16)

            for_tiles(tiles_ref[r], rows // TILE, body)
            each_block(r, lambda k: store(r, slot, 0, k).start())
            for j in range(1, 5):
                store(r, slot, j).start()
            return carry

        lax.fori_loop(0, TEAM, step, 0)
        for r in (TEAM - 2, TEAM - 1):
            for j in range(5):
                store(r, r % 2, j).wait()

    whole = TEAM * rows
    result = pl.pallas_call(
        kernel,
        out_shape=[struct((rows, width), BF16)] * TEAM
        + [
            struct((whole, width), BF16),
            struct((whole, cols), F32),
            struct((whole, TILE), F32),
            struct((whole, q_cols), BF16),
            struct((8, 128), jnp.int32),
        ],
        in_specs=[SMEM] + [ANY] * (TEAM + 3) + [VMEM] * 4 + [ANY],
        out_specs=[ANY] * (TEAM + 4) + [VMEM],
        scratch_shapes=[
            pltpu.VMEM((2, rows, width), BF16),
            pltpu.VMEM(weight_attn.shape, BF16),
            pltpu.VMEM(weight_head.shape, BF16),
            pltpu.VMEM(weight_out.shape, BF16),
            pltpu.VMEM((2, rows, width), BF16),
            pltpu.VMEM((2, rows, width), BF16),
            pltpu.VMEM((2, rows, cols), F32),
            pltpu.VMEM((2, rows, TILE), F32),
            pltpu.VMEM((2, rows, q_cols), BF16),
            pltpu.SemaphoreType.DMA((3,)),
            pltpu.SemaphoreType.DMA((2,)),
            pltpu.SemaphoreType.DMA((5, 2)),
        ],
        compiler_params=pltpu.CompilerParams(vmem_limit_bytes=48 << 20),
        cost_estimate=pl.CostEstimate(flops=30 << 30, bytes_accessed=60 << 20, transcendentals=1 << 20),
    )(tiles, *tokens, weight_attn, weight_head, weight_out, gain, gains, cosine, sine, after)
    return result[:TEAM], result[TEAM : TEAM + 4], result[TEAM + 4]


def attend_back(tiles, hidden, consts, saved, mine, after):
    weight_attn, weight_head, weight_out, gain, gains, cosine, sine = consts
    rows, width = hidden[0].shape
    size = gains.shape[1]
    q_cols = mine * size
    cols = weight_attn.shape[1]
    factor = size ** (-0.5)

    def kernel(*refs):
        tiles_ref, hids = refs[0], refs[1 : 1 + TEAM]
        wa, wh, wo, normed_all, qkv_all, logit_all, gated_all = refs[1 + TEAM : 8 + TEAM]
        gains_ref, cos_ref, sin_ref, _ = refs[8 + TEAM : 12 + TEAM]
        parts = refs[12 + TEAM : 12 + 2 * TEAM]
        attn_sum, out_sum, gain_sum, gains_sum = refs[12 + 2 * TEAM : 16 + 2 * TEAM]
        (
            hid_v, wa_v, wh_v, wo_v, normed_v, qkv_v, logit_v, gated_v, part_v, back_v,
            w_sem, in_sem, out_sem,
        ) = refs[16 + 2 * TEAM :]

        def loads(r, slot, k):
            yield pltpu.make_async_copy(hids[k], hid_v.at[slot], in_sem.at[0, slot])
            here = rows_of(r, rows)
            for j, (src, dst) in enumerate(
                ((qkv_all, qkv_v), (logit_all, logit_v), (normed_all, normed_v), (gated_all, gated_v))
            ):
                yield pltpu.make_async_copy(src.at[here], dst.at[slot], in_sem.at[1 + j, slot])

        def start_loads(r, slot):
            def body(k):
                for copy in loads(r, slot, k):
                    copy.start()

            each_block(r, body)

        def store(slot, k=0):
            return pltpu.make_async_copy(part_v.at[slot], parts[k], out_sem.at[slot])

        for copy in loads(0, 0, 0):
            copy.start()
        weights = [
            pltpu.make_async_copy(src, dst, w_sem.at[j])
            for j, (src, dst) in enumerate(((wo, wo_v), (wa, wa_v), (wh, wh_v)))
        ]
        for copy in weights:
            copy.start()
        for ref in (attn_sum, out_sum, gain_sum, gains_sum):
            ref[...] = jnp.zeros_like(ref)
        for copy in weights:
            copy.wait()

        def step(r, carry):
            slot = r % 2

            @pl.when(r + 1 < TEAM)
            def _():
                start_loads(r + 1, 1 - slot)

            for copy in loads(r, slot, 0):
                copy.wait()

            @pl.when(r >= 2)
            def _():
                store(slot).wait()

            def body(n):
                hidden_low = hid_v[slot, :n]
                normed = normed_v[slot, :n]
                out_sum[...] += product_tn(gated_v[slot, :n], hidden_low)
                gated_grad = product_nt(hidden_low, wo_v[...])
                cos, sin = cos_ref[:n], sin_ref[:n]
                key_raw = qkv_v[slot, :n, q_cols : q_cols + size]
                key = turned(key_raw * head_norm(key_raw) * gains_ref[1:2], cos, sin).astype(BF16)
                values = qkv_v[slot, :n, q_cols + size :].astype(BF16)
                lane = lax.broadcasted_iota(jnp.int32, (n, TILE), 1)
                logit_back = jnp.zeros((n, TILE), F32)
                values_back = jnp.zeros((n, size), F32)
                key_grad = jnp.zeros((n, size), F32)
                query_sum = jnp.zeros((1, size), F32)
                for h in range(mine):
                    span = slice(h * size, (h + 1) * size)
                    query_raw = qkv_v[slot, :n, span]
                    query = turned(query_raw * head_norm(query_raw) * gains_ref[0:1], cos, sin).astype(BF16)
                    attention = weights_of(query, key, factor)
                    attention_low = attention.astype(BF16)
                    mixture = product(attention_low, values)
                    gate = jax.nn.sigmoid(logit_v[slot, :n, h : h + 1])
                    head_grad = gated_grad[:, span]
                    mixture_back = (head_grad * gate).astype(BF16)
                    one = jnp.sum(head_grad * mixture, axis=-1, keepdims=True) * gate * (1.0 - gate)
                    logit_back = jnp.where(lane == h, one, logit_back)
                    values_back += product_tn(attention_low, mixture_back)
                    attention_grad = product_nt(mixture_back, values)
                    scores_back = (
                        attention
                        * (attention_grad - jnp.sum(attention_grad * attention, axis=-1, keepdims=True))
                    ).astype(BF16)
                    query_grad = product(scores_back, key) * factor
                    key_grad += product_tn(scores_back, query)
                    back, total = head_back(query_grad, query_raw, gains_ref[0:1], cos, sin)
                    back_v[:n, span] = back.astype(BF16)
                    query_sum += total
                back, key_sum = head_back(key_grad * factor, key_raw, gains_ref[1:2], cos, sin)
                back_v[:n, q_cols : q_cols + size] = back.astype(BF16)
                back_v[:n, q_cols + size : cols] = values_back.astype(BF16)
                logit_back = logit_back.astype(BF16)
                back_v[:n, cols:] = logit_back
                gains_sum[0:1] += query_sum
                gains_sum[1:2] += key_sum
                part = product_nt(back_v[:n, :cols], wa_v[...]) + product(logit_back, wh_v[...])
                part_v[slot, :n] = part.astype(BF16)
                gain_sum[0:1] += jnp.sum(part * normed.astype(F32), axis=0, keepdims=True)
                attn_sum[...] += product_tn(back_v[:n], normed)
                if n < rows:
                    part_v[slot, n:] = jnp.zeros((rows - n, width), BF16)

            for_tiles(tiles_ref[r], rows // TILE, body)
            each_block(r, lambda k: store(slot, k).start())
            return carry

        lax.fori_loop(0, TEAM, step, 0)
        store(0).wait()
        store(1).wait()

    result = pl.pallas_call(
        kernel,
        out_shape=[struct((rows, width), BF16)] * TEAM
        + [
            struct((cols + TILE, width), F32),
            struct((q_cols, width), F32),
            struct((8, width), F32),
            struct((8, size), F32),
        ],
        in_specs=[SMEM] + [ANY] * (TEAM + 7) + [VMEM] * 3 + [ANY],
        out_specs=[ANY] * TEAM + [VMEM] * 4,
        scratch_shapes=[
            pltpu.VMEM((2, rows, width), BF16),
            pltpu.VMEM(weight_attn.shape, BF16),
            pltpu.VMEM(weight_head.shape, BF16),
            pltpu.VMEM(weight_out.shape, BF16),
            pltpu.VMEM((2, rows, width), BF16),
            pltpu.VMEM((2, rows, cols), F32),
            pltpu.VMEM((2, rows, TILE), F32),
            pltpu.VMEM((2, rows, q_cols), BF16),
            pltpu.VMEM((2, rows, width), BF16),
            pltpu.VMEM((rows, cols + TILE), BF16),
            pltpu.SemaphoreType.DMA((3,)),
            pltpu.SemaphoreType.DMA((5, 2)),
            pltpu.SemaphoreType.DMA((2,)),
        ],
        compiler_params=pltpu.CompilerParams(vmem_limit_bytes=56 << 20),
        cost_estimate=pl.CostEstimate(flops=45 << 30, bytes_accessed=70 << 20, transcendentals=1 << 20),
    )(tiles, *hidden, weight_attn, weight_head, weight_out, *saved, gains, cosine, sine, after)
    return result[:TEAM], result[TEAM], result[TEAM + 1], result[TEAM + 2][0], result[TEAM + 3][:2]


def tile_places(tiles_ref, rows):
    places, total = [], 0
    for r in range(TEAM):
        count = tiles_ref[r]
        for j in range(rows // TILE):
            places.append((r, j, j < count, total + j))
        total = total + count
    return places, total


def feed(tiles, twos, upstreams, weight_gate, weight_up, weight_down):
    rows, width = twos[0].shape
    ff_cols = weight_down.shape[0]
    whole = TEAM * rows
    chunk = 2 * TILE
    chunks = whole // chunk

    def kernel(*refs):
        tiles_ref, twos_ref, ups_ref = refs[0], refs[1 : 1 + TEAM], refs[1 + TEAM : 1 + 2 * TEAM]
        weights_ref = refs[1 + 2 * TEAM : 4 + 2 * TEAM]
        outs_ref = refs[4 + 2 * TEAM : 4 + 3 * TEAM]
        grads_ref = refs[4 + 3 * TEAM : 4 + 4 * TEAM]
        inner_all, back_all, two_all, ups_all = refs[4 + 4 * TEAM : 8 + 4 * TEAM]
        (
            two_v, ups_v, wg_v, wu_v, wd_v, inner_v, back_v, out_v, grad_v, zero_v,
            w_sem, load_sem, keep_sem, tile_sem, dead_sem,
        ) = refs[8 + 4 * TEAM :]
        places, total = tile_places(tiles_ref, rows)
        used = (total + 1) // 2

        def loads(sources, packed, which):
            for k, (r, j, live, place) in enumerate(places):
                yield live, pltpu.make_async_copy(
                    sources[r].at[rows_of(j)], packed.at[rows_of(place)], load_sem.at[which, k]
                )

        weights = [
            pltpu.make_async_copy(src, dst, w_sem.at[j])
            for j, (src, dst) in enumerate(zip(weights_ref, (wg_v, wu_v, wd_v)))
        ]
        for live, copy in loads(twos_ref, two_v, 0):
            pl.when(live)(copy.start)
        for copy in weights:
            copy.start()
        for live, copy in loads(ups_ref, ups_v, 1):
            pl.when(live)(copy.start)
        zero_v[...] = jnp.zeros_like(zero_v)

        def dead(k, r, j):
            zeros = zero_v.at[:TILE]
            yield pltpu.make_async_copy(zeros, grads_ref[r].at[rows_of(j)], dead_sem.at[0, k])
            yield pltpu.make_async_copy(zeros, outs_ref[r].at[rows_of(j)], dead_sem.at[1, k])

        for k, (r, j, live, place) in enumerate(places):

            @pl.when(jnp.logical_not(live))
            def _(k=k, r=r, j=j):
                for copy in dead(k, r, j):
                    copy.start()

        def keeps(c, sources):
            for j, (src, dst) in enumerate(zip(sources, (two_all, ups_all, inner_all, back_all))):
                yield pltpu.make_async_copy(src, dst.at[rows_of(c, chunk)], keep_sem.at[j, c])

        zeros = (zero_v, zero_v, zero_v.at[:, :ff_cols], zero_v.at[:, : 2 * ff_cols])
        for c in range(TEAM // 2, chunks):

            @pl.when(c >= used)
            def _(c=c):
                for copy in keeps(c, zeros):
                    copy.start()

        @pl.when(total % 2 == 1)
        def _():
            two_v[rows_of(total)] = jnp.zeros((TILE, width), BF16)
            ups_v[rows_of(total)] = jnp.zeros((TILE, width), BF16)

        for live, copy in loads(twos_ref, two_v, 0):
            pl.when(live)(copy.wait)
        for copy in weights:
            copy.wait()
        for live, copy in loads(ups_ref, ups_v, 1):
            pl.when(live)(copy.wait)

        def tile_stores(r, j, slot, side):
            here = pl.ds(side * TILE, TILE)
            yield pltpu.make_async_copy(
                grad_v.at[slot, here], grads_ref[r].at[rows_of(j)], tile_sem.at[0, slot, side]
            )
            yield pltpu.make_async_copy(
                out_v.at[slot, here], outs_ref[r].at[rows_of(j)], tile_sem.at[1, slot, side]
            )

        def wait_tiles(c, slot):
            for side in range(2):

                @pl.when(2 * c + side < total)
                def _(side=side):
                    for copy in tile_stores(0, 0, slot, side):
                        copy.wait()

        def body(c, carry):
            slot = c % 2
            span = rows_of(c, chunk)

            @pl.when(c >= 2)
            def _():
                wait_tiles(c - 2, slot)
                for j, copy in enumerate(keeps(c - 2, zeros)):
                    if j >= 2:
                        copy.wait()

            gate_part = product(two_v[span], wg_v[...])
            up_part = product(two_v[span], wu_v[...])
            sig = jax.nn.sigmoid(gate_part)
            silu = gate_part * sig
            inner_v[slot] = (silu * up_part).astype(BF16)
            inner_grad = product_nt(ups_v[span], wd_v[...])
            back_v[slot, :, :ff_cols] = (inner_grad * up_part * (sig + silu * (1.0 - sig))).astype(BF16)
            back_v[slot, :, ff_cols:] = (inner_grad * silu).astype(BF16)
            for copy in keeps(c, (two_v.at[span], ups_v.at[span], inner_v.at[slot], back_v.at[slot])):
                copy.start()
            grad = product_nt(back_v[slot, :, :ff_cols], wg_v[...]) + product_nt(
                back_v[slot, :, ff_cols:], wu_v[...]
            )
            grad_v[slot] = grad.astype(BF16)
            out_v[slot] = product(inner_v[slot], wd_v[...]).astype(BF16)
            for k, (r, j, live, place) in enumerate(places):
                for side in range(2):

                    @pl.when(jnp.logical_and(live, place == 2 * c + side))
                    def _(r=r, j=j, side=side):
                        for copy in tile_stores(r, j, slot, side):
                            copy.start()

            return carry

        lax.fori_loop(0, used, body, 0)
        wait_tiles(used - 2, used % 2)
        wait_tiles(used - 1, (used - 1) % 2)
        for k, (r, j, live, place) in enumerate(places):

            @pl.when(jnp.logical_not(live))
            def _(k=k, r=r, j=j):
                for copy in dead(k, r, j):
                    copy.wait()

        for c in range(chunks):
            for j, copy in enumerate(keeps(c, zeros)):
                if j < 2:
                    copy.wait()
                else:
                    pl.when(c >= used - 2)(copy.wait)

    count = whole // TILE
    result = pl.pallas_call(
        kernel,
        out_shape=[struct((rows, width), BF16)] * (2 * TEAM)
        + [
            struct((whole, ff_cols), BF16),
            struct((whole, 2 * ff_cols), BF16),
            struct((whole, width), BF16),
            struct((whole, width), BF16),
        ],
        in_specs=[SMEM] + [ANY] * (3 + 2 * TEAM),
        out_specs=[ANY] * (2 * TEAM + 4),
        scratch_shapes=[
            pltpu.VMEM((whole, width), BF16),
            pltpu.VMEM((whole, width), BF16),
            pltpu.VMEM(weight_gate.shape, BF16),
            pltpu.VMEM(weight_up.shape, BF16),
            pltpu.VMEM(weight_down.shape, BF16),
            pltpu.VMEM((2, chunk, ff_cols), BF16),
            pltpu.VMEM((2, chunk, 2 * ff_cols), BF16),
            pltpu.VMEM((2, chunk, width), BF16),
            pltpu.VMEM((2, chunk, width), BF16),
            pltpu.VMEM((chunk, width), BF16),
            pltpu.SemaphoreType.DMA((3,)),
            pltpu.SemaphoreType.DMA((2, count)),
            pltpu.SemaphoreType.DMA((4, chunks)),
            pltpu.SemaphoreType.DMA((2, 2, 2)),
            pltpu.SemaphoreType.DMA((2, count)),
        ],
        compiler_params=pltpu.CompilerParams(vmem_limit_bytes=60 << 20),
        cost_estimate=pl.CostEstimate(flops=58 << 30, bytes_accessed=100 << 20, transcendentals=1 << 20),
    )(tiles, *twos, *upstreams, weight_gate, weight_up, weight_down)
    return result[:TEAM], result[TEAM : 2 * TEAM], result[2 * TEAM :]


def local(
    groups,
    tokens,
    lengths,
    cotangent,
    attention_gain,
    query_weight,
    key_matrix,
    value_matrix,
    head_gate_weight,
    output_weight,
    query_key_gain,
    feedforward_gain,
    gate_weight,
    up_weight,
    down_weight,
):
    t = member()
    everyone = groups * TEAM
    rows, width = tokens.shape
    rho = query_weight.shape[0]
    phi = down_weight.shape[0]
    ff = gate_weight.shape[1]
    pair_cols = query_key_gain.shape[1]
    size = pair_cols * everyone
    heads = query_weight.shape[1] // size
    mine = heads // TEAM
    q_cols = query_weight.shape[1] // TEAM
    k_cols = key_matrix.shape[1] // TEAM
    ff_cols = ff // TEAM

    def everyone_in_team(vector):
        return jnp.broadcast_to(vector.reshape(1, -1), (TEAM, vector.size))

    live_tiles = (lengths + (TILE - 1)) // TILE
    row = jnp.concatenate(
        [
            head_gate_weight.reshape(rho, TEAM, mine).transpose(1, 2, 0).reshape(TEAM, -1),
            everyone_in_team(attention_gain),
            everyone_in_team(feedforward_gain),
            everyone_in_team(query_key_gain),
            everyone_in_team(live_tiles.astype(BF16)),
        ],
        axis=1,
    )
    cols = q_cols + 2 * k_cols
    row = jnp.pad(row, ((0, 0), (0, cols - row.shape[1])))[:, None, :]
    attn = jnp.concatenate(
        [
            query_weight.reshape(rho, TEAM, q_cols),
            key_matrix.reshape(rho, TEAM, k_cols),
            value_matrix.reshape(rho, TEAM, k_cols),
        ],
        axis=2,
    ).transpose(1, 0, 2)
    attn = jnp.concatenate([attn, jnp.pad(row, ((0, 0), (0, 7), (0, 0)))], axis=1)
    attn = exchange(attn)
    head_lanes = mine * rho
    at_one, at_two, at_pair = head_lanes, head_lanes + rho, head_lanes + 2 * rho
    at_tiles = at_pair + 2 * pair_cols
    team_tiles = attn[:, rho, at_tiles].astype(jnp.int32)
    order = jnp.arange(TEAM, dtype=jnp.int32)
    tiles = jnp.sum(jnp.where((order[:, None] ^ t) == order[None, :], team_tiles[None, :], 0), axis=1)
    attn = line_gather(attn.reshape(TEAM * (rho + 8), cols)).reshape(everyone, rho + 8, cols)
    weight_attn = attn[:, :rho].reshape(width, cols)
    rows_small = attn[:, rho]
    weight_head = jnp.pad(
        rows_small[:, :head_lanes].reshape(everyone, mine, rho).transpose(1, 0, 2).reshape(mine, width),
        ((0, TILE - mine), (0, 0)),
    )
    gain_one = rows_small[:, at_one:at_two].reshape(1, width).astype(F32)
    gain_two = rows_small[:, at_two:at_pair].reshape(1, width).astype(F32)
    gain_pair = (
        rows_small[:, at_pair:at_tiles]
        .reshape(everyone, 2, pair_cols)
        .transpose(1, 0, 2)
        .reshape(2, size)
        .astype(F32)
    )
    weight_out = out_weight_in(output_weight, groups)

    def ff_split(w):
        return w.reshape(rho, groups, TEAM, phi).transpose(2, 0, 1, 3).reshape(TEAM, rho, ff_cols)

    feed_shard = jnp.concatenate([ff_split(gate_weight), ff_split(up_weight)], axis=2)
    feed_shard = exchange(feed_shard).reshape(TEAM * rho, -1)
    weight_gate = line_gather(feed_shard[:, :ff_cols])

    exponent = jnp.arange(size // 2, dtype=F32) * (-2.0 / size)
    frequency = jnp.power(ROPE_BASE, exponent)
    angles = jnp.arange(rows, dtype=F32)[:, None] * frequency[None, :]
    cosine = jnp.concatenate([jnp.cos(angles), jnp.cos(angles)], axis=1)
    sine = jnp.concatenate([-jnp.sin(angles), jnp.sin(angles)], axis=1)
    consts = (weight_attn, weight_head, weight_out, gain_one, gain_pair, cosine, sine)
    team_tokens = team_gather(tokens)
    live = lax.broadcasted_iota(jnp.int32, (rows, 1), 0) < lengths[0]
    live_rows = live.astype(F32)
    upstream = cotangent.astype(F32) * live_rows
    tick = mark([team_tokens[6]])
    later = lax.broadcasted_iota(jnp.int32, (rows, 1), 0) < lengths[0] + tick[0, 0]
    upstream_low = jnp.where(later, cotangent, jnp.zeros_like(cotangent))
    upstream_levels = TeamGather(upstream_low)
    parts, kept, tick = attend(tiles, team_tokens, consts, mine, mark([feed_shard, upstream_low]))
    normed, qkv, logit, gated = kept
    weight_up = line_gather(hold([feed_shard[:, ff_cols:]], tick)[0])
    parts = hold(parts, mark([upstream_levels.a1, upstream_levels.a2, upstream_levels.a4, weight_gate]))
    arrived = TeamSum(parts)
    arrived.first()
    weight_down = line_gather(hold([down_weight], arrived.low6)[0])
    team_upstream = upstream_levels.blocks()
    inputs = tokens.astype(F32)
    hidden_state = inputs + arrived.total()

    normed_two = rms(hidden_state, gain_two).astype(BF16)
    normed_two = hold([normed_two], mark(team_upstream + [weight_up]))[0]
    team_two = team_gather(normed_two)
    outs, grads, saved = feed(tiles, team_two, team_upstream, weight_gate, weight_up, weight_down)
    inner, feed_back, two_all, ups_all = saved
    arrived = TeamSum(grads)
    arrived.first()
    two_grad = arrived.total()
    inner, feed_back = hold([inner, feed_back], arrived.low6)
    down_part = product_tn(inner, ups_all).astype(BF16)
    gate_part = product_tn(two_all, feed_back[:, :ff_cols]).astype(BF16)
    up_part = product_tn(two_all, feed_back[:, ff_cols:]).astype(BF16)
    parts_made = mark([gate_part, up_part])
    down_grad = line_sum(down_part)
    gate_grad = line_sum(hold([gate_part], down_grad)[0])
    up_grad = line_sum(hold([up_part], gate_grad)[0])
    feed_done = up_grad
    hidden_grad = upstream + rms_pull(hidden_state, gain_two, two_grad)

    fed = TeamSum(outs)
    team_hidden = team_gather(hidden_grad.astype(BF16))
    two_scale = lax.rsqrt(jnp.mean(hidden_state * hidden_state, axis=-1, keepdims=True) + EPSILON)
    two_sum = jnp.sum(two_grad * hidden_state * two_scale, axis=0)
    first_hop = fed.first(mark(team_hidden + [parts_made]))
    parts, attn_sum, out_sum, one_sum, pair_sum = attend_back(
        tiles, team_hidden, consts, (normed, qkv, logit, gated), mine, mark(fed.sent + [down_grad])
    )
    parts = hold(parts, mark(first_hop + [gate_grad]))
    arrived = TeamSum(parts)
    arrived.first()
    normed_grad = arrived.total()
    layer_output = ((hidden_state + fed.total()) * live_rows).astype(BF16)
    tokens_grad = (hidden_grad + rms_pull(inputs, gain_one, normed_grad)).astype(BF16)
    head_part = attn_sum[cols : cols + mine]
    row = jnp.concatenate(
        [
            head_part.reshape(mine, everyone, rho).transpose(1, 0, 2).reshape(everyone, -1),
            (one_sum / gain_one[0]).reshape(everyone, rho),
            two_sum.reshape(everyone, rho),
            pair_sum.reshape(2, everyone, pair_cols).transpose(1, 0, 2).reshape(everyone, -1),
        ],
        axis=1,
    ).astype(BF16)
    row = jnp.pad(row, ((0, 0), (0, cols - row.shape[1])))[:, None, :]
    attn_part = attn_sum[:cols].astype(BF16).T
    packed = jnp.concatenate(
        [attn_part.reshape(everyone, rho, cols), jnp.pad(row, ((0, 0), (0, 7), (0, 0)))], axis=1
    )
    packed = packed.reshape(everyone * (rho + 8), cols)
    packed = line_sum(hold([packed], feed_done)[0])
    output_grad, packed = out_weight_back(out_sum.astype(BF16), groups, packed)
    packed = exchange(packed.reshape(TEAM, rho + 8, cols))
    feed_grad = jnp.concatenate([gate_grad, hold([up_grad], normed_grad)[0]], axis=1)
    feed_grad = exchange(feed_grad.reshape(TEAM, rho, 2 * ff_cols))

    def ff_join(w):
        return w.reshape(TEAM, rho, groups, phi).transpose(1, 2, 0, 3).reshape(rho, ff)

    gate_grad, up_grad = hold(
        [ff_join(feed_grad[:, :, :ff_cols]), ff_join(feed_grad[:, :, ff_cols:])], normed_grad
    )
    attn_grad = packed[:, :rho].transpose(1, 0, 2)
    rows_small = packed[:, rho].astype(F32)
    sums = jnp.sum(rows_small[:, head_lanes:], axis=0)
    head_gate_grad = rows_small[:, :head_lanes].reshape(heads, rho).T
    return (
        layer_output,
        tokens_grad,
        sums[:rho],
        attn_grad[:, :, :q_cols].reshape(rho, -1).astype(F32),
        attn_grad[:, :, q_cols : q_cols + k_cols].reshape(rho, -1).astype(F32),
        attn_grad[:, :, q_cols + k_cols :].reshape(rho, -1).astype(F32),
        head_gate_grad,
        output_grad.astype(F32),
        sums[2 * rho : 2 * rho + 2 * pair_cols].reshape(2, pair_cols),
        sums[rho : 2 * rho],
        gate_grad.astype(F32),
        up_grad.astype(F32),
        down_grad.astype(F32),
    )


def solution(mesh):
    groups = mesh.size // TEAM
    rows, vector, columns = P(ALL, None), P(ALL), P(None, ALL)

    def step(*args):
        return local(groups, *args)

    return jax.shard_map(
        step,
        mesh=mesh,
        in_specs=(
            rows, vector, rows, vector, rows, rows, rows, rows, rows, columns, vector, rows, rows, rows,
        ),
        out_specs=(
            rows, rows, vector, rows, rows, rows, rows, rows, columns, vector, rows, rows, rows,
        ),
        check_vma=False,
    )
```

time: 919 us -> 805 us (0.88)
  Pallas kernels: 210 us -> 153 us
  matrix products: 71.8 us -> 44.5 us
  starting transfers between devices: 120 us -> 102 us
  other arithmetic: 98 us -> 84.8 us
    pallas_call x11 -> x3, Pallas kernels: 206 us -> 148 us  [the longest x1 67.6 us: feed(): pl.pallas_call(kernel, out_shape=[struct((rows, width), BF16)] * (2 * TEA...]
    reduce_scatter x6 -> x5, waiting for transfers between devices: 31.9 us -> 0.03 us  [line_sum(): return lax.psum_scatter(array, 'dp', scatter_dimension=0, tiled=True)]
    dot_general x6 -> x3, matrix products: 71.8 us -> 44.5 us  [product_tn(): lax.dot_general(left, right, (((0,), (0,)), ((), ())), preferred_element_...]
    ppermute x80, waiting for transfers between devices: 221 us -> 239 us  [permute(): lax.ppermute(array, ALL, [(team[a], team[b]) for team in teams() for a, b...]
    convert_element_type x6 -> x0, local copies, waits for them, and re-layouts: 16.5 us -> none  [the longest x3 8.28 us: local(): gate_grad.astype(F32)]
    all_gather x5, waiting for transfers between devices: 0.05 us -> 14.5 us  [line_gather(): return lax.all_gather(shard, 'dp', axis=0, tiled=True)]
    ppermute x80, starting transfers between devices: 96.4 us -> 83.4 us  [permute(): lax.ppermute(array, ALL, [(team[a], team[b]) for team in teams() for a, b...]
    transpose x0 -> x4, local copies, waits for them, and re-layouts: none -> 9.37 us  [the longest x2 7.13 us: local(): attn_part = attn_sum[:cols].astype(BF16).T]
  transfers between devices with their start and end apart: 94 -> 93, of which waited for: 26 -> 26; matrix products, arithmetic and copies ran while one was open for 25% -> 27% of each run, Pallas kernels for 17% -> 11%
where the time goes in v1:
time: 805 us; the launch traced here: 790 us
  waiting for transfers between devices  265 us (33%)
  Pallas kernels  153 us (19%)
  local copies, waits for them, and re-layouts  108 us (13%)
  starting transfers between devices  102 us (13%)
  other arithmetic  84.8 us (11%)
  matrix products  44.5 us (6%)
  between operations  17.6 us (2%)
  blocking collectives  15.1 us (2%)
    ppermute x80, waiting for transfers between devices, permute(): lax.ppermute(array, ALL, [(team[a], team[b]) for team in teams() for a, b...  239 us
    ppermute x80, starting transfers between devices, permute(): lax.ppermute(array, ALL, [(team[a], team[b]) for team in teams() for a, b...  83.4 us
    pallas_call x1, Pallas kernels, feed(): pl.pallas_call(kernel, out_shape=[struct((rows, width), BF16)] * (2 * TEA...  67.6 us
    pallas_call x1, Pallas kernels, attend_back(): pl.pallas_call(kernel, out_shape=[struct((rows, width), BF16)] * TEAM + [...  51.8 us
    dot_general x3, matrix products, product_tn(): lax.dot_general(left, right, (((0,), (0,)), ((), ())), preferred_element_...  44.5 us
    unnamed x156, local copies, waits for them, and re-layouts  29.5 us
    pallas_call x1, Pallas kernels, attend(): pl.pallas_call(kernel, out_shape=[struct((rows, width), BF16)] * TEAM + [...  28.6 us
    all_to_all x3, starting transfers between devices, exchange(): return lax.all_to_all(blocks, 'fsdp', 0, 0, tiled=True)  17.6 us
  transfers between devices with their start and end apart: 93, of which 26 were waited for; matrix products, arithmetic and copies ran while one was open for 27% of the time, Pallas kernels for 11%

profile of v1, /device:TPU:1, one launch (start us, length us, event | category | flops | bytes accessed | tf_op | source)
XLA Modules:
  0.0 790.0 jit_solution(5972239143241476919)
XLA Ops:
  7.3 2.2 copy.221.refs_0_
  11.0 15.1 %all_to_all.20 = bf16[8,72,512]{2,1,0:T(8,128)(2,1)} all-to-all(bf16[8,72,512]{2,1,0:T(8,128)(2,1)S(1)} %copy.137), channel_id=1, replica_groups=mesh['dp'=4,'fsdp'=8] {'fsdp'}, dimensions={0} | all-to-all | bytes 1179648 | tf_op jit(solution)/shard_map/all_to_all | solution.py:60
  29.4 2.2 reshape.277
  34.3 4.8 all-to-all-start.1
  41.3 20.7 %collective-permute-done.3.refs_5_ = bf16[384,2048]{1,0:T(8,128)(2,1)} collective-permute-done((bf16[384,2048]{1,0:T(8,128)(2,1)}, bf16[384,2048]{1,0:T(8,128)(2,1)}, u32[]{:S(2)}, u32[]{:S(2)}) %collective-permute-start.3) | collective-permute-done | bytes 1572896 | tf_op jit(solution)/shard_map/ppermute | solution.py:49
  66.9 2.2 constant_dynamic-slice_fusion.4
  69.1 6.0 collective-permute-start.8
  78.7 7.9 collective-permute-start.9
  86.6 15.5 %collective-permute-done.8 = bf16[1,64,2048]{2,1,0:T(8,128)(2,1)} collective-permute-done((bf16[1,64,2048]{2,1,0:T(8,128)(2,1)}, bf16[1,64,2048]{2,1,0:T(8,128)(2,1)}, u32[]{:S(2)}, u32[]{:S(2)}) %collective-permute-start.8) | collective-permute-done | bytes 262176 | tf_op jit(solution)/shard_map/ppermute | solution.py:49
  104.2 3.5 collective-permute-start.11
  118.8 3.2 slice.262
  124.4 2.7 collective-permute-start.12
  127.1 28.6 %shard_map.239 = (bf16[384,2048]{1,0:T(8,128)(2,1)S(1)}, bf16[384,2048]{1,0:T(8,128)(2,1)S(1)}, bf16[384,2048]{1,0:T(8,128)(2,1)}, bf16[384,2048]{1,0:T(8,128)(2...) custom-call(s32[8]{0:T(128)S(1)} %select_reduce_fusion.refs_0_, ...), custom_call_target="tpu_custom_call" | custom-call | flops 32212254720 | bytes 62914560 | tf_op jit(solution)/shard_map/pallas_call | solution.py:334
  167.7 16.2 %collective-permute-done.27 = bf16[192,2048]{1,0:T(8,128)(2,1)} collective-permute-done((bf16[192,2048]{1,0:T(8,128)(2,1)}, bf16[192,2048]{1,0:T(8,128)(2,1)}, u32[]{:S(2)}, u32[]{:S(2)}) %collective-permute-start.27) | collective-permute-done | bytes 786464 | tf_op jit(solution)/shard_map/ppermute | solution.py:49
  189.7 2.4 collective-permute-done.16
  195.9 11.6 %collective-permute-done.20 = bf16[192,2048]{1,0:T(8,128)(2,1)S(1)} collective-permute-done((bf16[192,2048]{1,0:T(8,128)(2,1)S(1)}, bf16[192,2048]{1,0:T(8,128)(2,1)S(1)}, u32[]{:S(2)}, u32[]{:S(2)}) %collective-permute-start.20) | collective-permute-done | bytes 786464 | tf_op jit(solution)/shard_map/ppermute | solution.py:49
  214.7 14.5 %all-gather.11.cloned.1.call-done.refs_8_.refs_18_ = bf16[2048,768]{1,0:T(8,128)(2,1)} async-done(((bf16[512,768]{1,0:T(8,128)(2,1)}), bf16[2048,768]{1,0:T(8,128)(2,1)}) %all-gather.11.cloned.1.call-update) | async-done | bytes 3145744 | tf_op jit(solution)/shard_map/all_gather | solution.py:66
  231.2 14.9 %collective-permute-done.24 = bf16[192,2048]{1,0:T(8,128)(2,1)} collective-permute-done((bf16[192,2048]{1,0:T(8,128)(2,1)}, bf16[192,2048]{1,0:T(8,128)(2,1)}, u32[]{:S(2)}, u32[]{:S(2)}) %collective-permute-start.24) | collective-permute-done | bytes 786464 | tf_op jit(solution)/shard_map/ppermute | solution.py:49
  247.7 2.8 multiply_reduce_fusion.2
  253.5 32.8 %collective-permute-done.33.refs_5_ = bf16[384,2048]{1,0:T(8,128)(2,1)} collective-permute-done((bf16[384,2048]{1,0:T(8,128)(2,1)}, bf16[384,2048]{1,0:T(8,128)(2,1)}, u32[]{:S(2)}, u32[]{:S(2)}) %collective-permute-start.33) | collective-permute-done | bytes 1572896 | tf_op jit(solution)/shard_map/ppermute | solution.py:49
  290.2 3.5 collective-permute-start.30
  294.2 9.5 %collective-permute-done.35 = bf16[192,2048]{1,0:T(8,128)(2,1)S(1)} collective-permute-done((bf16[192,2048]{1,0:T(8,128)(2,1)S(1)}, bf16[192,2048]{1,0:T(8,128)(2,1)S(1)}, u32[]{:S(2)}, u32[]{:S(2)}) %collective-permute-start.35) | collective-permute-done | bytes 786464 | tf_op jit(solution)/shard_map/ppermute | solution.py:49
  306.3 4.2 collective-permute-start.37
  310.4 3.4 collective-permute-done.37.refs_8_
  313.8 67.6 %shard_map.246 = (bf16[384,2048]{1,0:T(8,128)(2,1)}, bf16[384,2048]{1,0:T(8,128)(2,1)}, bf16[384,2048]{1,0:T(8,128)(2,1)}, bf16[384,2048]{1,0:T(8,128)(2,1)}, bf...) custom-call(s32[8]{0:T(128)} %copy-done.11, ...), custom_call_target="tpu_custom_call" | custom-call | flops 62277025792 | bytes 104857600 | tf_op jit(solution)/shard_map/pallas_call | solution.py:676
  382.6 4.1 collective-permute-done.46
  386.7 3.2 add_convert_fusion.1.refs_2_
  389.9 15.6 %convolution_convert_fusion = bf16[768,2048]{1,0:T(8,128)(2,1)} fusion(bf16[3072,768]{1,0:T(8,128)(2,1)} %get-tuple-element.125, bf16[3072,2048]{1,0:T(8,128)(2,1)} %get-tuple-element.126), kind=kOutput, calls=%fused_computation.12 | convolution fusion | flops 9665249280 | bytes 20447232 | tf_op jit(solution)/shard_map/dot_general | solution.py:29
  414.6 11.5 %collective-permute-done.47 = bf16[192,2048]{1,0:T(8,128)(2,1)S(1)} collective-permute-done((bf16[192,2048]{1,0:T(8,128)(2,1)S(1)}, bf16[192,2048]{1,0:T(8,128)(2,1)S(1)}, u32[]{:S(2)}, u32[]{:S(2)}) %collective-permute-start.47) | collective-permute-done | bytes 786464 | tf_op jit(solution)/shard_map/ppermute | solution.py:49
  429.8 13.1 %collective-permute-done.44 = bf16[192,2048]{1,0:T(8,128)(2,1)S(1)} collective-permute-done((bf16[192,2048]{1,0:T(8,128)(2,1)S(1)}, bf16[192,2048]{1,0:T(8,128)(2,1)S(1)}, u32[]{:S(2)}, u32[]{:S(2)}) %collective-permute-start.44) | collective-permute-done | bytes 786464 | tf_op jit(solution)/shard_map/ppermute | solution.py:49
  442.9 19.8 %collective-permute-done.48 = bf16[192,2048]{1,0:T(8,128)(2,1)S(1)} collective-permute-done((bf16[192,2048]{1,0:T(8,128)(2,1)S(1)}, bf16[192,2048]{1,0:T(8,128)(2,1)S(1)}, u32[]{:S(2)}, u32[]{:S(2)}) %collective-permute-start.48) | collective-permute-done | bytes 786464 | tf_op jit(solution)/shard_map/ppermute | solution.py:49
  464.4 2.8 multiply_reduce_fusion
  467.2 5.0 fusion.44
  473.9 13.2 %fusion.5.refs_0_ = bf16[2048,768]{1,0:T(8,128)(2,1)S(1)} fusion(bf16[3072,2048]{1,0:T(8,128)(2,1)} %get-tuple-element.114, bf16[3072,1536]{1,0:T(8,128)(2,1)S(1)} %bitcast.88), kind=kOutput, calls=%fused_computation.10 | convolution fusion | flops 9665249280 | bytes 20447232 | tf_op jit(solution)/shard_map/dot_general | solution.py:29
  491.3 2.3 collective-permute-start.41
  494.0 12.5 %collective-permute-done.55.refs_4_.refs_5_ = bf16[384,2048]{1,0:T(8,128)(2,1)} collective-permute-done((bf16[384,2048]{1,0:T(8,128)(2,1)}, bf16[384,2048]{1,0:T(8,128)(2,1)}, u32[]{:S(2)}, u32[]{:S(2)}) %collective-permute-start.55) | collective-permute-done | bytes 1572896 | tf_op jit(solution)/shard_map/ppermute | solution.py:49
  512.6 15.7 %fusion.8.refs_1_.refs_0_ = bf16[2048,768]{1,0:T(8,128)(2,1)} fusion(bf16[3072,2048]{1,0:T(8,128)(2,1)} %get-tuple-element.114, bf16[3072,1536]{1,0:T(8,128)(2,1)} %get-tuple-element.117), kind=kOutput, calls=%fused_computation.11 | convolution fusion | flops 9665249280 | bytes 20447232 | tf_op jit(solution)/shard_map/dot_general | solution.py:29
  528.9 3.1 collective-permute-start.52
  532.1 2.1 constant_dynamic-update-slice_fusion.7
  546.0 3.2 add_convert_fusion.2.refs_0_
  549.9 2.7 fusion.47
  556.3 51.8 %shard_map.252 = (bf16[384,2048]{1,0:T(8,128)(2,1)}, bf16[384,2048]{1,0:T(8,128)(2,1)}, bf16[384,2048]{1,0:T(8,128)(2,1)}, bf16[384,2048]{1,0:T(8,128)(2,1)}, bf...) custom-call(s32[8]{0:T(128)} %copy-done.11, ...), custom_call_target="tpu_custom_call" | custom-call | flops 48318382080 | bytes 73400320 | tf_op jit(solution)/shard_map/pallas_call | solution.py:489
  608.1 2.9 convert.66
  614.8 3.2 slice_bitcast_fusion
  618.0 3.9 copy.143
  624.6 3.7 collective-permute-start.76
  631.4 2.9 collective-permute-start.77
  634.9 2.9 collective-permute-start.79
  639.4 2.7 fusion.24
  642.1 2.3 fusion.23
  664.6 11.6 %collective-permute-done.71 = bf16[192,2048]{1,0:T(8,128)(2,1)} collective-permute-done((bf16[192,2048]{1,0:T(8,128)(2,1)}, bf16[192,2048]{1,0:T(8,128)(2,1)}, u32[]{:S(2)}, u32[]{:S(2)}) %collective-permute-start.71) | collective-permute-done | bytes 786464 | tf_op jit(solution)/shard_map/ppermute | solution.py:49
  678.0 4.1 collective-permute-done.73
  685.0 2.7 convert_add_fusion.12
  687.7 5.3 collective-permute-done.68
  694.1 21.7 %collective-permute-done.72 = bf16[192,2048]{1,0:T(8,128)(2,1)S(1)} collective-permute-done((bf16[192,2048]{1,0:T(8,128)(2,1)S(1)}, bf16[192,2048]{1,0:T(8,128)(2,1)S(1)}, u32[]{:S(2)}, u32[]{:S(2)}) %collective-permute-start.72) | collective-permute-done | bytes 786464 | tf_op jit(solution)/shard_map/ppermute | solution.py:49
  718.7 4.7 fusion.11
  723.4 2.6 pad_maximum_fusion.1
  726.0 5.2 all-to-all-start.3
  731.2 3.2 collective-permute-done.64
  736.0 3.8 fusion.19
  739.9 9.4 %all-to-all-done.3 = bf16[8,64,1536]{2,1,0:T(8,128)(2,1)} async-done(((bf16[8,64,1536]{2,1,0:T(8,128)(2,1)}), bf16[8,64,1536]{2,1,0:T(8,128)(2,1)}, u32[]{:S(2)}, u32[]{:S(2)}) %all-to-all-start.3) | async-done | bytes 1572896 | tf_op jit(solution)/shard_map/all_to_all | solution.py:60
  749.3 7.6 all-to-all-start.2
  757.0 4.4 fusion.15
  770.9 2.5 convert_element_type.448
  (481 shorter events, 179.6 us)
Async XLA Ops:
  7.3 59.6 %all-gather.15.cloned.1.call-start = ((), (), s32[]{:S(2)}) async-start(), calls=%async_computation.18 | async-start | bytes 1310720 | tf_op jit(solution)/shard_map/all_gather | solution.py:66
  9.5 108.3 %all-gather.7.cloned.1.call-start = ((), (), s32[]{:S(2)}) async-start(), calls=%async_computation.9 | async-start | bytes 2949120 | tf_op jit(solution)/shard_map/all_gather | solution.py:66
  26.2 35.8 %collective-permute-start.3 = (bf16[384,2048]{1,0:T(8,128)(2,1)}, bf16[384,2048]{1,0:T(8,128)(2,1)}, u32[]{:S(2)}, u32[]{:S(2)}) collective-permute-start(bf16[384,2048]{1,0:T(8,128)(2,1)} %refs_1_.1), channel_id=1, source_target_pairs={{0,4},{1,5},{2,6},{3,7},{4,0},{5,1},{6,2},{7,3},{8,12},{9,13},{10,... | collective-permute-start | bytes 4718600 | tf_op jit(solution)/shard_map/ppermute | solution.py:49
  26.5 38.0 %collective-permute-start.1 = (bf16[384,2048]{1,0:T(8,128)(2,1)}, bf16[384,2048]{1,0:T(8,128)(2,1)}, u32[]{:S(2)}, u32[]{:S(2)}) collective-permute-start(bf16[384,2048]{1,0:T(8,128)(2,1)} %refs_1_.1), channel_id=1, source_target_pairs={{0,2},{1,3},{2,0},{3,1},{4,6},{5,7},{6,4},{7,5},{8,10},{9,11},{10,... | collective-permute-start | bytes 4718600 | tf_op jit(solution)/shard_map/ppermute | solution.py:49
  34.3 42.7 %all-to-all-start.1 = ((bf16[8,64,1536]{2,1,0:T(8,128)(2,1)}), bf16[8,64,1536]{2,1,0:T(8,128)(2,1)S(1)}, u32[]{:S(2)}, u32[]{:S(2)}) async-start(bf16[8,64,1536]{2,1,0:T(8,128)(2,1)} %pad_maximum_fusion), calls=%async_computation.1 | async-start | bytes 3145728 | tf_op jit(solution)/shard_map/all_to_all | solution.py:60
  39.0 120.7 %all-gather.9.cloned.1.call-start = ((), (), s32[]{:S(2)}) async-start(), calls=%async_computation.10 | async-start | bytes 3932160 | tf_op jit(solution)/shard_map/all_gather | solution.py:66
  39.1 84.6 %collective-permute-start = (bf16[384,2048]{1,0:T(8,128)(2,1)}, bf16[384,2048]{1,0:T(8,128)(2,1)}, u32[]{:S(2)}, u32[]{:S(2)}) collective-permute-start(bf16[384,2048]{1,0:T(8,128)(2,1)} %refs_1_.1), channel_id=1, source_target_pairs={{0,1},{1,0},{2,3},{3,2},{4,5},{5,4},{6,7},{7,6},{8,9},{9,8},{10,11... | collective-permute-start | bytes 4718600 | tf_op jit(solution)/shard_map/ppermute | solution.py:49
  64.0 40.2 %collective-permute-start.5 = (bf16[192,2048]{1,0:T(8,128)(2,1)}, bf16[192,2048]{1,0:T(8,128)(2,1)S(1)}, u32[]{:S(2)}, u32[]{:S(2)}) collective-permute-start(bf16[192,2048]{1,0:T(8,128)(2,1)} %slice.260), channel_id=1, source_target_pairs={{0,2},{1,3},{2,0},{3,1},{4,6},{5,7},{6,4},{7,5},{8,10},{9,11},{10,... | collective-permute-start | bytes 2359304 | tf_op jit(solution)/shard_map/ppermute | solution.py:49
  66.6 42.1 %collective-permute-start.6 = (bf16[192,2048]{1,0:T(8,128)(2,1)}, bf16[192,2048]{1,0:T(8,128)(2,1)S(1)}, u32[]{:S(2)}, u32[]{:S(2)}) collective-permute-start(bf16[192,2048]{1,0:T(8,128)(2,1)} %slice.261), channel_id=1, source_target_pairs={{0,4},{1,5},{2,6},{3,7},{4,0},{5,1},{6,2},{7,3},{8,12},{9,13},{10,... | collective-permute-start | bytes 2359304 | tf_op jit(solution)/shard_map/ppermute | solution.py:49
  69.1 33.0 %collective-permute-start.8 = (bf16[1,64,2048]{2,1,0:T(8,128)(2,1)}, bf16[1,64,2048]{2,1,0:T(8,128)(2,1)}, u32[]{:S(2)}, u32[]{:S(2)}) collective-permute-start(bf16[1,64,2048]{2,1,0:T(8,128)(2,1)} %get-tuple-element.177), channel_id=1, source_target_pairs={{0,0},{1,2},{2,4},{3,6},{4,1},{5,3},{6,5},{7,7},{8,8},{9,10},{10,1... | collective-permute-start | bytes 786440 | tf_op jit(solution)/shard_map/ppermute | solution.py:49
  78.6 150.6 %all-gather.11.cloned.1.call-start = ((), (), s32[]{:S(2)}) async-start(), calls=%async_computation.11 | async-start | bytes 3932160 | tf_op jit(solution)/shard_map/all_gather | solution.py:66
  78.7 31.5 %collective-permute-start.9 = (bf16[1,64,2048]{2,1,0:T(8,128)(2,1)}, bf16[1,64,2048]{2,1,0:T(8,128)(2,1)S(1)}, u32[]{:S(2)}, u32[]{:S(2)}) collective-permute-start(bf16[1,64,2048]{2,1,0:T(8,128)(2,1)} %get-tuple-element.176), channel_id=1, source_target_pairs={{0,2},{1,4},{2,6},{3,0},{4,3},{5,5},{6,7},{7,1},{8,10},{9,12},{10,... | collective-permute-start | bytes 786440 | tf_op jit(solution)/shard_map/ppermute | solution.py:49
  117.4 41.2 %collective-permute-start.14 = (bf16[384,2048]{1,0:T(8,128)(2,1)S(1)}, bf16[384,2048]{1,0:T(8,128)(2,1)}, u32[]{:S(2)}, u32[]{:S(2)}) collective-permute-start(bf16[384,2048]{1,0:T(8,128)(2,1)S(1)} %copy-done.14), channel_id=1, source_target_pairs={{0,4},{1,5},{2,6},{3,7},{4,0},{5,1},{6,2},{7,3},{8,12},{9,13},{10,... | collective-permute-start | bytes 4718600 | tf_op jit(solution)/shard_map/ppermute | solution.py:49
  123.6 35.0 %collective-permute-start.13 = (bf16[384,2048]{1,0:T(8,128)(2,1)S(1)}, bf16[384,2048]{1,0:T(8,128)(2,1)S(1)}, u32[]{:S(2)}, u32[]{:S(2)}) collective-permute-start(bf16[384,2048]{1,0:T(8,128)(2,1)S(1)} %copy-done.14), channel_id=1, source_target_pairs={{0,2},{1,3},{2,0},{3,1},{4,6},{5,7},{6,4},{7,5},{8,10},{9,11},{10,... | collective-permute-start | bytes 4718600 | tf_op jit(solution)/shard_map/ppermute | solution.py:49
  124.4 35.4 %collective-permute-start.12 = (bf16[384,2048]{1,0:T(8,128)(2,1)S(1)}, bf16[384,2048]{1,0:T(8,128)(2,1)}, u32[]{:S(2)}, u32[]{:S(2)}) collective-permute-start(bf16[384,2048]{1,0:T(8,128)(2,1)S(1)} %copy-done.14), channel_id=1, source_target_pairs={{0,1},{1,0},{2,3},{3,2},{4,5},{5,4},{6,7},{7,6},{8,9},{9,8},{10,11... | collective-permute-start | bytes 4718600 | tf_op jit(solution)/shard_map/ppermute | solution.py:49
  160.4 25.6 %collective-permute-start.19 = (bf16[384,2048]{1,0:T(8,128)(2,1)}, bf16[384,2048]{1,0:T(8,128)(2,1)S(1)}, u32[]{:S(2)}, u32[]{:S(2)}) collective-permute-start(bf16[384,2048]{1,0:T(8,128)(2,1)} %get-tuple-element.96), channel_id=1, source_target_pairs={{0,1},{1,0},{2,3},{3,2},{4,5},{5,4},{6,7},{7,6},{8,9},{9,8},{10,11... | collective-permute-start | bytes 4718600 | tf_op jit(solution)/shard_map/ppermute | solution.py:49
  165.1 145.3 %all-gather.13.cloned.1.call-start = ((), (), s32[]{:S(2)}) async-start(), calls=%async_computation.12 | async-start | bytes 3932160 | tf_op jit(solution)/shard_map/all_gather | solution.py:66
  165.8 20.0 %collective-permute-start.28 = (bf16[192,2048]{1,0:T(8,128)(2,1)S(1)}, bf16[192,2048]{1,0:T(8,128)(2,1)S(1)}, u32[]{:S(2)}, u32[]{:S(2)}) collective-permute-start(bf16[192,2048]{1,0:T(8,128)(2,1)S(1)} %slice.276), channel_id=1, source_target_pairs={{0,4},{1,5},{2,6},{3,7},{4,0},{5,1},{6,2},{7,3},{8,12},{9,13},{10,... | collective-permute-start | bytes 2359304 | tf_op jit(solution)/shard_map/ppermute | solution.py:49
  167.2 21.1 %collective-permute-start.18 = (bf16[384,2048]{1,0:T(8,128)(2,1)S(1)}, bf16[384,2048]{1,0:T(8,128)(2,1)S(1)}, u32[]{:S(2)}, u32[]{:S(2)}) collective-permute-start(bf16[384,2048]{1,0:T(8,128)(2,1)S(1)} %copy-done.54), channel_id=1, source_target_pairs={{0,1},{1,0},{2,3},{3,2},{4,5},{5,4},{6,7},{7,6},{8,9},{9,8},{10,11... | collective-permute-start | bytes 4718600 | tf_op jit(solution)/shard_map/ppermute | solution.py:49
  167.3 42.1 %collective-permute-start.25 = (bf16[384,2048]{1,0:T(8,128)(2,1)S(1)}, bf16[384,2048]{1,0:T(8,128)(2,1)S(1)}, u32[]{:S(2)}, u32[]{:S(2)}) collective-permute-start(bf16[384,2048]{1,0:T(8,128)(2,1)S(1)} %copy-done.18), channel_id=1, source_target_pairs={{0,1},{1,0},{2,3},{3,2},{4,5},{5,4},{6,7},{7,6},{8,9},{9,8},{10,11... | collective-permute-start | bytes 4718600 | tf_op jit(solution)/shard_map/ppermute | solution.py:49
  183.8 28.5 %collective-permute-start.26 = (bf16[384,2048]{1,0:T(8,128)(2,1)}, bf16[384,2048]{1,0:T(8,128)(2,1)S(1)}, u32[]{:S(2)}, u32[]{:S(2)}) collective-permute-start(bf16[384,2048]{1,0:T(8,128)(2,1)} %collective-permute-done.14.refs_2_.refs_4_.refs_13_), channel_id=1, source_target_pairs={{0,1},{1,0},{2,3},{3,2},{4,5},{5,4},{6,7},{7,6},{8,9},{9,8},{10,11... | collective-permute-start | bytes 4718600 | tf_op jit(solution)/shard_map/ppermute | solution.py:49
  185.9 26.8 %collective-permute-start.29 = (bf16[384,2048]{1,0:T(8,128)(2,1)S(1)}, bf16[384,2048]{1,0:T(8,128)(2,1)S(1)}, u32[]{:S(2)}, u32[]{:S(2)}) collective-permute-start(bf16[384,2048]{1,0:T(8,128)(2,1)S(1)} %constant_dynamic-update-slice_fusion.2.refs_6_.refs_15_), channel_id=1, source_target_pairs={{0,1},{1,0},{2,3},{3,2},{4,5},{5,4},{6,7},{7,6},{8,9},{9,8},{10,11... | collective-permute-start | bytes 4718600 | tf_op jit(solution)/shard_map/ppermute | solution.py:49
  207.5 40.2 %collective-permute-start.15 = (bf16[384,2048]{1,0:T(8,128)(2,1)S(1)}, bf16[384,2048]{1,0:T(8,128)(2,1)}, u32[]{:S(2)}, u32[]{:S(2)}) collective-permute-start(bf16[384,2048]{1,0:T(8,128)(2,1)S(1)} %copy-done.3), channel_id=1, source_target_pairs={{0,1},{1,0},{2,3},{3,2},{4,5},{5,4},{6,7},{7,6},{8,9},{9,8},{10,11... | collective-permute-start | bytes 4718600 | tf_op jit(solution)/shard_map/ppermute | solution.py:49
  209.4 20.5 %collective-permute-start.17 = (bf16[192,2048]{1,0:T(8,128)(2,1)}, bf16[192,2048]{1,0:T(8,128)(2,1)S(1)}, u32[]{:S(2)}, u32[]{:S(2)}) collective-permute-start(bf16[192,2048]{1,0:T(8,128)(2,1)} %slice.372), channel_id=1, source_target_pairs={{0,2},{1,3},{2,0},{3,1},{4,6},{5,7},{6,4},{7,5},{8,10},{9,11},{10,... | collective-permute-start | bytes 2359304 | tf_op jit(solution)/shard_map/ppermute | solution.py:49
  212.3 33.8 %collective-permute-start.24 = (bf16[192,2048]{1,0:T(8,128)(2,1)}, bf16[192,2048]{1,0:T(8,128)(2,1)}, u32[]{:S(2)}, u32[]{:S(2)}) collective-permute-start(bf16[192,2048]{1,0:T(8,128)(2,1)} %slice.371), channel_id=1, source_target_pairs={{0,4},{1,5},{2,6},{3,7},{4,0},{5,1},{6,2},{7,3},{8,12},{9,13},{10,... | collective-permute-start | bytes 2359304 | tf_op jit(solution)/shard_map/ppermute | solution.py:49
  213.5 32.7 %collective-permute-start.23 = (bf16[192,2048]{1,0:T(8,128)(2,1)S(1)}, bf16[192,2048]{1,0:T(8,128)(2,1)}, u32[]{:S(2)}, u32[]{:S(2)}) collective-permute-start(bf16[192,2048]{1,0:T(8,128)(2,1)S(1)} %fusion.27), channel_id=1, source_target_pairs={{0,2},{1,3},{2,0},{3,1},{4,6},{5,7},{6,4},{7,5},{8,10},{9,11},{10,... | collective-permute-start | bytes 2359304 | tf_op jit(solution)/shard_map/ppermute | solution.py:49
  214.7 275.8 %reduce-scatter.6.cloned.1.call-start = ((), (), s32[]{:S(2)}) async-start(), calls=%async_computation.13 | async-start | bytes 3932160 | tf_op jit(solution)/shard_map/reduce_scatter | solution.py:72
  252.1 34.2 %collective-permute-start.33 = (bf16[384,2048]{1,0:T(8,128)(2,1)}, bf16[384,2048]{1,0:T(8,128)(2,1)}, u32[]{:S(2)}, u32[]{:S(2)}) collective-permute-start(bf16[384,2048]{1,0:T(8,128)(2,1)} %shard_map.244.refs_1_), channel_id=1, source_target_pairs={{0,4},{1,5},{2,6},{3,7},{4,0},{5,1},{6,2},{7,3},{8,12},{9,13},{10,... | collective-permute-start | bytes 4718600 | tf_op jit(solution)/shard_map/ppermute | solution.py:49
  253.2 35.0 %collective-permute-start.31 = (bf16[384,2048]{1,0:T(8,128)(2,1)}, bf16[384,2048]{1,0:T(8,128)(2,1)}, u32[]{:S(2)}, u32[]{:S(2)}) collective-permute-start(bf16[384,2048]{1,0:T(8,128)(2,1)} %shard_map.244.refs_1_), channel_id=1, source_target_pairs={{0,2},{1,3},{2,0},{3,1},{4,6},{5,7},{6,4},{7,5},{8,10},{9,11},{10,... | collective-permute-start | bytes 4718600 | tf_op jit(solution)/shard_map/ppermute | solution.py:49
  290.2 20.2 %collective-permute-start.30 = (bf16[384,2048]{1,0:T(8,128)(2,1)S(1)}, bf16[384,2048]{1,0:T(8,128)(2,1)}, u32[]{:S(2)}, u32[]{:S(2)}) collective-permute-start(bf16[384,2048]{1,0:T(8,128)(2,1)S(1)} %copy-done.32), channel_id=1, source_target_pairs={{0,1},{1,0},{2,3},{3,2},{4,5},{5,4},{6,7},{7,6},{8,9},{9,8},{10,11... | collective-permute-start | bytes 4718600 | tf_op jit(solution)/shard_map/ppermute | solution.py:49
  382.0 29.5 %collective-permute-start.45 = (bf16[384,2048]{1,0:T(8,128)(2,1)}, bf16[384,2048]{1,0:T(8,128)(2,1)}, u32[]{:S(2)}, u32[]{:S(2)}) collective-permute-start(bf16[384,2048]{1,0:T(8,128)(2,1)} %get-tuple-element.111), channel_id=1, source_target_pairs={{0,1},{1,0},{2,3},{3,2},{4,5},{5,4},{6,7},{7,6},{8,9},{9,8},{10,11... | collective-permute-start | bytes 4718600 | tf_op jit(solution)/shard_map/ppermute | solution.py:49
  382.1 25.1 %collective-permute-start.43 = (bf16[384,2048]{1,0:T(8,128)(2,1)}, bf16[384,2048]{1,0:T(8,128)(2,1)}, u32[]{:S(2)}, u32[]{:S(2)}) collective-permute-start(bf16[384,2048]{1,0:T(8,128)(2,1)} %get-tuple-element.109), channel_id=1, source_target_pairs={{0,1},{1,0},{2,3},{3,2},{4,5},{5,4},{6,7},{7,6},{8,9},{9,8},{10,11... | collective-permute-start | bytes 4718600 | tf_op jit(solution)/shard_map/ppermute | solution.py:49
  382.5 80.7 %collective-permute-start.42 = (bf16[384,2048]{1,0:T(8,128)(2,1)}, bf16[384,2048]{1,0:T(8,128)(2,1)}, u32[]{:S(2)}, u32[]{:S(2)}) collective-permute-start(bf16[384,2048]{1,0:T(8,128)(2,1)} %get-tuple-element.107), channel_id=1, source_target_pairs={{0,1},{1,0},{2,3},{3,2},{4,5},{5,4},{6,7},{7,6},{8,9},{9,8},{10,11... | collective-permute-start | bytes 4718600 | tf_op jit(solution)/shard_map/ppermute | solution.py:49
  405.5 150.7 %reduce-scatter.8.cloned.1.call-start = ((), (), s32[]{:S(2)}) async-start(), calls=%async_computation.14 | async-start | bytes 3932160 | tf_op jit(solution)/shard_map/reduce_scatter | solution.py:72
  409.5 33.4 %collective-permute-start.44 = (bf16[192,2048]{1,0:T(8,128)(2,1)S(1)}, bf16[192,2048]{1,0:T(8,128)(2,1)S(1)}, u32[]{:S(2)}, u32[]{:S(2)}) collective-permute-start(bf16[192,2048]{1,0:T(8,128)(2,1)S(1)} %slice.368), channel_id=1, source_target_pairs={{0,2},{1,3},{2,0},{3,1},{4,6},{5,7},{6,4},{7,5},{8,10},{9,11},{10,... | collective-permute-start | bytes 2359304 | tf_op jit(solution)/shard_map/ppermute | solution.py:49
  413.6 49.4 %collective-permute-start.51 = (bf16[192,2048]{1,0:T(8,128)(2,1)S(1)}, bf16[192,2048]{1,0:T(8,128)(2,1)S(1)}, u32[]{:S(2)}, u32[]{:S(2)}) collective-permute-start(bf16[192,2048]{1,0:T(8,128)(2,1)S(1)} %slice.367), channel_id=1, source_target_pairs={{0,4},{1,5},{2,6},{3,7},{4,0},{5,1},{6,2},{7,3},{8,12},{9,13},{10,... | collective-permute-start | bytes 2359304 | tf_op jit(solution)/shard_map/ppermute | solution.py:49
  426.3 36.5 %collective-permute-start.48 = (bf16[192,2048]{1,0:T(8,128)(2,1)S(1)}, bf16[192,2048]{1,0:T(8,128)(2,1)S(1)}, u32[]{:S(2)}, u32[]{:S(2)}) collective-permute-start(bf16[192,2048]{1,0:T(8,128)(2,1)S(1)} %fusion.26), channel_id=1, source_target_pairs={{0,4},{1,5},{2,6},{3,7},{4,0},{5,1},{6,2},{7,3},{8,12},{9,13},{10,... | collective-permute-start | bytes 2359304 | tf_op jit(solution)/shard_map/ppermute | solution.py:49
  429.2 33.8 %collective-permute-start.50 = (bf16[192,2048]{1,0:T(8,128)(2,1)S(1)}, bf16[192,2048]{1,0:T(8,128)(2,1)S(1)}, u32[]{:S(2)}, u32[]{:S(2)}) collective-permute-start(bf16[192,2048]{1,0:T(8,128)(2,1)S(1)} %fusion.25), channel_id=1, source_target_pairs={{0,2},{1,3},{2,0},{3,1},{4,6},{5,7},{6,4},{7,5},{8,10},{9,11},{10,... | collective-permute-start | bytes 2359304 | tf_op jit(solution)/shard_map/ppermute | solution.py:49
  472.2 34.4 %collective-permute-start.55 = (bf16[384,2048]{1,0:T(8,128)(2,1)}, bf16[384,2048]{1,0:T(8,128)(2,1)}, u32[]{:S(2)}, u32[]{:S(2)}) collective-permute-start(bf16[384,2048]{1,0:T(8,128)(2,1)} %get-tuple-element.154.refs_0_.refs_1_), channel_id=1, source_target_pairs={{0,4},{1,5},{2,6},{3,7},{4,0},{5,1},{6,2},{7,3},{8,12},{9,13},{10,... | collective-permute-start | bytes 4718600 | tf_op jit(solution)/shard_map/ppermute | solution.py:49
  472.9 36.8 %collective-permute-start.53 = (bf16[384,2048]{1,0:T(8,128)(2,1)}, bf16[384,2048]{1,0:T(8,128)(2,1)}, u32[]{:S(2)}, u32[]{:S(2)}) collective-permute-start(bf16[384,2048]{1,0:T(8,128)(2,1)} %get-tuple-element.154.refs_0_.refs_1_), channel_id=1, source_target_pairs={{0,2},{1,3},{2,0},{3,1},{4,6},{5,7},{6,4},{7,5},{8,10},{9,11},{10,... | collective-permute-start | bytes 4718600 | tf_op jit(solution)/shard_map/ppermute | solution.py:49
  490.5 174.1 %reduce-scatter.10.cloned.1.call-start = ((), (), s32[]{:S(2)}) async-start(), calls=%async_computation.15 | async-start | bytes 3932160 | tf_op jit(solution)/shard_map/reduce_scatter | solution.py:72
  491.3 45.1 %collective-permute-start.41 = (bf16[384,2048]{1,0:T(8,128)(2,1)}, bf16[384,2048]{1,0:T(8,128)(2,1)}, u32[]{:S(2)}, u32[]{:S(2)}) collective-permute-start(bf16[384,2048]{1,0:T(8,128)(2,1)} %get-tuple-element.105), channel_id=1, source_target_pairs={{0,1},{1,0},{2,3},{3,2},{4,5},{5,4},{6,7},{7,6},{8,9},{9,8},{10,11... | collective-permute-start | bytes 4718600 | tf_op jit(solution)/shard_map/ppermute | solution.py:49
  493.5 43.3 %collective-permute-start.40 = (bf16[384,2048]{1,0:T(8,128)(2,1)}, bf16[384,2048]{1,0:T(8,128)(2,1)}, u32[]{:S(2)}, u32[]{:S(2)}) collective-permute-start(bf16[384,2048]{1,0:T(8,128)(2,1)} %get-tuple-element.103), channel_id=1, source_target_pairs={{0,1},{1,0},{2,3},{3,2},{4,5},{5,4},{6,7},{7,6},{8,9},{9,8},{10,11... | collective-permute-start | bytes 4718600 | tf_op jit(solution)/shard_map/ppermute | solution.py:49
  493.5 50.9 %collective-permute-start.39 = (bf16[384,2048]{1,0:T(8,128)(2,1)}, bf16[384,2048]{1,0:T(8,128)(2,1)}, u32[]{:S(2)}, u32[]{:S(2)}) collective-permute-start(bf16[384,2048]{1,0:T(8,128)(2,1)} %get-tuple-element.101), channel_id=1, source_target_pairs={{0,1},{1,0},{2,3},{3,2},{4,5},{5,4},{6,7},{7,6},{8,9},{9,8},{10,11... | collective-permute-start | bytes 4718600 | tf_op jit(solution)/shard_map/ppermute | solution.py:49
  508.7 20.3 %collective-permute-start.57 = (bf16[192,2048]{1,0:T(8,128)(2,1)}, bf16[192,2048]{1,0:T(8,128)(2,1)}, u32[]{:S(2)}, u32[]{:S(2)}) collective-permute-start(bf16[192,2048]{1,0:T(8,128)(2,1)} %slice.288), channel_id=1, source_target_pairs={{0,2},{1,3},{2,0},{3,1},{4,6},{5,7},{6,4},{7,5},{8,10},{9,11},{10,... | collective-permute-start | bytes 2359304 | tf_op jit(solution)/shard_map/ppermute | solution.py:49
  511.8 22.4 %collective-permute-start.58 = (bf16[192,2048]{1,0:T(8,128)(2,1)}, bf16[192,2048]{1,0:T(8,128)(2,1)}, u32[]{:S(2)}, u32[]{:S(2)}) collective-permute-start(bf16[192,2048]{1,0:T(8,128)(2,1)} %slice.289), channel_id=1, source_target_pairs={{0,4},{1,5},{2,6},{3,7},{4,0},{5,1},{6,2},{7,3},{8,12},{9,13},{10,... | collective-permute-start | bytes 2359304 | tf_op jit(solution)/shard_map/ppermute | solution.py:49
  528.9 20.4 %collective-permute-start.52 = (bf16[384,2048]{1,0:T(8,128)(2,1)}, bf16[384,2048]{1,0:T(8,128)(2,1)}, u32[]{:S(2)}, u32[]{:S(2)}) collective-permute-start(bf16[384,2048]{1,0:T(8,128)(2,1)} %get-tuple-element.154.refs_0_.refs_1_), channel_id=1, source_target_pairs={{0,1},{1,0},{2,3},{3,2},{4,5},{5,4},{6,7},{7,6},{8,9},{9,8},{10,11... | collective-permute-start | bytes 4718600 | tf_op jit(solution)/shard_map/ppermute | solution.py:49
  552.7 78.7 %collective-permute-start.61 = (bf16[192,2048]{1,0:T(8,128)(2,1)}, bf16[192,2048]{1,0:T(8,128)(2,1)}, u32[]{:S(2)}, u32[]{:S(2)}) collective-permute-start(bf16[192,2048]{1,0:T(8,128)(2,1)} %get-tuple-element.162), channel_id=1, source_target_pairs={{0,2},{1,3},{2,0},{3,1},{4,6},{5,7},{6,4},{7,5},{8,10},{9,11},{10,... | collective-permute-start | bytes 2359304 | tf_op jit(solution)/shard_map/ppermute | solution.py:49
  553.0 81.2 %collective-permute-start.63 = (bf16[192,2048]{1,0:T(8,128)(2,1)}, bf16[192,2048]{1,0:T(8,128)(2,1)}, u32[]{:S(2)}, u32[]{:S(2)}) collective-permute-start(bf16[192,2048]{1,0:T(8,128)(2,1)} %get-tuple-element.163), channel_id=1, source_target_pairs={{0,4},{1,5},{2,6},{3,7},{4,0},{5,1},{6,2},{7,3},{8,12},{9,13},{10,... | collective-permute-start | bytes 2359304 | tf_op jit(solution)/shard_map/ppermute | solution.py:49
  553.9 81.0 %collective-permute-start.60 = (bf16[192,2048]{1,0:T(8,128)(2,1)}, bf16[192,2048]{1,0:T(8,128)(2,1)}, u32[]{:S(2)}, u32[]{:S(2)}) collective-permute-start(bf16[192,2048]{1,0:T(8,128)(2,1)} %get-tuple-element.118.refs_1_), channel_id=1, source_target_pairs={{0,2},{1,3},{2,0},{3,1},{4,6},{5,7},{6,4},{7,5},{8,10},{9,11},{10,... | collective-permute-start | bytes 2359304 | tf_op jit(solution)/shard_map/ppermute | solution.py:49
  554.4 83.4 %collective-permute-start.65 = (bf16[192,2048]{1,0:T(8,128)(2,1)}, bf16[192,2048]{1,0:T(8,128)(2,1)}, u32[]{:S(2)}, u32[]{:S(2)}) collective-permute-start(bf16[192,2048]{1,0:T(8,128)(2,1)} %get-tuple-element.120.refs_2_), channel_id=1, source_target_pairs={{0,4},{1,5},{2,6},{3,7},{4,0},{5,1},{6,2},{7,3},{8,12},{9,13},{10,... | collective-permute-start | bytes 2359304 | tf_op jit(solution)/shard_map/ppermute | solution.py:49
  556.2 183.6 %reduce-scatter.12.cloned.1.call-start = ((), (), s32[]{:S(2)}) async-start(), calls=%async_computation.16 | async-start | bytes 2949120 | tf_op jit(solution)/shard_map/reduce_scatter | solution.py:72
  644.4 39.1 %collective-permute-start.62 = (bf16[192,2048]{1,0:T(8,128)(2,1)}, bf16[192,2048]{1,0:T(8,128)(2,1)}, u32[]{:S(2)}, u32[]{:S(2)}) collective-permute-start(bf16[192,2048]{1,0:T(8,128)(2,1)} %fusion.24), channel_id=1, source_target_pairs={{0,4},{1,5},{2,6},{3,7},{4,0},{5,1},{6,2},{7,3},{8,12},{9,13},{10,... | collective-permute-start | bytes 2359304 | tf_op jit(solution)/shard_map/ppermute | solution.py:49
  653.8 63.7 %collective-permute-start.66 = (bf16[384,2048]{1,0:T(8,128)(2,1)}, bf16[384,2048]{1,0:T(8,128)(2,1)}, u32[]{:S(2)}, u32[]{:S(2)}) collective-permute-start(bf16[384,2048]{1,0:T(8,128)(2,1)} %get-tuple-element.136), channel_id=1, source_target_pairs={{0,1},{1,0},{2,3},{3,2},{4,5},{5,4},{6,7},{7,6},{8,9},{9,8},{10,11... | collective-permute-start | bytes 4718600 | tf_op jit(solution)/shard_map/ppermute | solution.py:49
  656.2 20.0 %collective-permute-start.71 = (bf16[192,2048]{1,0:T(8,128)(2,1)}, bf16[192,2048]{1,0:T(8,128)(2,1)}, u32[]{:S(2)}, u32[]{:S(2)}) collective-permute-start(bf16[192,2048]{1,0:T(8,128)(2,1)} %get-tuple-element.160), channel_id=1, source_target_pairs={{0,2},{1,3},{2,0},{3,1},{4,6},{5,7},{6,4},{7,5},{8,10},{9,11},{10,... | collective-permute-start | bytes 2359304 | tf_op jit(solution)/shard_map/ppermute | solution.py:49
  659.7 33.4 %collective-permute-start.68 = (bf16[192,2048]{1,0:T(8,128)(2,1)}, bf16[192,2048]{1,0:T(8,128)(2,1)}, u32[]{:S(2)}, u32[]{:S(2)}) collective-permute-start(bf16[192,2048]{1,0:T(8,128)(2,1)} %slice.366), channel_id=1, source_target_pairs={{0,2},{1,3},{2,0},{3,1},{4,6},{5,7},{6,4},{7,5},{8,10},{9,11},{10,... | collective-permute-start | bytes 2359304 | tf_op jit(solution)/shard_map/ppermute | solution.py:49
  660.4 21.7 %collective-permute-start.73 = (bf16[192,2048]{1,0:T(8,128)(2,1)}, bf16[192,2048]{1,0:T(8,128)(2,1)}, u32[]{:S(2)}, u32[]{:S(2)}) collective-permute-start(bf16[192,2048]{1,0:T(8,128)(2,1)} %get-tuple-element.161), channel_id=1, source_target_pairs={{0,4},{1,5},{2,6},{3,7},{4,0},{5,1},{6,2},{7,3},{8,12},{9,13},{10,... | collective-permute-start | bytes 2359304 | tf_op jit(solution)/shard_map/ppermute | solution.py:49
  676.2 41.1 %collective-permute-start.75 = (bf16[192,2048]{1,0:T(8,128)(2,1)}, bf16[192,2048]{1,0:T(8,128)(2,1)S(1)}, u32[]{:S(2)}, u32[]{:S(2)}) collective-permute-start(bf16[192,2048]{1,0:T(8,128)(2,1)} %slice.365), channel_id=1, source_target_pairs={{0,4},{1,5},{2,6},{3,7},{4,0},{5,1},{6,2},{7,3},{8,12},{9,13},{10,... | collective-permute-start | bytes 2359304 | tf_op jit(solution)/shard_map/ppermute | solution.py:49
  682.1 33.6 %collective-permute-start.72 = (bf16[192,2048]{1,0:T(8,128)(2,1)S(1)}, bf16[192,2048]{1,0:T(8,128)(2,1)S(1)}, u32[]{:S(2)}, u32[]{:S(2)}) collective-permute-start(bf16[192,2048]{1,0:T(8,128)(2,1)S(1)} %fusion.22), channel_id=1, source_target_pairs={{0,4},{1,5},{2,6},{3,7},{4,0},{5,1},{6,2},{7,3},{8,12},{9,13},{10,... | collective-permute-start | bytes 2359304 | tf_op jit(solution)/shard_map/ppermute | solution.py:49
  683.5 33.8 %collective-permute-start.74 = (bf16[192,2048]{1,0:T(8,128)(2,1)S(1)}, bf16[192,2048]{1,0:T(8,128)(2,1)S(1)}, u32[]{:S(2)}, u32[]{:S(2)}) collective-permute-start(bf16[192,2048]{1,0:T(8,128)(2,1)S(1)} %fusion.21), channel_id=1, source_target_pairs={{0,2},{1,3},{2,0},{3,1},{4,6},{5,7},{6,4},{7,5},{8,10},{9,11},{10,... | collective-permute-start | bytes 2359304 | tf_op jit(solution)/shard_map/ppermute | solution.py:49
  693.1 43.0 %collective-permute-start.38 = (bf16[384,2048]{1,0:T(8,128)(2,1)}, bf16[384,2048]{1,0:T(8,128)(2,1)}, u32[]{:S(2)}, u32[]{:S(2)}) collective-permute-start(bf16[384,2048]{1,0:T(8,128)(2,1)} %get-tuple-element.99), channel_id=1, source_target_pairs={{0,1},{1,0},{2,3},{3,2},{4,5},{5,4},{6,7},{7,6},{8,9},{9,8},{10,11... | collective-permute-start | bytes 4718600 | tf_op jit(solution)/shard_map/ppermute | solution.py:49
  726.0 23.3 %all-to-all-start.3 = ((bf16[8,64,1536]{2,1,0:T(8,128)(2,1)}), bf16[8,64,1536]{2,1,0:T(8,128)(2,1)}, u32[]{:S(2)}, u32[]{:S(2)}) async-start(bf16[8,64,1536]{2,1,0:T(8,128)(2,1)} %bitcast.90), calls=%async_computation.8 | async-start | bytes 3145728 | tf_op jit(solution)/shard_map/all_to_all | solution.py:60
  731.2 49.7 %reduce-scatter.14.cloned.1.call-start = ((), (), s32[]{:S(2)}) async-start(), calls=%async_computation.17 | async-start | bytes 1310720 | tf_op jit(solution)/shard_map/reduce_scatter | solution.py:72
  749.3 25.3 %all-to-all-start.2 = ((bf16[8,72,512]{2,1,0:T(8,128)(2,1)}), bf16[8,72,512]{2,1,0:T(8,128)(2,1)}, u32[]{:S(2)}, u32[]{:S(2)}) async-start(bf16[8,72,512]{2,1,0:T(8,128)(2,1)} %bitcast.91), calls=%async_computation.6 | async-start | bytes 1179648 | tf_op jit(solution)/shard_map/all_to_all | solution.py:60
  (101 other events, 1153.4 us)
Sparse Core Ops, SparseCore 0:
  9.7 29.8 all-gather.14
  41.1 50.0 all-gather.6
  92.8 62.2 all-gather.8
  165.2 64.0 all-gather.10
  230.7 62.1 all-gather.12
  405.6 58.9 reduce-scatter.5
  490.6 60.6 reduce-scatter.7
  556.3 59.8 reduce-scatter.9
  664.7 50.2 reduce-scatter.11
  740.0 31.3 reduce-scatter.13

commit v2 on v1

--- a/solution.py
+++ b/solution.py
@@ -376,11 +376,11 @@
         wa, wh, wo, normed_all, qkv_all, logit_all, gated_all = refs[1 + TEAM : 8 + TEAM]
         gains_ref, cos_ref, sin_ref, _ = refs[8 + TEAM : 12 + TEAM]
         parts = refs[12 + TEAM : 12 + 2 * TEAM]
-        attn_sum, out_sum, gain_sum, gains_sum = refs[12 + 2 * TEAM : 16 + 2 * TEAM]
+        attn_part, head_sum, out_part, gain_sum, gains_sum = refs[12 + 2 * TEAM : 17 + 2 * TEAM]
         (
-            hid_v, wa_v, wh_v, wo_v, normed_v, qkv_v, logit_v, gated_v, part_v, back_v,
+            hid_v, wa_v, wh_v, wo_v, normed_v, qkv_v, logit_v, gated_v, part_v, back_v, attn_sum, out_sum,
             w_sem, in_sem, out_sem,
-        ) = refs[16 + 2 * TEAM :]
+        ) = refs[17 + 2 * TEAM :]
 
         def loads(r, slot, k):
             yield pltpu.make_async_copy(hids[k], hid_v.at[slot], in_sem.at[0, slot])
@@ -483,6 +483,9 @@
             return carry
 
         lax.fori_loop(0, TEAM, step, 0)
+        attn_part[...] = attn_sum[:cols].T.astype(BF16)
+        head_sum[...] = attn_sum[cols : cols + 8]
+        out_part[...] = out_sum[...].astype(BF16)
         store(0).wait()
         store(1).wait()
 
@@ -490,13 +493,14 @@
         kernel,
         out_shape=[struct((rows, width), BF16)] * TEAM
         + [
-            struct((cols + TILE, width), F32),
-            struct((q_cols, width), F32),
+            struct((width, cols), BF16),
+            struct((8, width), F32),
+            struct((q_cols, width), BF16),
             struct((8, width), F32),
             struct((8, size), F32),
         ],
         in_specs=[SMEM] + [ANY] * (TEAM + 7) + [VMEM] * 3 + [ANY],
-        out_specs=[ANY] * TEAM + [VMEM] * 4,
+        out_specs=[ANY] * TEAM + [VMEM] * 5,
         scratch_shapes=[
             pltpu.VMEM((2, rows, width), BF16),
             pltpu.VMEM(weight_attn.shape, BF16),
@@ -508,6 +512,8 @@
             pltpu.VMEM((2, rows, q_cols), BF16),
             pltpu.VMEM((2, rows, width), BF16),
             pltpu.VMEM((rows, cols + TILE), BF16),
+            pltpu.VMEM((cols + TILE, width), F32),
+            pltpu.VMEM((q_cols, width), F32),
             pltpu.SemaphoreType.DMA((3,)),
             pltpu.SemaphoreType.DMA((5, 2)),
             pltpu.SemaphoreType.DMA((2,)),
@@ -515,7 +521,7 @@
         compiler_params=pltpu.CompilerParams(vmem_limit_bytes=56 << 20),
         cost_estimate=pl.CostEstimate(flops=45 << 30, bytes_accessed=70 << 20, transcendentals=1 << 20),
     )(tiles, *hidden, weight_attn, weight_head, weight_out, *saved, gains, cosine, sine, after)
-    return result[:TEAM], result[TEAM], result[TEAM + 1], result[TEAM + 2][0], result[TEAM + 3][:2]
+    return result[:TEAM], *result[TEAM : TEAM + 3], result[TEAM + 3][0], result[TEAM + 4][:2]
 
 
 def tile_places(tiles_ref, rows):
@@ -792,7 +798,7 @@
         return w.reshape(rho, groups, TEAM, phi).transpose(2, 0, 1, 3).reshape(TEAM, rho, ff_cols)
 
     feed_shard = jnp.concatenate([ff_split(gate_weight), ff_split(up_weight)], axis=2)
-    feed_shard = exchange(feed_shard).reshape(TEAM * rho, -1)
+    feed_shard = exchange(hold([feed_shard], weight_out)[0]).reshape(TEAM * rho, -1)
     weight_gate = line_gather(feed_shard[:, :ff_cols])
 
     exponent = jnp.arange(size // 2, dtype=F32) * (-2.0 / size)
@@ -821,14 +827,14 @@
     hidden_state = inputs + arrived.total()
 
     normed_two = rms(hidden_state, gain_two).astype(BF16)
-    normed_two = hold([normed_two], mark(team_upstream + [weight_up]))[0]
-    team_two = team_gather(normed_two)
+    normed_two = hold([normed_two], mark(team_upstream))[0]
+    team_two = TeamGather(normed_two).blocks(mark([weight_up]))
     outs, grads, saved = feed(tiles, team_two, team_upstream, weight_gate, weight_up, weight_down)
     inner, feed_back, two_all, ups_all = saved
     arrived = TeamSum(grads)
     arrived.first()
     two_grad = arrived.total()
-    inner, feed_back = hold([inner, feed_back], arrived.low6)
+    inner, feed_back = hold([inner, feed_back], mark(arrived.ready))
     down_part = product_tn(inner, ups_all).astype(BF16)
     gate_part = product_tn(two_all, feed_back[:, :ff_cols]).astype(BF16)
     up_part = product_tn(two_all, feed_back[:, ff_cols:]).astype(BF16)
@@ -840,23 +846,16 @@
     hidden_grad = upstream + rms_pull(hidden_state, gain_two, two_grad)
 
     fed = TeamSum(outs)
-    team_hidden = team_gather(hidden_grad.astype(BF16))
+    team_hidden = TeamGather(hidden_grad.astype(BF16)).blocks(mark(fed.ready + [gate_part]))
     two_scale = lax.rsqrt(jnp.mean(hidden_state * hidden_state, axis=-1, keepdims=True) + EPSILON)
     two_sum = jnp.sum(two_grad * hidden_state * two_scale, axis=0)
     first_hop = fed.first(mark(team_hidden + [parts_made]))
-    parts, attn_sum, out_sum, one_sum, pair_sum = attend_back(
+    parts, attn_part, head_sum, out_part, one_sum, pair_sum = attend_back(
         tiles, team_hidden, consts, (normed, qkv, logit, gated), mine, mark(fed.sent + [down_grad])
     )
-    parts = hold(parts, mark(first_hop + [gate_grad]))
-    arrived = TeamSum(parts)
-    arrived.first()
-    normed_grad = arrived.total()
-    layer_output = ((hidden_state + fed.total()) * live_rows).astype(BF16)
-    tokens_grad = (hidden_grad + rms_pull(inputs, gain_one, normed_grad)).astype(BF16)
-    head_part = attn_sum[cols : cols + mine]
     row = jnp.concatenate(
         [
-            head_part.reshape(mine, everyone, rho).transpose(1, 0, 2).reshape(everyone, -1),
+            head_sum[:mine].reshape(mine, everyone, rho).transpose(1, 0, 2).reshape(everyone, -1),
             (one_sum / gain_one[0]).reshape(everyone, rho),
             two_sum.reshape(everyone, rho),
             pair_sum.reshape(2, everyone, pair_cols).transpose(1, 0, 2).reshape(everyone, -1),
@@ -864,13 +863,18 @@
         axis=1,
     ).astype(BF16)
     row = jnp.pad(row, ((0, 0), (0, cols - row.shape[1])))[:, None, :]
-    attn_part = attn_sum[:cols].astype(BF16).T
     packed = jnp.concatenate(
         [attn_part.reshape(everyone, rho, cols), jnp.pad(row, ((0, 0), (0, 7), (0, 0)))], axis=1
     )
-    packed = packed.reshape(everyone * (rho + 8), cols)
-    packed = line_sum(hold([packed], feed_done)[0])
-    output_grad, packed = out_weight_back(out_sum.astype(BF16), groups, packed)
+    packed = hold([packed.reshape(everyone * (rho + 8), cols)], feed_done)[0]
+    parts = hold(parts, mark(first_hop + [gate_grad]))
+    arrived = TeamSum(parts)
+    arrived.first(packed)
+    packed = line_sum(packed)
+    normed_grad = arrived.total()
+    layer_output = ((hidden_state + fed.total()) * live_rows).astype(BF16)
+    tokens_grad = (hidden_grad + rms_pull(inputs, gain_one, normed_grad)).astype(BF16)
+    output_grad, packed = out_weight_back(hold([out_part], arrived.u4)[0], groups, packed)
     packed = exchange(packed.reshape(TEAM, rho + 8, cols))
     feed_grad = jnp.concatenate([gate_grad, hold([up_grad], normed_grad)[0]], axis=1)
     feed_grad = exchange(feed_grad.reshape(TEAM, rho, 2 * ff_cols))

time: 805 us -> 832 us (1.034)
  waiting for transfers between devices: 265 us -> 302 us
  Pallas kernels: 153 us -> 136 us
    ppermute x80, waiting for transfers between devices: 239 us -> 272 us  [permute(): lax.ppermute(array, ALL, [(team[a], team[b]) for team in teams() for a, b...]
    reduce_scatter x5, waiting for transfers between devices: 0.03 us -> 13.5 us  [line_sum(): return lax.psum_scatter(array, 'dp', scatter_dimension=0, tiled=True)]
    all_to_all x3, waiting for transfers between devices: 11.3 us -> 0.01 us  [exchange(): return lax.all_to_all(blocks, 'fsdp', 0, 0, tiled=True)]
    pallas_call x1, Pallas kernels: 51.8 us -> 43.5 us  [attend_back(): pl.pallas_call(kernel, out_shape=[struct((rows, width), BF16)] * TEAM + [...]
    pallas_call x1, Pallas kernels: 67.6 us -> 59.2 us  [feed(): pl.pallas_call(kernel, out_shape=[struct((rows, width), BF16)] * (2 * TEA...]
    unnamed x156 -> x167, local copies, waits for them, and re-layouts: 29.5 us -> 34.3 us
  transfers between devices with their start and end apart: 93 -> 93, of which waited for: 26 -> 34; matrix products, arithmetic and copies ran while one was open for 27% -> 23% of each run, Pallas kernels for 11% -> 9%
where the time goes in v2:
time: 832 us; the launch traced here: 819 us
  waiting for transfers between devices  302 us (36%)
  Pallas kernels  136 us (16%)
  starting transfers between devices  109 us (13%)
  local copies, waits for them, and re-layouts  107 us (13%)
  other arithmetic  87.1 us (10%)
  matrix products  45.9 us (6%)
  between operations  17.2 us (2%)
  blocking collectives  15.1 us (2%)
    ppermute x80, waiting for transfers between devices, permute(): lax.ppermute(array, ALL, [(team[a], team[b]) for team in teams() for a, b...  272 us
    ppermute x80, starting transfers between devices, permute(): lax.ppermute(array, ALL, [(team[a], team[b]) for team in teams() for a, b...  86.5 us
    pallas_call x1, Pallas kernels, feed(): pl.pallas_call(kernel, out_shape=[struct((rows, width), BF16)] * (2 * TEA...  59.2 us
    dot_general x3, matrix products, product_tn(): lax.dot_general(left, right, (((0,), (0,)), ((), ())), preferred_element_...  45.9 us
    pallas_call x1, Pallas kernels, attend_back(): pl.pallas_call(kernel, out_shape=[struct((rows, width), BF16)] * TEAM + [...  43.5 us
    unnamed x167, local copies, waits for them, and re-layouts  34.3 us
    pallas_call x1, Pallas kernels, attend(): pl.pallas_call(kernel, out_shape=[struct((rows, width), BF16)] * TEAM + [...  26.3 us
    all_to_all x3, starting transfers between devices, exchange(): return lax.all_to_all(blocks, 'fsdp', 0, 0, tiled=True)  21.3 us
  transfers between devices with their start and end apart: 93, of which 34 were waited for; matrix products, arithmetic and copies ran while one was open for 23% of the time, Pallas kernels for 9%

profile of v2, /device:TPU:1, one launch (start us, length us, event | category | flops | bytes accessed | tf_op | source)
XLA Modules:
  0.0 818.9 jit_solution(2292445870920936195)
XLA Ops:
  7.3 2.2 copy.238.refs_0_
  11.1 15.1 %all_to_all.20 = bf16[8,72,512]{2,1,0:T(8,128)(2,1)} all-to-all(bf16[8,72,512]{2,1,0:T(8,128)(2,1)S(1)} %copy.141), channel_id=1, replica_groups=mesh['dp'=4,'fsdp'=8] {'fsdp'}, dimensions={0} | all-to-all | bytes 1179648 | tf_op jit(solution)/shard_map/all_to_all | solution.py:60
  26.9 2.2 reshape.275
  31.6 3.0 reshape.277
  41.7 3.8 collective-permute-start.8
  49.6 18.9 %collective-permute-done.8 = bf16[1,64,2048]{2,1,0:T(8,128)(2,1)} collective-permute-done((bf16[1,64,2048]{2,1,0:T(8,128)(2,1)S(1)}, bf16[1,64,2048]{2,1,0:T(8,128)(2,1)}, u32[]{:S(2)}, u32[]{:S(2)}) %collective-permute-start.8) | collective-permute-done | bytes 262176 | tf_op jit(solution)/shard_map/ppermute | solution.py:49
  72.5 3.7 collective-permute-done.11
  77.2 4.6 all-to-all-start.1
  88.3 29.6 %collective-permute-done.5 = bf16[192,2048]{1,0:T(8,128)(2,1)S(1)} collective-permute-done((bf16[192,2048]{1,0:T(8,128)(2,1)S(1)}, bf16[192,2048]{1,0:T(8,128)(2,1)S(1)}, u32[]{:S(2)}, u32[]{:S(2)}) %collective-permute-start.5) | collective-permute-done | bytes 786464 | tf_op jit(solution)/shard_map/ppermute | solution.py:49
  130.7 3.4 slice.257
  137.7 26.3 %shard_map.240 = (bf16[384,2048]{1,0:T(8,128)(2,1)S(1)}, bf16[384,2048]{1,0:T(8,128)(2,1)S(1)}, bf16[384,2048]{1,0:T(8,128)(2,1)}, bf16[384,2048]{1,0:T(8,128)(2...) custom-call(s32[8]{0:T(128)S(1)} %select_reduce_fusion.refs_0_, ...), custom_call_target="tpu_custom_call" | custom-call | flops 32212254720 | bytes 62914560 | tf_op jit(solution)/shard_map/pallas_call | solution.py:334
  166.8 4.8 collective-permute-done.14.refs_2_.refs_4_.refs_13_
  171.7 14.1 %all-gather.9.cloned.1.call-done.refs_3_.refs_17_ = bf16[2048,768]{1,0:T(8,128)(2,1)} async-done(((bf16[512,768]{1,0:T(8,128)(2,1)}), bf16[2048,768]{1,0:T(8,128)(2,1)}) %all-gather.9.cloned.1.call-update) | async-done | bytes 3145744 | tf_op jit(solution)/shard_map/all_gather | solution.py:66
  192.8 14.8 %collective-permute-done.27 = bf16[192,2048]{1,0:T(8,128)(2,1)S(1)} collective-permute-done((bf16[192,2048]{1,0:T(8,128)(2,1)S(1)}, bf16[192,2048]{1,0:T(8,128)(2,1)S(1)}, u32[]{:S(2)}, u32[]{:S(2)}) %collective-permute-start.27) | collective-permute-done | bytes 786464 | tf_op jit(solution)/shard_map/ppermute | solution.py:49
  220.2 11.7 %collective-permute-done.20 = bf16[192,2048]{1,0:T(8,128)(2,1)S(1)} collective-permute-done((bf16[192,2048]{1,0:T(8,128)(2,1)S(1)}, bf16[192,2048]{1,0:T(8,128)(2,1)S(1)}, u32[]{:S(2)}, u32[]{:S(2)}) %collective-permute-start.20) | collective-permute-done | bytes 786464 | tf_op jit(solution)/shard_map/ppermute | solution.py:49
  240.6 13.0 %collective-permute-done.17 = bf16[192,2048]{1,0:T(8,128)(2,1)} collective-permute-done((bf16[192,2048]{1,0:T(8,128)(2,1)}, bf16[192,2048]{1,0:T(8,128)(2,1)}, u32[]{:S(2)}, u32[]{:S(2)}) %collective-permute-start.17) | collective-permute-done | bytes 786464 | tf_op jit(solution)/shard_map/ppermute | solution.py:49
  255.2 15.2 %collective-permute-done.24 = bf16[192,2048]{1,0:T(8,128)(2,1)} collective-permute-done((bf16[192,2048]{1,0:T(8,128)(2,1)}, bf16[192,2048]{1,0:T(8,128)(2,1)}, u32[]{:S(2)}, u32[]{:S(2)}) %collective-permute-start.24) | collective-permute-done | bytes 786464 | tf_op jit(solution)/shard_map/ppermute | solution.py:49
  273.2 2.3 multiply_reduce_fusion.2
  279.3 31.8 %collective-permute-done.31.refs_0_ = bf16[384,2048]{1,0:T(8,128)(2,1)} collective-permute-done((bf16[384,2048]{1,0:T(8,128)(2,1)}, bf16[384,2048]{1,0:T(8,128)(2,1)}, u32[]{:S(2)}, u32[]{:S(2)}) %collective-permute-start.31) | collective-permute-done | bytes 1572896 | tf_op jit(solution)/shard_map/ppermute | solution.py:49
  316.2 3.8 collective-permute-start.30
  320.5 8.2 collective-permute-done.35
  331.6 4.4 collective-permute-start.37
  339.3 59.2 %shard_map.249 = (bf16[384,2048]{1,0:T(8,128)(2,1)}, bf16[384,2048]{1,0:T(8,128)(2,1)}, bf16[384,2048]{1,0:T(8,128)(2,1)}, bf16[384,2048]{1,0:T(8,128)(2,1)}, bf...) custom-call(s32[8]{0:T(128)} %copy-done.12, ...), custom_call_target="tpu_custom_call" | custom-call | flops 62277025792 | bytes 104857600 | tf_op jit(solution)/shard_map/pallas_call | solution.py:682
  399.6 2.7 collective-permute-done.43
  412.4 15.6 %convolution_convert_fusion = bf16[768,2048]{1,0:T(8,128)(2,1)} fusion(bf16[3072,768]{1,0:T(8,128)(2,1)} %get-tuple-element.137, bf16[3072,2048]{1,0:T(8,128)(2,1)} %get-tuple-element.138), kind=kOutput, calls=%fused_computation.12 | convolution fusion | flops 9665249280 | bytes 20447232 | tf_op jit(solution)/shard_map/dot_general | solution.py:29
  434.1 15.0 %collective-permute-done.47 = bf16[192,2048]{1,0:T(8,128)(2,1)S(1)} collective-permute-done((bf16[192,2048]{1,0:T(8,128)(2,1)S(1)}, bf16[192,2048]{1,0:T(8,128)(2,1)S(1)}, u32[]{:S(2)}, u32[]{:S(2)}) %collective-permute-start.47) | collective-permute-done | bytes 786464 | tf_op jit(solution)/shard_map/ppermute | solution.py:49
  451.3 14.6 %fusion.5.refs_3_.refs_0_ = bf16[2048,768]{1,0:T(8,128)(2,1)S(1)} fusion(bf16[3072,2048]{1,0:T(8,128)(2,1)} %get-tuple-element.124, bf16[3072,1536]{1,0:T(8,128)(2,1)} %get-tuple-element.127), kind=kOutput, calls=%fused_computation.10 | convolution fusion | flops 9665249280 | bytes 20447232 | tf_op jit(solution)/shard_map/dot_general | solution.py:29
  468.6 2.5 collective-permute-start.41
  471.0 11.9 %collective-permute-done.48 = bf16[192,2048]{1,0:T(8,128)(2,1)S(1)} collective-permute-done((bf16[192,2048]{1,0:T(8,128)(2,1)S(1)}, bf16[192,2048]{1,0:T(8,128)(2,1)S(1)}, u32[]{:S(2)}, u32[]{:S(2)}) %collective-permute-start.48) | collective-permute-done | bytes 786464 | tf_op jit(solution)/shard_map/ppermute | solution.py:49
  488.5 5.7 reduce-scatter.6.cloned.1.call-done.refs_3_.refs_1_
  494.5 7.0 fusion.44
  513.7 3.2 add_convert_fusion.2.refs_0_
  517.5 19.4 %collective-permute-done.53.refs_0_ = bf16[384,2048]{1,0:T(8,128)(2,1)} collective-permute-done((bf16[384,2048]{1,0:T(8,128)(2,1)}, bf16[384,2048]{1,0:T(8,128)(2,1)}, u32[]{:S(2)}, u32[]{:S(2)}) %collective-permute-start.53) | collective-permute-done | bytes 1572896 | tf_op jit(solution)/shard_map/ppermute | solution.py:49
  541.8 2.5 collective-permute-start.52
  544.9 11.3 %collective-permute-done.57 = bf16[192,2048]{1,0:T(8,128)(2,1)S(1)} collective-permute-done((bf16[192,2048]{1,0:T(8,128)(2,1)S(1)}, bf16[192,2048]{1,0:T(8,128)(2,1)S(1)}, u32[]{:S(2)}, u32[]{:S(2)}) %collective-permute-start.57) | collective-permute-done | bytes 786464 | tf_op jit(solution)/shard_map/ppermute | solution.py:49
  558.4 3.2 collective-permute-start.59
  561.5 15.8 %fusion.8.refs_1_.refs_0_ = bf16[2048,768]{1,0:T(8,128)(2,1)} fusion(bf16[3072,2048]{1,0:T(8,128)(2,1)} %get-tuple-element.124, bf16[3072,1536]{1,0:T(8,128)(2,1)} %get-tuple-element.127), kind=kOutput, calls=%fused_computation.11 | convolution fusion | flops 9665249280 | bytes 20447232 | tf_op jit(solution)/shard_map/dot_general | solution.py:29
  578.5 2.7 fusion.47
  584.8 43.5 %shard_map.258 = (bf16[384,2048]{1,0:T(8,128)(2,1)}, bf16[384,2048]{1,0:T(8,128)(2,1)}, bf16[384,2048]{1,0:T(8,128)(2,1)}, bf16[384,2048]{1,0:T(8,128)(2,1)}, bf...) custom-call(s32[8]{0:T(128)} %copy-done.12, ...), custom_call_target="tpu_custom_call" | custom-call | flops 48318382080 | bytes 73400320 | tf_op jit(solution)/shard_map/pallas_call | solution.py:492
  634.1 2.6 convert_element_type.445
  639.5 2.2 fusion.24
  653.2 2.8 fusion.46
  657.2 2.2 fusion.23
  661.0 2.7 convert_add_fusion.12
  666.0 9.1 %collective-permute-done.71.refs_1_ = bf16[192,2048]{1,0:T(8,128)(2,1)} collective-permute-done((bf16[192,2048]{1,0:T(8,128)(2,1)}, bf16[192,2048]{1,0:T(8,128)(2,1)}, u32[]{:S(2)}, u32[]{:S(2)}) %collective-permute-start.71) | collective-permute-done | bytes 786464 | tf_op jit(solution)/shard_map/ppermute | solution.py:49
  675.3 2.9 fusion.22
  679.2 2.2 fusion.21
  681.4 10.4 %collective-permute-done.64 = bf16[192,2048]{1,0:T(8,128)(2,1)} collective-permute-done((bf16[192,2048]{1,0:T(8,128)(2,1)}, bf16[192,2048]{1,0:T(8,128)(2,1)}, u32[]{:S(2)}, u32[]{:S(2)}) %collective-permute-start.64) | collective-permute-done | bytes 786464 | tf_op jit(solution)/shard_map/ppermute | solution.py:49
  693.0 2.7 convert_add_fusion.11
  697.8 10.9 %collective-permute-done.70 = bf16[192,2048]{1,0:T(8,128)(2,1)} collective-permute-done((bf16[192,2048]{1,0:T(8,128)(2,1)}, bf16[192,2048]{1,0:T(8,128)(2,1)}, u32[]{:S(2)}, u32[]{:S(2)}) %collective-permute-start.70) | collective-permute-done | bytes 786464 | tf_op jit(solution)/shard_map/ppermute | solution.py:49
  708.7 2.2 collective-permute-start.38
  711.8 3.9 collective-permute-start.76
  717.3 2.9 collective-permute-start.77
  720.3 5.3 collective-permute-done.74
  727.2 4.3 fusion.11
  731.5 2.6 pad_maximum_fusion.1
  734.1 6.3 all-to-all-start.3
  740.5 5.1 fusion.19
  745.6 2.6 collective-permute-start.78
  752.1 14.8 %collective-permute-done.78 = bf16[1,64,2048]{2,1,0:T(8,128)(2,1)S(1)} collective-permute-done((bf16[1,64,2048]{2,1,0:T(8,128)(2,1)S(1)}, bf16[1,64,2048]{2,1,0:T(8,128)(2,1)S(1)}, u32[]{:S(2)}, u32[]{:S(2)}) %collective-permute-start.78) | collective-permute-done | bytes 262176 | tf_op jit(solution)/shard_map/ppermute | solution.py:49
  768.0 10.4 %all-to-all-start.2 = ((bf16[8,72,512]{2,1,0:T(8,128)(2,1)}), bf16[8,72,512]{2,1,0:T(8,128)(2,1)}, u32[]{:S(2)}, u32[]{:S(2)}) async-start(bf16[8,72,512]{2,1,0:T(8,128)(2,1)} %bitcast.91), calls=%async_computation.6 | async-start | bytes 1179648 | tf_op jit(solution)/shard_map/all_to_all | solution.py:60
  778.4 4.4 fusion.15
  792.3 2.5 convert_element_type.443
  802.3 7.8 reduce-scatter.14.cloned.1.call-done
  (494 shorter events, 203.5 us)
Async XLA Ops:
  7.3 32.3 %all-gather.15.cloned.1.call-start = ((), (), s32[]{:S(2)}) async-start(), calls=%async_computation.18 | async-start | bytes 1310720 | tf_op jit(solution)/shard_map/all_gather | solution.py:66
  9.6 120.1 %all-gather.7.cloned.1.call-start = ((), (), s32[]{:S(2)}) async-start(), calls=%async_computation.9 | async-start | bytes 2949120 | tf_op jit(solution)/shard_map/all_gather | solution.py:66
  26.2 55.5 %collective-permute-start.3 = (bf16[384,2048]{1,0:T(8,128)(2,1)S(1)}, bf16[384,2048]{1,0:T(8,128)(2,1)}, u32[]{:S(2)}, u32[]{:S(2)}) collective-permute-start(bf16[384,2048]{1,0:T(8,128)(2,1)S(1)} %copy-done.20), channel_id=1, source_target_pairs={{0,4},{1,5},{2,6},{3,7},{4,0},{5,1},{6,2},{7,3},{8,12},{9,13},{10,... | collective-permute-start | bytes 4718600 | tf_op jit(solution)/shard_map/ppermute | solution.py:49
  26.6 57.8 %collective-permute-start.1 = (bf16[384,2048]{1,0:T(8,128)(2,1)S(1)}, bf16[384,2048]{1,0:T(8,128)(2,1)}, u32[]{:S(2)}, u32[]{:S(2)}) collective-permute-start(bf16[384,2048]{1,0:T(8,128)(2,1)S(1)} %copy-done.20), channel_id=1, source_target_pairs={{0,2},{1,3},{2,0},{3,1},{4,6},{5,7},{6,4},{7,5},{8,10},{9,11},{10,... | collective-permute-start | bytes 4718600 | tf_op jit(solution)/shard_map/ppermute | solution.py:49
  41.7 26.8 %collective-permute-start.8 = (bf16[1,64,2048]{2,1,0:T(8,128)(2,1)S(1)}, bf16[1,64,2048]{2,1,0:T(8,128)(2,1)}, u32[]{:S(2)}, u32[]{:S(2)}) collective-permute-start(bf16[1,64,2048]{2,1,0:T(8,128)(2,1)S(1)} %get-tuple-element.193), channel_id=1, source_target_pairs={{0,0},{1,2},{2,4},{3,6},{4,1},{5,3},{6,5},{7,7},{8,8},{9,10},{10,1... | collective-permute-start | bytes 786440 | tf_op jit(solution)/shard_map/ppermute | solution.py:49
  45.5 26.0 %collective-permute-start.9 = (bf16[1,64,2048]{2,1,0:T(8,128)(2,1)}, bf16[1,64,2048]{2,1,0:T(8,128)(2,1)}, u32[]{:S(2)}, u32[]{:S(2)}) collective-permute-start(bf16[1,64,2048]{2,1,0:T(8,128)(2,1)} %get-tuple-element.192), channel_id=1, source_target_pairs={{0,2},{1,4},{2,6},{3,0},{4,3},{5,5},{6,7},{7,1},{8,10},{9,12},{10,... | collective-permute-start | bytes 786440 | tf_op jit(solution)/shard_map/ppermute | solution.py:49
  48.7 23.8 %collective-permute-start.10 = (bf16[1,64,2048]{2,1,0:T(8,128)(2,1)}, bf16[1,64,2048]{2,1,0:T(8,128)(2,1)S(1)}, u32[]{:S(2)}, u32[]{:S(2)}) collective-permute-start(bf16[1,64,2048]{2,1,0:T(8,128)(2,1)} %get-tuple-element.191), channel_id=1, source_target_pairs={{0,4},{1,6},{2,0},{3,2},{4,5},{5,7},{6,1},{7,3},{8,12},{9,14},{10,... | collective-permute-start | bytes 786440 | tf_op jit(solution)/shard_map/ppermute | solution.py:49
  77.2 43.5 %all-to-all-start.1 = ((bf16[8,64,1536]{2,1,0:T(8,128)(2,1)}), bf16[8,64,1536]{2,1,0:T(8,128)(2,1)S(1)}, u32[]{:S(2)}, u32[]{:S(2)}) async-start(bf16[8,64,1536]{2,1,0:T(8,128)(2,1)} %shard_map.237), calls=%async_computation.1 | async-start | bytes 3145728 | tf_op jit(solution)/shard_map/all_to_all | solution.py:60
  81.8 104.0 %all-gather.9.cloned.1.call-start = ((), (), s32[]{:S(2)}) async-start(), calls=%async_computation.10 | async-start | bytes 3932160 | tf_op jit(solution)/shard_map/all_gather | solution.py:66
  83.0 34.9 %collective-permute-start.5 = (bf16[192,2048]{1,0:T(8,128)(2,1)S(1)}, bf16[192,2048]{1,0:T(8,128)(2,1)S(1)}, u32[]{:S(2)}, u32[]{:S(2)}) collective-permute-start(bf16[192,2048]{1,0:T(8,128)(2,1)S(1)} %slice.255), channel_id=1, source_target_pairs={{0,2},{1,3},{2,0},{3,1},{4,6},{5,7},{6,4},{7,5},{8,10},{9,11},{10,... | collective-permute-start | bytes 2359304 | tf_op jit(solution)/shard_map/ppermute | solution.py:49
  85.6 33.2 %collective-permute-start.6 = (bf16[192,2048]{1,0:T(8,128)(2,1)S(1)}, bf16[192,2048]{1,0:T(8,128)(2,1)S(1)}, u32[]{:S(2)}, u32[]{:S(2)}) collective-permute-start(bf16[192,2048]{1,0:T(8,128)(2,1)S(1)} %slice.256), channel_id=1, source_target_pairs={{0,4},{1,5},{2,6},{3,7},{4,0},{5,1},{6,2},{7,3},{8,12},{9,13},{10,... | collective-permute-start | bytes 2359304 | tf_op jit(solution)/shard_map/ppermute | solution.py:49
  86.9 48.8 %collective-permute-start = (bf16[384,2048]{1,0:T(8,128)(2,1)S(1)}, bf16[384,2048]{1,0:T(8,128)(2,1)}, u32[]{:S(2)}, u32[]{:S(2)}) collective-permute-start(bf16[384,2048]{1,0:T(8,128)(2,1)S(1)} %copy-done.20), channel_id=1, source_target_pairs={{0,1},{1,0},{2,3},{3,2},{4,5},{5,4},{6,7},{7,6},{8,9},{9,8},{10,11... | collective-permute-start | bytes 4718600 | tf_op jit(solution)/shard_map/ppermute | solution.py:49
  87.8 49.3 %collective-permute-start.2 = (bf16[384,2048]{1,0:T(8,128)(2,1)}, bf16[384,2048]{1,0:T(8,128)(2,1)}, u32[]{:S(2)}, u32[]{:S(2)}) collective-permute-start(bf16[384,2048]{1,0:T(8,128)(2,1)} %collective-permute-done.1.refs_3_), channel_id=1, source_target_pairs={{0,1},{1,0},{2,3},{3,2},{4,5},{5,4},{6,7},{7,6},{8,9},{9,8},{10,11... | collective-permute-start | bytes 4718600 | tf_op jit(solution)/shard_map/ppermute | solution.py:49
  87.9 49.8 %collective-permute-start.4 = (bf16[384,2048]{1,0:T(8,128)(2,1)}, bf16[384,2048]{1,0:T(8,128)(2,1)}, u32[]{:S(2)}, u32[]{:S(2)}) collective-permute-start(bf16[384,2048]{1,0:T(8,128)(2,1)} %collective-permute-done.3.refs_5_), channel_id=1, source_target_pairs={{0,1},{1,0},{2,3},{3,2},{4,5},{5,4},{6,7},{7,6},{8,9},{9,8},{10,11... | collective-permute-start | bytes 4718600 | tf_op jit(solution)/shard_map/ppermute | solution.py:49
  122.4 156.4 %all-gather.11.cloned.1.call-start = ((), (), s32[]{:S(2)}) async-start(), calls=%async_computation.11 | async-start | bytes 3932160 | tf_op jit(solution)/shard_map/all_gather | solution.py:66
  128.9 37.9 %collective-permute-start.13 = (bf16[384,2048]{1,0:T(8,128)(2,1)}, bf16[384,2048]{1,0:T(8,128)(2,1)}, u32[]{:S(2)}, u32[]{:S(2)}) collective-permute-start(bf16[384,2048]{1,0:T(8,128)(2,1)} %broadcast_select_fusion.refs_1_.refs_0_.refs_9_), channel_id=1, source_target_pairs={{0,2},{1,3},{2,0},{3,1},{4,6},{5,7},{6,4},{7,5},{8,10},{9,11},{10,... | collective-permute-start | bytes 4718600 | tf_op jit(solution)/shard_map/ppermute | solution.py:49
  135.7 36.0 %collective-permute-start.14 = (bf16[384,2048]{1,0:T(8,128)(2,1)}, bf16[384,2048]{1,0:T(8,128)(2,1)}, u32[]{:S(2)}, u32[]{:S(2)}) collective-permute-start(bf16[384,2048]{1,0:T(8,128)(2,1)} %broadcast_select_fusion.refs_1_.refs_0_.refs_9_), channel_id=1, source_target_pairs={{0,4},{1,5},{2,6},{3,7},{4,0},{5,1},{6,2},{7,3},{8,12},{9,13},{10,... | collective-permute-start | bytes 4718600 | tf_op jit(solution)/shard_map/ppermute | solution.py:49
  137.1 34.6 %collective-permute-start.12 = (bf16[384,2048]{1,0:T(8,128)(2,1)}, bf16[384,2048]{1,0:T(8,128)(2,1)S(1)}, u32[]{:S(2)}, u32[]{:S(2)}) collective-permute-start(bf16[384,2048]{1,0:T(8,128)(2,1)} %broadcast_select_fusion.refs_1_.refs_0_.refs_9_), channel_id=1, source_target_pairs={{0,1},{1,0},{2,3},{3,2},{4,5},{5,4},{6,7},{7,6},{8,9},{9,8},{10,11... | collective-permute-start | bytes 4718600 | tf_op jit(solution)/shard_map/ppermute | solution.py:49
  186.4 24.8 %collective-permute-start.19 = (bf16[384,2048]{1,0:T(8,128)(2,1)}, bf16[384,2048]{1,0:T(8,128)(2,1)S(1)}, u32[]{:S(2)}, u32[]{:S(2)}) collective-permute-start(bf16[384,2048]{1,0:T(8,128)(2,1)} %get-tuple-element.104), channel_id=1, source_target_pairs={{0,1},{1,0},{2,3},{3,2},{4,5},{5,4},{6,7},{7,6},{8,9},{9,8},{10,11... | collective-permute-start | bytes 4718600 | tf_op jit(solution)/shard_map/ppermute | solution.py:49
  189.5 148.8 %all-gather.13.cloned.1.call-start = ((), (), s32[]{:S(2)}) async-start(), calls=%async_computation.12 | async-start | bytes 3932160 | tf_op jit(solution)/shard_map/all_gather | solution.py:66
  192.2 20.8 %collective-permute-start.18 = (bf16[384,2048]{1,0:T(8,128)(2,1)}, bf16[384,2048]{1,0:T(8,128)(2,1)S(1)}, u32[]{:S(2)}, u32[]{:S(2)}) collective-permute-start(bf16[384,2048]{1,0:T(8,128)(2,1)} %get-tuple-element.102), channel_id=1, source_target_pairs={{0,1},{1,0},{2,3},{3,2},{4,5},{5,4},{6,7},{7,6},{8,9},{9,8},{10,11... | collective-permute-start | bytes 4718600 | tf_op jit(solution)/shard_map/ppermute | solution.py:49
  192.8 41.3 %collective-permute-start.25 = (bf16[384,2048]{1,0:T(8,128)(2,1)}, bf16[384,2048]{1,0:T(8,128)(2,1)S(1)}, u32[]{:S(2)}, u32[]{:S(2)}) collective-permute-start(bf16[384,2048]{1,0:T(8,128)(2,1)} %collective-permute-done.13.refs_1_.refs_2_.refs_11_), channel_id=1, source_target_pairs={{0,1},{1,0},{2,3},{3,2},{4,5},{5,4},{6,7},{7,6},{8,9},{9,8},{10,11... | collective-permute-start | bytes 4718600 | tf_op jit(solution)/shard_map/ppermute | solution.py:49
  207.6 29.9 %collective-permute-start.26 = (bf16[384,2048]{1,0:T(8,128)(2,1)}, bf16[384,2048]{1,0:T(8,128)(2,1)S(1)}, u32[]{:S(2)}, u32[]{:S(2)}) collective-permute-start(bf16[384,2048]{1,0:T(8,128)(2,1)} %collective-permute-done.14.refs_2_.refs_4_.refs_13_), channel_id=1, source_target_pairs={{0,1},{1,0},{2,3},{3,2},{4,5},{5,4},{6,7},{7,6},{8,9},{9,8},{10,11... | collective-permute-start | bytes 4718600 | tf_op jit(solution)/shard_map/ppermute | solution.py:49
  210.1 27.8 %collective-permute-start.29 = (bf16[384,2048]{1,0:T(8,128)(2,1)S(1)}, bf16[384,2048]{1,0:T(8,128)(2,1)S(1)}, u32[]{:S(2)}, u32[]{:S(2)}) collective-permute-start(bf16[384,2048]{1,0:T(8,128)(2,1)S(1)} %constant_dynamic-update-slice_fusion.2.refs_6_.refs_15_), channel_id=1, source_target_pairs={{0,1},{1,0},{2,3},{3,2},{4,5},{5,4},{6,7},{7,6},{8,9},{9,8},{10,11... | collective-permute-start | bytes 4718600 | tf_op jit(solution)/shard_map/ppermute | solution.py:49
  231.8 40.2 %collective-permute-start.15 = (bf16[384,2048]{1,0:T(8,128)(2,1)S(1)}, bf16[384,2048]{1,0:T(8,128)(2,1)S(1)}, u32[]{:S(2)}, u32[]{:S(2)}) collective-permute-start(bf16[384,2048]{1,0:T(8,128)(2,1)S(1)} %copy-done.5), channel_id=1, source_target_pairs={{0,1},{1,0},{2,3},{3,2},{4,5},{5,4},{6,7},{7,6},{8,9},{9,8},{10,11... | collective-permute-start | bytes 4718600 | tf_op jit(solution)/shard_map/ppermute | solution.py:49
  237.6 32.8 %collective-permute-start.24 = (bf16[192,2048]{1,0:T(8,128)(2,1)}, bf16[192,2048]{1,0:T(8,128)(2,1)}, u32[]{:S(2)}, u32[]{:S(2)}) collective-permute-start(bf16[192,2048]{1,0:T(8,128)(2,1)} %slice.359), channel_id=1, source_target_pairs={{0,4},{1,5},{2,6},{3,7},{4,0},{5,1},{6,2},{7,3},{8,12},{9,13},{10,... | collective-permute-start | bytes 2359304 | tf_op jit(solution)/shard_map/ppermute | solution.py:49
  238.7 31.7 %collective-permute-start.23 = (bf16[192,2048]{1,0:T(8,128)(2,1)}, bf16[192,2048]{1,0:T(8,128)(2,1)}, u32[]{:S(2)}, u32[]{:S(2)}) collective-permute-start(bf16[192,2048]{1,0:T(8,128)(2,1)} %fusion.27), channel_id=1, source_target_pairs={{0,2},{1,3},{2,0},{3,1},{4,6},{5,7},{6,4},{7,5},{8,10},{9,11},{10,... | collective-permute-start | bytes 2359304 | tf_op jit(solution)/shard_map/ppermute | solution.py:49
  240.5 253.7 %reduce-scatter.6.cloned.1.call-start = ((), (), s32[]{:S(2)}) async-start(), calls=%async_computation.13 | async-start | bytes 3932160 | tf_op jit(solution)/shard_map/reduce_scatter | solution.py:72
  277.0 34.2 %collective-permute-start.31 = (bf16[384,2048]{1,0:T(8,128)(2,1)}, bf16[384,2048]{1,0:T(8,128)(2,1)}, u32[]{:S(2)}, u32[]{:S(2)}) collective-permute-start(bf16[384,2048]{1,0:T(8,128)(2,1)} %shard_map.244.refs_1_), channel_id=1, source_target_pairs={{0,2},{1,3},{2,0},{3,1},{4,6},{5,7},{6,4},{7,5},{8,10},{9,11},{10,... | collective-permute-start | bytes 4718600 | tf_op jit(solution)/shard_map/ppermute | solution.py:49
  277.6 33.9 %collective-permute-start.32 = (bf16[384,2048]{1,0:T(8,128)(2,1)}, bf16[384,2048]{1,0:T(8,128)(2,1)}, u32[]{:S(2)}, u32[]{:S(2)}) collective-permute-start(bf16[384,2048]{1,0:T(8,128)(2,1)} %shard_map.244.refs_1_), channel_id=1, source_target_pairs={{0,4},{1,5},{2,6},{3,7},{4,0},{5,1},{6,2},{7,3},{8,12},{9,13},{10,... | collective-permute-start | bytes 4718600 | tf_op jit(solution)/shard_map/ppermute | solution.py:49
  428.0 156.8 %reduce-scatter.8.cloned.1.call-start = ((), (), s32[]{:S(2)}) async-start(), calls=%async_computation.14 | async-start | bytes 3932160 | tf_op jit(solution)/shard_map/reduce_scatter | solution.py:72
  430.7 19.8 %collective-permute-start.49 = (bf16[192,2048]{1,0:T(8,128)(2,1)S(1)}, bf16[192,2048]{1,0:T(8,128)(2,1)S(1)}, u32[]{:S(2)}, u32[]{:S(2)}) collective-permute-start(bf16[192,2048]{1,0:T(8,128)(2,1)S(1)} %get-tuple-element.181), channel_id=1, source_target_pairs={{0,4},{1,5},{2,6},{3,7},{4,0},{5,1},{6,2},{7,3},{8,12},{9,13},{10,... | collective-permute-start | bytes 2359304 | tf_op jit(solution)/shard_map/ppermute | solution.py:49
  431.9 53.0 %collective-permute-start.42 = (bf16[384,2048]{1,0:T(8,128)(2,1)}, bf16[384,2048]{1,0:T(8,128)(2,1)S(1)}, u32[]{:S(2)}, u32[]{:S(2)}) collective-permute-start(bf16[384,2048]{1,0:T(8,128)(2,1)} %get-tuple-element.117), channel_id=1, source_target_pairs={{0,1},{1,0},{2,3},{3,2},{4,5},{5,4},{6,7},{7,6},{8,9},{9,8},{10,11... | collective-permute-start | bytes 4718600 | tf_op jit(solution)/shard_map/ppermute | solution.py:49
  432.9 35.7 %collective-permute-start.44 = (bf16[192,2048]{1,0:T(8,128)(2,1)}, bf16[192,2048]{1,0:T(8,128)(2,1)S(1)}, u32[]{:S(2)}, u32[]{:S(2)}) collective-permute-start(bf16[192,2048]{1,0:T(8,128)(2,1)} %slice.356.refs_1_), channel_id=1, source_target_pairs={{0,2},{1,3},{2,0},{3,1},{4,6},{5,7},{6,4},{7,5},{8,10},{9,11},{10,... | collective-permute-start | bytes 2359304 | tf_op jit(solution)/shard_map/ppermute | solution.py:49
  433.8 50.8 %collective-permute-start.51 = (bf16[192,2048]{1,0:T(8,128)(2,1)}, bf16[192,2048]{1,0:T(8,128)(2,1)S(1)}, u32[]{:S(2)}, u32[]{:S(2)}) collective-permute-start(bf16[192,2048]{1,0:T(8,128)(2,1)} %slice.355.refs_2_), channel_id=1, source_target_pairs={{0,4},{1,5},{2,6},{3,7},{4,0},{5,1},{6,2},{7,3},{8,12},{9,13},{10,... | collective-permute-start | bytes 2359304 | tf_op jit(solution)/shard_map/ppermute | solution.py:49
  449.3 33.7 %collective-permute-start.48 = (bf16[192,2048]{1,0:T(8,128)(2,1)S(1)}, bf16[192,2048]{1,0:T(8,128)(2,1)S(1)}, u32[]{:S(2)}, u32[]{:S(2)}) collective-permute-start(bf16[192,2048]{1,0:T(8,128)(2,1)S(1)} %fusion.26), channel_id=1, source_target_pairs={{0,4},{1,5},{2,6},{3,7},{4,0},{5,1},{6,2},{7,3},{8,12},{9,13},{10,... | collective-permute-start | bytes 2359304 | tf_op jit(solution)/shard_map/ppermute | solution.py:49
  450.8 34.0 %collective-permute-start.50 = (bf16[192,2048]{1,0:T(8,128)(2,1)S(1)}, bf16[192,2048]{1,0:T(8,128)(2,1)S(1)}, u32[]{:S(2)}, u32[]{:S(2)}) collective-permute-start(bf16[192,2048]{1,0:T(8,128)(2,1)S(1)} %fusion.25), channel_id=1, source_target_pairs={{0,2},{1,3},{2,0},{3,1},{4,6},{5,7},{6,4},{7,5},{8,10},{9,11},{10,... | collective-permute-start | bytes 2359304 | tf_op jit(solution)/shard_map/ppermute | solution.py:49
  468.6 35.3 %collective-permute-start.41 = (bf16[384,2048]{1,0:T(8,128)(2,1)}, bf16[384,2048]{1,0:T(8,128)(2,1)}, u32[]{:S(2)}, u32[]{:S(2)}) collective-permute-start(bf16[384,2048]{1,0:T(8,128)(2,1)} %get-tuple-element.115), channel_id=1, source_target_pairs={{0,1},{1,0},{2,3},{3,2},{4,5},{5,4},{6,7},{7,6},{8,9},{9,8},{10,11... | collective-permute-start | bytes 4718600 | tf_op jit(solution)/shard_map/ppermute | solution.py:49
  483.0 23.9 %collective-permute-start.40 = (bf16[384,2048]{1,0:T(8,128)(2,1)}, bf16[384,2048]{1,0:T(8,128)(2,1)}, u32[]{:S(2)}, u32[]{:S(2)}) collective-permute-start(bf16[384,2048]{1,0:T(8,128)(2,1)} %get-tuple-element.113), channel_id=1, source_target_pairs={{0,1},{1,0},{2,3},{3,2},{4,5},{5,4},{6,7},{7,6},{8,9},{9,8},{10,11... | collective-permute-start | bytes 4718600 | tf_op jit(solution)/shard_map/ppermute | solution.py:49
  484.7 28.4 %collective-permute-start.39 = (bf16[384,2048]{1,0:T(8,128)(2,1)}, bf16[384,2048]{1,0:T(8,128)(2,1)}, u32[]{:S(2)}, u32[]{:S(2)}) collective-permute-start(bf16[384,2048]{1,0:T(8,128)(2,1)} %get-tuple-element.111), channel_id=1, source_target_pairs={{0,1},{1,0},{2,3},{3,2},{4,5},{5,4},{6,7},{7,6},{8,9},{9,8},{10,11... | collective-permute-start | bytes 4718600 | tf_op jit(solution)/shard_map/ppermute | solution.py:49
  494.3 158.9 %reduce-scatter.10.cloned.1.call-start = ((), (), s32[]{:S(2)}) async-start(), calls=%async_computation.15 | async-start | bytes 3932160 | tf_op jit(solution)/shard_map/reduce_scatter | solution.py:72
  501.5 35.4 %collective-permute-start.53 = (bf16[384,2048]{1,0:T(8,128)(2,1)}, bf16[384,2048]{1,0:T(8,128)(2,1)}, u32[]{:S(2)}, u32[]{:S(2)}) collective-permute-start(bf16[384,2048]{1,0:T(8,128)(2,1)} %get-tuple-element.170.refs_0_.refs_1_), channel_id=1, source_target_pairs={{0,2},{1,3},{2,0},{3,1},{4,6},{5,7},{6,4},{7,5},{8,10},{9,11},{10,... | collective-permute-start | bytes 4718600 | tf_op jit(solution)/shard_map/ppermute | solution.py:49
  502.7 35.1 %collective-permute-start.54 = (bf16[384,2048]{1,0:T(8,128)(2,1)}, bf16[384,2048]{1,0:T(8,128)(2,1)}, u32[]{:S(2)}, u32[]{:S(2)}) collective-permute-start(bf16[384,2048]{1,0:T(8,128)(2,1)} %get-tuple-element.170.refs_0_.refs_1_), channel_id=1, source_target_pairs={{0,4},{1,5},{2,6},{3,7},{4,0},{5,1},{6,2},{7,3},{8,12},{9,13},{10,... | collective-permute-start | bytes 4718600 | tf_op jit(solution)/shard_map/ppermute | solution.py:49
  541.8 36.1 %collective-permute-start.52 = (bf16[384,2048]{1,0:T(8,128)(2,1)}, bf16[384,2048]{1,0:T(8,128)(2,1)}, u32[]{:S(2)}, u32[]{:S(2)}) collective-permute-start(bf16[384,2048]{1,0:T(8,128)(2,1)} %get-tuple-element.170.refs_0_.refs_1_), channel_id=1, source_target_pairs={{0,1},{1,0},{2,3},{3,2},{4,5},{5,4},{6,7},{7,6},{8,9},{9,8},{10,11... | collective-permute-start | bytes 4718600 | tf_op jit(solution)/shard_map/ppermute | solution.py:49
  544.4 33.5 %collective-permute-start.55 = (bf16[384,2048]{1,0:T(8,128)(2,1)}, bf16[384,2048]{1,0:T(8,128)(2,1)}, u32[]{:S(2)}, u32[]{:S(2)}) collective-permute-start(bf16[384,2048]{1,0:T(8,128)(2,1)} %get-tuple-element.128.refs_2_.refs_3_), channel_id=1, source_target_pairs={{0,1},{1,0},{2,3},{3,2},{4,5},{5,4},{6,7},{7,6},{8,9},{9,8},{10,11... | collective-permute-start | bytes 4718600 | tf_op jit(solution)/shard_map/ppermute | solution.py:49
  544.4 33.5 %collective-permute-start.56 = (bf16[384,2048]{1,0:T(8,128)(2,1)}, bf16[384,2048]{1,0:T(8,128)(2,1)}, u32[]{:S(2)}, u32[]{:S(2)}) collective-permute-start(bf16[384,2048]{1,0:T(8,128)(2,1)} %get-tuple-element.129.refs_4_.refs_5_), channel_id=1, source_target_pairs={{0,1},{1,0},{2,3},{3,2},{4,5},{5,4},{6,7},{7,6},{8,9},{9,8},{10,11... | collective-permute-start | bytes 4718600 | tf_op jit(solution)/shard_map/ppermute | solution.py:49
  581.2 47.1 %collective-permute-start.61 = (bf16[192,2048]{1,0:T(8,128)(2,1)}, bf16[192,2048]{1,0:T(8,128)(2,1)}, u32[]{:S(2)}, u32[]{:S(2)}) collective-permute-start(bf16[192,2048]{1,0:T(8,128)(2,1)} %get-tuple-element.178), channel_id=1, source_target_pairs={{0,2},{1,3},{2,0},{3,1},{4,6},{5,7},{6,4},{7,5},{8,10},{9,11},{10,... | collective-permute-start | bytes 2359304 | tf_op jit(solution)/shard_map/ppermute | solution.py:49
  582.3 46.0 %collective-permute-start.63 = (bf16[192,2048]{1,0:T(8,128)(2,1)}, bf16[192,2048]{1,0:T(8,128)(2,1)}, u32[]{:S(2)}, u32[]{:S(2)}) collective-permute-start(bf16[192,2048]{1,0:T(8,128)(2,1)} %get-tuple-element.179), channel_id=1, source_target_pairs={{0,4},{1,5},{2,6},{3,7},{4,0},{5,1},{6,2},{7,3},{8,12},{9,13},{10,... | collective-permute-start | bytes 2359304 | tf_op jit(solution)/shard_map/ppermute | solution.py:49
  583.5 44.8 %collective-permute-start.60 = (bf16[192,2048]{1,0:T(8,128)(2,1)}, bf16[192,2048]{1,0:T(8,128)(2,1)}, u32[]{:S(2)}, u32[]{:S(2)}) collective-permute-start(bf16[192,2048]{1,0:T(8,128)(2,1)} %get-tuple-element.130.refs_1_), channel_id=1, source_target_pairs={{0,2},{1,3},{2,0},{3,1},{4,6},{5,7},{6,4},{7,5},{8,10},{9,11},{10,... | collective-permute-start | bytes 2359304 | tf_op jit(solution)/shard_map/ppermute | solution.py:49
  583.9 44.5 %collective-permute-start.65 = (bf16[192,2048]{1,0:T(8,128)(2,1)}, bf16[192,2048]{1,0:T(8,128)(2,1)}, u32[]{:S(2)}, u32[]{:S(2)}) collective-permute-start(bf16[192,2048]{1,0:T(8,128)(2,1)} %get-tuple-element.132.refs_2_), channel_id=1, source_target_pairs={{0,4},{1,5},{2,6},{3,7},{4,0},{5,1},{6,2},{7,3},{8,12},{9,13},{10,... | collective-permute-start | bytes 2359304 | tf_op jit(solution)/shard_map/ppermute | solution.py:49
  584.8 182.3 %reduce-scatter.12.cloned.1.call-start = ((), (), s32[]{:S(2)}) async-start(), calls=%async_computation.16 | async-start | bytes 2949120 | tf_op jit(solution)/shard_map/reduce_scatter | solution.py:72
  659.4 32.5 %collective-permute-start.64 = (bf16[192,2048]{1,0:T(8,128)(2,1)}, bf16[192,2048]{1,0:T(8,128)(2,1)}, u32[]{:S(2)}, u32[]{:S(2)}) collective-permute-start(bf16[192,2048]{1,0:T(8,128)(2,1)} %fusion.23), channel_id=1, source_target_pairs={{0,2},{1,3},{2,0},{3,1},{4,6},{5,7},{6,4},{7,5},{8,10},{9,11},{10,... | collective-permute-start | bytes 2359304 | tf_op jit(solution)/shard_map/ppermute | solution.py:49
  663.8 63.4 %collective-permute-start.66 = (bf16[384,2048]{1,0:T(8,128)(2,1)}, bf16[384,2048]{1,0:T(8,128)(2,1)}, u32[]{:S(2)}, u32[]{:S(2)}) collective-permute-start(bf16[384,2048]{1,0:T(8,128)(2,1)} %get-tuple-element.148), channel_id=1, source_target_pairs={{0,1},{1,0},{2,3},{3,2},{4,5},{5,4},{6,7},{7,6},{8,9},{9,8},{10,11... | collective-permute-start | bytes 4718600 | tf_op jit(solution)/shard_map/ppermute | solution.py:49
  664.7 44.0 %collective-permute-start.70 = (bf16[192,2048]{1,0:T(8,128)(2,1)}, bf16[192,2048]{1,0:T(8,128)(2,1)}, u32[]{:S(2)}, u32[]{:S(2)}) collective-permute-start(bf16[192,2048]{1,0:T(8,128)(2,1)} %get-tuple-element.159), channel_id=1, source_target_pairs={{0,2},{1,3},{2,0},{3,1},{4,6},{5,7},{6,4},{7,5},{8,10},{9,11},{10,... | collective-permute-start | bytes 2359304 | tf_op jit(solution)/shard_map/ppermute | solution.py:49
  675.0 42.3 %collective-permute-start.75 = (bf16[192,2048]{1,0:T(8,128)(2,1)}, bf16[192,2048]{1,0:T(8,128)(2,1)}, u32[]{:S(2)}, u32[]{:S(2)}) collective-permute-start(bf16[192,2048]{1,0:T(8,128)(2,1)} %get-tuple-element.161), channel_id=1, source_target_pairs={{0,4},{1,5},{2,6},{3,7},{4,0},{5,1},{6,2},{7,3},{8,12},{9,13},{10,... | collective-permute-start | bytes 2359304 | tf_op jit(solution)/shard_map/ppermute | solution.py:49
  678.2 33.6 %collective-permute-start.72 = (bf16[192,2048]{1,0:T(8,128)(2,1)}, bf16[192,2048]{1,0:T(8,128)(2,1)}, u32[]{:S(2)}, u32[]{:S(2)}) collective-permute-start(bf16[192,2048]{1,0:T(8,128)(2,1)} %fusion.22), channel_id=1, source_target_pairs={{0,4},{1,5},{2,6},{3,7},{4,0},{5,1},{6,2},{7,3},{8,12},{9,13},{10,... | collective-permute-start | bytes 2359304 | tf_op jit(solution)/shard_map/ppermute | solution.py:49
  691.9 33.7 %collective-permute-start.74 = (bf16[192,2048]{1,0:T(8,128)(2,1)}, bf16[192,2048]{1,0:T(8,128)(2,1)}, u32[]{:S(2)}, u32[]{:S(2)}) collective-permute-start(bf16[192,2048]{1,0:T(8,128)(2,1)} %fusion.21), channel_id=1, source_target_pairs={{0,2},{1,3},{2,0},{3,1},{4,6},{5,7},{6,4},{7,5},{8,10},{9,11},{10,... | collective-permute-start | bytes 2359304 | tf_op jit(solution)/shard_map/ppermute | solution.py:49
  708.7 31.7 %collective-permute-start.38 = (bf16[384,2048]{1,0:T(8,128)(2,1)}, bf16[384,2048]{1,0:T(8,128)(2,1)}, u32[]{:S(2)}, u32[]{:S(2)}) collective-permute-start(bf16[384,2048]{1,0:T(8,128)(2,1)} %get-tuple-element.109), channel_id=1, source_target_pairs={{0,1},{1,0},{2,3},{3,2},{4,5},{5,4},{6,7},{7,6},{8,9},{9,8},{10,11... | collective-permute-start | bytes 4718600 | tf_op jit(solution)/shard_map/ppermute | solution.py:49
  711.8 38.3 %collective-permute-start.76 = (bf16[1,64,2048]{2,1,0:T(8,128)(2,1)}, bf16[1,64,2048]{2,1,0:T(8,128)(2,1)}, u32[]{:S(2)}, u32[]{:S(2)}) collective-permute-start(bf16[1,64,2048]{2,1,0:T(8,128)(2,1)} %get-tuple-element.189), channel_id=1, source_target_pairs={{0,0},{2,1},{4,2},{6,3},{1,4},{3,5},{5,6},{7,7},{8,8},{10,9},{12,1... | collective-permute-start | bytes 786440 | tf_op jit(solution)/shard_map/ppermute | solution.py:49
  717.3 33.8 %collective-permute-start.77 = (bf16[1,64,2048]{2,1,0:T(8,128)(2,1)}, bf16[1,64,2048]{2,1,0:T(8,128)(2,1)}, u32[]{:S(2)}, u32[]{:S(2)}) collective-permute-start(bf16[1,64,2048]{2,1,0:T(8,128)(2,1)} %get-tuple-element.188), channel_id=1, source_target_pairs={{2,0},{4,1},{6,2},{0,3},{3,4},{5,5},{7,6},{1,7},{10,8},{12,9},{14,... | collective-permute-start | bytes 786440 | tf_op jit(solution)/shard_map/ppermute | solution.py:49
  734.1 34.0 %all-to-all-start.3 = ((bf16[8,64,1536]{2,1,0:T(8,128)(2,1)}), bf16[8,64,1536]{2,1,0:T(8,128)(2,1)}, u32[]{:S(2)}, u32[]{:S(2)}) async-start(bf16[8,64,1536]{2,1,0:T(8,128)(2,1)} %bitcast.90), calls=%async_computation.8 | async-start | bytes 3145728 | tf_op jit(solution)/shard_map/all_to_all | solution.py:60
  740.4 69.7 %reduce-scatter.14.cloned.1.call-start = ((), (), s32[]{:S(2)}) async-start(), calls=%async_computation.17 | async-start | bytes 1310720 | tf_op jit(solution)/shard_map/reduce_scatter | solution.py:72
  745.6 21.4 %collective-permute-start.78 = (bf16[1,64,2048]{2,1,0:T(8,128)(2,1)S(1)}, bf16[1,64,2048]{2,1,0:T(8,128)(2,1)S(1)}, u32[]{:S(2)}, u32[]{:S(2)}) collective-permute-start(bf16[1,64,2048]{2,1,0:T(8,128)(2,1)S(1)} %copy-done.62), channel_id=1, source_target_pairs={{4,0},{6,1},{0,2},{2,3},{5,4},{7,5},{1,6},{3,7},{12,8},{14,9},{8,1... | collective-permute-start | bytes 786440 | tf_op jit(solution)/shard_map/ppermute | solution.py:49
  768.0 28.0 %all-to-all-start.2 = ((bf16[8,72,512]{2,1,0:T(8,128)(2,1)}), bf16[8,72,512]{2,1,0:T(8,128)(2,1)}, u32[]{:S(2)}, u32[]{:S(2)}) async-start(bf16[8,72,512]{2,1,0:T(8,128)(2,1)} %bitcast.91), calls=%async_computation.6 | async-start | bytes 1179648 | tf_op jit(solution)/shard_map/all_to_all | solution.py:60
  (106 other events, 921.4 us)
Sparse Core Ops, SparseCore 0:
  9.7 29.8 all-gather.14
  41.2 50.0 all-gather.6
  122.5 63.2 all-gather.8
  189.7 60.8 all-gather.10
  251.9 62.1 all-gather.12
  428.1 66.0 reduce-scatter.5
  496.5 60.2 reduce-scatter.7
  584.9 62.7 reduce-scatter.9
  664.9 58.8 reduce-scatter.11
  768.1 41.9 reduce-scatter.13

commit v3 on v2

--- a/solution.py
+++ b/solution.py
@@ -114,50 +114,33 @@
         self.sent = [low6, x_top, y_low]
         return [self.u4, self.u2, self.x_top, self.y_low]
 
-    def total(self):
+    def total(self, tick=None):
         half = self.half
-        x_low = swap((self.total2[half:] + self.u2.astype(F32)).astype(BF16), 2).astype(F32)
-        y_top = swap((self.total4[:half] + self.u4.astype(F32)).astype(BF16), 4).astype(F32)
+        lasts = [
+            (self.total2[half:] + self.u2.astype(F32)).astype(BF16),
+            (self.total4[:half] + self.u4.astype(F32)).astype(BF16),
+        ]
+        x_low, y_top = lasts if tick is None else hold(lasts, tick)
+        x_low = swap(x_low, 2).astype(F32)
+        y_top = swap(y_top, 4).astype(F32)
         top = self.x_top.astype(F32) + y_top
         low = x_low + self.y_low.astype(F32)
         return self.total0 + jnp.concatenate([top, low], axis=0)
 
 
-def out_weight_in(shard, groups):
-    t = member()
-    if groups < TEAM:
-        gathered = line_gather(shard[None])
-        per = TEAM // groups
-        b, z = t % groups, t // per
-        result = jnp.zeros_like(gathered)
-        for j in range(groups):
-            perm = [(i, per * ((i % groups + j) % groups) + i // groups) for i in range(TEAM)]
-            piece = lax.dynamic_index_in_dim(gathered, (b + j) % groups, 0, keepdims=True)
-            piece = permute(piece, perm)
-            result = lax.dynamic_update_slice_in_dim(result, piece, (z - j + groups) % groups, 0)
-        return result.reshape(-1, shard.shape[1])
-    full = lax.all_gather(shard, ALL, axis=0, tiled=True)
-    rows = full.shape[0] // TEAM
-    return lax.dynamic_slice_in_dim(full, t * rows, rows, 0)
+def out_weight_routes(groups):
+    return [(i, TEAM * (i % groups) + i // groups) for i in range(groups * TEAM)]
+
+
+def out_weight_in(shard, groups, after):
+    routed = lax.ppermute(shard, ALL, out_weight_routes(groups))
+    return line_gather(hold([routed], after)[0]), routed
 
 
 def out_weight_back(grad, groups, done):
-    t = member()
-    if groups < TEAM:
-        per = TEAM // groups
-        b, z = t % groups, t // per
-        grad = grad.reshape(groups, -1, grad.shape[1])
-        placed = jnp.zeros_like(grad)
-        for j in range(groups):
-            perm = [(per * ((i % groups + j) % groups) + i // groups, i) for i in range(TEAM)]
-            piece = lax.dynamic_index_in_dim(grad, (z - j + groups) % groups, 0, keepdims=True)
-            piece = permute(piece, perm)
-            placed = lax.dynamic_update_slice_in_dim(placed, piece, (b + j) % groups, 0)
-        placed = hold([placed], done)[0]
-        return line_sum(placed)[0], hold([done], placed)[0]
-    whole = jnp.zeros((grad.shape[0] * TEAM, grad.shape[1]), grad.dtype)
-    whole = lax.dynamic_update_slice_in_dim(whole, grad, t * grad.shape[0], 0)
-    return lax.psum_scatter(whole, ALL, scatter_dimension=0, tiled=True), done
+    grad = hold([grad], done)[0]
+    routes = [(user, owner) for owner, user in out_weight_routes(groups)]
+    return lax.ppermute(line_sum(grad), ALL, routes), hold([done], grad)[0]
 
 
 def rms_pull(value, gain, grad):
@@ -770,6 +753,7 @@
     ).transpose(1, 0, 2)
     attn = jnp.concatenate([attn, jnp.pad(row, ((0, 0), (0, 7), (0, 0)))], axis=1)
     attn = exchange(attn)
+    exchanged = attn
     head_lanes = mine * rho
     at_one, at_two, at_pair = head_lanes, head_lanes + rho, head_lanes + 2 * rho
     at_tiles = at_pair + 2 * pair_cols
@@ -792,13 +776,13 @@
         .reshape(2, size)
         .astype(F32)
     )
-    weight_out = out_weight_in(output_weight, groups)
+    weight_out, routed = out_weight_in(output_weight, groups, exchanged)
 
     def ff_split(w):
         return w.reshape(rho, groups, TEAM, phi).transpose(2, 0, 1, 3).reshape(TEAM, rho, ff_cols)
 
     feed_shard = jnp.concatenate([ff_split(gate_weight), ff_split(up_weight)], axis=2)
-    feed_shard = exchange(hold([feed_shard], weight_out)[0]).reshape(TEAM * rho, -1)
+    feed_shard = exchange(hold([feed_shard], routed)[0]).reshape(TEAM * rho, -1)
     weight_gate = line_gather(feed_shard[:, :ff_cols])
 
     exponent = jnp.arange(size // 2, dtype=F32) * (-2.0 / size)
@@ -811,20 +795,20 @@
     live = lax.broadcasted_iota(jnp.int32, (rows, 1), 0) < lengths[0]
     live_rows = live.astype(F32)
     upstream = cotangent.astype(F32) * live_rows
-    tick = mark([team_tokens[6]])
+    tick = mark([team_tokens[6], feed_shard])
     later = lax.broadcasted_iota(jnp.int32, (rows, 1), 0) < lengths[0] + tick[0, 0]
     upstream_low = jnp.where(later, cotangent, jnp.zeros_like(cotangent))
     upstream_levels = TeamGather(upstream_low)
     parts, kept, tick = attend(tiles, team_tokens, consts, mine, mark([feed_shard, upstream_low]))
     normed, qkv, logit, gated = kept
     weight_up = line_gather(hold([feed_shard[:, ff_cols:]], tick)[0])
-    parts = hold(parts, mark([upstream_levels.a1, upstream_levels.a2, upstream_levels.a4, weight_gate]))
+    parts = hold(parts, mark([upstream_levels.a1, upstream_levels.a2, upstream_levels.a4, tick]))
     arrived = TeamSum(parts)
     arrived.first()
     weight_down = line_gather(hold([down_weight], arrived.low6)[0])
-    team_upstream = upstream_levels.blocks()
+    team_upstream = upstream_levels.blocks(mark([arrived.u4, arrived.u2]))
     inputs = tokens.astype(F32)
-    hidden_state = inputs + arrived.total()
+    hidden_state = inputs + arrived.total(weight_gate)
 
     normed_two = rms(hidden_state, gain_two).astype(BF16)
     normed_two = hold([normed_two], mark(team_upstream))[0]
@@ -834,8 +818,8 @@
     arrived = TeamSum(grads)
     arrived.first()
     two_grad = arrived.total()
-    inner, feed_back = hold([inner, feed_back], mark(arrived.ready))
     down_part = product_tn(inner, ups_all).astype(BF16)
+    feed_back = hold([feed_back], mark([arrived.x_top, arrived.y_low]))[0]
     gate_part = product_tn(two_all, feed_back[:, :ff_cols]).astype(BF16)
     up_part = product_tn(two_all, feed_back[:, ff_cols:]).astype(BF16)
     parts_made = mark([gate_part, up_part])
@@ -846,7 +830,7 @@
     hidden_grad = upstream + rms_pull(hidden_state, gain_two, two_grad)
 
     fed = TeamSum(outs)
-    team_hidden = TeamGather(hidden_grad.astype(BF16)).blocks(mark(fed.ready + [gate_part]))
+    team_hidden = TeamGather(hidden_grad.astype(BF16)).blocks(mark(fed.ready + [gate_part, up_part]))
     two_scale = lax.rsqrt(jnp.mean(hidden_state * hidden_state, axis=-1, keepdims=True) + EPSILON)
     two_sum = jnp.sum(two_grad * hidden_state * two_scale, axis=0)
     first_hop = fed.first(mark(team_hidden + [parts_made]))
@@ -874,9 +858,9 @@
     normed_grad = arrived.total()
     layer_output = ((hidden_state + fed.total()) * live_rows).astype(BF16)
     tokens_grad = (hidden_grad + rms_pull(inputs, gain_one, normed_grad)).astype(BF16)
-    output_grad, packed = out_weight_back(hold([out_part], arrived.u4)[0], groups, packed)
+    output_grad, packed = out_weight_back(out_part, groups, packed)
     packed = exchange(packed.reshape(TEAM, rho + 8, cols))
-    feed_grad = jnp.concatenate([gate_grad, hold([up_grad], normed_grad)[0]], axis=1)
+    feed_grad = jnp.concatenate([gate_grad, hold([up_grad], arrived.u4)[0]], axis=1)
     feed_grad = exchange(feed_grad.reshape(TEAM, rho, 2 * ff_cols))
 
     def ff_join(w):

time: 832 us -> 791 us (0.951)
  waiting for transfers between devices: 302 us -> 278 us
  local copies, waits for them, and re-layouts: 107 us -> 90 us
  starting transfers between devices: 109 us -> 92.3 us
  Pallas kernels: 136 us -> 152 us
    ppermute x80 -> x72, starting transfers between devices: 86.5 us -> 66 us  [permute(): lax.ppermute(array, ALL, [(team[a], team[b]) for team in teams() for a, b...]
    ppermute x80 -> x72, waiting for transfers between devices: 272 us -> 254 us  [permute(): lax.ppermute(array, ALL, [(team[a], team[b]) for team in teams() for a, b...]
    all_gather x5, waiting for transfers between devices: 15.6 us -> 0.02 us  [line_gather(): return lax.all_gather(shard, 'dp', axis=0, tiled=True)]
    ppermute x0 -> x2, waiting for transfers between devices: none -> 13.7 us  [the longest x1 13.7 us: out_weight_back(): return (lax.ppermute(line_sum(grad), ALL, routes), hold([done], grad)[0])]
    reduce_scatter x5, waiting for transfers between devices: 13.5 us -> 0.07 us  [line_sum(): return lax.psum_scatter(array, 'dp', scatter_dimension=0, tiled=True)]
    all_to_all x3, waiting for transfers between devices: 0.01 us -> 9.41 us  [exchange(): return lax.all_to_all(blocks, 'fsdp', 0, 0, tiled=True)]
    pallas_call x1, Pallas kernels: 43.5 us -> 52.1 us  [attend_back(): pl.pallas_call(kernel, out_shape=[struct((rows, width), BF16)] * TEAM + [...]
    unnamed x167 -> x160, local copies, waits for them, and re-layouts: 34.3 us -> 30.8 us
  transfers between devices with their start and end apart: 93 -> 87, of which waited for: 34 -> 31; matrix products, arithmetic and copies ran while one was open for 23% -> 25% of each run, Pallas kernels for 9% -> 11%
where the time goes in v3:
time: 791 us; the launch traced here: 776 us
  waiting for transfers between devices  278 us (35%)
  Pallas kernels  152 us (19%)
  starting transfers between devices  92.3 us (12%)
  local copies, waits for them, and re-layouts  90 us (11%)
  other arithmetic  85.3 us (11%)
  matrix products  46.5 us (6%)
  between operations  17.5 us (2%)
  blocking collectives  15 us (2%)
    ppermute x72, waiting for transfers between devices, permute(): lax.ppermute(array, ALL, [(team[a], team[b]) for team in teams() for a, b...  254 us
    ppermute x72, starting transfers between devices, permute(): lax.ppermute(array, ALL, [(team[a], team[b]) for team in teams() for a, b...  66 us
    pallas_call x1, Pallas kernels, feed(): pl.pallas_call(kernel, out_shape=[struct((rows, width), BF16)] * (2 * TEA...  63.5 us
    pallas_call x1, Pallas kernels, attend_back(): pl.pallas_call(kernel, out_shape=[struct((rows, width), BF16)] * TEAM + [...  52.1 us
    dot_general x3, matrix products, product_tn(): lax.dot_general(left, right, (((0,), (0,)), ((), ())), preferred_element_...  46.5 us
    unnamed x160, local copies, waits for them, and re-layouts  30.8 us
    pallas_call x1, Pallas kernels, attend(): pl.pallas_call(kernel, out_shape=[struct((rows, width), BF16)] * TEAM + [...  28.8 us
    all_to_all x3, starting transfers between devices, exchange(): return lax.all_to_all(blocks, 'fsdp', 0, 0, tiled=True)  16.9 us
  transfers between devices with their start and end apart: 87, of which 31 were waited for; matrix products, arithmetic and copies ran while one was open for 25% of the time, Pallas kernels for 11%

profile of v3, /device:TPU:1, one launch (start us, length us, event | category | flops | bytes accessed | tf_op | source)
XLA Modules:
  0.0 775.9 jit_solution(9044162875382094461)
XLA Ops:
  7.3 2.2 copy.233.refs_0_
  10.8 15.0 %all_to_all.20.refs_1_ = bf16[8,72,512]{2,1,0:T(8,128)(2,1)} all-to-all(bf16[8,72,512]{2,1,0:T(8,128)(2,1)S(1)} %fusion.30), channel_id=1, replica_groups=mesh['dp'=4,'fsdp'=8] {'fsdp'}, dimensions={0} | all-to-all | bytes 1179648 | tf_op jit(solution)/shard_map/all_to_all | solution.py:60
  26.5 4.2 collective-permute-start.8
  33.4 2.3 reshape.268
  37.0 25.4 %collective-permute-done.3.refs_5_ = bf16[384,2048]{1,0:T(8,128)(2,1)} collective-permute-done((bf16[384,2048]{1,0:T(8,128)(2,1)}, bf16[384,2048]{1,0:T(8,128)(2,1)}, u32[]{:S(2)}, u32[]{:S(2)}) %collective-permute-start.3) | collective-permute-done | bytes 1572896 | tf_op jit(solution)/shard_map/ppermute | solution.py:49
  64.5 2.4 collective-permute-start.5
  68.8 5.2 all-to-all-start.1
  79.5 4.1 collective-permute-done.5
  83.6 2.1 constant_dynamic-update-slice_fusion.1
  85.7 24.5 %collective-permute-done.6 = bf16[192,2048]{1,0:T(8,128)(2,1)S(1)} collective-permute-done((bf16[192,2048]{1,0:T(8,128)(2,1)S(1)}, bf16[192,2048]{1,0:T(8,128)(2,1)S(1)}, u32[]{:S(2)}, u32[]{:S(2)}) %collective-permute-start.6) | collective-permute-done | bytes 786464 | tf_op jit(solution)/shard_map/ppermute | solution.py:49
  120.8 3.4 slice.257
  128.2 28.8 %shard_map.241 = (bf16[384,2048]{1,0:T(8,128)(2,1)S(1)}, bf16[384,2048]{1,0:T(8,128)(2,1)S(1)}, bf16[384,2048]{1,0:T(8,128)(2,1)}, bf16[384,2048]{1,0:T(8,128)(2...) custom-call(s32[8]{0:T(128)S(1)} %select_reduce_fusion.refs_0_, ...), custom_call_target="tpu_custom_call" | custom-call | flops 32212254720 | bytes 62914560 | tf_op jit(solution)/shard_map/pallas_call | solution.py:317
  164.4 2.6 collective-permute-done.15
  175.2 12.5 %collective-permute-done.18.refs_0_ = bf16[192,2048]{1,0:T(8,128)(2,1)S(1)} collective-permute-done((bf16[192,2048]{1,0:T(8,128)(2,1)S(1)}, bf16[192,2048]{1,0:T(8,128)(2,1)S(1)}, u32[]{:S(2)}, u32[]{:S(2)}) %collective-permute-start.18) | collective-permute-done | bytes 786464 | tf_op jit(solution)/shard_map/ppermute | solution.py:49
  189.4 2.3 slice.213
  196.1 2.2 fusion.28.refs_0_
  200.9 2.5 collective-permute-start.12
  205.2 16.2 %collective-permute-done.24 = bf16[192,2048]{1,0:T(8,128)(2,1)} collective-permute-done((bf16[192,2048]{1,0:T(8,128)(2,1)}, bf16[192,2048]{1,0:T(8,128)(2,1)}, u32[]{:S(2)}, u32[]{:S(2)}) %collective-permute-start.24) | collective-permute-done | bytes 786464 | tf_op jit(solution)/shard_map/ppermute | solution.py:49
  228.9 5.8 collective-permute-start.23
  236.4 9.3 %collective-permute-done.21 = bf16[192,2048]{1,0:T(8,128)(2,1)S(1)} collective-permute-done((bf16[192,2048]{1,0:T(8,128)(2,1)S(1)}, bf16[192,2048]{1,0:T(8,128)(2,1)S(1)}, u32[]{:S(2)}, u32[]{:S(2)}) %collective-permute-start.21) | collective-permute-done | bytes 786464 | tf_op jit(solution)/shard_map/ppermute | solution.py:49
  245.7 3.1 collective-permute-start.26
  249.0 3.1 multiply_reduce_fusion.2
  258.6 34.3 %collective-permute-done.29.refs_1_ = bf16[384,2048]{1,0:T(8,128)(2,1)} collective-permute-done((bf16[384,2048]{1,0:T(8,128)(2,1)}, bf16[384,2048]{1,0:T(8,128)(2,1)}, u32[]{:S(2)}, u32[]{:S(2)}) %collective-permute-start.29) | collective-permute-done | bytes 1572896 | tf_op jit(solution)/shard_map/ppermute | solution.py:49
  299.1 14.0 %collective-permute-done.32 = bf16[192,2048]{1,0:T(8,128)(2,1)S(1)} collective-permute-done((bf16[192,2048]{1,0:T(8,128)(2,1)S(1)}, bf16[192,2048]{1,0:T(8,128)(2,1)S(1)}, u32[]{:S(2)}, u32[]{:S(2)}) %collective-permute-start.32) | collective-permute-done | bytes 786464 | tf_op jit(solution)/shard_map/ppermute | solution.py:49
  315.3 2.3 collective-permute-start.34
  317.7 3.3 collective-permute-done.34.refs_8_
  321.0 63.5 %shard_map.253 = (bf16[384,2048]{1,0:T(8,128)(2,1)}, bf16[384,2048]{1,0:T(8,128)(2,1)}, bf16[384,2048]{1,0:T(8,128)(2,1)}, bf16[384,2048]{1,0:T(8,128)(2,1)}, bf...) custom-call(s32[8]{0:T(128)} %copy-done.13, ...), custom_call_target="tpu_custom_call" | custom-call | flops 62277025792 | bytes 104857600 | tf_op jit(solution)/shard_map/pallas_call | solution.py:665
  386.2 15.6 %convolution_convert_fusion = bf16[768,2048]{1,0:T(8,128)(2,1)} fusion(bf16[3072,768]{1,0:T(8,128)(2,1)} %get-tuple-element.141, bf16[3072,2048]{1,0:T(8,128)(2,1)} %get-tuple-element.142), kind=kOutput, calls=%fused_computation.12 | convolution fusion | flops 9665249280 | bytes 20447232 | tf_op jit(solution)/shard_map/dot_general | solution.py:29
  402.2 2.6 convert_add_fusion.6
  405.4 2.6 add_convert_fusion.1
  409.5 2.1 convert_add_fusion.5
  414.2 3.2 add_convert_fusion.2.refs_0_
  422.9 4.1 collective-permute-done.44
  428.5 10.7 %collective-permute-done.46 = bf16[192,2048]{1,0:T(8,128)(2,1)S(1)} collective-permute-done((bf16[192,2048]{1,0:T(8,128)(2,1)S(1)}, bf16[192,2048]{1,0:T(8,128)(2,1)S(1)}, u32[]{:S(2)}, u32[]{:S(2)}) %collective-permute-start.46) | collective-permute-done | bytes 786464 | tf_op jit(solution)/shard_map/ppermute | solution.py:49
  440.3 3.6 collective-permute-done.41.refs_0_
  443.9 12.2 %collective-permute-done.48.refs_1_ = bf16[192,2048]{1,0:T(8,128)(2,1)} collective-permute-done((bf16[192,2048]{1,0:T(8,128)(2,1)S(1)}, bf16[192,2048]{1,0:T(8,128)(2,1)}, u32[]{:S(2)}, u32[]{:S(2)}) %collective-permute-start.48) | collective-permute-done | bytes 786464 | tf_op jit(solution)/shard_map/ppermute | solution.py:49
  456.7 14.6 %fusion.5.refs_3_.refs_0_ = bf16[2048,768]{1,0:T(8,128)(2,1)S(1)} fusion(bf16[3072,2048]{1,0:T(8,128)(2,1)} %get-tuple-element.130, bf16[3072,1536]{1,0:T(8,128)(2,1)} %shard_map.255), kind=kOutput, calls=%fused_computation.10 | convolution fusion | flops 9665249280 | bytes 20447232 | tf_op jit(solution)/shard_map/dot_general | solution.py:29
  475.5 2.2 convert_add_fusion.13
  478.0 2.9 multiply_reduce_fusion
  481.4 6.9 fusion.44
  489.4 16.3 %fusion.8.refs_4_.refs_1_.refs_0_ = bf16[2048,768]{1,0:T(8,128)(2,1)} fusion(bf16[3072,2048]{1,0:T(8,128)(2,1)} %get-tuple-element.130, bf16[3072,1536]{1,0:T(8,128)(2,1)} %shard_map.255), kind=kOutput, calls=%fused_computation.11 | convolution fusion | flops 9665249280 | bytes 20447232 | tf_op jit(solution)/shard_map/dot_general | solution.py:29
  506.3 15.6 %collective-permute-done.51.refs_1_ = bf16[384,2048]{1,0:T(8,128)(2,1)} collective-permute-done((bf16[384,2048]{1,0:T(8,128)(2,1)}, bf16[384,2048]{1,0:T(8,128)(2,1)}, u32[]{:S(2)}, u32[]{:S(2)}) %collective-permute-start.51) | collective-permute-done | bytes 1572896 | tf_op jit(solution)/shard_map/ppermute | solution.py:49
  526.2 3.9 collective-permute-start.49
  530.5 10.0 %collective-permute-done.54 = bf16[192,2048]{1,0:T(8,128)(2,1)S(1)} collective-permute-done((bf16[192,2048]{1,0:T(8,128)(2,1)S(1)}, bf16[192,2048]{1,0:T(8,128)(2,1)S(1)}, u32[]{:S(2)}, u32[]{:S(2)}) %collective-permute-start.54) | collective-permute-done | bytes 786464 | tf_op jit(solution)/shard_map/ppermute | solution.py:49
  542.6 4.3 collective-permute-start.56
  547.6 2.5 convert_element_type.441
  552.5 2.7 fusion.47
  557.1 52.1 %shard_map.262 = (bf16[384,2048]{1,0:T(8,128)(2,1)}, bf16[384,2048]{1,0:T(8,128)(2,1)}, bf16[384,2048]{1,0:T(8,128)(2,1)}, bf16[384,2048]{1,0:T(8,128)(2,1)}, bf...) custom-call(s32[8]{0:T(128)} %copy-done.13, ...), custom_call_target="tpu_custom_call" | custom-call | flops 48318382080 | bytes 73400320 | tf_op jit(solution)/shard_map/pallas_call | solution.py:475
  620.3 2.2 fusion.23
  623.9 12.4 %collective-permute-done.59 = bf16[192,2048]{1,0:T(8,128)(2,1)S(1)} collective-permute-done((bf16[192,2048]{1,0:T(8,128)(2,1)S(1)}, bf16[192,2048]{1,0:T(8,128)(2,1)S(1)}, u32[]{:S(2)}, u32[]{:S(2)}) %collective-permute-start.59) | collective-permute-done | bytes 786464 | tf_op jit(solution)/shard_map/ppermute | solution.py:49
  637.1 2.5 convert_add_fusion.12
  651.8 4.2 fusion.19
  657.8 9.7 %collective-permute-done.68.refs_1_ = bf16[192,2048]{1,0:T(8,128)(2,1)S(1)} collective-permute-done((bf16[192,2048]{1,0:T(8,128)(2,1)S(1)}, bf16[192,2048]{1,0:T(8,128)(2,1)S(1)}, u32[]{:S(2)}, u32[]{:S(2)}) %collective-permute-start.68) | collective-permute-done | bytes 786464 | tf_op jit(solution)/shard_map/ppermute | solution.py:49
  672.6 2.4 pad_maximum_fusion.1
  675.0 6.1 all-to-all-start.3
  681.1 3.2 collective-permute-done.67
  684.3 19.7 %collective-permute-done.69 = bf16[192,2048]{1,0:T(8,128)(2,1)} collective-permute-done((bf16[192,2048]{1,0:T(8,128)(2,1)}, bf16[192,2048]{1,0:T(8,128)(2,1)}, u32[]{:S(2)}, u32[]{:S(2)}) %collective-permute-start.69) | collective-permute-done | bytes 786464 | tf_op jit(solution)/shard_map/ppermute | solution.py:49
  708.3 3.1 fusion.11
  711.5 9.4 %all-to-all-done.3 = bf16[8,64,1536]{2,1,0:T(8,128)(2,1)} async-done(((bf16[8,64,1536]{2,1,0:T(8,128)(2,1)}), bf16[8,64,1536]{2,1,0:T(8,128)(2,1)}, u32[]{:S(2)}, u32[]{:S(2)}) %all-to-all-start.3) | async-done | bytes 1572896 | tf_op jit(solution)/shard_map/all_to_all | solution.py:60
  720.9 5.6 all-to-all-start.2
  726.5 4.4 fusion.15
  740.5 2.5 convert_element_type.439
  746.3 3.5 collective-permute-start.73
  754.1 13.7 %collective-permute-done.73 = bf16[64,2048]{1,0:T(8,128)(2,1)S(1)} collective-permute-done((bf16[64,2048]{1,0:T(8,128)(2,1)}, bf16[64,2048]{1,0:T(8,128)(2,1)S(1)}, u32[]{:S(2)}, u32[]{:S(2)}) %collective-permute-start.73) | collective-permute-done | bytes 262176 | tf_op jit(solution)/shard_map/ppermute | solution.py:143
  (468 shorter events, 166.8 us)
Async XLA Ops:
  7.3 112.6 %all-gather.6.cloned.1.call-start = ((), (), s32[]{:S(2)}) async-start(), calls=%async_computation.9 | async-start | bytes 2949120 | tf_op jit(solution)/shard_map/all_gather | solution.py:66
  25.7 36.6 %collective-permute-start.3 = (bf16[384,2048]{1,0:T(8,128)(2,1)}, bf16[384,2048]{1,0:T(8,128)(2,1)}, u32[]{:S(2)}, u32[]{:S(2)}) collective-permute-start(bf16[384,2048]{1,0:T(8,128)(2,1)} %refs_1_.1), channel_id=1, source_target_pairs={{0,4},{1,5},{2,6},{3,7},{4,0},{5,1},{6,2},{7,3},{8,12},{9,13},{10,... | collective-permute-start | bytes 4718600 | tf_op jit(solution)/shard_map/ppermute | solution.py:49
  26.2 48.8 %collective-permute-start.1 = (bf16[384,2048]{1,0:T(8,128)(2,1)}, bf16[384,2048]{1,0:T(8,128)(2,1)}, u32[]{:S(2)}, u32[]{:S(2)}) collective-permute-start(bf16[384,2048]{1,0:T(8,128)(2,1)} %refs_1_.1), channel_id=1, source_target_pairs={{0,2},{1,3},{2,0},{3,1},{4,6},{5,7},{6,4},{7,5},{8,10},{9,11},{10,... | collective-permute-start | bytes 4718600 | tf_op jit(solution)/shard_map/ppermute | solution.py:49
  26.5 41.6 %collective-permute-start.8 = (bf16[64,2048]{1,0:T(8,128)(2,1)S(1)}, bf16[64,2048]{1,0:T(8,128)(2,1)S(1)}, u32[]{:S(2)}, u32[]{:S(2)}) collective-permute-start(bf16[64,2048]{1,0:T(8,128)(2,1)S(1)} %copy-done.73), channel_id=1, source_target_pairs={{0,0},{1,8},{2,16},{3,24},{4,1},{5,9},{6,17},{7,25},{8,2},{9,10},{... | collective-permute-start | bytes 786440 | tf_op jit(solution)/shard_map/ppermute | solution.py:136
  64.5 19.1 %collective-permute-start.5 = (bf16[192,2048]{1,0:T(8,128)(2,1)}, bf16[192,2048]{1,0:T(8,128)(2,1)}, u32[]{:S(2)}, u32[]{:S(2)}) collective-permute-start(bf16[192,2048]{1,0:T(8,128)(2,1)} %slice.255), channel_id=1, source_target_pairs={{0,2},{1,3},{2,0},{3,1},{4,6},{5,7},{6,4},{7,5},{8,10},{9,11},{10,... | collective-permute-start | bytes 2359304 | tf_op jit(solution)/shard_map/ppermute | solution.py:49
  68.8 44.1 %all-to-all-start.1 = ((bf16[8,64,1536]{2,1,0:T(8,128)(2,1)}), bf16[8,64,1536]{2,1,0:T(8,128)(2,1)S(1)}, u32[]{:S(2)}, u32[]{:S(2)}) async-start(bf16[8,64,1536]{2,1,0:T(8,128)(2,1)} %shard_map.238), calls=%async_computation.1 | async-start | bytes 3145728 | tf_op jit(solution)/shard_map/all_to_all | solution.py:60
  74.0 52.9 %all-gather.8.cloned.1.call-start = ((), (), s32[]{:S(2)}) async-start(), calls=%async_computation.10 | async-start | bytes 1310720 | tf_op jit(solution)/shard_map/all_gather | solution.py:66
  74.8 124.7 %all-gather.10.cloned.1.call-start = ((), (), s32[]{:S(2)}) async-start(), calls=%async_computation.11 | async-start | bytes 3932160 | tf_op jit(solution)/shard_map/all_gather | solution.py:66
  74.8 50.1 %collective-permute-start = (bf16[384,2048]{1,0:T(8,128)(2,1)}, bf16[384,2048]{1,0:T(8,128)(2,1)}, u32[]{:S(2)}, u32[]{:S(2)}) collective-permute-start(bf16[384,2048]{1,0:T(8,128)(2,1)} %refs_1_.1), channel_id=1, source_target_pairs={{0,1},{1,0},{2,3},{3,2},{4,5},{5,4},{6,7},{7,6},{8,9},{9,8},{10,11... | collective-permute-start | bytes 4718600 | tf_op jit(solution)/shard_map/ppermute | solution.py:49
  76.2 34.0 %collective-permute-start.6 = (bf16[192,2048]{1,0:T(8,128)(2,1)S(1)}, bf16[192,2048]{1,0:T(8,128)(2,1)S(1)}, u32[]{:S(2)}, u32[]{:S(2)}) collective-permute-start(bf16[192,2048]{1,0:T(8,128)(2,1)S(1)} %slice.256), channel_id=1, source_target_pairs={{0,4},{1,5},{2,6},{3,7},{4,0},{5,1},{6,2},{7,3},{8,12},{9,13},{10,... | collective-permute-start | bytes 2359304 | tf_op jit(solution)/shard_map/ppermute | solution.py:49
  78.9 47.5 %collective-permute-start.2 = (bf16[384,2048]{1,0:T(8,128)(2,1)}, bf16[384,2048]{1,0:T(8,128)(2,1)}, u32[]{:S(2)}, u32[]{:S(2)}) collective-permute-start(bf16[384,2048]{1,0:T(8,128)(2,1)} %collective-permute-done.1.refs_3_), channel_id=1, source_target_pairs={{0,1},{1,0},{2,3},{3,2},{4,5},{5,4},{6,7},{7,6},{8,9},{9,8},{10,11... | collective-permute-start | bytes 4718600 | tf_op jit(solution)/shard_map/ppermute | solution.py:49
  79.4 47.6 %collective-permute-start.4 = (bf16[384,2048]{1,0:T(8,128)(2,1)}, bf16[384,2048]{1,0:T(8,128)(2,1)}, u32[]{:S(2)}, u32[]{:S(2)}) collective-permute-start(bf16[384,2048]{1,0:T(8,128)(2,1)} %collective-permute-done.3.refs_5_), channel_id=1, source_target_pairs={{0,1},{1,0},{2,3},{3,2},{4,5},{5,4},{6,7},{7,6},{8,9},{9,8},{10,11... | collective-permute-start | bytes 4718600 | tf_op jit(solution)/shard_map/ppermute | solution.py:49
  114.7 143.3 %all-gather.12.cloned.1.call-start = ((), (), s32[]{:S(2)}) async-start(), calls=%async_computation.12 | async-start | bytes 3932160 | tf_op jit(solution)/shard_map/all_gather | solution.py:66
  119.8 40.2 %collective-permute-start.11 = (bf16[384,2048]{1,0:T(8,128)(2,1)}, bf16[384,2048]{1,0:T(8,128)(2,1)}, u32[]{:S(2)}, u32[]{:S(2)}) collective-permute-start(bf16[384,2048]{1,0:T(8,128)(2,1)} %broadcast_select_fusion.refs_1_.refs_0_.refs_9_), channel_id=1, source_target_pairs={{0,4},{1,5},{2,6},{3,7},{4,0},{5,1},{6,2},{7,3},{8,12},{9,13},{10,... | collective-permute-start | bytes 4718600 | tf_op jit(solution)/shard_map/ppermute | solution.py:49
  124.9 36.1 %collective-permute-start.10 = (bf16[384,2048]{1,0:T(8,128)(2,1)}, bf16[384,2048]{1,0:T(8,128)(2,1)S(1)}, u32[]{:S(2)}, u32[]{:S(2)}) collective-permute-start(bf16[384,2048]{1,0:T(8,128)(2,1)} %broadcast_select_fusion.refs_1_.refs_0_.refs_9_), channel_id=1, source_target_pairs={{0,2},{1,3},{2,0},{3,1},{4,6},{5,7},{6,4},{7,5},{8,10},{9,11},{10,... | collective-permute-start | bytes 4718600 | tf_op jit(solution)/shard_map/ppermute | solution.py:49
  126.4 34.6 %collective-permute-start.9 = (bf16[384,2048]{1,0:T(8,128)(2,1)}, bf16[384,2048]{1,0:T(8,128)(2,1)}, u32[]{:S(2)}, u32[]{:S(2)}) collective-permute-start(bf16[384,2048]{1,0:T(8,128)(2,1)} %broadcast_select_fusion.refs_1_.refs_0_.refs_9_), channel_id=1, source_target_pairs={{0,1},{1,0},{2,3},{3,2},{4,5},{5,4},{6,7},{7,6},{8,9},{9,8},{10,11... | collective-permute-start | bytes 4718600 | tf_op jit(solution)/shard_map/ppermute | solution.py:49
  163.8 153.8 %all-gather.14.cloned.1.call-start = ((), (), s32[]{:S(2)}) async-start(), calls=%async_computation.13 | async-start | bytes 3932160 | tf_op jit(solution)/shard_map/all_gather | solution.py:66
  173.1 53.4 %collective-permute-start.14 = (bf16[192,2048]{1,0:T(8,128)(2,1)}, bf16[192,2048]{1,0:T(8,128)(2,1)}, u32[]{:S(2)}, u32[]{:S(2)}) collective-permute-start(bf16[192,2048]{1,0:T(8,128)(2,1)} %slice.360), channel_id=1, source_target_pairs={{0,2},{1,3},{2,0},{3,1},{4,6},{5,7},{6,4},{7,5},{8,10},{9,11},{10,... | collective-permute-start | bytes 2359304 | tf_op jit(solution)/shard_map/ppermute | solution.py:49
  193.7 27.7 %collective-permute-start.24 = (bf16[192,2048]{1,0:T(8,128)(2,1)}, bf16[192,2048]{1,0:T(8,128)(2,1)}, u32[]{:S(2)}, u32[]{:S(2)}) collective-permute-start(bf16[192,2048]{1,0:T(8,128)(2,1)} %slice.212), channel_id=1, source_target_pairs={{0,2},{1,3},{2,0},{3,1},{4,6},{5,7},{6,4},{7,5},{8,10},{9,11},{10,... | collective-permute-start | bytes 2359304 | tf_op jit(solution)/shard_map/ppermute | solution.py:49
  194.9 27.9 %collective-permute-start.25 = (bf16[192,2048]{1,0:T(8,128)(2,1)}, bf16[192,2048]{1,0:T(8,128)(2,1)}, u32[]{:S(2)}, u32[]{:S(2)}) collective-permute-start(bf16[192,2048]{1,0:T(8,128)(2,1)} %slice.213), channel_id=1, source_target_pairs={{0,4},{1,5},{2,6},{3,7},{4,0},{5,1},{6,2},{7,3},{8,12},{9,13},{10,... | collective-permute-start | bytes 2359304 | tf_op jit(solution)/shard_map/ppermute | solution.py:49
  199.5 29.5 %collective-permute-start.19 = (bf16[192,2048]{1,0:T(8,128)(2,1)}, bf16[192,2048]{1,0:T(8,128)(2,1)}, u32[]{:S(2)}, u32[]{:S(2)}) collective-permute-start(bf16[192,2048]{1,0:T(8,128)(2,1)} %get-tuple-element.108), channel_id=1, source_target_pairs={{0,4},{1,5},{2,6},{3,7},{4,0},{5,1},{6,2},{7,3},{8,12},{9,13},{10,... | collective-permute-start | bytes 2359304 | tf_op jit(solution)/shard_map/ppermute | solution.py:49
  200.9 48.1 %collective-permute-start.12 = (bf16[384,2048]{1,0:T(8,128)(2,1)S(1)}, bf16[384,2048]{1,0:T(8,128)(2,1)}, u32[]{:S(2)}, u32[]{:S(2)}) collective-permute-start(bf16[384,2048]{1,0:T(8,128)(2,1)S(1)} %copy-done.5), channel_id=1, source_target_pairs={{0,1},{1,0},{2,3},{3,2},{4,5},{5,4},{6,7},{7,6},{8,9},{9,8},{10,11... | collective-permute-start | bytes 4718600 | tf_op jit(solution)/shard_map/ppermute | solution.py:49
  205.0 275.9 %reduce-scatter.6.cloned.1.call-start = ((), (), s32[]{:S(2)}) async-start(), calls=%async_computation.14 | async-start | bytes 3932160 | tf_op jit(solution)/shard_map/reduce_scatter | solution.py:72
  221.4 24.3 %collective-permute-start.21 = (bf16[192,2048]{1,0:T(8,128)(2,1)S(1)}, bf16[192,2048]{1,0:T(8,128)(2,1)S(1)}, u32[]{:S(2)}, u32[]{:S(2)}) collective-permute-start(bf16[192,2048]{1,0:T(8,128)(2,1)S(1)} %slice.359), channel_id=1, source_target_pairs={{0,4},{1,5},{2,6},{3,7},{4,0},{5,1},{6,2},{7,3},{8,12},{9,13},{10,... | collective-permute-start | bytes 2359304 | tf_op jit(solution)/shard_map/ppermute | solution.py:49
  222.8 26.0 %collective-permute-start.20 = (bf16[192,2048]{1,0:T(8,128)(2,1)S(1)}, bf16[192,2048]{1,0:T(8,128)(2,1)S(1)}, u32[]{:S(2)}, u32[]{:S(2)}) collective-permute-start(bf16[192,2048]{1,0:T(8,128)(2,1)S(1)} %copy-done.46), channel_id=1, source_target_pairs={{0,2},{1,3},{2,0},{3,1},{4,6},{5,7},{6,4},{7,5},{8,10},{9,11},{10,... | collective-permute-start | bytes 2359304 | tf_op jit(solution)/shard_map/ppermute | solution.py:49
  226.5 27.1 %collective-permute-start.22 = (bf16[384,2048]{1,0:T(8,128)(2,1)S(1)}, bf16[384,2048]{1,0:T(8,128)(2,1)S(1)}, u32[]{:S(2)}, u32[]{:S(2)}) collective-permute-start(bf16[384,2048]{1,0:T(8,128)(2,1)S(1)} %copy-done.18), channel_id=1, source_target_pairs={{0,1},{1,0},{2,3},{3,2},{4,5},{5,4},{6,7},{7,6},{8,9},{9,8},{10,11... | collective-permute-start | bytes 4718600 | tf_op jit(solution)/shard_map/ppermute | solution.py:49
  228.9 25.8 %collective-permute-start.23 = (bf16[384,2048]{1,0:T(8,128)(2,1)}, bf16[384,2048]{1,0:T(8,128)(2,1)S(1)}, u32[]{:S(2)}, u32[]{:S(2)}) collective-permute-start(bf16[384,2048]{1,0:T(8,128)(2,1)} %get-tuple-element.111.refs_4_.refs_13_), channel_id=1, source_target_pairs={{0,1},{1,0},{2,3},{3,2},{4,5},{5,4},{6,7},{7,6},{8,9},{9,8},{10,11... | collective-permute-start | bytes 4718600 | tf_op jit(solution)/shard_map/ppermute | solution.py:49
  256.5 36.3 %collective-permute-start.29 = (bf16[384,2048]{1,0:T(8,128)(2,1)}, bf16[384,2048]{1,0:T(8,128)(2,1)}, u32[]{:S(2)}, u32[]{:S(2)}) collective-permute-start(bf16[384,2048]{1,0:T(8,128)(2,1)} %shard_map.248.refs_1_), channel_id=1, source_target_pairs={{0,4},{1,5},{2,6},{3,7},{4,0},{5,1},{6,2},{7,3},{8,12},{9,13},{10,... | collective-permute-start | bytes 4718600 | tf_op jit(solution)/shard_map/ppermute | solution.py:49
  257.7 36.0 %collective-permute-start.28 = (bf16[384,2048]{1,0:T(8,128)(2,1)}, bf16[384,2048]{1,0:T(8,128)(2,1)}, u32[]{:S(2)}, u32[]{:S(2)}) collective-permute-start(bf16[384,2048]{1,0:T(8,128)(2,1)} %shard_map.248.refs_1_), channel_id=1, source_target_pairs={{0,2},{1,3},{2,0},{3,1},{4,6},{5,7},{6,4},{7,5},{8,10},{9,11},{10,... | collective-permute-start | bytes 4718600 | tf_op jit(solution)/shard_map/ppermute | solution.py:49
  297.0 20.6 %collective-permute-start.27 = (bf16[384,2048]{1,0:T(8,128)(2,1)S(1)}, bf16[384,2048]{1,0:T(8,128)(2,1)}, u32[]{:S(2)}, u32[]{:S(2)}) collective-permute-start(bf16[384,2048]{1,0:T(8,128)(2,1)S(1)} %copy-done.36), channel_id=1, source_target_pairs={{0,1},{1,0},{2,3},{3,2},{4,5},{5,4},{6,7},{7,6},{8,9},{9,8},{10,11... | collective-permute-start | bytes 4718600 | tf_op jit(solution)/shard_map/ppermute | solution.py:49
  384.5 27.7 %collective-permute-start.36 = (bf16[384,2048]{1,0:T(8,128)(2,1)}, bf16[384,2048]{1,0:T(8,128)(2,1)}, u32[]{:S(2)}, u32[]{:S(2)}) collective-permute-start(bf16[384,2048]{1,0:T(8,128)(2,1)} %get-tuple-element.117), channel_id=1, source_target_pairs={{0,1},{1,0},{2,3},{3,2},{4,5},{5,4},{6,7},{7,6},{8,9},{9,8},{10,11... | collective-permute-start | bytes 4718600 | tf_op jit(solution)/shard_map/ppermute | solution.py:49
  385.3 22.9 %collective-permute-start.38 = (bf16[384,2048]{1,0:T(8,128)(2,1)}, bf16[384,2048]{1,0:T(8,128)(2,1)}, u32[]{:S(2)}, u32[]{:S(2)}) collective-permute-start(bf16[384,2048]{1,0:T(8,128)(2,1)} %get-tuple-element.121), channel_id=1, source_target_pairs={{0,1},{1,0},{2,3},{3,2},{4,5},{5,4},{6,7},{7,6},{8,9},{9,8},{10,11... | collective-permute-start | bytes 4718600 | tf_op jit(solution)/shard_map/ppermute | solution.py:49
  385.7 92.0 %collective-permute-start.39 = (bf16[384,2048]{1,0:T(8,128)(2,1)}, bf16[384,2048]{1,0:T(8,128)(2,1)}, u32[]{:S(2)}, u32[]{:S(2)}) collective-permute-start(bf16[384,2048]{1,0:T(8,128)(2,1)} %get-tuple-element.123), channel_id=1, source_target_pairs={{0,1},{1,0},{2,3},{3,2},{4,5},{5,4},{6,7},{7,6},{8,9},{9,8},{10,11... | collective-permute-start | bytes 4718600 | tf_op jit(solution)/shard_map/ppermute | solution.py:49
  401.8 155.2 %reduce-scatter.8.cloned.1.call-start = ((), (), s32[]{:S(2)}) async-start(), calls=%async_computation.15 | async-start | bytes 3932160 | tf_op jit(solution)/shard_map/reduce_scatter | solution.py:72
  419.5 24.4 %collective-permute-start.41 = (bf16[192,2048]{1,0:T(8,128)(2,1)S(1)}, bf16[192,2048]{1,0:T(8,128)(2,1)}, u32[]{:S(2)}, u32[]{:S(2)}) collective-permute-start(bf16[192,2048]{1,0:T(8,128)(2,1)S(1)} %slice.356), channel_id=1, source_target_pairs={{0,2},{1,3},{2,0},{3,1},{4,6},{5,7},{6,4},{7,5},{8,10},{9,11},{10,... | collective-permute-start | bytes 2359304 | tf_op jit(solution)/shard_map/ppermute | solution.py:49
  422.2 33.9 %collective-permute-start.48 = (bf16[192,2048]{1,0:T(8,128)(2,1)S(1)}, bf16[192,2048]{1,0:T(8,128)(2,1)}, u32[]{:S(2)}, u32[]{:S(2)}) collective-permute-start(bf16[192,2048]{1,0:T(8,128)(2,1)S(1)} %slice.355), channel_id=1, source_target_pairs={{0,4},{1,5},{2,6},{3,7},{4,0},{5,1},{6,2},{7,3},{8,12},{9,13},{10,... | collective-permute-start | bytes 2359304 | tf_op jit(solution)/shard_map/ppermute | solution.py:49
  428.1 45.8 %collective-permute-start.45 = (bf16[192,2048]{1,0:T(8,128)(2,1)}, bf16[192,2048]{1,0:T(8,128)(2,1)}, u32[]{:S(2)}, u32[]{:S(2)}) collective-permute-start(bf16[192,2048]{1,0:T(8,128)(2,1)} %fusion.26), channel_id=1, source_target_pairs={{0,4},{1,5},{2,6},{3,7},{4,0},{5,1},{6,2},{7,3},{8,12},{9,13},{10,... | collective-permute-start | bytes 2359304 | tf_op jit(solution)/shard_map/ppermute | solution.py:49
  440.3 35.2 %collective-permute-start.47 = (bf16[192,2048]{1,0:T(8,128)(2,1)}, bf16[192,2048]{1,0:T(8,128)(2,1)}, u32[]{:S(2)}, u32[]{:S(2)}) collective-permute-start(bf16[192,2048]{1,0:T(8,128)(2,1)} %fusion.25), channel_id=1, source_target_pairs={{0,2},{1,3},{2,0},{3,1},{4,6},{5,7},{6,4},{7,5},{8,10},{9,11},{10,... | collective-permute-start | bytes 2359304 | tf_op jit(solution)/shard_map/ppermute | solution.py:49
  481.0 165.8 %reduce-scatter.10.cloned.1.call-start = ((), (), s32[]{:S(2)}) async-start(), calls=%async_computation.16 | async-start | bytes 3932160 | tf_op jit(solution)/shard_map/reduce_scatter | solution.py:72
  488.3 33.6 %collective-permute-start.51 = (bf16[384,2048]{1,0:T(8,128)(2,1)}, bf16[384,2048]{1,0:T(8,128)(2,1)}, u32[]{:S(2)}, u32[]{:S(2)}) collective-permute-start(bf16[384,2048]{1,0:T(8,128)(2,1)} %get-tuple-element.174.refs_0_.refs_1_), channel_id=1, source_target_pairs={{0,4},{1,5},{2,6},{3,7},{4,0},{5,1},{6,2},{7,3},{8,12},{9,13},{10,... | collective-permute-start | bytes 4718600 | tf_op jit(solution)/shard_map/ppermute | solution.py:49
  489.4 34.0 %collective-permute-start.50 = (bf16[384,2048]{1,0:T(8,128)(2,1)}, bf16[384,2048]{1,0:T(8,128)(2,1)}, u32[]{:S(2)}, u32[]{:S(2)}) collective-permute-start(bf16[384,2048]{1,0:T(8,128)(2,1)} %get-tuple-element.174.refs_0_.refs_1_), channel_id=1, source_target_pairs={{0,2},{1,3},{2,0},{3,1},{4,6},{5,7},{6,4},{7,5},{8,10},{9,11},{10,... | collective-permute-start | bytes 4718600 | tf_op jit(solution)/shard_map/ppermute | solution.py:49
  526.2 23.9 %collective-permute-start.49 = (bf16[384,2048]{1,0:T(8,128)(2,1)}, bf16[384,2048]{1,0:T(8,128)(2,1)}, u32[]{:S(2)}, u32[]{:S(2)}) collective-permute-start(bf16[384,2048]{1,0:T(8,128)(2,1)} %get-tuple-element.174.refs_0_.refs_1_), channel_id=1, source_target_pairs={{0,1},{1,0},{2,3},{3,2},{4,5},{5,4},{6,7},{7,6},{8,9},{9,8},{10,11... | collective-permute-start | bytes 4718600 | tf_op jit(solution)/shard_map/ppermute | solution.py:49
  530.0 20.0 %collective-permute-start.52 = (bf16[384,2048]{1,0:T(8,128)(2,1)}, bf16[384,2048]{1,0:T(8,128)(2,1)}, u32[]{:S(2)}, u32[]{:S(2)}) collective-permute-start(bf16[384,2048]{1,0:T(8,128)(2,1)} %get-tuple-element.132.refs_2_.refs_3_), channel_id=1, source_target_pairs={{0,1},{1,0},{2,3},{3,2},{4,5},{5,4},{6,7},{7,6},{8,9},{9,8},{10,11... | collective-permute-start | bytes 4718600 | tf_op jit(solution)/shard_map/ppermute | solution.py:49
  530.0 20.0 %collective-permute-start.53 = (bf16[384,2048]{1,0:T(8,128)(2,1)}, bf16[384,2048]{1,0:T(8,128)(2,1)}, u32[]{:S(2)}, u32[]{:S(2)}) collective-permute-start(bf16[384,2048]{1,0:T(8,128)(2,1)} %get-tuple-element.133.refs_4_.refs_5_), channel_id=1, source_target_pairs={{0,1},{1,0},{2,3},{3,2},{4,5},{5,4},{6,7},{7,6},{8,9},{9,8},{10,11... | collective-permute-start | bytes 4718600 | tf_op jit(solution)/shard_map/ppermute | solution.py:49
  546.9 104.8 %collective-permute-start.35 = (bf16[384,2048]{1,0:T(8,128)(2,1)}, bf16[384,2048]{1,0:T(8,128)(2,1)}, u32[]{:S(2)}, u32[]{:S(2)}) collective-permute-start(bf16[384,2048]{1,0:T(8,128)(2,1)} %get-tuple-element.115), channel_id=1, source_target_pairs={{0,1},{1,0},{2,3},{3,2},{4,5},{5,4},{6,7},{7,6},{8,9},{9,8},{10,11... | collective-permute-start | bytes 4718600 | tf_op jit(solution)/shard_map/ppermute | solution.py:49
  550.8 62.2 %collective-permute-start.57 = (bf16[192,2048]{1,0:T(8,128)(2,1)}, bf16[192,2048]{1,0:T(8,128)(2,1)}, u32[]{:S(2)}, u32[]{:S(2)}) collective-permute-start(bf16[192,2048]{1,0:T(8,128)(2,1)} %get-tuple-element.134.refs_1_), channel_id=1, source_target_pairs={{0,2},{1,3},{2,0},{3,1},{4,6},{5,7},{6,4},{7,5},{8,10},{9,11},{10,... | collective-permute-start | bytes 2359304 | tf_op jit(solution)/shard_map/ppermute | solution.py:49
  552.3 60.7 %collective-permute-start.62 = (bf16[192,2048]{1,0:T(8,128)(2,1)}, bf16[192,2048]{1,0:T(8,128)(2,1)}, u32[]{:S(2)}, u32[]{:S(2)}) collective-permute-start(bf16[192,2048]{1,0:T(8,128)(2,1)} %get-tuple-element.136.refs_2_), channel_id=1, source_target_pairs={{0,4},{1,5},{2,6},{3,7},{4,0},{5,1},{6,2},{7,3},{8,12},{9,13},{10,... | collective-permute-start | bytes 2359304 | tf_op jit(solution)/shard_map/ppermute | solution.py:49
  555.2 57.8 %collective-permute-start.58 = (bf16[192,2048]{1,0:T(8,128)(2,1)}, bf16[192,2048]{1,0:T(8,128)(2,1)}, u32[]{:S(2)}, u32[]{:S(2)}) collective-permute-start(bf16[192,2048]{1,0:T(8,128)(2,1)} %get-tuple-element.182), channel_id=1, source_target_pairs={{0,2},{1,3},{2,0},{3,1},{4,6},{5,7},{6,4},{7,5},{8,10},{9,11},{10,... | collective-permute-start | bytes 2359304 | tf_op jit(solution)/shard_map/ppermute | solution.py:49
  555.2 57.8 %collective-permute-start.60 = (bf16[192,2048]{1,0:T(8,128)(2,1)}, bf16[192,2048]{1,0:T(8,128)(2,1)}, u32[]{:S(2)}, u32[]{:S(2)}) collective-permute-start(bf16[192,2048]{1,0:T(8,128)(2,1)} %get-tuple-element.183), channel_id=1, source_target_pairs={{0,4},{1,5},{2,6},{3,7},{4,0},{5,1},{6,2},{7,3},{8,12},{9,13},{10,... | collective-permute-start | bytes 2359304 | tf_op jit(solution)/shard_map/ppermute | solution.py:49
  557.1 154.3 %reduce-scatter.12.cloned.1.call-start = ((), (), s32[]{:S(2)}) async-start(), calls=%async_computation.17 | async-start | bytes 2949120 | tf_op jit(solution)/shard_map/reduce_scatter | solution.py:72
  613.6 26.0 %collective-permute-start.65 = (bf16[384,2048]{1,0:T(8,128)(2,1)}, bf16[384,2048]{1,0:T(8,128)(2,1)S(1)}, u32[]{:S(2)}, u32[]{:S(2)}) collective-permute-start(bf16[384,2048]{1,0:T(8,128)(2,1)} %get-tuple-element.156), channel_id=1, source_target_pairs={{0,1},{1,0},{2,3},{3,2},{4,5},{5,4},{6,7},{7,6},{8,9},{9,8},{10,11... | collective-permute-start | bytes 4718600 | tf_op jit(solution)/shard_map/ppermute | solution.py:49
  617.0 19.3 %collective-permute-start.59 = (bf16[192,2048]{1,0:T(8,128)(2,1)S(1)}, bf16[192,2048]{1,0:T(8,128)(2,1)S(1)}, u32[]{:S(2)}, u32[]{:S(2)}) collective-permute-start(bf16[192,2048]{1,0:T(8,128)(2,1)S(1)} %fusion.24), channel_id=1, source_target_pairs={{0,4},{1,5},{2,6},{3,7},{4,0},{5,1},{6,2},{7,3},{8,12},{9,13},{10,... | collective-permute-start | bytes 2359304 | tf_op jit(solution)/shard_map/ppermute | solution.py:49
  619.1 21.0 %collective-permute-start.66 = (bf16[384,2048]{1,0:T(8,128)(2,1)S(1)}, bf16[384,2048]{1,0:T(8,128)(2,1)S(1)}, u32[]{:S(2)}, u32[]{:S(2)}) collective-permute-start(bf16[384,2048]{1,0:T(8,128)(2,1)S(1)} %copy-done.60), channel_id=1, source_target_pairs={{0,1},{1,0},{2,3},{3,2},{4,5},{5,4},{6,7},{7,6},{8,9},{9,8},{10,11... | collective-permute-start | bytes 4718600 | tf_op jit(solution)/shard_map/ppermute | solution.py:49
  622.5 27.3 %collective-permute-start.61 = (bf16[192,2048]{1,0:T(8,128)(2,1)}, bf16[192,2048]{1,0:T(8,128)(2,1)}, u32[]{:S(2)}, u32[]{:S(2)}) collective-permute-start(bf16[192,2048]{1,0:T(8,128)(2,1)} %fusion.23), channel_id=1, source_target_pairs={{0,2},{1,3},{2,0},{3,1},{4,6},{5,7},{6,4},{7,5},{8,10},{9,11},{10,... | collective-permute-start | bytes 2359304 | tf_op jit(solution)/shard_map/ppermute | solution.py:49
  648.3 19.2 %collective-permute-start.68 = (bf16[192,2048]{1,0:T(8,128)(2,1)S(1)}, bf16[192,2048]{1,0:T(8,128)(2,1)S(1)}, u32[]{:S(2)}, u32[]{:S(2)}) collective-permute-start(bf16[192,2048]{1,0:T(8,128)(2,1)S(1)} %get-tuple-element.180), channel_id=1, source_target_pairs={{0,2},{1,3},{2,0},{3,1},{4,6},{5,7},{6,4},{7,5},{8,10},{9,11},{10,... | collective-permute-start | bytes 2359304 | tf_op jit(solution)/shard_map/ppermute | solution.py:49
  656.0 51.1 %collective-permute-start.63 = (bf16[384,2048]{1,0:T(8,128)(2,1)}, bf16[384,2048]{1,0:T(8,128)(2,1)S(1)}, u32[]{:S(2)}, u32[]{:S(2)}) collective-permute-start(bf16[384,2048]{1,0:T(8,128)(2,1)} %get-tuple-element.152), channel_id=1, source_target_pairs={{0,1},{1,0},{2,3},{3,2},{4,5},{5,4},{6,7},{7,6},{8,9},{9,8},{10,11... | collective-permute-start | bytes 4718600 | tf_op jit(solution)/shard_map/ppermute | solution.py:49
  656.5 27.9 %collective-permute-start.67 = (bf16[192,2048]{1,0:T(8,128)(2,1)}, bf16[192,2048]{1,0:T(8,128)(2,1)}, u32[]{:S(2)}, u32[]{:S(2)}) collective-permute-start(bf16[192,2048]{1,0:T(8,128)(2,1)} %get-tuple-element.163), channel_id=1, source_target_pairs={{0,2},{1,3},{2,0},{3,1},{4,6},{5,7},{6,4},{7,5},{8,10},{9,11},{10,... | collective-permute-start | bytes 2359304 | tf_op jit(solution)/shard_map/ppermute | solution.py:49
  656.6 49.1 %collective-permute-start.72 = (bf16[192,2048]{1,0:T(8,128)(2,1)}, bf16[192,2048]{1,0:T(8,128)(2,1)S(1)}, u32[]{:S(2)}, u32[]{:S(2)}) collective-permute-start(bf16[192,2048]{1,0:T(8,128)(2,1)} %get-tuple-element.165), channel_id=1, source_target_pairs={{0,4},{1,5},{2,6},{3,7},{4,0},{5,1},{6,2},{7,3},{8,12},{9,13},{10,... | collective-permute-start | bytes 2359304 | tf_op jit(solution)/shard_map/ppermute | solution.py:49
  668.6 35.4 %collective-permute-start.69 = (bf16[192,2048]{1,0:T(8,128)(2,1)}, bf16[192,2048]{1,0:T(8,128)(2,1)}, u32[]{:S(2)}, u32[]{:S(2)}) collective-permute-start(bf16[192,2048]{1,0:T(8,128)(2,1)} %fusion.22), channel_id=1, source_target_pairs={{0,4},{1,5},{2,6},{3,7},{4,0},{5,1},{6,2},{7,3},{8,12},{9,13},{10,... | collective-permute-start | bytes 2359304 | tf_op jit(solution)/shard_map/ppermute | solution.py:49
  671.4 34.2 %collective-permute-start.71 = (bf16[192,2048]{1,0:T(8,128)(2,1)}, bf16[192,2048]{1,0:T(8,128)(2,1)}, u32[]{:S(2)}, u32[]{:S(2)}) collective-permute-start(bf16[192,2048]{1,0:T(8,128)(2,1)} %fusion.21), channel_id=1, source_target_pairs={{0,2},{1,3},{2,0},{3,1},{4,6},{5,7},{6,4},{7,5},{8,10},{9,11},{10,... | collective-permute-start | bytes 2359304 | tf_op jit(solution)/shard_map/ppermute | solution.py:49
  675.0 45.9 %all-to-all-start.3 = ((bf16[8,64,1536]{2,1,0:T(8,128)(2,1)}), bf16[8,64,1536]{2,1,0:T(8,128)(2,1)}, u32[]{:S(2)}, u32[]{:S(2)}) async-start(bf16[8,64,1536]{2,1,0:T(8,128)(2,1)} %bitcast.25), calls=%async_computation.8 | async-start | bytes 3145728 | tf_op jit(solution)/shard_map/all_to_all | solution.py:60
  681.1 65.2 %reduce-scatter.14.cloned.1.call-start = ((), (), s32[]{:S(2)}) async-start(), calls=%async_computation.18 | async-start | bytes 1310720 | tf_op jit(solution)/shard_map/reduce_scatter | solution.py:72
  720.9 23.3 %all-to-all-start.2 = ((bf16[8,72,512]{2,1,0:T(8,128)(2,1)}), bf16[8,72,512]{2,1,0:T(8,128)(2,1)}, u32[]{:S(2)}, u32[]{:S(2)}) async-start(bf16[8,72,512]{2,1,0:T(8,128)(2,1)} %bitcast.91), calls=%async_computation.6 | async-start | bytes 1179648 | tf_op jit(solution)/shard_map/all_to_all | solution.py:60
  746.3 21.5 %collective-permute-start.73 = (bf16[64,2048]{1,0:T(8,128)(2,1)}, bf16[64,2048]{1,0:T(8,128)(2,1)S(1)}, u32[]{:S(2)}, u32[]{:S(2)}) collective-permute-start(bf16[64,2048]{1,0:T(8,128)(2,1)} %reduce-scatter.14.cloned.1.call-done), channel_id=1, source_target_pairs={{0,0},{8,1},{16,2},{24,3},{1,4},{9,5},{17,6},{25,7},{2,8},{10,9},{... | collective-permute-start | bytes 786440 | tf_op jit(solution)/shard_map/ppermute | solution.py:143
  (98 other events, 944.4 us)
Sparse Core Ops, SparseCore 0:
  25.9 57.8 all-gather.5
  85.9 26.3 all-gather.7
  114.8 63.2 all-gather.9
  179.5 62.1 all-gather.11
  243.1 62.1 all-gather.13
  401.9 60.9 reduce-scatter.5
  481.1 63.0 reduce-scatter.7
  557.2 62.3 reduce-scatter.9
  646.9 47.1 reduce-scatter.11
  711.6 31.1 reduce-scatter.13

commit v4 on v3

--- a/solution.py
+++ b/solution.py
@@ -98,11 +98,11 @@
         half = parts[0].shape[0] // 2
         odd = {r: swap(parts[r + 1], 1) for r in (6, 2, 4, 0)}
         self.total6, self.total2, self.total4, self.total0 = (
-            parts[r].astype(F32) + odd[r].astype(F32) for r in (6, 2, 4, 0)
+            (parts[r].astype(F32) + odd[r].astype(F32)).astype(BF16) for r in (6, 2, 4, 0)
         )
         self.half = half
-        self.low6 = self.total6.astype(BF16)
-        self.ready = [self.low6, self.total2[:half].astype(BF16), self.total4[half:].astype(BF16)]
+        self.low6 = self.total6
+        self.ready = [self.low6, self.total2[:half], self.total4[half:]]
 
     def first(self, tick=None):
         half = self.half
@@ -117,30 +117,20 @@
     def total(self, tick=None):
         half = self.half
         lasts = [
-            (self.total2[half:] + self.u2.astype(F32)).astype(BF16),
-            (self.total4[:half] + self.u4.astype(F32)).astype(BF16),
+            (self.total2[half:].astype(F32) + self.u2.astype(F32)).astype(BF16),
+            (self.total4[:half].astype(F32) + self.u4.astype(F32)).astype(BF16),
         ]
         x_low, y_top = lasts if tick is None else hold(lasts, tick)
+        self.last_sent = [x_low, y_top]
         x_low = swap(x_low, 2).astype(F32)
         y_top = swap(y_top, 4).astype(F32)
         top = self.x_top.astype(F32) + y_top
         low = x_low + self.y_low.astype(F32)
-        return self.total0 + jnp.concatenate([top, low], axis=0)
+        return self.total0.astype(F32) + jnp.concatenate([top, low], axis=0)
 
 
 def out_weight_routes(groups):
     return [(i, TEAM * (i % groups) + i // groups) for i in range(groups * TEAM)]
-
-
-def out_weight_in(shard, groups, after):
-    routed = lax.ppermute(shard, ALL, out_weight_routes(groups))
-    return line_gather(hold([routed], after)[0]), routed
-
-
-def out_weight_back(grad, groups, done):
-    grad = hold([grad], done)[0]
-    routes = [(user, owner) for owner, user in out_weight_routes(groups)]
-    return lax.ppermute(line_sum(grad), ALL, routes), hold([done], grad)[0]
 
 
 def rms_pull(value, gain, grad):
@@ -753,14 +743,18 @@
     ).transpose(1, 0, 2)
     attn = jnp.concatenate([attn, jnp.pad(row, ((0, 0), (0, 7), (0, 0)))], axis=1)
     attn = exchange(attn)
-    exchanged = attn
     head_lanes = mine * rho
     at_one, at_two, at_pair = head_lanes, head_lanes + rho, head_lanes + 2 * rho
     at_tiles = at_pair + 2 * pair_cols
     team_tiles = attn[:, rho, at_tiles].astype(jnp.int32)
     order = jnp.arange(TEAM, dtype=jnp.int32)
     tiles = jnp.sum(jnp.where((order[:, None] ^ t) == order[None, :], team_tiles[None, :], 0), axis=1)
-    attn = line_gather(attn.reshape(TEAM * (rho + 8), cols)).reshape(everyone, rho + 8, cols)
+    routed = lax.ppermute(output_weight, ALL, out_weight_routes(groups))
+    team_rows = TEAM * (rho + 8)
+    attn = jnp.concatenate([attn.reshape(team_rows, cols), routed.reshape(-1, cols)], axis=0)
+    attn = line_gather(attn).reshape(groups, -1, cols)
+    weight_out = attn[:, team_rows:].reshape(-1, width)
+    attn = attn[:, :team_rows].reshape(everyone, rho + 8, cols)
     weight_attn = attn[:, :rho].reshape(width, cols)
     rows_small = attn[:, rho]
     weight_head = jnp.pad(
@@ -776,14 +770,10 @@
         .reshape(2, size)
         .astype(F32)
     )
-    weight_out, routed = out_weight_in(output_weight, groups, exchanged)
-
     def ff_split(w):
         return w.reshape(rho, groups, TEAM, phi).transpose(2, 0, 1, 3).reshape(TEAM, rho, ff_cols)
 
     feed_shard = jnp.concatenate([ff_split(gate_weight), ff_split(up_weight)], axis=2)
-    feed_shard = exchange(hold([feed_shard], routed)[0]).reshape(TEAM * rho, -1)
-    weight_gate = line_gather(feed_shard[:, :ff_cols])
 
     exponent = jnp.arange(size // 2, dtype=F32) * (-2.0 / size)
     frequency = jnp.power(ROPE_BASE, exponent)
@@ -792,27 +782,28 @@
     sine = jnp.concatenate([-jnp.sin(angles), jnp.sin(angles)], axis=1)
     consts = (weight_attn, weight_head, weight_out, gain_one, gain_pair, cosine, sine)
     team_tokens = team_gather(tokens)
+    feed_shard = exchange(hold([feed_shard], team_tokens[6])[0]).reshape(TEAM * rho, -1)
+    weight_gate = line_gather(feed_shard[:, :ff_cols])
     live = lax.broadcasted_iota(jnp.int32, (rows, 1), 0) < lengths[0]
     live_rows = live.astype(F32)
     upstream = cotangent.astype(F32) * live_rows
-    tick = mark([team_tokens[6], feed_shard])
+    tick = mark([team_tokens[6]])
     later = lax.broadcasted_iota(jnp.int32, (rows, 1), 0) < lengths[0] + tick[0, 0]
     upstream_low = jnp.where(later, cotangent, jnp.zeros_like(cotangent))
     upstream_levels = TeamGather(upstream_low)
-    parts, kept, tick = attend(tiles, team_tokens, consts, mine, mark([feed_shard, upstream_low]))
+    parts, kept, tick = attend(tiles, team_tokens, consts, mine, mark([upstream_low]))
     normed, qkv, logit, gated = kept
     weight_up = line_gather(hold([feed_shard[:, ff_cols:]], tick)[0])
     parts = hold(parts, mark([upstream_levels.a1, upstream_levels.a2, upstream_levels.a4, tick]))
     arrived = TeamSum(parts)
     arrived.first()
     weight_down = line_gather(hold([down_weight], arrived.low6)[0])
-    team_upstream = upstream_levels.blocks(mark([arrived.u4, arrived.u2]))
     inputs = tokens.astype(F32)
     hidden_state = inputs + arrived.total(weight_gate)
+    team_upstream = upstream_levels.blocks(mark(arrived.last_sent))
 
     normed_two = rms(hidden_state, gain_two).astype(BF16)
-    normed_two = hold([normed_two], mark(team_upstream))[0]
-    team_two = TeamGather(normed_two).blocks(mark([weight_up]))
+    team_two = TeamGather(normed_two).blocks(mark(team_upstream + [weight_up]))
     outs, grads, saved = feed(tiles, team_two, team_upstream, weight_gate, weight_up, weight_down)
     inner, feed_back, two_all, ups_all = saved
     arrived = TeamSum(grads)
@@ -850,16 +841,20 @@
     packed = jnp.concatenate(
         [attn_part.reshape(everyone, rho, cols), jnp.pad(row, ((0, 0), (0, 7), (0, 0)))], axis=1
     )
-    packed = hold([packed.reshape(everyone * (rho + 8), cols)], feed_done)[0]
+    packed = jnp.concatenate(
+        [packed.reshape(groups, team_rows, cols), out_part.reshape(groups, -1, cols)], axis=1
+    )
     parts = hold(parts, mark(first_hop + [gate_grad]))
     arrived = TeamSum(parts)
-    arrived.first(packed)
+    arrived.first()
+    packed = hold([packed.reshape(-1, cols)], mark([feed_done, arrived.u4, arrived.u2] + arrived.sent))[0]
+    normed_grad = arrived.total(packed)
     packed = line_sum(packed)
-    normed_grad = arrived.total()
     layer_output = ((hidden_state + fed.total()) * live_rows).astype(BF16)
     tokens_grad = (hidden_grad + rms_pull(inputs, gain_one, normed_grad)).astype(BF16)
-    output_grad, packed = out_weight_back(out_part, groups, packed)
-    packed = exchange(packed.reshape(TEAM, rho + 8, cols))
+    routes = [(user, owner) for owner, user in out_weight_routes(groups)]
+    output_grad = lax.ppermute(packed[team_rows:].reshape(rho, width), ALL, routes)
+    packed = exchange(packed[:team_rows].reshape(TEAM, rho + 8, cols))
     feed_grad = jnp.concatenate([gate_grad, hold([up_grad], arrived.u4)[0]], axis=1)
     feed_grad = exchange(feed_grad.reshape(TEAM, rho, 2 * ff_cols))
 

time: 791 us -> 813 us (1.028)
  the two profiles are of different devices: /device:TPU:1 before, /device:TPU:26 now
where the time goes in v4:
time: 813 us; the launch traced here: 799 us
  waiting for transfers between devices  326 us (40%)
  Pallas kernels  150 us (18%)
  other arithmetic  94.7 us (12%)
  local copies, waits for them, and re-layouts  83.2 us (10%)
  starting transfers between devices  82.7 us (10%)
  matrix products  45.9 us (6%)
  between operations  17.2 us (2%)
    ppermute x72, waiting for transfers between devices, permute(): lax.ppermute(array, ALL, [(team[a], team[b]) for team in teams() for a, b...  297 us
    pallas_call x1, Pallas kernels, feed(): pl.pallas_call(kernel, out_shape=[struct((rows, width), BF16)] * (2 * TEA...  63.7 us
    pallas_call x1, Pallas kernels, attend_back(): pl.pallas_call(kernel, out_shape=[struct((rows, width), BF16)] * TEAM + [...  50.1 us
    dot_general x3, matrix products, product_tn(): lax.dot_general(left, right, (((0,), (0,)), ((), ())), preferred_element_...  45.9 us
    ppermute x72, starting transfers between devices, permute(): lax.ppermute(array, ALL, [(team[a], team[b]) for team in teams() for a, b...  42.4 us
    pallas_call x1, Pallas kernels, attend(): pl.pallas_call(kernel, out_shape=[struct((rows, width), BF16)] * TEAM + [...  28.6 us
    unnamed x141, local copies, waits for them, and re-layouts  19.5 us
    all_to_all x4, starting transfers between devices, exchange(): return lax.all_to_all(blocks, 'fsdp', 0, 0, tiled=True)  19.1 us
  transfers between devices with their start and end apart: 86, of which 31 were waited for; matrix products, arithmetic and copies ran while one was open for 25% of the time, Pallas kernels for 11%

profile of v4, /device:TPU:26, one launch (start us, length us, event | category | flops | bytes accessed | tf_op | source)
XLA Modules:
  0.0 799.3 jit_solution(15294867256513550894)
XLA Ops:
  7.3 2.2 copy.221.refs_0_
  11.7 4.3 all-to-all-start
  16.0 3.3 collective-permute-start.8
  19.2 13.3 %collective-permute-done.8 = bf16[64,2048]{1,0:T(8,128)(2,1)S(1)} collective-permute-done((bf16[64,2048]{1,0:T(8,128)(2,1)S(1)}, bf16[64,2048]{1,0:T(8,128)(2,1)S(1)}, u32[]{:S(2)}, u32[]{:S(2)}) %collective-permute-start.8) | collective-permute-done | bytes 262176 | tf_op jit(solution)/shard_map/ppermute | solution.py:752
  34.0 36.9 %collective-permute-done.3.refs_5_ = bf16[384,2048]{1,0:T(8,128)(2,1)S(1)} collective-permute-done((bf16[384,2048]{1,0:T(8,128)(2,1)}, bf16[384,2048]{1,0:T(8,128)(2,1)S(1)}, u32[]{:S(2)}, u32[]{:S(2)}) %collective-permute-start.3) | collective-permute-done | bytes 1572896 | tf_op jit(solution)/shard_map/ppermute | solution.py:49
  76.6 2.2 reshape.289
  81.5 10.0 %collective-permute-done.5 = bf16[192,2048]{1,0:T(8,128)(2,1)} collective-permute-done((bf16[192,2048]{1,0:T(8,128)(2,1)}, bf16[192,2048]{1,0:T(8,128)(2,1)}, u32[]{:S(2)}, u32[]{:S(2)}) %collective-permute-start.5) | collective-permute-done | bytes 786464 | tf_op jit(solution)/shard_map/ppermute | solution.py:49
  91.5 2.1 constant_dynamic-update-slice_fusion.1
  93.5 2.1 constant_dynamic-update-slice_fusion.refs_0_.refs_7_.refs_1_
  95.6 4.5 all-to-all-start.1
  105.9 13.8 %all-to-all-done.1 = bf16[8,64,1536]{2,1,0:T(8,128)(2,1)S(1)} async-done(((bf16[8,64,1536]{2,1,0:T(8,128)(2,1)}), bf16[8,64,1536]{2,1,0:T(8,128)(2,1)S(1)}, u32[]{:S(2)}, u32[]{:S(2)}) %all-to-all-start.1) | async-done | bytes 1572896 | tf_op jit(solution)/shard_map/all_to_all | solution.py:60
  124.3 2.3 slice.269
  134.2 28.6 %shard_map.239 = (bf16[384,2048]{1,0:T(8,128)(2,1)S(1)}, bf16[384,2048]{1,0:T(8,128)(2,1)S(1)}, bf16[384,2048]{1,0:T(8,128)(2,1)}, bf16[384,2048]{1,0:T(8,128)(2...) custom-call(s32[8]{0:T(128)S(1)} %select_reduce_fusion.refs_0_, ...), custom_call_target="tpu_custom_call" | custom-call | flops 32212254720 | bytes 62914560 | tf_op jit(solution)/shard_map/pallas_call | solution.py:307
  165.8 2.9 collective-permute-done.10.refs_1_.refs_0_
  170.0 2.9 collective-permute-done.15
  180.0 14.4 %collective-permute-done.16 = bf16[192,2048]{1,0:T(8,128)(2,1)S(1)} collective-permute-done((bf16[192,2048]{1,0:T(8,128)(2,1)S(1)}, bf16[192,2048]{1,0:T(8,128)(2,1)S(1)}, u32[]{:S(2)}, u32[]{:S(2)}) %collective-permute-start.16) | collective-permute-done | bytes 786464 | tf_op jit(solution)/shard_map/ppermute | solution.py:49
  195.5 17.9 %collective-permute-done.18 = bf16[192,2048]{1,0:T(8,128)(2,1)S(1)} collective-permute-done((bf16[192,2048]{1,0:T(8,128)(2,1)S(1)}, bf16[192,2048]{1,0:T(8,128)(2,1)S(1)}, u32[]{:S(2)}, u32[]{:S(2)}) %collective-permute-start.18) | collective-permute-done | bytes 786464 | tf_op jit(solution)/shard_map/ppermute | solution.py:49
  222.4 13.0 %collective-permute-done.19 = bf16[192,2048]{1,0:T(8,128)(2,1)} collective-permute-done((bf16[192,2048]{1,0:T(8,128)(2,1)}, bf16[192,2048]{1,0:T(8,128)(2,1)}, u32[]{:S(2)}, u32[]{:S(2)}) %collective-permute-start.19) | collective-permute-done | bytes 786464 | tf_op jit(solution)/shard_map/ppermute | solution.py:49
  237.0 13.3 %collective-permute-done.21 = bf16[192,2048]{1,0:T(8,128)(2,1)} collective-permute-done((bf16[192,2048]{1,0:T(8,128)(2,1)}, bf16[192,2048]{1,0:T(8,128)(2,1)}, u32[]{:S(2)}, u32[]{:S(2)}) %collective-permute-start.21) | collective-permute-done | bytes 786464 | tf_op jit(solution)/shard_map/ppermute | solution.py:49
  253.6 2.9 multiply_reduce_fusion.2
  256.5 11.5 %collective-permute-done.27 = bf16[192,2048]{1,0:T(8,128)(2,1)S(1)} collective-permute-done((bf16[192,2048]{1,0:T(8,128)(2,1)S(1)}, bf16[192,2048]{1,0:T(8,128)(2,1)S(1)}, u32[]{:S(2)}, u32[]{:S(2)}) %collective-permute-start.27) | collective-permute-done | bytes 786464 | tf_op jit(solution)/shard_map/ppermute | solution.py:49
  274.4 34.0 %collective-permute-done.24.refs_1_ = bf16[384,2048]{1,0:T(8,128)(2,1)} collective-permute-done((bf16[384,2048]{1,0:T(8,128)(2,1)}, bf16[384,2048]{1,0:T(8,128)(2,1)}, u32[]{:S(2)}, u32[]{:S(2)}) %collective-permute-start.24) | collective-permute-done | bytes 1572896 | tf_op jit(solution)/shard_map/ppermute | solution.py:49
  314.0 15.9 %collective-permute-done.32 = bf16[192,2048]{1,0:T(8,128)(2,1)S(1)} collective-permute-done((bf16[192,2048]{1,0:T(8,128)(2,1)S(1)}, bf16[192,2048]{1,0:T(8,128)(2,1)S(1)}, u32[]{:S(2)}, u32[]{:S(2)}) %collective-permute-start.32) | collective-permute-done | bytes 786464 | tf_op jit(solution)/shard_map/ppermute | solution.py:49
  332.8 3.7 collective-permute-done.34.refs_8_
  336.4 63.7 %shard_map.250 = (bf16[384,2048]{1,0:T(8,128)(2,1)}, bf16[384,2048]{1,0:T(8,128)(2,1)}, bf16[384,2048]{1,0:T(8,128)(2,1)}, bf16[384,2048]{1,0:T(8,128)(2,1)}, bf...) custom-call(s32[8]{0:T(128)} %copy-done.11, ...), custom_call_target="tpu_custom_call" | custom-call | flops 62277025792 | bytes 104857600 | tf_op jit(solution)/shard_map/pallas_call | solution.py:655
  401.3 15.6 %convolution_convert_fusion = bf16[768,2048]{1,0:T(8,128)(2,1)} fusion(bf16[3072,768]{1,0:T(8,128)(2,1)} %get-tuple-element.140, bf16[3072,2048]{1,0:T(8,128)(2,1)} %get-tuple-element.141), kind=kOutput, calls=%fused_computation.13 | convolution fusion | flops 9665249280 | bytes 20447232 | tf_op jit(solution)/shard_map/dot_general | solution.py:29
  417.7 3.8 add_convert_fusion.10.refs_0_
  425.1 2.1 add_convert_fusion.9
  427.3 2.6 add_convert_fusion.8
  436.9 7.3 collective-permute-done.44
  446.0 8.4 %collective-permute-done.46 = bf16[192,2048]{1,0:T(8,128)(2,1)S(1)} collective-permute-done((bf16[192,2048]{1,0:T(8,128)(2,1)S(1)}, bf16[192,2048]{1,0:T(8,128)(2,1)S(1)}, u32[]{:S(2)}, u32[]{:S(2)}) %collective-permute-start.46) | collective-permute-done | bytes 786464 | tf_op jit(solution)/shard_map/ppermute | solution.py:49
  456.3 4.9 collective-permute-done.41.refs_0_
  461.2 10.2 %collective-permute-done.48.refs_1_ = bf16[192,2048]{1,0:T(8,128)(2,1)} collective-permute-done((bf16[192,2048]{1,0:T(8,128)(2,1)S(1)}, bf16[192,2048]{1,0:T(8,128)(2,1)}, u32[]{:S(2)}, u32[]{:S(2)}) %collective-permute-start.48) | collective-permute-done | bytes 786464 | tf_op jit(solution)/shard_map/ppermute | solution.py:49
  472.0 14.6 %fusion.5.refs_3_.refs_0_ = bf16[2048,768]{1,0:T(8,128)(2,1)S(1)} fusion(bf16[3072,2048]{1,0:T(8,128)(2,1)} %get-tuple-element.129, bf16[3072,1536]{1,0:T(8,128)(2,1)} %shard_map.252), kind=kOutput, calls=%fused_computation.11 | convolution fusion | flops 9665249280 | bytes 20447232 | tf_op jit(solution)/shard_map/dot_general | solution.py:29
  490.9 2.2 convert_add_fusion.5
  493.3 2.9 multiply_reduce_fusion
  496.6 6.9 fusion.36
  504.8 15.7 %fusion.8.refs_4_.refs_1_.refs_0_ = bf16[2048,768]{1,0:T(8,128)(2,1)} fusion(bf16[3072,2048]{1,0:T(8,128)(2,1)} %get-tuple-element.129, bf16[3072,1536]{1,0:T(8,128)(2,1)} %shard_map.252), kind=kOutput, calls=%fused_computation.12 | convolution fusion | flops 9665249280 | bytes 20447232 | tf_op jit(solution)/shard_map/dot_general | solution.py:29
  521.0 17.7 %collective-permute-done.51.refs_1_ = bf16[384,2048]{1,0:T(8,128)(2,1)} collective-permute-done((bf16[384,2048]{1,0:T(8,128)(2,1)}, bf16[384,2048]{1,0:T(8,128)(2,1)}, u32[]{:S(2)}, u32[]{:S(2)}) %collective-permute-start.51) | collective-permute-done | bytes 1572896 | tf_op jit(solution)/shard_map/ppermute | solution.py:49
  543.9 13.3 %collective-permute-done.54 = bf16[192,2048]{1,0:T(8,128)(2,1)S(1)} collective-permute-done((bf16[192,2048]{1,0:T(8,128)(2,1)S(1)}, bf16[192,2048]{1,0:T(8,128)(2,1)S(1)}, u32[]{:S(2)}, u32[]{:S(2)}) %collective-permute-start.54) | collective-permute-done | bytes 786464 | tf_op jit(solution)/shard_map/ppermute | solution.py:49
  560.0 3.1 collective-permute-done.56.refs_7_.refs_8_
  567.0 2.7 fusion.39
  571.2 50.1 %shard_map.259 = (bf16[384,2048]{1,0:T(8,128)(2,1)}, bf16[384,2048]{1,0:T(8,128)(2,1)}, bf16[384,2048]{1,0:T(8,128)(2,1)}, bf16[384,2048]{1,0:T(8,128)(2,1)}, bf...) custom-call(s32[8]{0:T(128)} %copy-done.11, ...), custom_call_target="tpu_custom_call" | custom-call | flops 48318382080 | bytes 73400320 | tf_op jit(solution)/shard_map/pallas_call | solution.py:465
  625.7 2.5 reshape.299
  646.0 10.0 %collective-permute-done.69.refs_1_ = bf16[192,2048]{1,0:T(8,128)(2,1)} collective-permute-done((bf16[192,2048]{1,0:T(8,128)(2,1)S(1)}, bf16[192,2048]{1,0:T(8,128)(2,1)}, u32[]{:S(2)}, u32[]{:S(2)}) %collective-permute-start.69) | collective-permute-done | bytes 786464 | tf_op jit(solution)/shard_map/ppermute | solution.py:49
  658.0 2.6 add_convert_fusion.19
  662.1 2.3 add_convert_fusion.18
  664.8 2.5 convert_element_type.529
  667.3 12.0 %collective-permute-done.59 = bf16[192,2048]{1,0:T(8,128)(2,1)} collective-permute-done((bf16[192,2048]{1,0:T(8,128)(2,1)}, bf16[192,2048]{1,0:T(8,128)(2,1)}, u32[]{:S(2)}, u32[]{:S(2)}) %collective-permute-start.59) | collective-permute-done | bytes 786464 | tf_op jit(solution)/shard_map/ppermute | solution.py:49
  679.3 2.7 convert_add_fusion.4
  682.8 2.7 convert_add_fusion.3
  686.1 2.3 add_convert_fusion.17.refs_0_
  688.4 2.3 add_convert_fusion.16.refs_1_
  691.5 5.1 fusion.19
  699.3 2.4 pad_maximum_fusion.2
  701.7 4.8 all-to-all-start.3
  706.4 4.9 collective-permute-done.70
  713.0 23.6 %collective-permute-done.72 = bf16[192,2048]{1,0:T(8,128)(2,1)S(1)} collective-permute-done((bf16[192,2048]{1,0:T(8,128)(2,1)}, bf16[192,2048]{1,0:T(8,128)(2,1)S(1)}, u32[]{:S(2)}, u32[]{:S(2)}) %collective-permute-start.72) | collective-permute-done | bytes 786464 | tf_op jit(solution)/shard_map/ppermute | solution.py:49
  736.8 3.1 fusion.11
  740.0 2.3 slice.300
  744.4 5.5 all-to-all-start.2
  749.9 4.4 fusion.15
  755.2 16.7 %collective-permute-start.73 = (bf16[64,2048]{1,0:T(8,128)(2,1)}, bf16[64,2048]{1,0:T(8,128)(2,1)S(1)}, u32[]{:S(2)}, u32[]{:S(2)}) collective-permute-start(bf16[64,2048]{1,0:T(8,128)(2,1)} %reshape.303), channel_id=1, source_target_pairs={{0,0},{8,1},{16,2},{24,3},{1,4},{9,5},{17,6},{25,7},{2,8},{10,9},{... | collective-permute-start | bytes 786440 | tf_op jit(solution)/shard_map/ppermute | solution.py:856
  781.4 2.5 convert_element_type.527
  (449 shorter events, 159.2 us)
Async XLA Ops:
  11.7 21.0 %all-to-all-start = ((bf16[8,72,512]{2,1,0:T(8,128)(2,1)}), bf16[8,72,512]{2,1,0:T(8,128)(2,1)S(1)}, u32[]{:S(2)}, u32[]{:S(2)}) async-start(bf16[8,72,512]{2,1,0:T(8,128)(2,1)} %copy.135), calls=%async_computation | async-start | bytes 1179648 | tf_op jit(solution)/shard_map/all_to_all | solution.py:60
  15.9 108.3 %all-gather.5.cloned.1.call-start = ((), (), s32[]{:S(2)}) async-start(), calls=%async_computation.8 | async-start | bytes 4259840 | tf_op jit(solution)/shard_map/all_gather | solution.py:66
  33.8 37.0 %collective-permute-start.3 = (bf16[384,2048]{1,0:T(8,128)(2,1)}, bf16[384,2048]{1,0:T(8,128)(2,1)S(1)}, u32[]{:S(2)}, u32[]{:S(2)}) collective-permute-start(bf16[384,2048]{1,0:T(8,128)(2,1)} %refs_1_.1), channel_id=1, source_target_pairs={{0,4},{1,5},{2,6},{3,7},{4,0},{5,1},{6,2},{7,3},{8,12},{9,13},{10,... | collective-permute-start | bytes 4718600 | tf_op jit(solution)/shard_map/ppermute | solution.py:49
  33.9 38.0 %collective-permute-start.1 = (bf16[384,2048]{1,0:T(8,128)(2,1)}, bf16[384,2048]{1,0:T(8,128)(2,1)S(1)}, u32[]{:S(2)}, u32[]{:S(2)}) collective-permute-start(bf16[384,2048]{1,0:T(8,128)(2,1)} %refs_1_.1), channel_id=1, source_target_pairs={{0,2},{1,3},{2,0},{3,1},{4,6},{5,7},{6,4},{7,5},{8,10},{9,11},{10,... | collective-permute-start | bytes 4718600 | tf_op jit(solution)/shard_map/ppermute | solution.py:49
  71.9 19.6 %collective-permute-start.5 = (bf16[192,2048]{1,0:T(8,128)(2,1)}, bf16[192,2048]{1,0:T(8,128)(2,1)}, u32[]{:S(2)}, u32[]{:S(2)}) collective-permute-start(bf16[192,2048]{1,0:T(8,128)(2,1)} %slice.263), channel_id=1, source_target_pairs={{0,2},{1,3},{2,0},{3,1},{4,6},{5,7},{6,4},{7,5},{8,10},{9,11},{10,... | collective-permute-start | bytes 2359304 | tf_op jit(solution)/shard_map/ppermute | solution.py:49
  73.3 20.2 %collective-permute-start.6 = (bf16[192,2048]{1,0:T(8,128)(2,1)}, bf16[192,2048]{1,0:T(8,128)(2,1)}, u32[]{:S(2)}, u32[]{:S(2)}) collective-permute-start(bf16[192,2048]{1,0:T(8,128)(2,1)} %slice.264), channel_id=1, source_target_pairs={{0,4},{1,5},{2,6},{3,7},{4,0},{5,1},{6,2},{7,3},{8,12},{9,13},{10,... | collective-permute-start | bytes 2359304 | tf_op jit(solution)/shard_map/ppermute | solution.py:49
  95.6 24.1 %all-to-all-start.1 = ((bf16[8,64,1536]{2,1,0:T(8,128)(2,1)}), bf16[8,64,1536]{2,1,0:T(8,128)(2,1)S(1)}, u32[]{:S(2)}, u32[]{:S(2)}) async-start(bf16[8,64,1536]{2,1,0:T(8,128)(2,1)} %shard_map.242), calls=%async_computation.1 | async-start | bytes 3145728 | tf_op jit(solution)/shard_map/all_to_all | solution.py:60
  100.2 114.4 %all-gather.7.cloned.1.call-start = ((), (), s32[]{:S(2)}) async-start(), calls=%async_computation.9 | async-start | bytes 3932160 | tf_op jit(solution)/shard_map/all_gather | solution.py:66
  100.2 32.4 %collective-permute-start = (bf16[384,2048]{1,0:T(8,128)(2,1)}, bf16[384,2048]{1,0:T(8,128)(2,1)}, u32[]{:S(2)}, u32[]{:S(2)}) collective-permute-start(bf16[384,2048]{1,0:T(8,128)(2,1)} %refs_1_.1), channel_id=1, source_target_pairs={{0,1},{1,0},{2,3},{3,2},{4,5},{5,4},{6,7},{7,6},{8,9},{9,8},{10,11... | collective-permute-start | bytes 4718600 | tf_op jit(solution)/shard_map/ppermute | solution.py:49
  101.3 32.8 %collective-permute-start.2 = (bf16[384,2048]{1,0:T(8,128)(2,1)}, bf16[384,2048]{1,0:T(8,128)(2,1)}, u32[]{:S(2)}, u32[]{:S(2)}) collective-permute-start(bf16[384,2048]{1,0:T(8,128)(2,1)} %copy-done.50), channel_id=1, source_target_pairs={{0,1},{1,0},{2,3},{3,2},{4,5},{5,4},{6,7},{7,6},{8,9},{9,8},{10,11... | collective-permute-start | bytes 4718600 | tf_op jit(solution)/shard_map/ppermute | solution.py:49
  101.7 32.4 %collective-permute-start.4 = (bf16[384,2048]{1,0:T(8,128)(2,1)}, bf16[384,2048]{1,0:T(8,128)(2,1)}, u32[]{:S(2)}, u32[]{:S(2)}) collective-permute-start(bf16[384,2048]{1,0:T(8,128)(2,1)} %copy-done.49), channel_id=1, source_target_pairs={{0,1},{1,0},{2,3},{3,2},{4,5},{5,4},{6,7},{7,6},{8,9},{9,8},{10,11... | collective-permute-start | bytes 4718600 | tf_op jit(solution)/shard_map/ppermute | solution.py:49
  101.9 32.3 %collective-permute-start.7 = (bf16[384,2048]{1,0:T(8,128)(2,1)}, bf16[384,2048]{1,0:T(8,128)(2,1)}, u32[]{:S(2)}, u32[]{:S(2)}) collective-permute-start(bf16[384,2048]{1,0:T(8,128)(2,1)} %constant_dynamic-update-slice_fusion.refs_0_.refs_7_.refs_1_), channel_id=1, source_target_pairs={{0,1},{1,0},{2,3},{3,2},{4,5},{5,4},{6,7},{7,6},{8,9},{9,8},{10,11... | collective-permute-start | bytes 4718600 | tf_op jit(solution)/shard_map/ppermute | solution.py:49
  121.0 152.7 %all-gather.9.cloned.1.call-start = ((), (), s32[]{:S(2)}) async-start(), calls=%async_computation.10 | async-start | bytes 3932160 | tf_op jit(solution)/shard_map/all_gather | solution.py:66
  123.6 42.1 %collective-permute-start.11 = (bf16[384,2048]{1,0:T(8,128)(2,1)}, bf16[384,2048]{1,0:T(8,128)(2,1)S(1)}, u32[]{:S(2)}, u32[]{:S(2)}) collective-permute-start(bf16[384,2048]{1,0:T(8,128)(2,1)} %broadcast_select_fusion.refs_0_.refs_9_), channel_id=1, source_target_pairs={{0,4},{1,5},{2,6},{3,7},{4,0},{5,1},{6,2},{7,3},{8,12},{9,13},{10,... | collective-permute-start | bytes 4718600 | tf_op jit(solution)/shard_map/ppermute | solution.py:49
  132.6 36.1 %collective-permute-start.10 = (bf16[384,2048]{1,0:T(8,128)(2,1)}, bf16[384,2048]{1,0:T(8,128)(2,1)}, u32[]{:S(2)}, u32[]{:S(2)}) collective-permute-start(bf16[384,2048]{1,0:T(8,128)(2,1)} %broadcast_select_fusion.refs_0_.refs_9_), channel_id=1, source_target_pairs={{0,2},{1,3},{2,0},{3,1},{4,6},{5,7},{6,4},{7,5},{8,10},{9,11},{10,... | collective-permute-start | bytes 4718600 | tf_op jit(solution)/shard_map/ppermute | solution.py:49
  134.1 34.5 %collective-permute-start.9 = (bf16[384,2048]{1,0:T(8,128)(2,1)}, bf16[384,2048]{1,0:T(8,128)(2,1)}, u32[]{:S(2)}, u32[]{:S(2)}) collective-permute-start(bf16[384,2048]{1,0:T(8,128)(2,1)} %broadcast_select_fusion.refs_0_.refs_9_), channel_id=1, source_target_pairs={{0,1},{1,0},{2,3},{3,2},{4,5},{5,4},{6,7},{7,6},{8,9},{9,8},{10,11... | collective-permute-start | bytes 4718600 | tf_op jit(solution)/shard_map/ppermute | solution.py:49
  169.3 163.4 %all-gather.11.cloned.1.call-start = ((), (), s32[]{:S(2)}) async-start(), calls=%async_computation.11 | async-start | bytes 3932160 | tf_op jit(solution)/shard_map/all_gather | solution.py:66
  174.7 19.6 %collective-permute-start.16 = (bf16[192,2048]{1,0:T(8,128)(2,1)S(1)}, bf16[192,2048]{1,0:T(8,128)(2,1)S(1)}, u32[]{:S(2)}, u32[]{:S(2)}) collective-permute-start(bf16[192,2048]{1,0:T(8,128)(2,1)S(1)} %get-tuple-element.187), channel_id=1, source_target_pairs={{0,4},{1,5},{2,6},{3,7},{4,0},{5,1},{6,2},{7,3},{8,12},{9,13},{10,... | collective-permute-start | bytes 2359304 | tf_op jit(solution)/shard_map/ppermute | solution.py:49
  177.2 45.2 %collective-permute-start.14 = (bf16[192,2048]{1,0:T(8,128)(2,1)S(1)}, bf16[192,2048]{1,0:T(8,128)(2,1)}, u32[]{:S(2)}, u32[]{:S(2)}) collective-permute-start(bf16[192,2048]{1,0:T(8,128)(2,1)S(1)} %slice.272), channel_id=1, source_target_pairs={{0,2},{1,3},{2,0},{3,1},{4,6},{5,7},{6,4},{7,5},{8,10},{9,11},{10,... | collective-permute-start | bytes 2359304 | tf_op jit(solution)/shard_map/ppermute | solution.py:49
  177.5 35.9 %collective-permute-start.18 = (bf16[192,2048]{1,0:T(8,128)(2,1)S(1)}, bf16[192,2048]{1,0:T(8,128)(2,1)S(1)}, u32[]{:S(2)}, u32[]{:S(2)}) collective-permute-start(bf16[192,2048]{1,0:T(8,128)(2,1)S(1)} %get-tuple-element.186), channel_id=1, source_target_pairs={{0,2},{1,3},{2,0},{3,1},{4,6},{5,7},{6,4},{7,5},{8,10},{9,11},{10,... | collective-permute-start | bytes 2359304 | tf_op jit(solution)/shard_map/ppermute | solution.py:49
  214.6 20.8 %collective-permute-start.19 = (bf16[192,2048]{1,0:T(8,128)(2,1)}, bf16[192,2048]{1,0:T(8,128)(2,1)}, u32[]{:S(2)}, u32[]{:S(2)}) collective-permute-start(bf16[192,2048]{1,0:T(8,128)(2,1)} %get-tuple-element.107.refs_1_), channel_id=1, source_target_pairs={{0,4},{1,5},{2,6},{3,7},{4,0},{5,1},{6,2},{7,3},{8,12},{9,13},{10,... | collective-permute-start | bytes 2359304 | tf_op jit(solution)/shard_map/ppermute | solution.py:49
  216.0 37.5 %collective-permute-start.12 = (bf16[384,2048]{1,0:T(8,128)(2,1)S(1)}, bf16[384,2048]{1,0:T(8,128)(2,1)}, u32[]{:S(2)}, u32[]{:S(2)}) collective-permute-start(bf16[384,2048]{1,0:T(8,128)(2,1)S(1)} %copy-done.3), channel_id=1, source_target_pairs={{0,1},{1,0},{2,3},{3,2},{4,5},{5,4},{6,7},{7,6},{8,9},{9,8},{10,11... | collective-permute-start | bytes 4718600 | tf_op jit(solution)/shard_map/ppermute | solution.py:49
  218.1 32.2 %collective-permute-start.21 = (bf16[192,2048]{1,0:T(8,128)(2,1)}, bf16[192,2048]{1,0:T(8,128)(2,1)}, u32[]{:S(2)}, u32[]{:S(2)}) collective-permute-start(bf16[192,2048]{1,0:T(8,128)(2,1)} %slice.278), channel_id=1, source_target_pairs={{0,4},{1,5},{2,6},{3,7},{4,0},{5,1},{6,2},{7,3},{8,12},{9,13},{10,... | collective-permute-start | bytes 2359304 | tf_op jit(solution)/shard_map/ppermute | solution.py:49
  219.2 31.5 %collective-permute-start.20 = (bf16[192,2048]{1,0:T(8,128)(2,1)S(1)}, bf16[192,2048]{1,0:T(8,128)(2,1)}, u32[]{:S(2)}, u32[]{:S(2)}) collective-permute-start(bf16[192,2048]{1,0:T(8,128)(2,1)S(1)} %copy-done.20), channel_id=1, source_target_pairs={{0,2},{1,3},{2,0},{3,1},{4,6},{5,7},{6,4},{7,5},{8,10},{9,11},{10,... | collective-permute-start | bytes 2359304 | tf_op jit(solution)/shard_map/ppermute | solution.py:49
  219.5 276.7 %reduce-scatter.5.cloned.1.call-start = ((), (), s32[]{:S(2)}) async-start(), calls=%async_computation.12 | async-start | bytes 3932160 | tf_op jit(solution)/shard_map/reduce_scatter | solution.py:72
  222.3 51.4 %collective-permute-start.25 = (bf16[384,2048]{1,0:T(8,128)(2,1)}, bf16[384,2048]{1,0:T(8,128)(2,1)}, u32[]{:S(2)}, u32[]{:S(2)}) collective-permute-start(bf16[384,2048]{1,0:T(8,128)(2,1)} %get-tuple-element.109.refs_2_.refs_11_), channel_id=1, source_target_pairs={{0,1},{1,0},{2,3},{3,2},{4,5},{5,4},{6,7},{7,6},{8,9},{9,8},{10,11... | collective-permute-start | bytes 4718600 | tf_op jit(solution)/shard_map/ppermute | solution.py:49
  235.4 38.4 %collective-permute-start.26 = (bf16[384,2048]{1,0:T(8,128)(2,1)S(1)}, bf16[384,2048]{1,0:T(8,128)(2,1)}, u32[]{:S(2)}, u32[]{:S(2)}) collective-permute-start(bf16[384,2048]{1,0:T(8,128)(2,1)S(1)} %copy-done.15), channel_id=1, source_target_pairs={{0,1},{1,0},{2,3},{3,2},{4,5},{5,4},{6,7},{7,6},{8,9},{9,8},{10,11... | collective-permute-start | bytes 4718600 | tf_op jit(solution)/shard_map/ppermute | solution.py:49
  271.3 37.1 %collective-permute-start.24 = (bf16[384,2048]{1,0:T(8,128)(2,1)}, bf16[384,2048]{1,0:T(8,128)(2,1)}, u32[]{:S(2)}, u32[]{:S(2)}) collective-permute-start(bf16[384,2048]{1,0:T(8,128)(2,1)} %multiply_convert_fusion.refs_1_), channel_id=1, source_target_pairs={{0,4},{1,5},{2,6},{3,7},{4,0},{5,1},{6,2},{7,3},{8,12},{9,13},{10,... | collective-permute-start | bytes 4718600 | tf_op jit(solution)/shard_map/ppermute | solution.py:49
  273.0 36.8 %collective-permute-start.23 = (bf16[384,2048]{1,0:T(8,128)(2,1)}, bf16[384,2048]{1,0:T(8,128)(2,1)}, u32[]{:S(2)}, u32[]{:S(2)}) collective-permute-start(bf16[384,2048]{1,0:T(8,128)(2,1)} %multiply_convert_fusion.refs_1_), channel_id=1, source_target_pairs={{0,2},{1,3},{2,0},{3,1},{4,6},{5,7},{6,4},{7,5},{8,10},{9,11},{10,... | collective-permute-start | bytes 4718600 | tf_op jit(solution)/shard_map/ppermute | solution.py:49
  311.0 18.9 %collective-permute-start.32 = (bf16[192,2048]{1,0:T(8,128)(2,1)S(1)}, bf16[192,2048]{1,0:T(8,128)(2,1)S(1)}, u32[]{:S(2)}, u32[]{:S(2)}) collective-permute-start(bf16[192,2048]{1,0:T(8,128)(2,1)S(1)} %slice.221), channel_id=1, source_target_pairs={{0,2},{1,3},{2,0},{3,1},{4,6},{5,7},{6,4},{7,5},{8,10},{9,11},{10,... | collective-permute-start | bytes 2359304 | tf_op jit(solution)/shard_map/ppermute | solution.py:49
  313.1 18.6 %collective-permute-start.33 = (bf16[192,2048]{1,0:T(8,128)(2,1)S(1)}, bf16[192,2048]{1,0:T(8,128)(2,1)S(1)}, u32[]{:S(2)}, u32[]{:S(2)}) collective-permute-start(bf16[192,2048]{1,0:T(8,128)(2,1)S(1)} %slice.222), channel_id=1, source_target_pairs={{0,4},{1,5},{2,6},{3,7},{4,0},{5,1},{6,2},{7,3},{8,12},{9,13},{10,... | collective-permute-start | bytes 2359304 | tf_op jit(solution)/shard_map/ppermute | solution.py:49
  313.5 19.2 %collective-permute-start.22 = (bf16[384,2048]{1,0:T(8,128)(2,1)}, bf16[384,2048]{1,0:T(8,128)(2,1)}, u32[]{:S(2)}, u32[]{:S(2)}) collective-permute-start(bf16[384,2048]{1,0:T(8,128)(2,1)} %multiply_convert_fusion.refs_1_), channel_id=1, source_target_pairs={{0,1},{1,0},{2,3},{3,2},{4,5},{5,4},{6,7},{7,6},{8,9},{9,8},{10,11... | collective-permute-start | bytes 4718600 | tf_op jit(solution)/shard_map/ppermute | solution.py:49
  313.5 19.2 %collective-permute-start.30 = (bf16[384,2048]{1,0:T(8,128)(2,1)}, bf16[384,2048]{1,0:T(8,128)(2,1)}, u32[]{:S(2)}, u32[]{:S(2)}) collective-permute-start(bf16[384,2048]{1,0:T(8,128)(2,1)} %get-tuple-element.111.refs_3_), channel_id=1, source_target_pairs={{0,1},{1,0},{2,3},{3,2},{4,5},{5,4},{6,7},{7,6},{8,9},{9,8},{10,11... | collective-permute-start | bytes 4718600 | tf_op jit(solution)/shard_map/ppermute | solution.py:49
  314.0 18.7 %collective-permute-start.31 = (bf16[384,2048]{1,0:T(8,128)(2,1)}, bf16[384,2048]{1,0:T(8,128)(2,1)}, u32[]{:S(2)}, u32[]{:S(2)}) collective-permute-start(bf16[384,2048]{1,0:T(8,128)(2,1)} %get-tuple-element.112.refs_5_), channel_id=1, source_target_pairs={{0,1},{1,0},{2,3},{3,2},{4,5},{5,4},{6,7},{7,6},{8,9},{9,8},{10,11... | collective-permute-start | bytes 4718600 | tf_op jit(solution)/shard_map/ppermute | solution.py:49
  400.3 23.5 %collective-permute-start.37 = (bf16[384,2048]{1,0:T(8,128)(2,1)}, bf16[384,2048]{1,0:T(8,128)(2,1)}, u32[]{:S(2)}, u32[]{:S(2)}) collective-permute-start(bf16[384,2048]{1,0:T(8,128)(2,1)} %get-tuple-element.118), channel_id=1, source_target_pairs={{0,1},{1,0},{2,3},{3,2},{4,5},{5,4},{6,7},{7,6},{8,9},{9,8},{10,11... | collective-permute-start | bytes 4718600 | tf_op jit(solution)/shard_map/ppermute | solution.py:49
  400.8 26.5 %collective-permute-start.38 = (bf16[384,2048]{1,0:T(8,128)(2,1)}, bf16[384,2048]{1,0:T(8,128)(2,1)}, u32[]{:S(2)}, u32[]{:S(2)}) collective-permute-start(bf16[384,2048]{1,0:T(8,128)(2,1)} %get-tuple-element.120), channel_id=1, source_target_pairs={{0,1},{1,0},{2,3},{3,2},{4,5},{5,4},{6,7},{7,6},{8,9},{9,8},{10,11... | collective-permute-start | bytes 4718600 | tf_op jit(solution)/shard_map/ppermute | solution.py:49
  400.8 92.2 %collective-permute-start.39 = (bf16[384,2048]{1,0:T(8,128)(2,1)}, bf16[384,2048]{1,0:T(8,128)(2,1)}, u32[]{:S(2)}, u32[]{:S(2)}) collective-permute-start(bf16[384,2048]{1,0:T(8,128)(2,1)} %get-tuple-element.122), channel_id=1, source_target_pairs={{0,1},{1,0},{2,3},{3,2},{4,5},{5,4},{6,7},{7,6},{8,9},{9,8},{10,11... | collective-permute-start | bytes 4718600 | tf_op jit(solution)/shard_map/ppermute | solution.py:49
  401.3 20.3 %collective-permute-start.43 = (bf16[384,2048]{1,0:T(8,128)(2,1)}, bf16[384,2048]{1,0:T(8,128)(2,1)}, u32[]{:S(2)}, u32[]{:S(2)}) collective-permute-start(bf16[384,2048]{1,0:T(8,128)(2,1)} %get-tuple-element.128), channel_id=1, source_target_pairs={{0,1},{1,0},{2,3},{3,2},{4,5},{5,4},{6,7},{7,6},{8,9},{9,8},{10,11... | collective-permute-start | bytes 4718600 | tf_op jit(solution)/shard_map/ppermute | solution.py:49
  417.0 154.1 %reduce-scatter.7.cloned.1.call-start = ((), (), s32[]{:S(2)}) async-start(), calls=%async_computation.13 | async-start | bytes 3932160 | tf_op jit(solution)/shard_map/reduce_scatter | solution.py:72
  423.8 20.4 %collective-permute-start.44 = (bf16[192,2048]{1,0:T(8,128)(2,1)S(1)}, bf16[192,2048]{1,0:T(8,128)(2,1)S(1)}, u32[]{:S(2)}, u32[]{:S(2)}) collective-permute-start(bf16[192,2048]{1,0:T(8,128)(2,1)S(1)} %get-tuple-element.182), channel_id=1, source_target_pairs={{0,2},{1,3},{2,0},{3,1},{4,6},{5,7},{6,4},{7,5},{8,10},{9,11},{10,... | collective-permute-start | bytes 2359304 | tf_op jit(solution)/shard_map/ppermute | solution.py:49
  432.7 28.5 %collective-permute-start.41 = (bf16[192,2048]{1,0:T(8,128)(2,1)S(1)}, bf16[192,2048]{1,0:T(8,128)(2,1)}, u32[]{:S(2)}, u32[]{:S(2)}) collective-permute-start(bf16[192,2048]{1,0:T(8,128)(2,1)S(1)} %slice.283), channel_id=1, source_target_pairs={{0,2},{1,3},{2,0},{3,1},{4,6},{5,7},{6,4},{7,5},{8,10},{9,11},{10,... | collective-permute-start | bytes 2359304 | tf_op jit(solution)/shard_map/ppermute | solution.py:49
  434.1 20.4 %collective-permute-start.46 = (bf16[192,2048]{1,0:T(8,128)(2,1)S(1)}, bf16[192,2048]{1,0:T(8,128)(2,1)S(1)}, u32[]{:S(2)}, u32[]{:S(2)}) collective-permute-start(bf16[192,2048]{1,0:T(8,128)(2,1)S(1)} %get-tuple-element.183), channel_id=1, source_target_pairs={{0,4},{1,5},{2,6},{3,7},{4,0},{5,1},{6,2},{7,3},{8,12},{9,13},{10,... | collective-permute-start | bytes 2359304 | tf_op jit(solution)/shard_map/ppermute | solution.py:49
  435.2 36.2 %collective-permute-start.48 = (bf16[192,2048]{1,0:T(8,128)(2,1)S(1)}, bf16[192,2048]{1,0:T(8,128)(2,1)}, u32[]{:S(2)}, u32[]{:S(2)}) collective-permute-start(bf16[192,2048]{1,0:T(8,128)(2,1)S(1)} %slice.288), channel_id=1, source_target_pairs={{0,4},{1,5},{2,6},{3,7},{4,0},{5,1},{6,2},{7,3},{8,12},{9,13},{10,... | collective-permute-start | bytes 2359304 | tf_op jit(solution)/shard_map/ppermute | solution.py:49
  445.4 43.9 %collective-permute-start.45 = (bf16[192,2048]{1,0:T(8,128)(2,1)}, bf16[192,2048]{1,0:T(8,128)(2,1)}, u32[]{:S(2)}, u32[]{:S(2)}) collective-permute-start(bf16[192,2048]{1,0:T(8,128)(2,1)} %add_convert_fusion.21), channel_id=1, source_target_pairs={{0,4},{1,5},{2,6},{3,7},{4,0},{5,1},{6,2},{7,3},{8,12},{9,13},{10,... | collective-permute-start | bytes 2359304 | tf_op jit(solution)/shard_map/ppermute | solution.py:49
  455.6 35.3 %collective-permute-start.47 = (bf16[192,2048]{1,0:T(8,128)(2,1)}, bf16[192,2048]{1,0:T(8,128)(2,1)}, u32[]{:S(2)}, u32[]{:S(2)}) collective-permute-start(bf16[192,2048]{1,0:T(8,128)(2,1)} %add_convert_fusion.20), channel_id=1, source_target_pairs={{0,2},{1,3},{2,0},{3,1},{4,6},{5,7},{6,4},{7,5},{8,10},{9,11},{10,... | collective-permute-start | bytes 2359304 | tf_op jit(solution)/shard_map/ppermute | solution.py:49
  496.3 161.1 %reduce-scatter.9.cloned.1.call-start = ((), (), s32[]{:S(2)}) async-start(), calls=%async_computation.14 | async-start | bytes 3932160 | tf_op jit(solution)/shard_map/reduce_scatter | solution.py:72
  503.4 35.3 %collective-permute-start.51 = (bf16[384,2048]{1,0:T(8,128)(2,1)}, bf16[384,2048]{1,0:T(8,128)(2,1)}, u32[]{:S(2)}, u32[]{:S(2)}) collective-permute-start(bf16[384,2048]{1,0:T(8,128)(2,1)} %get-tuple-element.172.refs_0_.refs_1_), channel_id=1, source_target_pairs={{0,4},{1,5},{2,6},{3,7},{4,0},{5,1},{6,2},{7,3},{8,12},{9,13},{10,... | collective-permute-start | bytes 4718600 | tf_op jit(solution)/shard_map/ppermute | solution.py:49
  503.8 34.9 %collective-permute-start.50 = (bf16[384,2048]{1,0:T(8,128)(2,1)}, bf16[384,2048]{1,0:T(8,128)(2,1)}, u32[]{:S(2)}, u32[]{:S(2)}) collective-permute-start(bf16[384,2048]{1,0:T(8,128)(2,1)} %get-tuple-element.172.refs_0_.refs_1_), channel_id=1, source_target_pairs={{0,2},{1,3},{2,0},{3,1},{4,6},{5,7},{6,4},{7,5},{8,10},{9,11},{10,... | collective-permute-start | bytes 4718600 | tf_op jit(solution)/shard_map/ppermute | solution.py:49
  563.8 57.5 %collective-permute-start.57 = (bf16[192,2048]{1,0:T(8,128)(2,1)}, bf16[192,2048]{1,0:T(8,128)(2,1)}, u32[]{:S(2)}, u32[]{:S(2)}) collective-permute-start(bf16[192,2048]{1,0:T(8,128)(2,1)} %get-tuple-element.133.refs_1_), channel_id=1, source_target_pairs={{0,2},{1,3},{2,0},{3,1},{4,6},{5,7},{6,4},{7,5},{8,10},{9,11},{10,... | collective-permute-start | bytes 2359304 | tf_op jit(solution)/shard_map/ppermute | solution.py:49
  565.5 55.8 %collective-permute-start.62 = (bf16[192,2048]{1,0:T(8,128)(2,1)}, bf16[192,2048]{1,0:T(8,128)(2,1)}, u32[]{:S(2)}, u32[]{:S(2)}) collective-permute-start(bf16[192,2048]{1,0:T(8,128)(2,1)} %get-tuple-element.135.refs_2_), channel_id=1, source_target_pairs={{0,4},{1,5},{2,6},{3,7},{4,0},{5,1},{6,2},{7,3},{8,12},{9,13},{10,... | collective-permute-start | bytes 2359304 | tf_op jit(solution)/shard_map/ppermute | solution.py:49
  569.7 51.6 %collective-permute-start.58 = (bf16[192,2048]{1,0:T(8,128)(2,1)}, bf16[192,2048]{1,0:T(8,128)(2,1)}, u32[]{:S(2)}, u32[]{:S(2)}) collective-permute-start(bf16[192,2048]{1,0:T(8,128)(2,1)} %get-tuple-element.180), channel_id=1, source_target_pairs={{0,2},{1,3},{2,0},{3,1},{4,6},{5,7},{6,4},{7,5},{8,10},{9,11},{10,... | collective-permute-start | bytes 2359304 | tf_op jit(solution)/shard_map/ppermute | solution.py:49
  569.9 51.4 %collective-permute-start.60 = (bf16[192,2048]{1,0:T(8,128)(2,1)}, bf16[192,2048]{1,0:T(8,128)(2,1)}, u32[]{:S(2)}, u32[]{:S(2)}) collective-permute-start(bf16[192,2048]{1,0:T(8,128)(2,1)} %get-tuple-element.181), channel_id=1, source_target_pairs={{0,4},{1,5},{2,6},{3,7},{4,0},{5,1},{6,2},{7,3},{8,12},{9,13},{10,... | collective-permute-start | bytes 2359304 | tf_op jit(solution)/shard_map/ppermute | solution.py:49
  571.1 168.8 %reduce-scatter.11.cloned.1.call-start = ((), (), s32[]{:S(2)}) async-start(), calls=%async_computation.15 | async-start | bytes 4259840 | tf_op jit(solution)/shard_map/reduce_scatter | solution.py:72
  636.4 19.6 %collective-permute-start.69 = (bf16[192,2048]{1,0:T(8,128)(2,1)S(1)}, bf16[192,2048]{1,0:T(8,128)(2,1)}, u32[]{:S(2)}, u32[]{:S(2)}) collective-permute-start(bf16[192,2048]{1,0:T(8,128)(2,1)S(1)} %get-tuple-element.178), channel_id=1, source_target_pairs={{0,2},{1,3},{2,0},{3,1},{4,6},{5,7},{6,4},{7,5},{8,10},{9,11},{10,... | collective-permute-start | bytes 2359304 | tf_op jit(solution)/shard_map/ppermute | solution.py:49
  638.1 19.3 %collective-permute-start.67 = (bf16[192,2048]{1,0:T(8,128)(2,1)S(1)}, bf16[192,2048]{1,0:T(8,128)(2,1)}, u32[]{:S(2)}, u32[]{:S(2)}) collective-permute-start(bf16[192,2048]{1,0:T(8,128)(2,1)S(1)} %get-tuple-element.179), channel_id=1, source_target_pairs={{0,4},{1,5},{2,6},{3,7},{4,0},{5,1},{6,2},{7,3},{8,12},{9,13},{10,... | collective-permute-start | bytes 2359304 | tf_op jit(solution)/shard_map/ppermute | solution.py:49
  664.8 26.7 %collective-permute-start.35 = (bf16[384,2048]{1,0:T(8,128)(2,1)}, bf16[384,2048]{1,0:T(8,128)(2,1)}, u32[]{:S(2)}, u32[]{:S(2)}) collective-permute-start(bf16[384,2048]{1,0:T(8,128)(2,1)} %get-tuple-element.114), channel_id=1, source_target_pairs={{0,1},{1,0},{2,3},{3,2},{4,5},{5,4},{6,7},{7,6},{8,9},{9,8},{10,11... | collective-permute-start | bytes 4718600 | tf_op jit(solution)/shard_map/ppermute | solution.py:49
  685.5 51.3 %collective-permute-start.63 = (bf16[384,2048]{1,0:T(8,128)(2,1)}, bf16[384,2048]{1,0:T(8,128)(2,1)}, u32[]{:S(2)}, u32[]{:S(2)}) collective-permute-start(bf16[384,2048]{1,0:T(8,128)(2,1)} %get-tuple-element.151), channel_id=1, source_target_pairs={{0,1},{1,0},{2,3},{3,2},{4,5},{5,4},{6,7},{7,6},{8,9},{9,8},{10,11... | collective-permute-start | bytes 4718600 | tf_op jit(solution)/shard_map/ppermute | solution.py:49
  685.5 20.9 %collective-permute-start.65 = (bf16[192,2048]{1,0:T(8,128)(2,1)}, bf16[192,2048]{1,0:T(8,128)(2,1)}, u32[]{:S(2)}, u32[]{:S(2)}) collective-permute-start(bf16[192,2048]{1,0:T(8,128)(2,1)} %slice.293.refs_4_), channel_id=1, source_target_pairs={{0,2},{1,3},{2,0},{3,1},{4,6},{5,7},{6,4},{7,5},{8,10},{9,11},{10,... | collective-permute-start | bytes 2359304 | tf_op jit(solution)/shard_map/ppermute | solution.py:49
  690.7 20.7 %collective-permute-start.70 = (bf16[192,2048]{1,0:T(8,128)(2,1)}, bf16[192,2048]{1,0:T(8,128)(2,1)}, u32[]{:S(2)}, u32[]{:S(2)}) collective-permute-start(bf16[192,2048]{1,0:T(8,128)(2,1)} %get-tuple-element.163), channel_id=1, source_target_pairs={{0,4},{1,5},{2,6},{3,7},{4,0},{5,1},{6,2},{7,3},{8,12},{9,13},{10,... | collective-permute-start | bytes 2359304 | tf_op jit(solution)/shard_map/ppermute | solution.py:49
  696.6 39.9 %collective-permute-start.72 = (bf16[192,2048]{1,0:T(8,128)(2,1)}, bf16[192,2048]{1,0:T(8,128)(2,1)S(1)}, u32[]{:S(2)}, u32[]{:S(2)}) collective-permute-start(bf16[192,2048]{1,0:T(8,128)(2,1)} %slice.299.refs_5_), channel_id=1, source_target_pairs={{0,4},{1,5},{2,6},{3,7},{4,0},{5,1},{6,2},{7,3},{8,12},{9,13},{10,... | collective-permute-start | bytes 2359304 | tf_op jit(solution)/shard_map/ppermute | solution.py:49
  697.8 38.7 %collective-permute-start.71 = (bf16[192,2048]{1,0:T(8,128)(2,1)}, bf16[192,2048]{1,0:T(8,128)(2,1)S(1)}, u32[]{:S(2)}, u32[]{:S(2)}) collective-permute-start(bf16[192,2048]{1,0:T(8,128)(2,1)} %get-tuple-element.164), channel_id=1, source_target_pairs={{0,2},{1,3},{2,0},{3,1},{4,6},{5,7},{6,4},{7,5},{8,10},{9,11},{10,... | collective-permute-start | bytes 2359304 | tf_op jit(solution)/shard_map/ppermute | solution.py:49
  701.7 42.7 %all-to-all-start.3 = ((bf16[8,64,1536]{2,1,0:T(8,128)(2,1)}), bf16[8,64,1536]{2,1,0:T(8,128)(2,1)}, u32[]{:S(2)}, u32[]{:S(2)}) async-start(bf16[8,64,1536]{2,1,0:T(8,128)(2,1)} %bitcast.27), calls=%async_computation.7 | async-start | bytes 3145728 | tf_op jit(solution)/shard_map/all_to_all | solution.py:60
  744.4 41.6 %all-to-all-start.2 = ((bf16[8,72,512]{2,1,0:T(8,128)(2,1)}), bf16[8,72,512]{2,1,0:T(8,128)(2,1)}, u32[]{:S(2)}, u32[]{:S(2)}) async-start(bf16[8,72,512]{2,1,0:T(8,128)(2,1)} %bitcast.92), calls=%async_computation.6 | async-start | bytes 1179648 | tf_op jit(solution)/shard_map/all_to_all | solution.py:60
  755.2 30.0 %collective-permute-start.73 = (bf16[64,2048]{1,0:T(8,128)(2,1)}, bf16[64,2048]{1,0:T(8,128)(2,1)S(1)}, u32[]{:S(2)}, u32[]{:S(2)}) collective-permute-start(bf16[64,2048]{1,0:T(8,128)(2,1)} %reshape.303), channel_id=1, source_target_pairs={{0,0},{8,1},{16,2},{24,3},{1,4},{9,5},{17,6},{25,7},{2,8},{10,9},{... | collective-permute-start | bytes 786440 | tf_op jit(solution)/shard_map/ppermute | solution.py:856
  (87 other events, 840.3 us)
Sparse Core Ops, SparseCore 0:
  33.9 65.5 all-gather.4
  121.2 61.2 all-gather.6
  184.0 62.1 all-gather.8
  247.6 62.1 all-gather.10
  417.1 65.7 reduce-scatter.4
  496.4 65.6 reduce-scatter.6
  571.2 66.1 reduce-scatter.8
  658.1 76.7 reduce-scatter.10

commit v5 on v4

--- a/solution.py
+++ b/solution.py
@@ -217,22 +217,46 @@
         pl.when(r == k)(lambda k=k: body(k))
 
 
+def load_weights(gathered, weight_head, wa_v, wo_v, wh_v, sems):
+    groups, _, cols = gathered.shape
+    width = wo_v.shape[1]
+    rho = width // (groups * TEAM)
+    copies = [pltpu.make_async_copy(weight_head, wh_v, sems.at[0])]
+    for g in range(groups):
+        copies.append(
+            pltpu.make_async_copy(
+                gathered.at[g, pl.ds(0, TEAM * rho)],
+                wa_v.at[pl.ds(g * TEAM * rho, TEAM * rho)],
+                sems.at[len(copies)],
+            )
+        )
+        for k in range(width // cols):
+            copies.append(
+                pltpu.make_async_copy(
+                    gathered.at[g, pl.ds(TEAM * rho + k * rho, rho)],
+                    wo_v.at[pl.ds(g * rho, rho), pl.ds(k * cols, cols)],
+                    sems.at[len(copies)],
+                )
+            )
+    return copies
+
+
 def attend(tiles, tokens, consts, mine, after):
-    weight_attn, weight_head, weight_out, gain, gains, cosine, sine = consts
+    gathered, weight_head, gain, gains, cosine, sine = consts
     rows, width = tokens[0].shape
     size = gains.shape[1]
     q_cols = mine * size
-    cols = weight_attn.shape[1]
+    cols = gathered.shape[2]
     factor = size ** (-0.5)
 
     def kernel(*refs):
         tiles_ref, toks = refs[0], refs[1 : 1 + TEAM]
-        wa, wh, wo, gain_ref, gains_ref, cos_ref, sin_ref, _ = refs[1 + TEAM : 9 + TEAM]
-        parts = refs[9 + TEAM : 9 + 2 * TEAM]
-        normed_all, qkv_all, logit_all, gated_all, tick = refs[9 + 2 * TEAM : 14 + 2 * TEAM]
+        wa, wh, gain_ref, gains_ref, cos_ref, sin_ref, _ = refs[1 + TEAM : 8 + TEAM]
+        parts = refs[8 + TEAM : 8 + 2 * TEAM]
+        normed_all, qkv_all, logit_all, gated_all, tick = refs[8 + 2 * TEAM : 13 + 2 * TEAM]
         (
             tok_v, wa_v, wh_v, wo_v, part_v, normed_v, qkv_v, logit_v, gated_v, w_sem, in_sem, out_sem,
-        ) = refs[14 + 2 * TEAM :]
+        ) = refs[13 + 2 * TEAM :]
         tick[...] = jnp.zeros_like(tick)
 
         def load(k, slot):
@@ -244,10 +268,7 @@
             return pltpu.make_async_copy(src, dst, out_sem.at[j, slot])
 
         load(0, 0).start()
-        weights = [
-            pltpu.make_async_copy(src, dst, w_sem.at[j])
-            for j, (src, dst) in enumerate(((wa, wa_v), (wh, wh_v), (wo, wo_v)))
-        ]
+        weights = load_weights(wa, wh, wa_v, wo_v, wh_v, w_sem)
         for copy in weights:
             copy.start()
         for copy in weights:
@@ -314,46 +335,46 @@
             struct((whole, q_cols), BF16),
             struct((8, 128), jnp.int32),
         ],
-        in_specs=[SMEM] + [ANY] * (TEAM + 3) + [VMEM] * 4 + [ANY],
+        in_specs=[SMEM] + [ANY] * (TEAM + 2) + [VMEM] * 4 + [ANY],
         out_specs=[ANY] * (TEAM + 4) + [VMEM],
         scratch_shapes=[
             pltpu.VMEM((2, rows, width), BF16),
-            pltpu.VMEM(weight_attn.shape, BF16),
+            pltpu.VMEM((width, cols), BF16),
             pltpu.VMEM(weight_head.shape, BF16),
-            pltpu.VMEM(weight_out.shape, BF16),
+            pltpu.VMEM((q_cols, width), BF16),
             pltpu.VMEM((2, rows, width), BF16),
             pltpu.VMEM((2, rows, width), BF16),
             pltpu.VMEM((2, rows, cols), F32),
             pltpu.VMEM((2, rows, TILE), F32),
             pltpu.VMEM((2, rows, q_cols), BF16),
-            pltpu.SemaphoreType.DMA((3,)),
+            pltpu.SemaphoreType.DMA((1 + gathered.shape[0] * (1 + width // cols),)),
             pltpu.SemaphoreType.DMA((2,)),
             pltpu.SemaphoreType.DMA((5, 2)),
         ],
         compiler_params=pltpu.CompilerParams(vmem_limit_bytes=48 << 20),
         cost_estimate=pl.CostEstimate(flops=30 << 30, bytes_accessed=60 << 20, transcendentals=1 << 20),
-    )(tiles, *tokens, weight_attn, weight_head, weight_out, gain, gains, cosine, sine, after)
+    )(tiles, *tokens, gathered, weight_head, gain, gains, cosine, sine, after)
     return result[:TEAM], result[TEAM : TEAM + 4], result[TEAM + 4]
 
 
 def attend_back(tiles, hidden, consts, saved, mine, after):
-    weight_attn, weight_head, weight_out, gain, gains, cosine, sine = consts
+    gathered, weight_head, gain, gains, cosine, sine = consts
     rows, width = hidden[0].shape
     size = gains.shape[1]
     q_cols = mine * size
-    cols = weight_attn.shape[1]
+    cols = gathered.shape[2]
     factor = size ** (-0.5)
 
     def kernel(*refs):
         tiles_ref, hids = refs[0], refs[1 : 1 + TEAM]
-        wa, wh, wo, normed_all, qkv_all, logit_all, gated_all = refs[1 + TEAM : 8 + TEAM]
-        gains_ref, cos_ref, sin_ref, _ = refs[8 + TEAM : 12 + TEAM]
-        parts = refs[12 + TEAM : 12 + 2 * TEAM]
-        attn_part, head_sum, out_part, gain_sum, gains_sum = refs[12 + 2 * TEAM : 17 + 2 * TEAM]
+        wa, wh, normed_all, qkv_all, logit_all, gated_all = refs[1 + TEAM : 7 + TEAM]
+        gains_ref, cos_ref, sin_ref, _ = refs[7 + TEAM : 11 + TEAM]
+        parts = refs[11 + TEAM : 11 + 2 * TEAM]
+        packed, head_sum, gain_sum, gains_sum = refs[11 + 2 * TEAM : 15 + 2 * TEAM]
         (
             hid_v, wa_v, wh_v, wo_v, normed_v, qkv_v, logit_v, gated_v, part_v, back_v, attn_sum, out_sum,
             w_sem, in_sem, out_sem,
-        ) = refs[17 + 2 * TEAM :]
+        ) = refs[15 + 2 * TEAM :]
 
         def loads(r, slot, k):
             yield pltpu.make_async_copy(hids[k], hid_v.at[slot], in_sem.at[0, slot])
@@ -375,10 +396,7 @@
 
         for copy in loads(0, 0, 0):
             copy.start()
-        weights = [
-            pltpu.make_async_copy(src, dst, w_sem.at[j])
-            for j, (src, dst) in enumerate(((wo, wo_v), (wa, wa_v), (wh, wh_v)))
-        ]
+        weights = load_weights(wa, wh, wa_v, wo_v, wh_v, w_sem)
         for copy in weights:
             copy.start()
         for ref in (attn_sum, out_sum, gain_sum, gains_sum):
@@ -456,9 +474,18 @@
             return carry
 
         lax.fori_loop(0, TEAM, step, 0)
-        attn_part[...] = attn_sum[:cols].T.astype(BF16)
         head_sum[...] = attn_sum[cols : cols + 8]
-        out_part[...] = out_sum[...].astype(BF16)
+        turned_sum = attn_sum[:cols].T.astype(BF16)
+        groups, height, _ = packed.shape
+        rho = width // (groups * TEAM)
+        for g in range(groups):
+            packed[g, : TEAM * rho] = turned_sum[g * TEAM * rho : (g + 1) * TEAM * rho]
+            for k in range(width // cols):
+                top = TEAM * rho + k * rho
+                packed[g, top : top + rho] = out_sum[
+                    g * rho : (g + 1) * rho, k * cols : (k + 1) * cols
+                ].astype(BF16)
+            packed[g, height - 16 :] = jnp.zeros((16, cols), BF16)
         store(0).wait()
         store(1).wait()
 
@@ -466,19 +493,18 @@
         kernel,
         out_shape=[struct((rows, width), BF16)] * TEAM
         + [
-            struct((width, cols), BF16),
+            struct(gathered.shape, BF16),
             struct((8, width), F32),
-            struct((q_cols, width), BF16),
             struct((8, width), F32),
             struct((8, size), F32),
         ],
-        in_specs=[SMEM] + [ANY] * (TEAM + 7) + [VMEM] * 3 + [ANY],
-        out_specs=[ANY] * TEAM + [VMEM] * 5,
+        in_specs=[SMEM] + [ANY] * (TEAM + 6) + [VMEM] * 3 + [ANY],
+        out_specs=[ANY] * TEAM + [VMEM] * 4,
         scratch_shapes=[
             pltpu.VMEM((2, rows, width), BF16),
-            pltpu.VMEM(weight_attn.shape, BF16),
+            pltpu.VMEM((width, cols), BF16),
             pltpu.VMEM(weight_head.shape, BF16),
-            pltpu.VMEM(weight_out.shape, BF16),
+            pltpu.VMEM((q_cols, width), BF16),
             pltpu.VMEM((2, rows, width), BF16),
             pltpu.VMEM((2, rows, cols), F32),
             pltpu.VMEM((2, rows, TILE), F32),
@@ -487,14 +513,14 @@
             pltpu.VMEM((rows, cols + TILE), BF16),
             pltpu.VMEM((cols + TILE, width), F32),
             pltpu.VMEM((q_cols, width), F32),
-            pltpu.SemaphoreType.DMA((3,)),
+            pltpu.SemaphoreType.DMA((1 + gathered.shape[0] * (1 + width // cols),)),
             pltpu.SemaphoreType.DMA((5, 2)),
             pltpu.SemaphoreType.DMA((2,)),
         ],
         compiler_params=pltpu.CompilerParams(vmem_limit_bytes=56 << 20),
         cost_estimate=pl.CostEstimate(flops=45 << 30, bytes_accessed=70 << 20, transcendentals=1 << 20),
-    )(tiles, *hidden, weight_attn, weight_head, weight_out, *saved, gains, cosine, sine, after)
-    return result[:TEAM], *result[TEAM : TEAM + 3], result[TEAM + 3][0], result[TEAM + 4][:2]
+    )(tiles, *hidden, gathered, weight_head, *saved, gains, cosine, sine, after)
+    return result[:TEAM], *result[TEAM : TEAM + 2], result[TEAM + 2][0], result[TEAM + 3][:2]
 
 
 def tile_places(tiles_ref, rows):
@@ -750,13 +776,16 @@
     order = jnp.arange(TEAM, dtype=jnp.int32)
     tiles = jnp.sum(jnp.where((order[:, None] ^ t) == order[None, :], team_tiles[None, :], 0), axis=1)
     routed = lax.ppermute(output_weight, ALL, out_weight_routes(groups))
-    team_rows = TEAM * (rho + 8)
-    attn = jnp.concatenate([attn.reshape(team_rows, cols), routed.reshape(-1, cols)], axis=0)
-    attn = line_gather(attn).reshape(groups, -1, cols)
-    weight_out = attn[:, team_rows:].reshape(-1, width)
-    attn = attn[:, :team_rows].reshape(everyone, rho + 8, cols)
-    weight_attn = attn[:, :rho].reshape(width, cols)
-    rows_small = attn[:, rho]
+    team_rows = TEAM * rho
+    small_at = team_rows + (width // cols) * rho
+    stacked = jnp.concatenate(
+        [attn[:, :rho].reshape(team_rows, cols)]
+        + [routed[:, k : k + cols] for k in range(0, width, cols)]
+        + [attn[:, rho], jnp.zeros((16 - TEAM, cols), BF16)],
+        axis=0,
+    )
+    gathered = line_gather(stacked).reshape(groups, -1, cols)
+    rows_small = gathered[:, small_at : small_at + TEAM].reshape(everyone, cols)
     weight_head = jnp.pad(
         rows_small[:, :head_lanes].reshape(everyone, mine, rho).transpose(1, 0, 2).reshape(mine, width),
         ((0, TILE - mine), (0, 0)),
@@ -780,9 +809,9 @@
     angles = jnp.arange(rows, dtype=F32)[:, None] * frequency[None, :]
     cosine = jnp.concatenate([jnp.cos(angles), jnp.cos(angles)], axis=1)
     sine = jnp.concatenate([-jnp.sin(angles), jnp.sin(angles)], axis=1)
-    consts = (weight_attn, weight_head, weight_out, gain_one, gain_pair, cosine, sine)
+    consts = (gathered, weight_head, gain_one, gain_pair, cosine, sine)
     team_tokens = team_gather(tokens)
-    feed_shard = exchange(hold([feed_shard], team_tokens[6])[0]).reshape(TEAM * rho, -1)
+    feed_shard = exchange(feed_shard).reshape(TEAM * rho, -1)
     weight_gate = line_gather(feed_shard[:, :ff_cols])
     live = lax.broadcasted_iota(jnp.int32, (rows, 1), 0) < lengths[0]
     live_rows = live.astype(F32)
@@ -825,7 +854,7 @@
     two_scale = lax.rsqrt(jnp.mean(hidden_state * hidden_state, axis=-1, keepdims=True) + EPSILON)
     two_sum = jnp.sum(two_grad * hidden_state * two_scale, axis=0)
     first_hop = fed.first(mark(team_hidden + [parts_made]))
-    parts, attn_part, head_sum, out_part, one_sum, pair_sum = attend_back(
+    parts, packed, head_sum, one_sum, pair_sum = attend_back(
         tiles, team_hidden, consts, (normed, qkv, logit, gated), mine, mark(fed.sent + [down_grad])
     )
     row = jnp.concatenate(
@@ -837,13 +866,8 @@
         ],
         axis=1,
     ).astype(BF16)
-    row = jnp.pad(row, ((0, 0), (0, cols - row.shape[1])))[:, None, :]
-    packed = jnp.concatenate(
-        [attn_part.reshape(everyone, rho, cols), jnp.pad(row, ((0, 0), (0, 7), (0, 0)))], axis=1
-    )
-    packed = jnp.concatenate(
-        [packed.reshape(groups, team_rows, cols), out_part.reshape(groups, -1, cols)], axis=1
-    )
+    row = jnp.pad(row, ((0, 0), (0, cols - row.shape[1]))).reshape(groups, TEAM, cols)
+    packed = lax.dynamic_update_slice(packed, row, (0, small_at, 0))
     parts = hold(parts, mark(first_hop + [gate_grad]))
     arrived = TeamSum(parts)
     arrived.first()
@@ -852,9 +876,6 @@
     packed = line_sum(packed)
     layer_output = ((hidden_state + fed.total()) * live_rows).astype(BF16)
     tokens_grad = (hidden_grad + rms_pull(inputs, gain_one, normed_grad)).astype(BF16)
-    routes = [(user, owner) for owner, user in out_weight_routes(groups)]
-    output_grad = lax.ppermute(packed[team_rows:].reshape(rho, width), ALL, routes)
-    packed = exchange(packed[:team_rows].reshape(TEAM, rho + 8, cols))
     feed_grad = jnp.concatenate([gate_grad, hold([up_grad], arrived.u4)[0]], axis=1)
     feed_grad = exchange(feed_grad.reshape(TEAM, rho, 2 * ff_cols))
 
@@ -862,8 +883,20 @@
         return w.reshape(TEAM, rho, groups, phi).transpose(1, 2, 0, 3).reshape(rho, ff)
 
     gate_grad, up_grad = hold(
-        [ff_join(feed_grad[:, :, :ff_cols]), ff_join(feed_grad[:, :, ff_cols:])], normed_grad
+        [ff_join(feed_grad[:, :, :ff_cols]), ff_join(feed_grad[:, :, ff_cols:])], arrived.u4
     )
+    packed = hold([packed], mark([gate_grad, up_grad]))[0]
+    routes = [(user, owner) for owner, user in out_weight_routes(groups)]
+    output_grad = packed[team_rows:small_at].reshape(-1, rho, cols).transpose(1, 0, 2).reshape(rho, width)
+    output_grad = lax.ppermute(output_grad, ALL, routes)
+    packed = jnp.concatenate(
+        [
+            packed[:team_rows].reshape(TEAM, rho, cols),
+            jnp.pad(packed[small_at : small_at + TEAM][:, None], ((0, 0), (0, 7), (0, 0))),
+        ],
+        axis=1,
+    )
+    packed = exchange(packed)
     attn_grad = packed[:, :rho].transpose(1, 0, 2)
     rows_small = packed[:, rho].astype(F32)
     sums = jnp.sum(rows_small[:, head_lanes:], axis=0)

time: 813 us -> 823 us (1.012); the launches traced: 799 us -> 818 us
  Pallas kernels: 150 us -> 165 us
  local copies, waits for them, and re-layouts: 83.2 us -> 97.4 us
  starting transfers between devices: 82.7 us -> 70.5 us
    ppermute x1, starting transfers between devices: 16.7 us -> 1.91 us  [local(): output_grad = lax.ppermute(output_grad, ALL, routes)]
    ppermute x1, waiting for transfers between devices: 0.01 us -> 13 us  [local(): output_grad = lax.ppermute(output_grad, ALL, routes)]
    ppermute x1, waiting for transfers between devices: 13.3 us -> 3.67 us  [local(): routed = lax.ppermute(output_weight, ALL, out_weight_routes(groups))]
    pallas_call x1, Pallas kernels: 63.7 us -> 72.1 us  [feed(): pl.pallas_call(kernel, out_shape=[struct((rows, width), BF16)] * (2 * TEA...]
    unnamed x141 -> x144, local copies, waits for them, and re-layouts: 19.5 us -> 26.1 us
  transfers between devices with their start and end apart: 86 -> 86, of which waited for: 31 -> 33; matrix products, arithmetic and copies ran while one was open for 25% -> 25% of each run, Pallas kernels for 11% -> 11%
where the time goes in v5:
time: 823 us; the launch traced here: 818 us
  waiting for transfers between devices  326 us (40%)
  Pallas kernels  165 us (20%)
  local copies, waits for them, and re-layouts  97.4 us (12%)
  other arithmetic  95.8 us (12%)
  starting transfers between devices  70.5 us (9%)
  matrix products  45.9 us (6%)
  between operations  17.1 us (2%)
    ppermute x72, waiting for transfers between devices, permute(): lax.ppermute(array, ALL, [(team[a], team[b]) for team in teams() for a, b...  298 us
    pallas_call x1, Pallas kernels, feed(): pl.pallas_call(kernel, out_shape=[struct((rows, width), BF16)] * (2 * TEA...  72.1 us
    pallas_call x1, Pallas kernels, attend_back(): pl.pallas_call(kernel, out_shape=[struct((rows, width), BF16)] * TEAM + [...  54.3 us
    dot_general x3, matrix products, product_tn(): lax.dot_general(left, right, (((0,), (0,)), ((), ())), preferred_element_...  45.9 us
    ppermute x72, starting transfers between devices, permute(): lax.ppermute(array, ALL, [(team[a], team[b]) for team in teams() for a, b...  43.9 us
    pallas_call x1, Pallas kernels, attend(): pl.pallas_call(kernel, out_shape=[struct((rows, width), BF16)] * TEAM + [...  30.6 us
    unnamed x144, local copies, waits for them, and re-layouts  26.1 us
    convert_element_type x12, other arithmetic, __init__(): (parts[r].astype(F32) + odd[r].astype(F32)).astype(BF16)  20.4 us
  transfers between devices with their start and end apart: 86, of which 33 were waited for; matrix products, arithmetic and copies ran while one was open for 25% of the time, Pallas kernels for 11%

profile of v5, /device:TPU:26, one launch (start us, length us, event | category | flops | bytes accessed | tf_op | source)
XLA Modules:
  0.0 817.7 jit_solution(15973829137413101656)
XLA Ops:
  11.7 4.3 all-to-all-start
  15.9 3.3 collective-permute-start.8
  19.2 9.5 %all-to-all-done = bf16[8,72,512]{2,1,0:T(8,128)(2,1)S(1)} async-done(((bf16[8,72,512]{2,1,0:T(8,128)(2,1)}), bf16[8,72,512]{2,1,0:T(8,128)(2,1)S(1)}, u32[]{:S(2)}, u32[]{:S(2)}) %all-to-all-start) | async-done | bytes 589856 | tf_op jit(solution)/shard_map/all_to_all | solution.py:60
  28.8 3.7 collective-permute-done.8
  36.3 2.2 reshape.274
  41.2 5.4 all-to-all-start.1
  46.8 24.3 %collective-permute-done.3.refs_5_ = bf16[384,2048]{1,0:T(8,128)(2,1)} collective-permute-done((bf16[384,2048]{1,0:T(8,128)(2,1)}, bf16[384,2048]{1,0:T(8,128)(2,1)}, u32[]{:S(2)}, u32[]{:S(2)}) %collective-permute-start.3) | collective-permute-done | bytes 1572896 | tf_op jit(solution)/shard_map/ppermute | solution.py:49
  76.4 28.0 %collective-permute-done.5 = bf16[192,2048]{1,0:T(8,128)(2,1)S(1)} collective-permute-done((bf16[192,2048]{1,0:T(8,128)(2,1)S(1)}, bf16[192,2048]{1,0:T(8,128)(2,1)S(1)}, u32[]{:S(2)}, u32[]{:S(2)}) %collective-permute-start.5) | collective-permute-done | bytes 786464 | tf_op jit(solution)/shard_map/ppermute | solution.py:49
  127.3 30.6 %shard_map.239 = (bf16[384,2048]{1,0:T(8,128)(2,1)S(1)}, bf16[384,2048]{1,0:T(8,128)(2,1)S(1)}, bf16[384,2048]{1,0:T(8,128)(2,1)S(1)}, bf16[384,2048]{1,0:T(8,12...) custom-call(s32[8]{0:T(128)S(1)} %select_reduce_fusion.refs_0_, ...), custom_call_target="tpu_custom_call" | custom-call | flops 32212254720 | bytes 62914560 | tf_op jit(solution)/shard_map/pallas_call | solution.py:328
  165.5 2.8 collective-permute-done.15
  177.0 15.3 %collective-permute-done.16 = bf16[192,2048]{1,0:T(8,128)(2,1)S(1)} collective-permute-done((bf16[192,2048]{1,0:T(8,128)(2,1)S(1)}, bf16[192,2048]{1,0:T(8,128)(2,1)S(1)}, u32[]{:S(2)}, u32[]{:S(2)}) %collective-permute-start.16) | collective-permute-done | bytes 786464 | tf_op jit(solution)/shard_map/ppermute | solution.py:49
  193.4 17.3 %collective-permute-done.18 = bf16[192,2048]{1,0:T(8,128)(2,1)S(1)} collective-permute-done((bf16[192,2048]{1,0:T(8,128)(2,1)S(1)}, bf16[192,2048]{1,0:T(8,128)(2,1)S(1)}, u32[]{:S(2)}, u32[]{:S(2)}) %collective-permute-start.18) | collective-permute-done | bytes 786464 | tf_op jit(solution)/shard_map/ppermute | solution.py:49
  221.1 11.7 %collective-permute-done.19 = bf16[192,2048]{1,0:T(8,128)(2,1)} collective-permute-done((bf16[192,2048]{1,0:T(8,128)(2,1)}, bf16[192,2048]{1,0:T(8,128)(2,1)}, u32[]{:S(2)}, u32[]{:S(2)}) %collective-permute-start.19) | collective-permute-done | bytes 786464 | tf_op jit(solution)/shard_map/ppermute | solution.py:49
  234.4 13.7 %collective-permute-done.21 = bf16[192,2048]{1,0:T(8,128)(2,1)} collective-permute-done((bf16[192,2048]{1,0:T(8,128)(2,1)}, bf16[192,2048]{1,0:T(8,128)(2,1)}, u32[]{:S(2)}, u32[]{:S(2)}) %collective-permute-start.21) | collective-permute-done | bytes 786464 | tf_op jit(solution)/shard_map/ppermute | solution.py:49
  252.3 2.8 multiply_reduce_fusion.2
  255.1 11.4 %collective-permute-done.27 = bf16[192,2048]{1,0:T(8,128)(2,1)S(1)} collective-permute-done((bf16[192,2048]{1,0:T(8,128)(2,1)S(1)}, bf16[192,2048]{1,0:T(8,128)(2,1)S(1)}, u32[]{:S(2)}, u32[]{:S(2)}) %collective-permute-start.27) | collective-permute-done | bytes 786464 | tf_op jit(solution)/shard_map/ppermute | solution.py:49
  273.3 34.2 %collective-permute-done.24.refs_1_ = bf16[384,2048]{1,0:T(8,128)(2,1)} collective-permute-done((bf16[384,2048]{1,0:T(8,128)(2,1)}, bf16[384,2048]{1,0:T(8,128)(2,1)}, u32[]{:S(2)}, u32[]{:S(2)}) %collective-permute-start.24) | collective-permute-done | bytes 1572896 | tf_op jit(solution)/shard_map/ppermute | solution.py:49
  313.5 14.4 %collective-permute-done.32 = bf16[192,2048]{1,0:T(8,128)(2,1)S(1)} collective-permute-done((bf16[192,2048]{1,0:T(8,128)(2,1)S(1)}, bf16[192,2048]{1,0:T(8,128)(2,1)S(1)}, u32[]{:S(2)}, u32[]{:S(2)}) %collective-permute-start.32) | collective-permute-done | bytes 786464 | tf_op jit(solution)/shard_map/ppermute | solution.py:49
  331.2 3.7 collective-permute-done.34.refs_8_
  334.9 72.1 %shard_map.249 = (bf16[384,2048]{1,0:T(8,128)(2,1)}, bf16[384,2048]{1,0:T(8,128)(2,1)}, bf16[384,2048]{1,0:T(8,128)(2,1)}, bf16[384,2048]{1,0:T(8,128)(2,1)}, bf...) custom-call(s32[8]{0:T(128)} %copy-done.12, ...), custom_call_target="tpu_custom_call" | custom-call | flops 62277025792 | bytes 104857600 | tf_op jit(solution)/shard_map/pallas_call | solution.py:681
  408.1 15.6 %convolution_convert_fusion = bf16[768,2048]{1,0:T(8,128)(2,1)} fusion(bf16[3072,768]{1,0:T(8,128)(2,1)} %get-tuple-element.139, bf16[3072,2048]{1,0:T(8,128)(2,1)} %get-tuple-element.140), kind=kOutput, calls=%fused_computation.10 | convolution fusion | flops 9665249280 | bytes 20447232 | tf_op jit(solution)/shard_map/dot_general | solution.py:29
  424.5 3.8 add_convert_fusion.10.refs_0_
  434.4 2.6 add_convert_fusion.8
  443.3 7.7 collective-permute-done.44
  453.6 7.3 collective-permute-done.46
  463.3 4.6 collective-permute-done.41.refs_0_
  468.0 9.9 %collective-permute-done.48.refs_1_ = bf16[192,2048]{1,0:T(8,128)(2,1)} collective-permute-done((bf16[192,2048]{1,0:T(8,128)(2,1)S(1)}, bf16[192,2048]{1,0:T(8,128)(2,1)}, u32[]{:S(2)}, u32[]{:S(2)}) %collective-permute-start.48) | collective-permute-done | bytes 786464 | tf_op jit(solution)/shard_map/ppermute | solution.py:49
  478.4 14.6 %fusion.4.refs_3_.refs_0_ = bf16[2048,768]{1,0:T(8,128)(2,1)S(1)} fusion(bf16[3072,2048]{1,0:T(8,128)(2,1)} %get-tuple-element.128, bf16[3072,1536]{1,0:T(8,128)(2,1)} %shard_map.251), kind=kOutput, calls=%fused_computation.8 | convolution fusion | flops 9665249280 | bytes 20447232 | tf_op jit(solution)/shard_map/dot_general | solution.py:29
  497.3 2.2 convert_add_fusion.5
  499.7 2.9 multiply_reduce_fusion
  503.0 6.9 fusion.38
  512.6 15.7 %fusion.7.refs_4_.refs_1_.refs_0_ = bf16[2048,768]{1,0:T(8,128)(2,1)} fusion(bf16[3072,2048]{1,0:T(8,128)(2,1)} %get-tuple-element.128, bf16[3072,1536]{1,0:T(8,128)(2,1)} %shard_map.251), kind=kOutput, calls=%fused_computation.9 | convolution fusion | flops 9665249280 | bytes 20447232 | tf_op jit(solution)/shard_map/dot_general | solution.py:29
  528.9 15.9 %collective-permute-done.51.refs_1_ = bf16[384,2048]{1,0:T(8,128)(2,1)} collective-permute-done((bf16[384,2048]{1,0:T(8,128)(2,1)}, bf16[384,2048]{1,0:T(8,128)(2,1)}, u32[]{:S(2)}, u32[]{:S(2)}) %collective-permute-start.51) | collective-permute-done | bytes 1572896 | tf_op jit(solution)/shard_map/ppermute | solution.py:49
  551.0 12.8 %collective-permute-done.54 = bf16[192,2048]{1,0:T(8,128)(2,1)S(1)} collective-permute-done((bf16[192,2048]{1,0:T(8,128)(2,1)S(1)}, bf16[192,2048]{1,0:T(8,128)(2,1)S(1)}, u32[]{:S(2)}, u32[]{:S(2)}) %collective-permute-start.54) | collective-permute-done | bytes 786464 | tf_op jit(solution)/shard_map/ppermute | solution.py:49
  567.8 3.1 collective-permute-done.56.refs_7_.refs_8_
  572.7 2.7 fusion.41
  579.0 54.3 %shard_map.258 = (bf16[384,2048]{1,0:T(8,128)(2,1)}, bf16[384,2048]{1,0:T(8,128)(2,1)}, bf16[384,2048]{1,0:T(8,128)(2,1)}, bf16[384,2048]{1,0:T(8,128)(2,1)}, bf...) custom-call(s32[8]{0:T(128)} %copy-done.12, ...), custom_call_target="tpu_custom_call" | custom-call | flops 48318382080 | bytes 73400320 | tf_op jit(solution)/shard_map/pallas_call | solution.py:492
  638.4 2.5 add_convert_fusion.1.refs_3_
  649.6 12.5 %collective-permute-done.69.refs_1_.refs_2_ = bf16[192,2048]{1,0:T(8,128)(2,1)} collective-permute-done((bf16[192,2048]{1,0:T(8,128)(2,1)S(1)}, bf16[192,2048]{1,0:T(8,128)(2,1)}, u32[]{:S(2)}, u32[]{:S(2)}) %collective-permute-start.69) | collective-permute-done | bytes 786464 | tf_op jit(solution)/shard_map/ppermute | solution.py:49
  662.9 2.6 add_convert_fusion.19
  666.2 2.3 add_convert_fusion.18
  670.0 2.5 convert_element_type.528
  672.5 12.3 %collective-permute-done.59 = bf16[192,2048]{1,0:T(8,128)(2,1)} collective-permute-done((bf16[192,2048]{1,0:T(8,128)(2,1)}, bf16[192,2048]{1,0:T(8,128)(2,1)}, u32[]{:S(2)}, u32[]{:S(2)}) %collective-permute-start.59) | collective-permute-done | bytes 786464 | tf_op jit(solution)/shard_map/ppermute | solution.py:49
  684.8 2.7 convert_add_fusion.4
  687.6 2.9 convert_add_fusion.3
  691.9 2.3 add_convert_fusion.17.refs_0_
  694.2 2.3 add_convert_fusion.16.refs_1_
  697.6 5.1 fusion.18
  704.1 2.4 pad_maximum_fusion.1
  706.5 5.9 all-to-all-start.2
  712.4 4.7 collective-permute-done.70
  718.7 23.6 %collective-permute-done.72 = bf16[192,2048]{1,0:T(8,128)(2,1)S(1)} collective-permute-done((bf16[192,2048]{1,0:T(8,128)(2,1)}, bf16[192,2048]{1,0:T(8,128)(2,1)S(1)}, u32[]{:S(2)}, u32[]{:S(2)}) %collective-permute-start.72) | collective-permute-done | bytes 786464 | tf_op jit(solution)/shard_map/ppermute | solution.py:49
  744.8 3.1 fusion.10
  747.9 2.2 all-to-all-done.2
  750.1 2.6 fusion.39
  752.8 3.4 reshape.287
  756.2 3.3 copy.154
  759.5 2.9 reshape.288.refs_1_
  762.3 3.4 reshape.285
  765.7 3.3 copy.153
  769.1 2.9 reshape.286.refs_0_
  776.2 4.7 all-to-all-start.3
  782.8 5.0 fusion.14
  790.5 13.0 %collective-permute-done.73 = bf16[64,2048]{1,0:T(8,128)(2,1)S(1)} collective-permute-done((bf16[64,2048]{1,0:T(8,128)(2,1)S(1)}, bf16[64,2048]{1,0:T(8,128)(2,1)S(1)}, u32[]{:S(2)}, u32[]{:S(2)}) %collective-permute-start.73) | collective-permute-done | bytes 262176 | tf_op jit(solution)/shard_map/ppermute | solution.py:891
  (448 shorter events, 170.9 us)
Async XLA Ops:
  15.9 98.8 %all-gather.5.cloned.1.call-start = ((), (), s32[]{:S(2)}) async-start(), calls=%async_computation.8 | async-start | bytes 4014080 | tf_op jit(solution)/shard_map/all_gather | solution.py:66
  33.5 37.6 %collective-permute-start.3 = (bf16[384,2048]{1,0:T(8,128)(2,1)}, bf16[384,2048]{1,0:T(8,128)(2,1)}, u32[]{:S(2)}, u32[]{:S(2)}) collective-permute-start(bf16[384,2048]{1,0:T(8,128)(2,1)} %refs_1_.1), channel_id=1, source_target_pairs={{0,4},{1,5},{2,6},{3,7},{4,0},{5,1},{6,2},{7,3},{8,12},{9,13},{10,... | collective-permute-start | bytes 4718600 | tf_op jit(solution)/shard_map/ppermute | solution.py:49
  33.6 38.8 %collective-permute-start.1 = (bf16[384,2048]{1,0:T(8,128)(2,1)}, bf16[384,2048]{1,0:T(8,128)(2,1)}, u32[]{:S(2)}, u32[]{:S(2)}) collective-permute-start(bf16[384,2048]{1,0:T(8,128)(2,1)} %refs_1_.1), channel_id=1, source_target_pairs={{0,2},{1,3},{2,0},{3,1},{4,6},{5,7},{6,4},{7,5},{8,10},{9,11},{10,... | collective-permute-start | bytes 4718600 | tf_op jit(solution)/shard_map/ppermute | solution.py:49
  41.2 65.1 %all-to-all-start.1 = ((bf16[8,64,1536]{2,1,0:T(8,128)(2,1)}), bf16[8,64,1536]{2,1,0:T(8,128)(2,1)S(1)}, u32[]{:S(2)}, u32[]{:S(2)}) async-start(bf16[8,64,1536]{2,1,0:T(8,128)(2,1)} %pad_maximum_fusion), calls=%async_computation.1 | async-start | bytes 3145728 | tf_op jit(solution)/shard_map/all_to_all | solution.py:60
  46.6 165.3 %all-gather.7.cloned.1.call-start = ((), (), s32[]{:S(2)}) async-start(), calls=%async_computation.9 | async-start | bytes 3932160 | tf_op jit(solution)/shard_map/all_gather | solution.py:66
  46.6 79.5 %collective-permute-start = (bf16[384,2048]{1,0:T(8,128)(2,1)}, bf16[384,2048]{1,0:T(8,128)(2,1)}, u32[]{:S(2)}, u32[]{:S(2)}) collective-permute-start(bf16[384,2048]{1,0:T(8,128)(2,1)} %refs_1_.1), channel_id=1, source_target_pairs={{0,1},{1,0},{2,3},{3,2},{4,5},{5,4},{6,7},{7,6},{8,9},{9,8},{10,11... | collective-permute-start | bytes 4718600 | tf_op jit(solution)/shard_map/ppermute | solution.py:49
  72.3 32.1 %collective-permute-start.5 = (bf16[192,2048]{1,0:T(8,128)(2,1)S(1)}, bf16[192,2048]{1,0:T(8,128)(2,1)S(1)}, u32[]{:S(2)}, u32[]{:S(2)}) collective-permute-start(bf16[192,2048]{1,0:T(8,128)(2,1)S(1)} %slice.279), channel_id=1, source_target_pairs={{0,2},{1,3},{2,0},{3,1},{4,6},{5,7},{6,4},{7,5},{8,10},{9,11},{10,... | collective-permute-start | bytes 2359304 | tf_op jit(solution)/shard_map/ppermute | solution.py:49
  73.6 31.7 %collective-permute-start.6 = (bf16[192,2048]{1,0:T(8,128)(2,1)S(1)}, bf16[192,2048]{1,0:T(8,128)(2,1)S(1)}, u32[]{:S(2)}, u32[]{:S(2)}) collective-permute-start(bf16[192,2048]{1,0:T(8,128)(2,1)S(1)} %slice.280), channel_id=1, source_target_pairs={{0,4},{1,5},{2,6},{3,7},{4,0},{5,1},{6,2},{7,3},{8,12},{9,13},{10,... | collective-permute-start | bytes 2359304 | tf_op jit(solution)/shard_map/ppermute | solution.py:49
  75.9 50.7 %collective-permute-start.2 = (bf16[384,2048]{1,0:T(8,128)(2,1)}, bf16[384,2048]{1,0:T(8,128)(2,1)}, u32[]{:S(2)}, u32[]{:S(2)}) collective-permute-start(bf16[384,2048]{1,0:T(8,128)(2,1)} %collective-permute-done.1.refs_3_), channel_id=1, source_target_pairs={{0,1},{1,0},{2,3},{3,2},{4,5},{5,4},{6,7},{7,6},{8,9},{9,8},{10,11... | collective-permute-start | bytes 4718600 | tf_op jit(solution)/shard_map/ppermute | solution.py:49
  75.9 50.6 %collective-permute-start.4 = (bf16[384,2048]{1,0:T(8,128)(2,1)}, bf16[384,2048]{1,0:T(8,128)(2,1)}, u32[]{:S(2)}, u32[]{:S(2)}) collective-permute-start(bf16[384,2048]{1,0:T(8,128)(2,1)} %collective-permute-done.3.refs_5_), channel_id=1, source_target_pairs={{0,1},{1,0},{2,3},{3,2},{4,5},{5,4},{6,7},{7,6},{8,9},{9,8},{10,11... | collective-permute-start | bytes 4718600 | tf_op jit(solution)/shard_map/ppermute | solution.py:49
  106.3 20.3 %collective-permute-start.7 = (bf16[384,2048]{1,0:T(8,128)(2,1)}, bf16[384,2048]{1,0:T(8,128)(2,1)}, u32[]{:S(2)}, u32[]{:S(2)}) collective-permute-start(bf16[384,2048]{1,0:T(8,128)(2,1)} %constant_dynamic-update-slice_fusion.refs_0_.refs_7_), channel_id=1, source_target_pairs={{0,1},{1,0},{2,3},{3,2},{4,5},{5,4},{6,7},{7,6},{8,9},{9,8},{10,11... | collective-permute-start | bytes 4718600 | tf_op jit(solution)/shard_map/ppermute | solution.py:49
  107.6 164.3 %all-gather.9.cloned.1.call-start = ((), (), s32[]{:S(2)}) async-start(), calls=%async_computation.10 | async-start | bytes 3932160 | tf_op jit(solution)/shard_map/all_gather | solution.py:66
  113.0 49.1 %collective-permute-start.11 = (bf16[384,2048]{1,0:T(8,128)(2,1)S(1)}, bf16[384,2048]{1,0:T(8,128)(2,1)S(1)}, u32[]{:S(2)}, u32[]{:S(2)}) collective-permute-start(bf16[384,2048]{1,0:T(8,128)(2,1)S(1)} %copy-done.18), channel_id=1, source_target_pairs={{0,4},{1,5},{2,6},{3,7},{4,0},{5,1},{6,2},{7,3},{8,12},{9,13},{10,... | collective-permute-start | bytes 4718600 | tf_op jit(solution)/shard_map/ppermute | solution.py:49
  126.2 36.7 %collective-permute-start.10 = (bf16[384,2048]{1,0:T(8,128)(2,1)S(1)}, bf16[384,2048]{1,0:T(8,128)(2,1)}, u32[]{:S(2)}, u32[]{:S(2)}) collective-permute-start(bf16[384,2048]{1,0:T(8,128)(2,1)S(1)} %copy-done.18), channel_id=1, source_target_pairs={{0,2},{1,3},{2,0},{3,1},{4,6},{5,7},{6,4},{7,5},{8,10},{9,11},{10,... | collective-permute-start | bytes 4718600 | tf_op jit(solution)/shard_map/ppermute | solution.py:49
  126.6 36.3 %collective-permute-start.9 = (bf16[384,2048]{1,0:T(8,128)(2,1)S(1)}, bf16[384,2048]{1,0:T(8,128)(2,1)S(1)}, u32[]{:S(2)}, u32[]{:S(2)}) collective-permute-start(bf16[384,2048]{1,0:T(8,128)(2,1)S(1)} %copy-done.18), channel_id=1, source_target_pairs={{0,1},{1,0},{2,3},{3,2},{4,5},{5,4},{6,7},{7,6},{8,9},{9,8},{10,11... | collective-permute-start | bytes 4718600 | tf_op jit(solution)/shard_map/ppermute | solution.py:49
  164.9 166.3 %all-gather.11.cloned.1.call-start = ((), (), s32[]{:S(2)}) async-start(), calls=%async_computation.11 | async-start | bytes 3932160 | tf_op jit(solution)/shard_map/all_gather | solution.py:66
  172.6 19.7 %collective-permute-start.16 = (bf16[192,2048]{1,0:T(8,128)(2,1)S(1)}, bf16[192,2048]{1,0:T(8,128)(2,1)S(1)}, u32[]{:S(2)}, u32[]{:S(2)}) collective-permute-start(bf16[192,2048]{1,0:T(8,128)(2,1)S(1)} %get-tuple-element.184), channel_id=1, source_target_pairs={{0,4},{1,5},{2,6},{3,7},{4,0},{5,1},{6,2},{7,3},{8,12},{9,13},{10,... | collective-permute-start | bytes 2359304 | tf_op jit(solution)/shard_map/ppermute | solution.py:49
  174.2 46.8 %collective-permute-start.14 = (bf16[192,2048]{1,0:T(8,128)(2,1)S(1)}, bf16[192,2048]{1,0:T(8,128)(2,1)}, u32[]{:S(2)}, u32[]{:S(2)}) collective-permute-start(bf16[192,2048]{1,0:T(8,128)(2,1)S(1)} %slice.291), channel_id=1, source_target_pairs={{0,2},{1,3},{2,0},{3,1},{4,6},{5,7},{6,4},{7,5},{8,10},{9,11},{10,... | collective-permute-start | bytes 2359304 | tf_op jit(solution)/shard_map/ppermute | solution.py:49
  175.9 34.9 %collective-permute-start.18 = (bf16[192,2048]{1,0:T(8,128)(2,1)S(1)}, bf16[192,2048]{1,0:T(8,128)(2,1)S(1)}, u32[]{:S(2)}, u32[]{:S(2)}) collective-permute-start(bf16[192,2048]{1,0:T(8,128)(2,1)S(1)} %get-tuple-element.183), channel_id=1, source_target_pairs={{0,2},{1,3},{2,0},{3,1},{4,6},{5,7},{6,4},{7,5},{8,10},{9,11},{10,... | collective-permute-start | bytes 2359304 | tf_op jit(solution)/shard_map/ppermute | solution.py:49
  212.0 20.9 %collective-permute-start.19 = (bf16[192,2048]{1,0:T(8,128)(2,1)}, bf16[192,2048]{1,0:T(8,128)(2,1)}, u32[]{:S(2)}, u32[]{:S(2)}) collective-permute-start(bf16[192,2048]{1,0:T(8,128)(2,1)} %get-tuple-element.106.refs_1_), channel_id=1, source_target_pairs={{0,4},{1,5},{2,6},{3,7},{4,0},{5,1},{6,2},{7,3},{8,12},{9,13},{10,... | collective-permute-start | bytes 2359304 | tf_op jit(solution)/shard_map/ppermute | solution.py:49
  213.4 38.9 %collective-permute-start.12 = (bf16[384,2048]{1,0:T(8,128)(2,1)S(1)}, bf16[384,2048]{1,0:T(8,128)(2,1)}, u32[]{:S(2)}, u32[]{:S(2)}) collective-permute-start(bf16[384,2048]{1,0:T(8,128)(2,1)S(1)} %copy-done.5), channel_id=1, source_target_pairs={{0,1},{1,0},{2,3},{3,2},{4,5},{5,4},{6,7},{7,6},{8,9},{9,8},{10,11... | collective-permute-start | bytes 4718600 | tf_op jit(solution)/shard_map/ppermute | solution.py:49
  215.4 32.7 %collective-permute-start.21 = (bf16[192,2048]{1,0:T(8,128)(2,1)}, bf16[192,2048]{1,0:T(8,128)(2,1)}, u32[]{:S(2)}, u32[]{:S(2)}) collective-permute-start(bf16[192,2048]{1,0:T(8,128)(2,1)} %slice.297), channel_id=1, source_target_pairs={{0,4},{1,5},{2,6},{3,7},{4,0},{5,1},{6,2},{7,3},{8,12},{9,13},{10,... | collective-permute-start | bytes 2359304 | tf_op jit(solution)/shard_map/ppermute | solution.py:49
  216.4 33.7 %collective-permute-start.20 = (bf16[192,2048]{1,0:T(8,128)(2,1)S(1)}, bf16[192,2048]{1,0:T(8,128)(2,1)}, u32[]{:S(2)}, u32[]{:S(2)}) collective-permute-start(bf16[192,2048]{1,0:T(8,128)(2,1)S(1)} %copy-done.24), channel_id=1, source_target_pairs={{0,2},{1,3},{2,0},{3,1},{4,6},{5,7},{6,4},{7,5},{8,10},{9,11},{10,... | collective-permute-start | bytes 2359304 | tf_op jit(solution)/shard_map/ppermute | solution.py:49
  218.2 284.5 %reduce-scatter.5.cloned.1.call-start = ((), (), s32[]{:S(2)}) async-start(), calls=%async_computation.12 | async-start | bytes 3932160 | tf_op jit(solution)/shard_map/reduce_scatter | solution.py:72
  221.0 50.9 %collective-permute-start.25 = (bf16[384,2048]{1,0:T(8,128)(2,1)}, bf16[384,2048]{1,0:T(8,128)(2,1)}, u32[]{:S(2)}, u32[]{:S(2)}) collective-permute-start(bf16[384,2048]{1,0:T(8,128)(2,1)} %get-tuple-element.108.refs_2_.refs_11_), channel_id=1, source_target_pairs={{0,1},{1,0},{2,3},{3,2},{4,5},{5,4},{6,7},{7,6},{8,9},{9,8},{10,11... | collective-permute-start | bytes 4718600 | tf_op jit(solution)/shard_map/ppermute | solution.py:49
  232.8 39.0 %collective-permute-start.26 = (bf16[384,2048]{1,0:T(8,128)(2,1)S(1)}, bf16[384,2048]{1,0:T(8,128)(2,1)}, u32[]{:S(2)}, u32[]{:S(2)}) collective-permute-start(bf16[384,2048]{1,0:T(8,128)(2,1)S(1)} %copy-done.15), channel_id=1, source_target_pairs={{0,1},{1,0},{2,3},{3,2},{4,5},{5,4},{6,7},{7,6},{8,9},{9,8},{10,11... | collective-permute-start | bytes 4718600 | tf_op jit(solution)/shard_map/ppermute | solution.py:49
  248.2 18.4 %collective-permute-start.27 = (bf16[192,2048]{1,0:T(8,128)(2,1)S(1)}, bf16[192,2048]{1,0:T(8,128)(2,1)S(1)}, u32[]{:S(2)}, u32[]{:S(2)}) collective-permute-start(bf16[192,2048]{1,0:T(8,128)(2,1)S(1)} %slice.233), channel_id=1, source_target_pairs={{0,2},{1,3},{2,0},{3,1},{4,6},{5,7},{6,4},{7,5},{8,10},{9,11},{10,... | collective-permute-start | bytes 2359304 | tf_op jit(solution)/shard_map/ppermute | solution.py:49
  270.4 37.1 %collective-permute-start.24 = (bf16[384,2048]{1,0:T(8,128)(2,1)}, bf16[384,2048]{1,0:T(8,128)(2,1)}, u32[]{:S(2)}, u32[]{:S(2)}) collective-permute-start(bf16[384,2048]{1,0:T(8,128)(2,1)} %multiply_convert_fusion.refs_1_), channel_id=1, source_target_pairs={{0,4},{1,5},{2,6},{3,7},{4,0},{5,1},{6,2},{7,3},{8,12},{9,13},{10,... | collective-permute-start | bytes 4718600 | tf_op jit(solution)/shard_map/ppermute | solution.py:49
  270.7 36.8 %collective-permute-start.23 = (bf16[384,2048]{1,0:T(8,128)(2,1)}, bf16[384,2048]{1,0:T(8,128)(2,1)}, u32[]{:S(2)}, u32[]{:S(2)}) collective-permute-start(bf16[384,2048]{1,0:T(8,128)(2,1)} %multiply_convert_fusion.refs_1_), channel_id=1, source_target_pairs={{0,2},{1,3},{2,0},{3,1},{4,6},{5,7},{6,4},{7,5},{8,10},{9,11},{10,... | collective-permute-start | bytes 4718600 | tf_op jit(solution)/shard_map/ppermute | solution.py:49
  308.7 19.2 %collective-permute-start.32 = (bf16[192,2048]{1,0:T(8,128)(2,1)S(1)}, bf16[192,2048]{1,0:T(8,128)(2,1)S(1)}, u32[]{:S(2)}, u32[]{:S(2)}) collective-permute-start(bf16[192,2048]{1,0:T(8,128)(2,1)S(1)} %slice.236), channel_id=1, source_target_pairs={{0,2},{1,3},{2,0},{3,1},{4,6},{5,7},{6,4},{7,5},{8,10},{9,11},{10,... | collective-permute-start | bytes 2359304 | tf_op jit(solution)/shard_map/ppermute | solution.py:49
  311.2 19.0 %collective-permute-start.33 = (bf16[192,2048]{1,0:T(8,128)(2,1)S(1)}, bf16[192,2048]{1,0:T(8,128)(2,1)S(1)}, u32[]{:S(2)}, u32[]{:S(2)}) collective-permute-start(bf16[192,2048]{1,0:T(8,128)(2,1)S(1)} %slice.237), channel_id=1, source_target_pairs={{0,4},{1,5},{2,6},{3,7},{4,0},{5,1},{6,2},{7,3},{8,12},{9,13},{10,... | collective-permute-start | bytes 2359304 | tf_op jit(solution)/shard_map/ppermute | solution.py:49
  313.0 18.1 %collective-permute-start.30 = (bf16[384,2048]{1,0:T(8,128)(2,1)}, bf16[384,2048]{1,0:T(8,128)(2,1)}, u32[]{:S(2)}, u32[]{:S(2)}) collective-permute-start(bf16[384,2048]{1,0:T(8,128)(2,1)} %get-tuple-element.110.refs_3_), channel_id=1, source_target_pairs={{0,1},{1,0},{2,3},{3,2},{4,5},{5,4},{6,7},{7,6},{8,9},{9,8},{10,11... | collective-permute-start | bytes 4718600 | tf_op jit(solution)/shard_map/ppermute | solution.py:49
  407.1 23.5 %collective-permute-start.37 = (bf16[384,2048]{1,0:T(8,128)(2,1)}, bf16[384,2048]{1,0:T(8,128)(2,1)}, u32[]{:S(2)}, u32[]{:S(2)}) collective-permute-start(bf16[384,2048]{1,0:T(8,128)(2,1)} %get-tuple-element.117), channel_id=1, source_target_pairs={{0,1},{1,0},{2,3},{3,2},{4,5},{5,4},{6,7},{7,6},{8,9},{9,8},{10,11... | collective-permute-start | bytes 4718600 | tf_op jit(solution)/shard_map/ppermute | solution.py:49
  407.5 26.8 %collective-permute-start.38 = (bf16[384,2048]{1,0:T(8,128)(2,1)}, bf16[384,2048]{1,0:T(8,128)(2,1)}, u32[]{:S(2)}, u32[]{:S(2)}) collective-permute-start(bf16[384,2048]{1,0:T(8,128)(2,1)} %get-tuple-element.119), channel_id=1, source_target_pairs={{0,1},{1,0},{2,3},{3,2},{4,5},{5,4},{6,7},{7,6},{8,9},{9,8},{10,11... | collective-permute-start | bytes 4718600 | tf_op jit(solution)/shard_map/ppermute | solution.py:49
  407.6 91.9 %collective-permute-start.39 = (bf16[384,2048]{1,0:T(8,128)(2,1)}, bf16[384,2048]{1,0:T(8,128)(2,1)}, u32[]{:S(2)}, u32[]{:S(2)}) collective-permute-start(bf16[384,2048]{1,0:T(8,128)(2,1)} %get-tuple-element.121), channel_id=1, source_target_pairs={{0,1},{1,0},{2,3},{3,2},{4,5},{5,4},{6,7},{7,6},{8,9},{9,8},{10,11... | collective-permute-start | bytes 4718600 | tf_op jit(solution)/shard_map/ppermute | solution.py:49
  408.1 20.3 %collective-permute-start.43 = (bf16[384,2048]{1,0:T(8,128)(2,1)}, bf16[384,2048]{1,0:T(8,128)(2,1)}, u32[]{:S(2)}, u32[]{:S(2)}) collective-permute-start(bf16[384,2048]{1,0:T(8,128)(2,1)} %get-tuple-element.127), channel_id=1, source_target_pairs={{0,1},{1,0},{2,3},{3,2},{4,5},{5,4},{6,7},{7,6},{8,9},{9,8},{10,11... | collective-permute-start | bytes 4718600 | tf_op jit(solution)/shard_map/ppermute | solution.py:49
  423.7 155.2 %reduce-scatter.7.cloned.1.call-start = ((), (), s32[]{:S(2)}) async-start(), calls=%async_computation.13 | async-start | bytes 3932160 | tf_op jit(solution)/shard_map/reduce_scatter | solution.py:72
  430.6 20.4 %collective-permute-start.44 = (bf16[192,2048]{1,0:T(8,128)(2,1)S(1)}, bf16[192,2048]{1,0:T(8,128)(2,1)S(1)}, u32[]{:S(2)}, u32[]{:S(2)}) collective-permute-start(bf16[192,2048]{1,0:T(8,128)(2,1)S(1)} %get-tuple-element.179), channel_id=1, source_target_pairs={{0,2},{1,3},{2,0},{3,1},{4,6},{5,7},{6,4},{7,5},{8,10},{9,11},{10,... | collective-permute-start | bytes 2359304 | tf_op jit(solution)/shard_map/ppermute | solution.py:49
  439.7 28.3 %collective-permute-start.41 = (bf16[192,2048]{1,0:T(8,128)(2,1)S(1)}, bf16[192,2048]{1,0:T(8,128)(2,1)}, u32[]{:S(2)}, u32[]{:S(2)}) collective-permute-start(bf16[192,2048]{1,0:T(8,128)(2,1)S(1)} %slice.302), channel_id=1, source_target_pairs={{0,2},{1,3},{2,0},{3,1},{4,6},{5,7},{6,4},{7,5},{8,10},{9,11},{10,... | collective-permute-start | bytes 2359304 | tf_op jit(solution)/shard_map/ppermute | solution.py:49
  440.5 20.4 %collective-permute-start.46 = (bf16[192,2048]{1,0:T(8,128)(2,1)S(1)}, bf16[192,2048]{1,0:T(8,128)(2,1)S(1)}, u32[]{:S(2)}, u32[]{:S(2)}) collective-permute-start(bf16[192,2048]{1,0:T(8,128)(2,1)S(1)} %get-tuple-element.180), channel_id=1, source_target_pairs={{0,4},{1,5},{2,6},{3,7},{4,0},{5,1},{6,2},{7,3},{8,12},{9,13},{10,... | collective-permute-start | bytes 2359304 | tf_op jit(solution)/shard_map/ppermute | solution.py:49
  442.7 35.1 %collective-permute-start.48 = (bf16[192,2048]{1,0:T(8,128)(2,1)S(1)}, bf16[192,2048]{1,0:T(8,128)(2,1)}, u32[]{:S(2)}, u32[]{:S(2)}) collective-permute-start(bf16[192,2048]{1,0:T(8,128)(2,1)S(1)} %slice.307), channel_id=1, source_target_pairs={{0,4},{1,5},{2,6},{3,7},{4,0},{5,1},{6,2},{7,3},{8,12},{9,13},{10,... | collective-permute-start | bytes 2359304 | tf_op jit(solution)/shard_map/ppermute | solution.py:49
  452.2 43.5 %collective-permute-start.45 = (bf16[192,2048]{1,0:T(8,128)(2,1)}, bf16[192,2048]{1,0:T(8,128)(2,1)}, u32[]{:S(2)}, u32[]{:S(2)}) collective-permute-start(bf16[192,2048]{1,0:T(8,128)(2,1)} %add_convert_fusion.21), channel_id=1, source_target_pairs={{0,4},{1,5},{2,6},{3,7},{4,0},{5,1},{6,2},{7,3},{8,12},{9,13},{10,... | collective-permute-start | bytes 2359304 | tf_op jit(solution)/shard_map/ppermute | solution.py:49
  462.0 35.3 %collective-permute-start.47 = (bf16[192,2048]{1,0:T(8,128)(2,1)}, bf16[192,2048]{1,0:T(8,128)(2,1)}, u32[]{:S(2)}, u32[]{:S(2)}) collective-permute-start(bf16[192,2048]{1,0:T(8,128)(2,1)} %add_convert_fusion.20), channel_id=1, source_target_pairs={{0,2},{1,3},{2,0},{3,1},{4,6},{5,7},{6,4},{7,5},{8,10},{9,11},{10,... | collective-permute-start | bytes 2359304 | tf_op jit(solution)/shard_map/ppermute | solution.py:49
  502.7 159.5 %reduce-scatter.9.cloned.1.call-start = ((), (), s32[]{:S(2)}) async-start(), calls=%async_computation.14 | async-start | bytes 3932160 | tf_op jit(solution)/shard_map/reduce_scatter | solution.py:72
  509.9 34.9 %collective-permute-start.51 = (bf16[384,2048]{1,0:T(8,128)(2,1)}, bf16[384,2048]{1,0:T(8,128)(2,1)}, u32[]{:S(2)}, u32[]{:S(2)}) collective-permute-start(bf16[384,2048]{1,0:T(8,128)(2,1)} %get-tuple-element.169.refs_0_.refs_1_), channel_id=1, source_target_pairs={{0,4},{1,5},{2,6},{3,7},{4,0},{5,1},{6,2},{7,3},{8,12},{9,13},{10,... | collective-permute-start | bytes 4718600 | tf_op jit(solution)/shard_map/ppermute | solution.py:49
  511.3 34.6 %collective-permute-start.50 = (bf16[384,2048]{1,0:T(8,128)(2,1)}, bf16[384,2048]{1,0:T(8,128)(2,1)}, u32[]{:S(2)}, u32[]{:S(2)}) collective-permute-start(bf16[384,2048]{1,0:T(8,128)(2,1)} %get-tuple-element.169.refs_0_.refs_1_), channel_id=1, source_target_pairs={{0,2},{1,3},{2,0},{3,1},{4,6},{5,7},{6,4},{7,5},{8,10},{9,11},{10,... | collective-permute-start | bytes 4718600 | tf_op jit(solution)/shard_map/ppermute | solution.py:49
  571.6 61.8 %collective-permute-start.57 = (bf16[192,2048]{1,0:T(8,128)(2,1)}, bf16[192,2048]{1,0:T(8,128)(2,1)}, u32[]{:S(2)}, u32[]{:S(2)}) collective-permute-start(bf16[192,2048]{1,0:T(8,128)(2,1)} %get-tuple-element.132.refs_1_), channel_id=1, source_target_pairs={{0,2},{1,3},{2,0},{3,1},{4,6},{5,7},{6,4},{7,5},{8,10},{9,11},{10,... | collective-permute-start | bytes 2359304 | tf_op jit(solution)/shard_map/ppermute | solution.py:49
  572.1 61.3 %collective-permute-start.62 = (bf16[192,2048]{1,0:T(8,128)(2,1)}, bf16[192,2048]{1,0:T(8,128)(2,1)}, u32[]{:S(2)}, u32[]{:S(2)}) collective-permute-start(bf16[192,2048]{1,0:T(8,128)(2,1)} %get-tuple-element.134.refs_2_), channel_id=1, source_target_pairs={{0,4},{1,5},{2,6},{3,7},{4,0},{5,1},{6,2},{7,3},{8,12},{9,13},{10,... | collective-permute-start | bytes 2359304 | tf_op jit(solution)/shard_map/ppermute | solution.py:49
  575.4 57.9 %collective-permute-start.58 = (bf16[192,2048]{1,0:T(8,128)(2,1)}, bf16[192,2048]{1,0:T(8,128)(2,1)}, u32[]{:S(2)}, u32[]{:S(2)}) collective-permute-start(bf16[192,2048]{1,0:T(8,128)(2,1)} %get-tuple-element.177), channel_id=1, source_target_pairs={{0,2},{1,3},{2,0},{3,1},{4,6},{5,7},{6,4},{7,5},{8,10},{9,11},{10,... | collective-permute-start | bytes 2359304 | tf_op jit(solution)/shard_map/ppermute | solution.py:49
  576.9 56.5 %collective-permute-start.60 = (bf16[192,2048]{1,0:T(8,128)(2,1)}, bf16[192,2048]{1,0:T(8,128)(2,1)}, u32[]{:S(2)}, u32[]{:S(2)}) collective-permute-start(bf16[192,2048]{1,0:T(8,128)(2,1)} %get-tuple-element.178), channel_id=1, source_target_pairs={{0,4},{1,5},{2,6},{3,7},{4,0},{5,1},{6,2},{7,3},{8,12},{9,13},{10,... | collective-permute-start | bytes 2359304 | tf_op jit(solution)/shard_map/ppermute | solution.py:49
  579.0 193.6 %reduce-scatter.11.cloned.1.call-start = ((), (), s32[]{:S(2)}) async-start(), calls=%async_computation.15 | async-start | bytes 4014080 | tf_op jit(solution)/shard_map/reduce_scatter | solution.py:72
  642.0 20.1 %collective-permute-start.69 = (bf16[192,2048]{1,0:T(8,128)(2,1)S(1)}, bf16[192,2048]{1,0:T(8,128)(2,1)}, u32[]{:S(2)}, u32[]{:S(2)}) collective-permute-start(bf16[192,2048]{1,0:T(8,128)(2,1)S(1)} %get-tuple-element.175), channel_id=1, source_target_pairs={{0,2},{1,3},{2,0},{3,1},{4,6},{5,7},{6,4},{7,5},{8,10},{9,11},{10,... | collective-permute-start | bytes 2359304 | tf_op jit(solution)/shard_map/ppermute | solution.py:49
  642.5 19.8 %collective-permute-start.67 = (bf16[192,2048]{1,0:T(8,128)(2,1)S(1)}, bf16[192,2048]{1,0:T(8,128)(2,1)}, u32[]{:S(2)}, u32[]{:S(2)}) collective-permute-start(bf16[192,2048]{1,0:T(8,128)(2,1)S(1)} %get-tuple-element.176), channel_id=1, source_target_pairs={{0,4},{1,5},{2,6},{3,7},{4,0},{5,1},{6,2},{7,3},{8,12},{9,13},{10,... | collective-permute-start | bytes 2359304 | tf_op jit(solution)/shard_map/ppermute | solution.py:49
  665.5 19.3 %collective-permute-start.59 = (bf16[192,2048]{1,0:T(8,128)(2,1)}, bf16[192,2048]{1,0:T(8,128)(2,1)}, u32[]{:S(2)}, u32[]{:S(2)}) collective-permute-start(bf16[192,2048]{1,0:T(8,128)(2,1)} %add_convert_fusion.19), channel_id=1, source_target_pairs={{0,4},{1,5},{2,6},{3,7},{4,0},{5,1},{6,2},{7,3},{8,12},{9,13},{10,... | collective-permute-start | bytes 2359304 | tf_op jit(solution)/shard_map/ppermute | solution.py:49
  668.5 19.1 %collective-permute-start.61 = (bf16[192,2048]{1,0:T(8,128)(2,1)}, bf16[192,2048]{1,0:T(8,128)(2,1)}, u32[]{:S(2)}, u32[]{:S(2)}) collective-permute-start(bf16[192,2048]{1,0:T(8,128)(2,1)} %add_convert_fusion.18), channel_id=1, source_target_pairs={{0,2},{1,3},{2,0},{3,1},{4,6},{5,7},{6,4},{7,5},{8,10},{9,11},{10,... | collective-permute-start | bytes 2359304 | tf_op jit(solution)/shard_map/ppermute | solution.py:49
  670.0 27.6 %collective-permute-start.35 = (bf16[384,2048]{1,0:T(8,128)(2,1)}, bf16[384,2048]{1,0:T(8,128)(2,1)}, u32[]{:S(2)}, u32[]{:S(2)}) collective-permute-start(bf16[384,2048]{1,0:T(8,128)(2,1)} %get-tuple-element.113), channel_id=1, source_target_pairs={{0,1},{1,0},{2,3},{3,2},{4,5},{5,4},{6,7},{7,6},{8,9},{9,8},{10,11... | collective-permute-start | bytes 4718600 | tf_op jit(solution)/shard_map/ppermute | solution.py:49
  690.4 54.3 %collective-permute-start.63 = (bf16[384,2048]{1,0:T(8,128)(2,1)}, bf16[384,2048]{1,0:T(8,128)(2,1)}, u32[]{:S(2)}, u32[]{:S(2)}) collective-permute-start(bf16[384,2048]{1,0:T(8,128)(2,1)} %get-tuple-element.150), channel_id=1, source_target_pairs={{0,1},{1,0},{2,3},{3,2},{4,5},{5,4},{6,7},{7,6},{8,9},{9,8},{10,11... | collective-permute-start | bytes 4718600 | tf_op jit(solution)/shard_map/ppermute | solution.py:49
  690.4 22.0 %collective-permute-start.65 = (bf16[192,2048]{1,0:T(8,128)(2,1)}, bf16[192,2048]{1,0:T(8,128)(2,1)}, u32[]{:S(2)}, u32[]{:S(2)}) collective-permute-start(bf16[192,2048]{1,0:T(8,128)(2,1)} %slice.312.refs_4_), channel_id=1, source_target_pairs={{0,2},{1,3},{2,0},{3,1},{4,6},{5,7},{6,4},{7,5},{8,10},{9,11},{10,... | collective-permute-start | bytes 2359304 | tf_op jit(solution)/shard_map/ppermute | solution.py:49
  696.4 20.7 %collective-permute-start.70 = (bf16[192,2048]{1,0:T(8,128)(2,1)}, bf16[192,2048]{1,0:T(8,128)(2,1)}, u32[]{:S(2)}, u32[]{:S(2)}) collective-permute-start(bf16[192,2048]{1,0:T(8,128)(2,1)} %get-tuple-element.161), channel_id=1, source_target_pairs={{0,4},{1,5},{2,6},{3,7},{4,0},{5,1},{6,2},{7,3},{8,12},{9,13},{10,... | collective-permute-start | bytes 2359304 | tf_op jit(solution)/shard_map/ppermute | solution.py:49
  702.7 39.6 %collective-permute-start.72 = (bf16[192,2048]{1,0:T(8,128)(2,1)}, bf16[192,2048]{1,0:T(8,128)(2,1)S(1)}, u32[]{:S(2)}, u32[]{:S(2)}) collective-permute-start(bf16[192,2048]{1,0:T(8,128)(2,1)} %slice.318.refs_5_), channel_id=1, source_target_pairs={{0,4},{1,5},{2,6},{3,7},{4,0},{5,1},{6,2},{7,3},{8,12},{9,13},{10,... | collective-permute-start | bytes 2359304 | tf_op jit(solution)/shard_map/ppermute | solution.py:49
  703.5 39.6 %collective-permute-start.71 = (bf16[192,2048]{1,0:T(8,128)(2,1)}, bf16[192,2048]{1,0:T(8,128)(2,1)}, u32[]{:S(2)}, u32[]{:S(2)}) collective-permute-start(bf16[192,2048]{1,0:T(8,128)(2,1)} %get-tuple-element.162), channel_id=1, source_target_pairs={{0,2},{1,3},{2,0},{3,1},{4,6},{5,7},{6,4},{7,5},{8,10},{9,11},{10,... | collective-permute-start | bytes 2359304 | tf_op jit(solution)/shard_map/ppermute | solution.py:49
  706.5 43.6 %all-to-all-start.2 = ((bf16[8,64,1536]{2,1,0:T(8,128)(2,1)}), bf16[8,64,1536]{2,1,0:T(8,128)(2,1)}, u32[]{:S(2)}, u32[]{:S(2)}) async-start(bf16[8,64,1536]{2,1,0:T(8,128)(2,1)} %bitcast.22), calls=%async_computation.6 | async-start | bytes 3145728 | tf_op jit(solution)/shard_map/all_to_all | solution.py:60
  776.2 28.2 %all-to-all-start.3 = ((bf16[8,72,512]{2,1,0:T(8,128)(2,1)}), bf16[8,72,512]{2,1,0:T(8,128)(2,1)}, u32[]{:S(2)}, u32[]{:S(2)}) async-start(bf16[8,72,512]{2,1,0:T(8,128)(2,1)} %fusion.22), calls=%async_computation.7 | async-start | bytes 1179648 | tf_op jit(solution)/shard_map/all_to_all | solution.py:60
  780.9 22.6 %collective-permute-start.73 = (bf16[64,2048]{1,0:T(8,128)(2,1)S(1)}, bf16[64,2048]{1,0:T(8,128)(2,1)S(1)}, u32[]{:S(2)}, u32[]{:S(2)}) collective-permute-start(bf16[64,2048]{1,0:T(8,128)(2,1)S(1)} %bitcast.98), channel_id=1, source_target_pairs={{0,0},{8,1},{16,2},{24,3},{1,4},{9,5},{17,6},{25,7},{2,8},{10,9},{... | collective-permute-start | bytes 786440 | tf_op jit(solution)/shard_map/ppermute | solution.py:891
  (85 other events, 707.7 us)
Sparse Core Ops, SparseCore 0:
  33.6 62.3 all-gather.4
  107.7 62.3 all-gather.6
  171.7 62.1 all-gather.8
  235.3 62.1 all-gather.10
  423.8 60.1 reduce-scatter.4
  502.9 60.1 reduce-scatter.6
  579.1 59.2 reduce-scatter.8
  663.0 60.3 reduce-scatter.10

commit v6 on v5

--- a/solution.py
+++ b/solution.py
@@ -101,31 +101,28 @@
             (parts[r].astype(F32) + odd[r].astype(F32)).astype(BF16) for r in (6, 2, 4, 0)
         )
         self.half = half
-        self.low6 = self.total6
-        self.ready = [self.low6, self.total2[:half], self.total4[half:]]
+        self.ready = [
+            jnp.concatenate([self.total6[:half], self.total2[:half]], axis=0),
+            jnp.concatenate([self.total6[half:], self.total4[half:]], axis=0),
+        ]
 
     def first(self, tick=None):
-        half = self.half
-        low6, x_top, y_low = self.ready if tick is None else hold(self.ready, tick)
-        self.u4 = swap(low6[:half], 2)
-        self.u2 = swap(low6[half:], 4)
-        self.x_top = swap(x_top, 2)
-        self.y_low = swap(y_low, 4)
-        self.sent = [low6, x_top, y_low]
-        return [self.u4, self.u2, self.x_top, self.y_low]
+        self.sent = self.ready if tick is None else list(hold(self.ready, tick))
+        self.over_x, self.over_y = swap(self.sent[0], 2), swap(self.sent[1], 4)
+        return [self.over_x, self.over_y]
 
     def total(self, tick=None):
         half = self.half
         lasts = [
-            (self.total2[half:].astype(F32) + self.u2.astype(F32)).astype(BF16),
-            (self.total4[:half].astype(F32) + self.u4.astype(F32)).astype(BF16),
+            (self.total2[half:].astype(F32) + self.over_y[:half].astype(F32)).astype(BF16),
+            (self.total4[:half].astype(F32) + self.over_x[:half].astype(F32)).astype(BF16),
         ]
         x_low, y_top = lasts if tick is None else hold(lasts, tick)
         self.last_sent = [x_low, y_top]
         x_low = swap(x_low, 2).astype(F32)
         y_top = swap(y_top, 4).astype(F32)
-        top = self.x_top.astype(F32) + y_top
-        low = x_low + self.y_low.astype(F32)
+        top = self.over_x[half:].astype(F32) + y_top
+        low = x_low + self.over_y[half:].astype(F32)
         return self.total0.astype(F32) + jnp.concatenate([top, low], axis=0)
 
 
@@ -826,20 +823,20 @@
     parts = hold(parts, mark([upstream_levels.a1, upstream_levels.a2, upstream_levels.a4, tick]))
     arrived = TeamSum(parts)
     arrived.first()
-    weight_down = line_gather(hold([down_weight], arrived.low6)[0])
+    weight_down = line_gather(hold([down_weight], arrived.sent[0])[0])
     inputs = tokens.astype(F32)
     hidden_state = inputs + arrived.total(weight_gate)
-    team_upstream = upstream_levels.blocks(mark(arrived.last_sent))
 
     normed_two = rms(hidden_state, gain_two).astype(BF16)
-    team_two = TeamGather(normed_two).blocks(mark(team_upstream + [weight_up]))
+    team_upstream = upstream_levels.blocks(normed_two)
+    team_two = TeamGather(normed_two).blocks(weight_up)
     outs, grads, saved = feed(tiles, team_two, team_upstream, weight_gate, weight_up, weight_down)
     inner, feed_back, two_all, ups_all = saved
     arrived = TeamSum(grads)
     arrived.first()
     two_grad = arrived.total()
     down_part = product_tn(inner, ups_all).astype(BF16)
-    feed_back = hold([feed_back], mark([arrived.x_top, arrived.y_low]))[0]
+    feed_back = hold([feed_back], mark([arrived.over_x, arrived.over_y]))[0]
     gate_part = product_tn(two_all, feed_back[:, :ff_cols]).astype(BF16)
     up_part = product_tn(two_all, feed_back[:, ff_cols:]).astype(BF16)
     parts_made = mark([gate_part, up_part])
@@ -871,21 +868,20 @@
     parts = hold(parts, mark(first_hop + [gate_grad]))
     arrived = TeamSum(parts)
     arrived.first()
-    packed = hold([packed.reshape(-1, cols)], mark([feed_done, arrived.u4, arrived.u2] + arrived.sent))[0]
+    packed = hold([packed.reshape(-1, cols)], mark([feed_done] + arrived.sent))[0]
     normed_grad = arrived.total(packed)
     packed = line_sum(packed)
-    layer_output = ((hidden_state + fed.total()) * live_rows).astype(BF16)
+    layer_output = ((hidden_state + fed.total(mark(arrived.last_sent))) * live_rows).astype(BF16)
     tokens_grad = (hidden_grad + rms_pull(inputs, gain_one, normed_grad)).astype(BF16)
-    feed_grad = jnp.concatenate([gate_grad, hold([up_grad], arrived.u4)[0]], axis=1)
+    feed_grad = jnp.concatenate([gate_grad, hold([up_grad], mark(arrived.last_sent))[0]], axis=1)
     feed_grad = exchange(feed_grad.reshape(TEAM, rho, 2 * ff_cols))
 
     def ff_join(w):
         return w.reshape(TEAM, rho, groups, phi).transpose(1, 2, 0, 3).reshape(rho, ff)
 
     gate_grad, up_grad = hold(
-        [ff_join(feed_grad[:, :, :ff_cols]), ff_join(feed_grad[:, :, ff_cols:])], arrived.u4
+        [ff_join(feed_grad[:, :, :ff_cols]), ff_join(feed_grad[:, :, ff_cols:])], normed_grad
     )
-    packed = hold([packed], mark([gate_grad, up_grad]))[0]
     routes = [(user, owner) for owner, user in out_weight_routes(groups)]
     output_grad = packed[team_rows:small_at].reshape(-1, rho, cols).transpose(1, 0, 2).reshape(rho, width)
     output_grad = lax.ppermute(output_grad, ALL, routes)

time: 823 us -> 770 us (0.936)
  the two profiles are of different devices: /device:TPU:26 before, /device:TPU:1 now
where the time goes in v6:
time: 770 us; the launch traced here: 766 us
  waiting for transfers between devices  262 us (34%)
  Pallas kernels  157 us (20%)
  other arithmetic  105 us (14%)
  starting transfers between devices  91.4 us (12%)
  local copies, waits for them, and re-layouts  89.7 us (12%)
  matrix products  44.5 us (6%)
  between operations  17.3 us (2%)
    ppermute x64, waiting for transfers between devices, permute(): lax.ppermute(array, ALL, [(team[a], team[b]) for team in teams() for a, b...  249 us
    pallas_call x1, Pallas kernels, feed(): pl.pallas_call(kernel, out_shape=[struct((rows, width), BF16)] * (2 * TEA...  67.7 us
    ppermute x64, starting transfers between devices, permute(): lax.ppermute(array, ALL, [(team[a], team[b]) for team in teams() for a, b...  59.3 us
    pallas_call x1, Pallas kernels, attend_back(): pl.pallas_call(kernel, out_shape=[struct((rows, width), BF16)] * TEAM + [...  52.9 us
    dot_general x3, matrix products, product_tn(): lax.dot_general(left, right, (((0,), (0,)), ((), ())), preferred_element_...  44.5 us
    unnamed x144, local copies, waits for them, and re-layouts  29.6 us
    pallas_call x1, Pallas kernels, attend(): pl.pallas_call(kernel, out_shape=[struct((rows, width), BF16)] * TEAM + [...  29.3 us
    convert_element_type x12, other arithmetic, __init__(): (parts[r].astype(F32) + odd[r].astype(F32)).astype(BF16)  23.9 us
  transfers between devices with their start and end apart: 78, of which 28 were waited for; matrix products, arithmetic and copies ran while one was open for 27% of the time, Pallas kernels for 12%

profile of v6, /device:TPU:1, one launch (start us, length us, event | category | flops | bytes accessed | tf_op | source)
XLA Modules:
  0.0 766.5 jit_solution(15507332240380955481)
XLA Ops:
  11.6 5.2 all-to-all-start
  16.9 3.1 collective-permute-start.8
  20.0 7.4 all-to-all-done
  29.5 6.8 collective-permute-start.3
  36.4 3.0 reshape.272
  39.3 2.6 copy.148
  41.9 2.3 reshape.273
  44.3 3.0 reshape.274
  47.3 2.6 copy.149
  49.9 3.0 reshape.275
  52.9 2.4 pad_maximum_fusion.2
  55.3 6.0 all-to-all-start.1
  61.5 8.1 %collective-permute-done.3.refs_5_ = bf16[384,2048]{1,0:T(8,128)(2,1)} collective-permute-done((bf16[384,2048]{1,0:T(8,128)(2,1)S(1)}, bf16[384,2048]{1,0:T(8,128)(2,1)}, u32[]{:S(2)}, u32[]{:S(2)}) %collective-permute-start.3) | collective-permute-done | bytes 1572896 | tf_op jit(solution)/shard_map/ppermute | solution.py:49
  74.9 4.9 collective-permute-start.2
  79.8 24.3 %collective-permute-done.5 = bf16[192,2048]{1,0:T(8,128)(2,1)S(1)} collective-permute-done((bf16[192,2048]{1,0:T(8,128)(2,1)S(1)}, bf16[192,2048]{1,0:T(8,128)(2,1)S(1)}, u32[]{:S(2)}, u32[]{:S(2)}) %collective-permute-start.5) | collective-permute-done | bytes 786464 | tf_op jit(solution)/shard_map/ppermute | solution.py:49
  106.1 2.7 collective-permute-start.7
  108.8 2.6 fusion.42
  114.4 2.7 broadcast_select_fusion.refs_0_.refs_9_
  121.3 29.3 %shard_map.239 = (bf16[384,2048]{1,0:T(8,128)(2,1)S(1)}, bf16[384,2048]{1,0:T(8,128)(2,1)S(1)}, bf16[384,2048]{1,0:T(8,128)(2,1)S(1)}, bf16[384,2048]{1,0:T(8,12...) custom-call(s32[8]{0:T(128)S(1)} %select_reduce_fusion.refs_0_, ...), custom_call_target="tpu_custom_call" | custom-call | flops 32212254720 | bytes 62914560 | tf_op jit(solution)/shard_map/pallas_call | solution.py:325
  158.3 4.9 collective-permute-done.13
  164.3 2.7 add_convert_fusion.14
  174.9 30.3 %collective-permute-done.15 = bf16[384,2048]{1,0:T(8,128)(2,1)S(1)} collective-permute-done((bf16[384,2048]{1,0:T(8,128)(2,1)S(1)}, bf16[384,2048]{1,0:T(8,128)(2,1)S(1)}, u32[]{:S(2)}, u32[]{:S(2)}) %collective-permute-start.15) | collective-permute-done | bytes 1572896 | tf_op jit(solution)/shard_map/ppermute | solution.py:49
  206.7 2.6 collective-permute-done.17
  214.6 15.1 %collective-permute-done.18 = bf16[192,2048]{1,0:T(8,128)(2,1)} collective-permute-done((bf16[192,2048]{1,0:T(8,128)(2,1)}, bf16[192,2048]{1,0:T(8,128)(2,1)}, u32[]{:S(2)}, u32[]{:S(2)}) %collective-permute-start.18) | collective-permute-done | bytes 786464 | tf_op jit(solution)/shard_map/ppermute | solution.py:49
  231.2 2.6 collective-permute-done.19
  235.2 2.3 multiply_reduce_fusion.2
  247.4 27.0 %collective-permute-done.22.refs_1_ = bf16[384,2048]{1,0:T(8,128)(2,1)} collective-permute-done((bf16[384,2048]{1,0:T(8,128)(2,1)}, bf16[384,2048]{1,0:T(8,128)(2,1)}, u32[]{:S(2)}, u32[]{:S(2)}) %collective-permute-start.22) | collective-permute-done | bytes 1572896 | tf_op jit(solution)/shard_map/ppermute | solution.py:49
  278.1 14.0 %collective-permute-done.30 = bf16[192,2048]{1,0:T(8,128)(2,1)} collective-permute-done((bf16[192,2048]{1,0:T(8,128)(2,1)}, bf16[192,2048]{1,0:T(8,128)(2,1)}, u32[]{:S(2)}, u32[]{:S(2)}) %collective-permute-start.30) | collective-permute-done | bytes 786464 | tf_op jit(solution)/shard_map/ppermute | solution.py:49
  294.5 3.9 collective-permute-start.20
  300.5 8.4 %collective-permute-done.25 = bf16[192,2048]{1,0:T(8,128)(2,1)S(1)} collective-permute-done((bf16[192,2048]{1,0:T(8,128)(2,1)S(1)}, bf16[192,2048]{1,0:T(8,128)(2,1)S(1)}, u32[]{:S(2)}, u32[]{:S(2)}) %collective-permute-start.25) | collective-permute-done | bytes 786464 | tf_op jit(solution)/shard_map/ppermute | solution.py:49
  320.9 67.7 %shard_map.247 = (bf16[384,2048]{1,0:T(8,128)(2,1)}, bf16[384,2048]{1,0:T(8,128)(2,1)}, bf16[384,2048]{1,0:T(8,128)(2,1)}, bf16[384,2048]{1,0:T(8,128)(2,1)}, bf...) custom-call(s32[8]{0:T(128)} %copy-done.12, ...), custom_call_target="tpu_custom_call" | custom-call | flops 62277025792 | bytes 104857600 | tf_op jit(solution)/shard_map/pallas_call | solution.py:678
  390.1 15.6 %convolution_convert_fusion = bf16[768,2048]{1,0:T(8,128)(2,1)} fusion(bf16[3072,768]{1,0:T(8,128)(2,1)} %get-tuple-element.139, bf16[3072,2048]{1,0:T(8,128)(2,1)} %get-tuple-element.140), kind=kOutput, calls=%fused_computation.10 | convolution fusion | flops 9665249280 | bytes 20447232 | tf_op jit(solution)/shard_map/dot_general | solution.py:29
  406.2 2.5 add_convert_fusion.5
  420.3 2.6 add_convert_fusion.8
  427.3 21.0 %collective-permute-done.40.refs_0_ = bf16[384,2048]{1,0:T(8,128)(2,1)S(1)} collective-permute-done((bf16[384,2048]{1,0:T(8,128)(2,1)S(1)}, bf16[384,2048]{1,0:T(8,128)(2,1)S(1)}, u32[]{:S(2)}, u32[]{:S(2)}) %collective-permute-start.40) | collective-permute-done | bytes 1572896 | tf_op jit(solution)/shard_map/ppermute | solution.py:49
  453.5 14.6 %fusion.4.refs_2_.refs_0_ = bf16[2048,768]{1,0:T(8,128)(2,1)S(1)} fusion(bf16[3072,2048]{1,0:T(8,128)(2,1)} %get-tuple-element.129, bf16[3072,1536]{1,0:T(8,128)(2,1)} %shard_map.249), kind=kOutput, calls=%fused_computation.8 | convolution fusion | flops 9665249280 | bytes 20447232 | tf_op jit(solution)/shard_map/dot_general | solution.py:29
  470.8 2.6 convert_add_fusion.6
  473.5 2.5 convert_add_fusion.5
  476.5 4.1 multiply_reduce_fusion
  480.6 6.6 fusion.37
  489.5 14.3 %fusion.7.refs_3_.refs_1_.refs_0_ = bf16[2048,768]{1,0:T(8,128)(2,1)} fusion(bf16[3072,2048]{1,0:T(8,128)(2,1)} %get-tuple-element.129, bf16[3072,1536]{1,0:T(8,128)(2,1)S(1)} %bitcast.84), kind=kOutput, calls=%fused_computation.9 | convolution fusion | flops 9665249280 | bytes 20447232 | tf_op jit(solution)/shard_map/dot_general | solution.py:29
  504.5 17.9 %collective-permute-done.47.refs_1_ = bf16[384,2048]{1,0:T(8,128)(2,1)} collective-permute-done((bf16[384,2048]{1,0:T(8,128)(2,1)}, bf16[384,2048]{1,0:T(8,128)(2,1)}, u32[]{:S(2)}, u32[]{:S(2)}) %collective-permute-start.47) | collective-permute-done | bytes 1572896 | tf_op jit(solution)/shard_map/ppermute | solution.py:49
  527.6 2.8 collective-permute-start.45
  530.9 10.0 %collective-permute-done.50 = bf16[192,2048]{1,0:T(8,128)(2,1)S(1)} collective-permute-done((bf16[192,2048]{1,0:T(8,128)(2,1)S(1)}, bf16[192,2048]{1,0:T(8,128)(2,1)S(1)}, u32[]{:S(2)}, u32[]{:S(2)}) %collective-permute-start.50) | collective-permute-done | bytes 786464 | tf_op jit(solution)/shard_map/ppermute | solution.py:49
  544.4 3.5 collective-permute-start.52
  548.5 2.8 collective-permute-done.52.refs_7_.refs_8_
  553.2 52.9 %shard_map.256 = (bf16[384,2048]{1,0:T(8,128)(2,1)}, bf16[384,2048]{1,0:T(8,128)(2,1)}, bf16[384,2048]{1,0:T(8,128)(2,1)}, bf16[384,2048]{1,0:T(8,128)(2,1)}, bf...) custom-call(s32[8]{0:T(128)} %copy-done.12, ...), custom_call_target="tpu_custom_call" | custom-call | flops 48318382080 | bytes 73400320 | tf_op jit(solution)/shard_map/pallas_call | solution.py:489
  611.8 2.5 add_convert_fusion.3
  625.3 2.6 add_convert_fusion.18.refs_1_
  628.0 2.6 add_convert_fusion.19.refs_0_
  630.6 25.3 %collective-permute-done.59 = bf16[384,2048]{1,0:T(8,128)(2,1)} collective-permute-done((bf16[384,2048]{1,0:T(8,128)(2,1)}, bf16[384,2048]{1,0:T(8,128)(2,1)}, u32[]{:S(2)}, u32[]{:S(2)}) %collective-permute-start.59) | collective-permute-done | bytes 1572896 | tf_op jit(solution)/shard_map/ppermute | solution.py:49
  664.4 2.5 convert_element_type.528
  668.3 2.6 pad_maximum_fusion.9
  671.0 5.2 all-to-all-start.3
  676.2 4.1 collective-permute-done.60
  681.0 2.7 convert_add_fusion.4
  683.8 18.9 %collective-permute-done.61 = bf16[192,2048]{1,0:T(8,128)(2,1)} collective-permute-done((bf16[192,2048]{1,0:T(8,128)(2,1)}, bf16[192,2048]{1,0:T(8,128)(2,1)}, u32[]{:S(2)}, u32[]{:S(2)}) %collective-permute-start.61) | collective-permute-done | bytes 786464 | tf_op jit(solution)/shard_map/ppermute | solution.py:49
  702.7 2.7 convert_add_fusion.3
  709.1 2.8 fusion.10
  718.3 7.3 all-to-all-start.2
  725.7 5.1 fusion.18
  730.8 3.8 collective-permute-start.65
  744.2 2.5 convert_element_type.526
  747.9 4.2 collective-permute-done.65
  (442 shorter events, 171.5 us)
Async XLA Ops:
  11.6 15.8 %all-to-all-start = ((bf16[8,72,512]{2,1,0:T(8,128)(2,1)}), bf16[8,72,512]{2,1,0:T(8,128)(2,1)S(1)}, u32[]{:S(2)}, u32[]{:S(2)}) async-start(bf16[8,72,512]{2,1,0:T(8,128)(2,1)} %copy.143), calls=%async_computation | async-start | bytes 1179648 | tf_op jit(solution)/shard_map/all_to_all | solution.py:60
  16.9 100.9 %all-gather.5.cloned.1.call-start = ((), (), s32[]{:S(2)}) async-start(), calls=%async_computation.8 | async-start | bytes 4014080 | tf_op jit(solution)/shard_map/all_gather | solution.py:66
  29.5 40.1 %collective-permute-start.3 = (bf16[384,2048]{1,0:T(8,128)(2,1)S(1)}, bf16[384,2048]{1,0:T(8,128)(2,1)}, u32[]{:S(2)}, u32[]{:S(2)}) collective-permute-start(bf16[384,2048]{1,0:T(8,128)(2,1)S(1)} %copy-done.17), channel_id=1, source_target_pairs={{0,4},{1,5},{2,6},{3,7},{4,0},{5,1},{6,2},{7,3},{8,12},{9,13},{10,... | collective-permute-start | bytes 4718600 | tf_op jit(solution)/shard_map/ppermute | solution.py:49
  36.4 34.6 %collective-permute-start.1 = (bf16[384,2048]{1,0:T(8,128)(2,1)S(1)}, bf16[384,2048]{1,0:T(8,128)(2,1)}, u32[]{:S(2)}, u32[]{:S(2)}) collective-permute-start(bf16[384,2048]{1,0:T(8,128)(2,1)S(1)} %copy-done.17), channel_id=1, source_target_pairs={{0,2},{1,3},{2,0},{3,1},{4,6},{5,7},{6,4},{7,5},{8,10},{9,11},{10,... | collective-permute-start | bytes 4718600 | tf_op jit(solution)/shard_map/ppermute | solution.py:49
  55.3 53.5 %all-to-all-start.1 = ((bf16[8,64,1536]{2,1,0:T(8,128)(2,1)}), bf16[8,64,1536]{2,1,0:T(8,128)(2,1)}, u32[]{:S(2)}, u32[]{:S(2)}) async-start(bf16[8,64,1536]{2,1,0:T(8,128)(2,1)} %pad_maximum_fusion.2), calls=%async_computation.1 | async-start | bytes 3145728 | tf_op jit(solution)/shard_map/all_to_all | solution.py:60
  61.3 150.3 %all-gather.7.cloned.1.call-start = ((), (), s32[]{:S(2)}) async-start(), calls=%async_computation.9 | async-start | bytes 3932160 | tf_op jit(solution)/shard_map/all_gather | solution.py:66
  61.3 58.6 %collective-permute-start = (bf16[384,2048]{1,0:T(8,128)(2,1)S(1)}, bf16[384,2048]{1,0:T(8,128)(2,1)}, u32[]{:S(2)}, u32[]{:S(2)}) collective-permute-start(bf16[384,2048]{1,0:T(8,128)(2,1)S(1)} %copy-done.17), channel_id=1, source_target_pairs={{0,1},{1,0},{2,3},{3,2},{4,5},{5,4},{6,7},{7,6},{8,9},{9,8},{10,11... | collective-permute-start | bytes 4718600 | tf_op jit(solution)/shard_map/ppermute | solution.py:49
  70.8 33.3 %collective-permute-start.5 = (bf16[192,2048]{1,0:T(8,128)(2,1)S(1)}, bf16[192,2048]{1,0:T(8,128)(2,1)S(1)}, u32[]{:S(2)}, u32[]{:S(2)}) collective-permute-start(bf16[192,2048]{1,0:T(8,128)(2,1)S(1)} %slice.343), channel_id=1, source_target_pairs={{0,2},{1,3},{2,0},{3,1},{4,6},{5,7},{6,4},{7,5},{8,10},{9,11},{10,... | collective-permute-start | bytes 2359304 | tf_op jit(solution)/shard_map/ppermute | solution.py:49
  72.2 32.9 %collective-permute-start.6 = (bf16[192,2048]{1,0:T(8,128)(2,1)S(1)}, bf16[192,2048]{1,0:T(8,128)(2,1)S(1)}, u32[]{:S(2)}, u32[]{:S(2)}) collective-permute-start(bf16[192,2048]{1,0:T(8,128)(2,1)S(1)} %slice.344), channel_id=1, source_target_pairs={{0,4},{1,5},{2,6},{3,7},{4,0},{5,1},{6,2},{7,3},{8,12},{9,13},{10,... | collective-permute-start | bytes 2359304 | tf_op jit(solution)/shard_map/ppermute | solution.py:49
  74.9 45.1 %collective-permute-start.2 = (bf16[384,2048]{1,0:T(8,128)(2,1)}, bf16[384,2048]{1,0:T(8,128)(2,1)}, u32[]{:S(2)}, u32[]{:S(2)}) collective-permute-start(bf16[384,2048]{1,0:T(8,128)(2,1)} %collective-permute-done.1.refs_3_), channel_id=1, source_target_pairs={{0,1},{1,0},{2,3},{3,2},{4,5},{5,4},{6,7},{7,6},{8,9},{9,8},{10,11... | collective-permute-start | bytes 4718600 | tf_op jit(solution)/shard_map/ppermute | solution.py:49
  79.7 40.8 %collective-permute-start.4 = (bf16[384,2048]{1,0:T(8,128)(2,1)}, bf16[384,2048]{1,0:T(8,128)(2,1)}, u32[]{:S(2)}, u32[]{:S(2)}) collective-permute-start(bf16[384,2048]{1,0:T(8,128)(2,1)} %collective-permute-done.3.refs_5_), channel_id=1, source_target_pairs={{0,1},{1,0},{2,3},{3,2},{4,5},{5,4},{6,7},{7,6},{8,9},{9,8},{10,11... | collective-permute-start | bytes 4718600 | tf_op jit(solution)/shard_map/ppermute | solution.py:49
  111.4 164.1 %all-gather.9.cloned.1.call-start = ((), (), s32[]{:S(2)}) async-start(), calls=%async_computation.10 | async-start | bytes 3932160 | tf_op jit(solution)/shard_map/all_gather | solution.py:66
  117.7 37.0 %collective-permute-start.11 = (bf16[384,2048]{1,0:T(8,128)(2,1)}, bf16[384,2048]{1,0:T(8,128)(2,1)}, u32[]{:S(2)}, u32[]{:S(2)}) collective-permute-start(bf16[384,2048]{1,0:T(8,128)(2,1)} %broadcast_select_fusion.refs_0_.refs_9_), channel_id=1, source_target_pairs={{0,4},{1,5},{2,6},{3,7},{4,0},{5,1},{6,2},{7,3},{8,12},{9,13},{10,... | collective-permute-start | bytes 4718600 | tf_op jit(solution)/shard_map/ppermute | solution.py:49
  119.9 36.1 %collective-permute-start.10 = (bf16[384,2048]{1,0:T(8,128)(2,1)}, bf16[384,2048]{1,0:T(8,128)(2,1)}, u32[]{:S(2)}, u32[]{:S(2)}) collective-permute-start(bf16[384,2048]{1,0:T(8,128)(2,1)} %broadcast_select_fusion.refs_0_.refs_9_), channel_id=1, source_target_pairs={{0,2},{1,3},{2,0},{3,1},{4,6},{5,7},{6,4},{7,5},{8,10},{9,11},{10,... | collective-permute-start | bytes 4718600 | tf_op jit(solution)/shard_map/ppermute | solution.py:49
  120.0 36.0 %collective-permute-start.9 = (bf16[384,2048]{1,0:T(8,128)(2,1)}, bf16[384,2048]{1,0:T(8,128)(2,1)}, u32[]{:S(2)}, u32[]{:S(2)}) collective-permute-start(bf16[384,2048]{1,0:T(8,128)(2,1)} %broadcast_select_fusion.refs_0_.refs_9_), channel_id=1, source_target_pairs={{0,1},{1,0},{2,3},{3,2},{4,5},{5,4},{6,7},{7,6},{8,9},{9,8},{10,11... | collective-permute-start | bytes 4718600 | tf_op jit(solution)/shard_map/ppermute | solution.py:49
  158.2 155.3 %all-gather.11.cloned.1.call-start = ((), (), s32[]{:S(2)}) async-start(), calls=%async_computation.11 | async-start | bytes 3932160 | tf_op jit(solution)/shard_map/all_gather | solution.py:66
  169.4 35.8 %collective-permute-start.15 = (bf16[384,2048]{1,0:T(8,128)(2,1)S(1)}, bf16[384,2048]{1,0:T(8,128)(2,1)S(1)}, u32[]{:S(2)}, u32[]{:S(2)}) collective-permute-start(bf16[384,2048]{1,0:T(8,128)(2,1)S(1)} %pad_maximum_fusion.refs_1_), channel_id=1, source_target_pairs={{0,2},{1,3},{2,0},{3,1},{4,6},{5,7},{6,4},{7,5},{8,10},{9,11},{10,... | collective-permute-start | bytes 4718600 | tf_op jit(solution)/shard_map/ppermute | solution.py:49
  173.4 35.8 %collective-permute-start.17 = (bf16[384,2048]{1,0:T(8,128)(2,1)S(1)}, bf16[384,2048]{1,0:T(8,128)(2,1)S(1)}, u32[]{:S(2)}, u32[]{:S(2)}) collective-permute-start(bf16[384,2048]{1,0:T(8,128)(2,1)S(1)} %pad_maximum_fusion.1), channel_id=1, source_target_pairs={{0,4},{1,5},{2,6},{3,7},{4,0},{5,1},{6,2},{7,3},{8,12},{9,13},{10,... | collective-permute-start | bytes 4718600 | tf_op jit(solution)/shard_map/ppermute | solution.py:49
  211.5 18.3 %collective-permute-start.18 = (bf16[192,2048]{1,0:T(8,128)(2,1)}, bf16[192,2048]{1,0:T(8,128)(2,1)}, u32[]{:S(2)}, u32[]{:S(2)}) collective-permute-start(bf16[192,2048]{1,0:T(8,128)(2,1)} %get-tuple-element.107), channel_id=1, source_target_pairs={{0,4},{1,5},{2,6},{3,7},{4,0},{5,1},{6,2},{7,3},{8,12},{9,13},{10,... | collective-permute-start | bytes 2359304 | tf_op jit(solution)/shard_map/ppermute | solution.py:49
  212.9 22.2 %collective-permute-start.12 = (bf16[384,2048]{1,0:T(8,128)(2,1)S(1)}, bf16[384,2048]{1,0:T(8,128)(2,1)}, u32[]{:S(2)}, u32[]{:S(2)}) collective-permute-start(bf16[384,2048]{1,0:T(8,128)(2,1)S(1)} %copy-done.5), channel_id=1, source_target_pairs={{0,1},{1,0},{2,3},{3,2},{4,5},{5,4},{6,7},{7,6},{8,9},{9,8},{10,11... | collective-permute-start | bytes 4718600 | tf_op jit(solution)/shard_map/ppermute | solution.py:49
  214.3 19.5 %collective-permute-start.19 = (bf16[192,2048]{1,0:T(8,128)(2,1)}, bf16[192,2048]{1,0:T(8,128)(2,1)}, u32[]{:S(2)}, u32[]{:S(2)}) collective-permute-start(bf16[192,2048]{1,0:T(8,128)(2,1)} %get-tuple-element.108), channel_id=1, source_target_pairs={{0,2},{1,3},{2,0},{3,1},{4,6},{5,7},{6,4},{7,5},{8,10},{9,11},{10,... | collective-permute-start | bytes 2359304 | tf_op jit(solution)/shard_map/ppermute | solution.py:49
  214.4 261.6 %reduce-scatter.5.cloned.1.call-start = ((), (), s32[]{:S(2)}) async-start(), calls=%async_computation.12 | async-start | bytes 3932160 | tf_op jit(solution)/shard_map/reduce_scatter | solution.py:72
  239.0 35.5 %collective-permute-start.22 = (bf16[384,2048]{1,0:T(8,128)(2,1)}, bf16[384,2048]{1,0:T(8,128)(2,1)}, u32[]{:S(2)}, u32[]{:S(2)}) collective-permute-start(bf16[384,2048]{1,0:T(8,128)(2,1)} %multiply_convert_fusion.refs_2_.refs_1_), channel_id=1, source_target_pairs={{0,4},{1,5},{2,6},{3,7},{4,0},{5,1},{6,2},{7,3},{8,12},{9,13},{10,... | collective-permute-start | bytes 4718600 | tf_op jit(solution)/shard_map/ppermute | solution.py:49
  240.1 35.5 %collective-permute-start.21 = (bf16[384,2048]{1,0:T(8,128)(2,1)}, bf16[384,2048]{1,0:T(8,128)(2,1)}, u32[]{:S(2)}, u32[]{:S(2)}) collective-permute-start(bf16[384,2048]{1,0:T(8,128)(2,1)} %multiply_convert_fusion.refs_2_.refs_1_), channel_id=1, source_target_pairs={{0,2},{1,3},{2,0},{3,1},{4,6},{5,7},{6,4},{7,5},{8,10},{9,11},{10,... | collective-permute-start | bytes 4718600 | tf_op jit(solution)/shard_map/ppermute | solution.py:49
  242.2 49.9 %collective-permute-start.30 = (bf16[192,2048]{1,0:T(8,128)(2,1)}, bf16[192,2048]{1,0:T(8,128)(2,1)}, u32[]{:S(2)}, u32[]{:S(2)}) collective-permute-start(bf16[192,2048]{1,0:T(8,128)(2,1)} %slice.288), channel_id=1, source_target_pairs={{0,2},{1,3},{2,0},{3,1},{4,6},{5,7},{6,4},{7,5},{8,10},{9,11},{10,... | collective-permute-start | bytes 2359304 | tf_op jit(solution)/shard_map/ppermute | solution.py:49
  243.7 69.4 %collective-permute-start.28 = (bf16[384,2048]{1,0:T(8,128)(2,1)}, bf16[384,2048]{1,0:T(8,128)(2,1)}, u32[]{:S(2)}, u32[]{:S(2)}) collective-permute-start(bf16[384,2048]{1,0:T(8,128)(2,1)} %get-tuple-element.111.refs_11_), channel_id=1, source_target_pairs={{0,1},{1,0},{2,3},{3,2},{4,5},{5,4},{6,7},{7,6},{8,9},{9,8},{10,11... | collective-permute-start | bytes 4718600 | tf_op jit(solution)/shard_map/ppermute | solution.py:49
  245.3 68.0 %collective-permute-start.29 = (bf16[384,2048]{1,0:T(8,128)(2,1)}, bf16[384,2048]{1,0:T(8,128)(2,1)}, u32[]{:S(2)}, u32[]{:S(2)}) collective-permute-start(bf16[384,2048]{1,0:T(8,128)(2,1)} %get-tuple-element.112.refs_13_), channel_id=1, source_target_pairs={{0,1},{1,0},{2,3},{3,2},{4,5},{5,4},{6,7},{7,6},{8,9},{9,8},{10,11... | collective-permute-start | bytes 4718600 | tf_op jit(solution)/shard_map/ppermute | solution.py:49
  274.4 20.1 %collective-permute-start.31 = (bf16[192,2048]{1,0:T(8,128)(2,1)}, bf16[192,2048]{1,0:T(8,128)(2,1)}, u32[]{:S(2)}, u32[]{:S(2)}) collective-permute-start(bf16[192,2048]{1,0:T(8,128)(2,1)} %slice.289), channel_id=1, source_target_pairs={{0,4},{1,5},{2,6},{3,7},{4,0},{5,1},{6,2},{7,3},{8,12},{9,13},{10,... | collective-permute-start | bytes 2359304 | tf_op jit(solution)/shard_map/ppermute | solution.py:49
  276.8 32.1 %collective-permute-start.25 = (bf16[192,2048]{1,0:T(8,128)(2,1)S(1)}, bf16[192,2048]{1,0:T(8,128)(2,1)S(1)}, u32[]{:S(2)}, u32[]{:S(2)}) collective-permute-start(bf16[192,2048]{1,0:T(8,128)(2,1)S(1)} %slice.286), channel_id=1, source_target_pairs={{0,2},{1,3},{2,0},{3,1},{4,6},{5,7},{6,4},{7,5},{8,10},{9,11},{10,... | collective-permute-start | bytes 2359304 | tf_op jit(solution)/shard_map/ppermute | solution.py:49
  292.1 19.7 %collective-permute-start.26 = (bf16[192,2048]{1,0:T(8,128)(2,1)S(1)}, bf16[192,2048]{1,0:T(8,128)(2,1)S(1)}, u32[]{:S(2)}, u32[]{:S(2)}) collective-permute-start(bf16[192,2048]{1,0:T(8,128)(2,1)S(1)} %slice.287), channel_id=1, source_target_pairs={{0,4},{1,5},{2,6},{3,7},{4,0},{5,1},{6,2},{7,3},{8,12},{9,13},{10,... | collective-permute-start | bytes 2359304 | tf_op jit(solution)/shard_map/ppermute | solution.py:49
  294.5 19.0 %collective-permute-start.20 = (bf16[384,2048]{1,0:T(8,128)(2,1)}, bf16[384,2048]{1,0:T(8,128)(2,1)}, u32[]{:S(2)}, u32[]{:S(2)}) collective-permute-start(bf16[384,2048]{1,0:T(8,128)(2,1)} %multiply_convert_fusion.refs_2_.refs_1_), channel_id=1, source_target_pairs={{0,1},{1,0},{2,3},{3,2},{4,5},{5,4},{6,7},{7,6},{8,9},{9,8},{10,11... | collective-permute-start | bytes 4718600 | tf_op jit(solution)/shard_map/ppermute | solution.py:49
  388.7 25.9 %collective-permute-start.34 = (bf16[384,2048]{1,0:T(8,128)(2,1)}, bf16[384,2048]{1,0:T(8,128)(2,1)}, u32[]{:S(2)}, u32[]{:S(2)}) collective-permute-start(bf16[384,2048]{1,0:T(8,128)(2,1)} %get-tuple-element.116), channel_id=1, source_target_pairs={{0,1},{1,0},{2,3},{3,2},{4,5},{5,4},{6,7},{7,6},{8,9},{9,8},{10,11... | collective-permute-start | bytes 4718600 | tf_op jit(solution)/shard_map/ppermute | solution.py:49
  389.1 29.0 %collective-permute-start.35 = (bf16[384,2048]{1,0:T(8,128)(2,1)}, bf16[384,2048]{1,0:T(8,128)(2,1)}, u32[]{:S(2)}, u32[]{:S(2)}) collective-permute-start(bf16[384,2048]{1,0:T(8,128)(2,1)} %get-tuple-element.118), channel_id=1, source_target_pairs={{0,1},{1,0},{2,3},{3,2},{4,5},{5,4},{6,7},{7,6},{8,9},{9,8},{10,11... | collective-permute-start | bytes 4718600 | tf_op jit(solution)/shard_map/ppermute | solution.py:49
  389.3 31.0 %collective-permute-start.36 = (bf16[384,2048]{1,0:T(8,128)(2,1)}, bf16[384,2048]{1,0:T(8,128)(2,1)}, u32[]{:S(2)}, u32[]{:S(2)}) collective-permute-start(bf16[384,2048]{1,0:T(8,128)(2,1)} %get-tuple-element.120), channel_id=1, source_target_pairs={{0,1},{1,0},{2,3},{3,2},{4,5},{5,4},{6,7},{7,6},{8,9},{9,8},{10,11... | collective-permute-start | bytes 4718600 | tf_op jit(solution)/shard_map/ppermute | solution.py:49
  389.6 19.3 %collective-permute-start.38 = (bf16[384,2048]{1,0:T(8,128)(2,1)}, bf16[384,2048]{1,0:T(8,128)(2,1)}, u32[]{:S(2)}, u32[]{:S(2)}) collective-permute-start(bf16[384,2048]{1,0:T(8,128)(2,1)} %get-tuple-element.124), channel_id=1, source_target_pairs={{0,1},{1,0},{2,3},{3,2},{4,5},{5,4},{6,7},{7,6},{8,9},{9,8},{10,11... | collective-permute-start | bytes 4718600 | tf_op jit(solution)/shard_map/ppermute | solution.py:49
  389.8 16.2 %collective-permute-start.39 = (bf16[384,2048]{1,0:T(8,128)(2,1)}, bf16[384,2048]{1,0:T(8,128)(2,1)}, u32[]{:S(2)}, u32[]{:S(2)}) collective-permute-start(bf16[384,2048]{1,0:T(8,128)(2,1)} %get-tuple-element.126), channel_id=1, source_target_pairs={{0,1},{1,0},{2,3},{3,2},{4,5},{5,4},{6,7},{7,6},{8,9},{9,8},{10,11... | collective-permute-start | bytes 4718600 | tf_op jit(solution)/shard_map/ppermute | solution.py:49
  405.7 147.4 %reduce-scatter.7.cloned.1.call-start = ((), (), s32[]{:S(2)}) async-start(), calls=%async_computation.13 | async-start | bytes 3932160 | tf_op jit(solution)/shard_map/reduce_scatter | solution.py:72
  408.8 67.6 %collective-permute-start.37 = (bf16[384,2048]{1,0:T(8,128)(2,1)}, bf16[384,2048]{1,0:T(8,128)(2,1)}, u32[]{:S(2)}, u32[]{:S(2)}) collective-permute-start(bf16[384,2048]{1,0:T(8,128)(2,1)} %get-tuple-element.122), channel_id=1, source_target_pairs={{0,1},{1,0},{2,3},{3,2},{4,5},{5,4},{6,7},{7,6},{8,9},{9,8},{10,11... | collective-permute-start | bytes 4718600 | tf_op jit(solution)/shard_map/ppermute | solution.py:49
  412.5 35.8 %collective-permute-start.40 = (bf16[384,2048]{1,0:T(8,128)(2,1)S(1)}, bf16[384,2048]{1,0:T(8,128)(2,1)S(1)}, u32[]{:S(2)}, u32[]{:S(2)}) collective-permute-start(bf16[384,2048]{1,0:T(8,128)(2,1)S(1)} %pad_maximum_fusion.5), channel_id=1, source_target_pairs={{0,2},{1,3},{2,0},{3,1},{4,6},{5,7},{6,4},{7,5},{8,10},{9,11},{10,... | collective-permute-start | bytes 4718600 | tf_op jit(solution)/shard_map/ppermute | solution.py:49
  414.6 35.9 %collective-permute-start.43 = (bf16[384,2048]{1,0:T(8,128)(2,1)S(1)}, bf16[384,2048]{1,0:T(8,128)(2,1)S(1)}, u32[]{:S(2)}, u32[]{:S(2)}) collective-permute-start(bf16[384,2048]{1,0:T(8,128)(2,1)S(1)} %pad_maximum_fusion.6), channel_id=1, source_target_pairs={{0,4},{1,5},{2,6},{3,7},{4,0},{5,1},{6,2},{7,3},{8,12},{9,13},{10,... | collective-permute-start | bytes 4718600 | tf_op jit(solution)/shard_map/ppermute | solution.py:49
  449.7 21.2 %collective-permute-start.42 = (bf16[192,2048]{1,0:T(8,128)(2,1)}, bf16[192,2048]{1,0:T(8,128)(2,1)}, u32[]{:S(2)}, u32[]{:S(2)}) collective-permute-start(bf16[192,2048]{1,0:T(8,128)(2,1)} %add_convert_fusion.21), channel_id=1, source_target_pairs={{0,4},{1,5},{2,6},{3,7},{4,0},{5,1},{6,2},{7,3},{8,12},{9,13},{10,... | collective-permute-start | bytes 2359304 | tf_op jit(solution)/shard_map/ppermute | solution.py:49
  452.9 20.6 %collective-permute-start.44 = (bf16[192,2048]{1,0:T(8,128)(2,1)}, bf16[192,2048]{1,0:T(8,128)(2,1)}, u32[]{:S(2)}, u32[]{:S(2)}) collective-permute-start(bf16[192,2048]{1,0:T(8,128)(2,1)} %add_convert_fusion.20), channel_id=1, source_target_pairs={{0,2},{1,3},{2,0},{3,1},{4,6},{5,7},{6,4},{7,5},{8,10},{9,11},{10,... | collective-permute-start | bytes 2359304 | tf_op jit(solution)/shard_map/ppermute | solution.py:49
  476.0 148.7 %reduce-scatter.9.cloned.1.call-start = ((), (), s32[]{:S(2)}) async-start(), calls=%async_computation.14 | async-start | bytes 3932160 | tf_op jit(solution)/shard_map/reduce_scatter | solution.py:72
  487.3 35.1 %collective-permute-start.47 = (bf16[384,2048]{1,0:T(8,128)(2,1)}, bf16[384,2048]{1,0:T(8,128)(2,1)}, u32[]{:S(2)}, u32[]{:S(2)}) collective-permute-start(bf16[384,2048]{1,0:T(8,128)(2,1)} %get-tuple-element.172.refs_0_.refs_1_), channel_id=1, source_target_pairs={{0,4},{1,5},{2,6},{3,7},{4,0},{5,1},{6,2},{7,3},{8,12},{9,13},{10,... | collective-permute-start | bytes 4718600 | tf_op jit(solution)/shard_map/ppermute | solution.py:49
  488.1 34.7 %collective-permute-start.46 = (bf16[384,2048]{1,0:T(8,128)(2,1)}, bf16[384,2048]{1,0:T(8,128)(2,1)}, u32[]{:S(2)}, u32[]{:S(2)}) collective-permute-start(bf16[384,2048]{1,0:T(8,128)(2,1)} %get-tuple-element.172.refs_0_.refs_1_), channel_id=1, source_target_pairs={{0,2},{1,3},{2,0},{3,1},{4,6},{5,7},{6,4},{7,5},{8,10},{9,11},{10,... | collective-permute-start | bytes 4718600 | tf_op jit(solution)/shard_map/ppermute | solution.py:49
  524.0 16.9 %collective-permute-start.50 = (bf16[192,2048]{1,0:T(8,128)(2,1)S(1)}, bf16[192,2048]{1,0:T(8,128)(2,1)S(1)}, u32[]{:S(2)}, u32[]{:S(2)}) collective-permute-start(bf16[192,2048]{1,0:T(8,128)(2,1)S(1)} %slice.306), channel_id=1, source_target_pairs={{0,2},{1,3},{2,0},{3,1},{4,6},{5,7},{6,4},{7,5},{8,10},{9,11},{10,... | collective-permute-start | bytes 2359304 | tf_op jit(solution)/shard_map/ppermute | solution.py:49
  526.9 16.6 %collective-permute-start.51 = (bf16[192,2048]{1,0:T(8,128)(2,1)S(1)}, bf16[192,2048]{1,0:T(8,128)(2,1)S(1)}, u32[]{:S(2)}, u32[]{:S(2)}) collective-permute-start(bf16[192,2048]{1,0:T(8,128)(2,1)S(1)} %slice.307), channel_id=1, source_target_pairs={{0,4},{1,5},{2,6},{3,7},{4,0},{5,1},{6,2},{7,3},{8,12},{9,13},{10,... | collective-permute-start | bytes 2359304 | tf_op jit(solution)/shard_map/ppermute | solution.py:49
  527.6 20.9 %collective-permute-start.45 = (bf16[384,2048]{1,0:T(8,128)(2,1)}, bf16[384,2048]{1,0:T(8,128)(2,1)}, u32[]{:S(2)}, u32[]{:S(2)}) collective-permute-start(bf16[384,2048]{1,0:T(8,128)(2,1)} %get-tuple-element.172.refs_0_.refs_1_), channel_id=1, source_target_pairs={{0,1},{1,0},{2,3},{3,2},{4,5},{5,4},{6,7},{7,6},{8,9},{9,8},{10,11... | collective-permute-start | bytes 4718600 | tf_op jit(solution)/shard_map/ppermute | solution.py:49
  530.4 18.1 %collective-permute-start.48 = (bf16[384,2048]{1,0:T(8,128)(2,1)}, bf16[384,2048]{1,0:T(8,128)(2,1)}, u32[]{:S(2)}, u32[]{:S(2)}) collective-permute-start(bf16[384,2048]{1,0:T(8,128)(2,1)} %get-tuple-element.131.refs_2_.refs_3_), channel_id=1, source_target_pairs={{0,1},{1,0},{2,3},{3,2},{4,5},{5,4},{6,7},{7,6},{8,9},{9,8},{10,11... | collective-permute-start | bytes 4718600 | tf_op jit(solution)/shard_map/ppermute | solution.py:49
  530.4 18.1 %collective-permute-start.49 = (bf16[384,2048]{1,0:T(8,128)(2,1)}, bf16[384,2048]{1,0:T(8,128)(2,1)}, u32[]{:S(2)}, u32[]{:S(2)}) collective-permute-start(bf16[384,2048]{1,0:T(8,128)(2,1)} %get-tuple-element.132.refs_4_.refs_5_), channel_id=1, source_target_pairs={{0,1},{1,0},{2,3},{3,2},{4,5},{5,4},{6,7},{7,6},{8,9},{9,8},{10,11... | collective-permute-start | bytes 4718600 | tf_op jit(solution)/shard_map/ppermute | solution.py:49
  551.9 54.3 %collective-permute-start.53 = (bf16[384,2048]{1,0:T(8,128)(2,1)}, bf16[384,2048]{1,0:T(8,128)(2,1)}, u32[]{:S(2)}, u32[]{:S(2)}) collective-permute-start(bf16[384,2048]{1,0:T(8,128)(2,1)} %get-tuple-element.133.refs_0_), channel_id=1, source_target_pairs={{0,2},{1,3},{2,0},{3,1},{4,6},{5,7},{6,4},{7,5},{8,10},{9,11},{10,... | collective-permute-start | bytes 4718600 | tf_op jit(solution)/shard_map/ppermute | solution.py:49
  551.9 54.3 %collective-permute-start.54 = (bf16[384,2048]{1,0:T(8,128)(2,1)}, bf16[384,2048]{1,0:T(8,128)(2,1)}, u32[]{:S(2)}, u32[]{:S(2)}) collective-permute-start(bf16[384,2048]{1,0:T(8,128)(2,1)} %get-tuple-element.134.refs_1_), channel_id=1, source_target_pairs={{0,4},{1,5},{2,6},{3,7},{4,0},{5,1},{6,2},{7,3},{8,12},{9,13},{10,... | collective-permute-start | bytes 4718600 | tf_op jit(solution)/shard_map/ppermute | solution.py:49
  553.2 162.5 %reduce-scatter.11.cloned.1.call-start = ((), (), s32[]{:S(2)}) async-start(), calls=%async_computation.15 | async-start | bytes 4014080 | tf_op jit(solution)/shard_map/reduce_scatter | solution.py:72
  619.7 36.3 %collective-permute-start.59 = (bf16[384,2048]{1,0:T(8,128)(2,1)}, bf16[384,2048]{1,0:T(8,128)(2,1)}, u32[]{:S(2)}, u32[]{:S(2)}) collective-permute-start(bf16[384,2048]{1,0:T(8,128)(2,1)} %pad_maximum_fusion.8.refs_1_), channel_id=1, source_target_pairs={{0,2},{1,3},{2,0},{3,1},{4,6},{5,7},{6,4},{7,5},{8,10},{9,11},{10,... | collective-permute-start | bytes 4718600 | tf_op jit(solution)/shard_map/ppermute | solution.py:49
  623.3 35.9 %collective-permute-start.58 = (bf16[384,2048]{1,0:T(8,128)(2,1)}, bf16[384,2048]{1,0:T(8,128)(2,1)}, u32[]{:S(2)}, u32[]{:S(2)}) collective-permute-start(bf16[384,2048]{1,0:T(8,128)(2,1)} %pad_maximum_fusion.7.refs_2_), channel_id=1, source_target_pairs={{0,4},{1,5},{2,6},{3,7},{4,0},{5,1},{6,2},{7,3},{8,12},{9,13},{10,... | collective-permute-start | bytes 4718600 | tf_op jit(solution)/shard_map/ppermute | solution.py:49
  662.2 18.2 %collective-permute-start.60 = (bf16[192,2048]{1,0:T(8,128)(2,1)}, bf16[192,2048]{1,0:T(8,128)(2,1)}, u32[]{:S(2)}, u32[]{:S(2)}) collective-permute-start(bf16[192,2048]{1,0:T(8,128)(2,1)} %get-tuple-element.161), channel_id=1, source_target_pairs={{0,4},{1,5},{2,6},{3,7},{4,0},{5,1},{6,2},{7,3},{8,12},{9,13},{10,... | collective-permute-start | bytes 2359304 | tf_op jit(solution)/shard_map/ppermute | solution.py:49
  662.9 62.7 %collective-permute-start.33 = (bf16[384,2048]{1,0:T(8,128)(2,1)}, bf16[384,2048]{1,0:T(8,128)(2,1)}, u32[]{:S(2)}, u32[]{:S(2)}) collective-permute-start(bf16[384,2048]{1,0:T(8,128)(2,1)} %get-tuple-element.114), channel_id=1, source_target_pairs={{0,1},{1,0},{2,3},{3,2},{4,5},{5,4},{6,7},{7,6},{8,9},{9,8},{10,11... | collective-permute-start | bytes 4718600 | tf_op jit(solution)/shard_map/ppermute | solution.py:49
  666.9 41.7 %collective-permute-start.62 = (bf16[384,2048]{1,0:T(8,128)(2,1)}, bf16[384,2048]{1,0:T(8,128)(2,1)}, u32[]{:S(2)}, u32[]{:S(2)}) collective-permute-start(bf16[384,2048]{1,0:T(8,128)(2,1)} %get-tuple-element.164), channel_id=1, source_target_pairs={{0,1},{1,0},{2,3},{3,2},{4,5},{5,4},{6,7},{7,6},{8,9},{9,8},{10,11... | collective-permute-start | bytes 4718600 | tf_op jit(solution)/shard_map/ppermute | solution.py:49
  666.9 38.5 %collective-permute-start.64 = (bf16[192,2048]{1,0:T(8,128)(2,1)}, bf16[192,2048]{1,0:T(8,128)(2,1)}, u32[]{:S(2)}, u32[]{:S(2)}) collective-permute-start(bf16[192,2048]{1,0:T(8,128)(2,1)} %get-tuple-element.159.refs_0_), channel_id=1, source_target_pairs={{0,2},{1,3},{2,0},{3,1},{4,6},{5,7},{6,4},{7,5},{8,10},{9,11},{10,... | collective-permute-start | bytes 2359304 | tf_op jit(solution)/shard_map/ppermute | solution.py:49
  667.6 35.1 %collective-permute-start.61 = (bf16[192,2048]{1,0:T(8,128)(2,1)}, bf16[192,2048]{1,0:T(8,128)(2,1)}, u32[]{:S(2)}, u32[]{:S(2)}) collective-permute-start(bf16[192,2048]{1,0:T(8,128)(2,1)} %get-tuple-element.162), channel_id=1, source_target_pairs={{0,2},{1,3},{2,0},{3,1},{4,6},{5,7},{6,4},{7,5},{8,10},{9,11},{10,... | collective-permute-start | bytes 2359304 | tf_op jit(solution)/shard_map/ppermute | solution.py:49
  671.0 47.4 %all-to-all-start.3 = ((bf16[8,64,1536]{2,1,0:T(8,128)(2,1)}), bf16[8,64,1536]{2,1,0:T(8,128)(2,1)}, u32[]{:S(2)}, u32[]{:S(2)}) async-start(bf16[8,64,1536]{2,1,0:T(8,128)(2,1)} %bitcast.85), calls=%async_computation.7 | async-start | bytes 3145728 | tf_op jit(solution)/shard_map/all_to_all | solution.py:60
  680.3 26.7 %collective-permute-start.63 = (bf16[192,2048]{1,0:T(8,128)(2,1)}, bf16[192,2048]{1,0:T(8,128)(2,1)S(1)}, u32[]{:S(2)}, u32[]{:S(2)}) collective-permute-start(bf16[192,2048]{1,0:T(8,128)(2,1)} %get-tuple-element.160.refs_1_), channel_id=1, source_target_pairs={{0,4},{1,5},{2,6},{3,7},{4,0},{5,1},{6,2},{7,3},{8,12},{9,13},{10,... | collective-permute-start | bytes 2359304 | tf_op jit(solution)/shard_map/ppermute | solution.py:49
  718.3 34.6 %all-to-all-start.2 = ((bf16[8,72,512]{2,1,0:T(8,128)(2,1)}), bf16[8,72,512]{2,1,0:T(8,128)(2,1)}, u32[]{:S(2)}, u32[]{:S(2)}) async-start(bf16[8,72,512]{2,1,0:T(8,128)(2,1)} %fusion.21), calls=%async_computation.6 | async-start | bytes 1179648 | tf_op jit(solution)/shard_map/all_to_all | solution.py:60
  730.8 21.3 %collective-permute-start.65 = (bf16[64,2048]{1,0:T(8,128)(2,1)S(1)}, bf16[64,2048]{1,0:T(8,128)(2,1)S(1)}, u32[]{:S(2)}, u32[]{:S(2)}) collective-permute-start(bf16[64,2048]{1,0:T(8,128)(2,1)S(1)} %bitcast.98), channel_id=1, source_target_pairs={{0,0},{8,1},{16,2},{24,3},{1,4},{9,5},{17,6},{25,7},{2,8},{10,9},{... | collective-permute-start | bytes 786440 | tf_op jit(solution)/shard_map/ppermute | solution.py:887
  (80 other events, 561.1 us)
Sparse Core Ops, SparseCore 0:
  29.6 69.9 all-gather.4
  111.6 63.3 all-gather.6
  176.5 62.1 all-gather.8
  240.1 62.1 all-gather.10
  405.8 56.0 reduce-scatter.4
  476.1 58.8 reduce-scatter.6
  553.3 58.3 reduce-scatter.8
  625.5 57.9 reduce-scatter.10
